TPU v7x, 32 devices: a whole 2x2x4 slice. The times are simulated.
32 devices in a mesh: row: 4 (over y, x), col: 8 (over z, core).
Axes of the slice: x: 2, y: 2, z: 4, core: 2. Of those that a mesh axis runs over, the one named last changes fastest.
Arguments:
- embed: bfloat16 [16384, 128], P(('row', 'col')), may hold values from -6 to 6
- degree: int32 [16384], P(('row', 'col')), may hold values from 1 to 256
- tile_row: int32 [4, 8, 256], P('row', 'col'), may hold values from 0 to 31
- tile_col: int32 [4, 8, 256], P('row', 'col'), may hold values from 0 to 15
- tile_count: int32 [4, 8], P('row', 'col'), may hold values from 64 to 256, as said below
- tile_values: bfloat16 [4, 8, 256, 128, 128], P('row', 'col'), may hold values from 0 to 1
- new_rows: int32 [8192], P(('row', 'col')), may hold values from 0 to 16383, as said below
- new_bucket: int32 [8192], P(('row', 'col')), may hold values from 0 to 15
- bucket_norm: float32 [16], replicated, may hold values from 0.5 to 4
Outputs:
- new_embed: float32 [8192, 128], P(('row', 'col'))
Inputs may be any that keep to these rules, and one draw needn't show every extreme that they name: `tile_count`: at least 64 slots live on each device, and some device has all 256 live. `new_rows`: the new nodes of one device lie in that device's row block.
All inputs are finite; a program needn't handle non-finite values.
Results may differ from a plain program's by a relative error of at most 0.0026.
Values may be sent and summed in bfloat16 or wider, within the bound.
No kernel may reach another device: no remote copies, remote signals or barrier semaphores. Data moves between devices by JAX's collectives and lax.ppermute only.
A program may use at most 128 MiB of HBM per device.

v0:
```python
import jax
import jax.numpy as jnp
from jax import lax
from jax.sharding import PartitionSpec as P

HOPS = 3


def tile_products(gathered, weights, tile_row, tile_col, tile_count, block_rows):
    tile_size = weights.shape[1]
    width = gathered.shape[1]
    col_tiles = gathered.reshape(gathered.shape[0] // tile_size, tile_size, width)
    picked = jnp.take(col_tiles, tile_col, axis=0)
    prod = jnp.einsum("tij,tjk->tik", weights, picked, preferred_element_type=jnp.float32)
    slots = jnp.arange(tile_row.shape[0], dtype=jnp.int32)
    live = slots < tile_count
    prod = jnp.where(live[:, None, None], prod, jnp.float32(0.0))
    row_tiles = block_rows // tile_size
    targets = jnp.clip(tile_row, 0, row_tiles - 1)
    sums = jax.ops.segment_sum(prod, targets, num_segments=row_tiles)
    return sums.reshape(block_rows, width)


def local(
    embed, degree, tile_row, tile_col, tile_count, tile_values, new_rows, new_bucket, bucket_norm
):
    rows_here = embed.shape[0]
    ncols = lax.axis_size("col")
    block_rows = ncols * rows_here
    weights = tile_values[0, 0]
    row_ids = tile_row[0, 0]
    col_ids = tile_col[0, 0]
    live_count = tile_count[0, 0]
    scale = lax.rsqrt(degree.astype(jnp.float32))
    state = (scale[:, None] * embed.astype(jnp.float32)).astype(jnp.bfloat16)

    def spread(current):
        gathered = lax.all_gather(current, "row", axis=0, tiled=True)
        return tile_products(gathered, weights, row_ids, col_ids, live_count, block_rows)

    for hop in range(HOPS - 1):
        summed = lax.psum_scatter(spread(state), "col", scatter_dimension=0, tiled=True)
        state = ((scale * scale)[:, None] * summed).astype(jnp.bfloat16)
    partial_value = spread(state)
    block = lax.psum(partial_value, "col")
    local_ids = new_rows - lax.axis_index("row") * block_rows
    picked = jnp.take(block, local_ids, axis=0)
    buckets = jnp.arange(bucket_norm.shape[0], dtype=jnp.int32)
    target = jnp.sum(
        jnp.where(new_bucket[:, None] == buckets[None, :], bucket_norm[None, :], jnp.float32(0.0)),
        axis=1,
    )
    return (
        target[:, None]
        * picked
        * lax.rsqrt(jnp.sum(picked * picked, axis=1, keepdims=True) + 1e-06)
    )


def solution(mesh):
    in_specs = (
        P(("row", "col"), None),
        P(("row", "col")),
        P("row", "col", None),
        P("row", "col", None),
        P("row", "col"),
        P("row", "col", None, None, None),
        P(("row", "col")),
        P(("row", "col")),
        P(),
    )
    out_specs = P(("row", "col"), None)
    return jax.shard_map(local, mesh=mesh, in_specs=in_specs, out_specs=out_specs, check_vma=False)
```

profile of v0, /device:TPU:0, one launch (start us, length us, event | category | flops | bytes accessed | tf_op | source)
XLA Modules:
  0.0 410.9 jit_solution(16219009823697693874)
XLA Ops:
  6.5 0.0 reduce-scatter.3.cloned.1.call-start
  6.5 0.7 compare_select_fusion
  7.2 0.7 fusion.15
  7.9 1.0 multiply_convert_fusion.2
  9.0 11.5 %all_gather.9 = bf16[2048,128]{1,0:T(8,128)(2,1)S(1)} all-gather(bf16[512,128]{1,0:T(8,128)(2,1)S(1)} %multiply_convert_fusion.2), channel_id=1, replica_groups=mesh['row'=4,'col'=8] {'row'}, dimensions={0}, use_global_device_ids=true | all-gather | bytes 655360 | tf_op jit(solution)/shard_map/all_gather | solution.py:38
  21.1 0.7 compare_and_fusion
  21.8 8.6 %gather_fusion.1 = bf16[256,128,128]{2,1,0:T(8,128)(2,1)} fusion(bf16[16,128,128]{2,1,0:T(8,128)(2,1)S(1)} %bitcast.26, s32[1024]{0:T(1024)S(1)} %pad_clamp_fusion.1), kind=kCustom, calls=%fused_computation.clone | custom fusion | bytes 16778240 | tf_op jit(solution)/shard_map/jit(_take)/gather | solution.py:13
  30.4 13.9 %select_bitcast_fusion.2 = f32[256,128,128]{1,2,0:T(8,128)} fusion(bf16[1,1,256,128,128]{4,3,2,1,0:T(8,128)(2,1)} %param.16, bf16[256,128,128]{2,1,0:T(8,128)(2,1)} %gather_fusion.1, pred[256]{0:T(512)(128)(4,1)S(1)} %get-tuple-element.10, pred[256]{0:T(512)(128)(4,1)S(1)} %get-tuple-element.11), kind=kOutput, calls=%fused_computation.9 | convolution fusion | flops 1082130432 | bytes 33554944 | tf_op jit(solution)/shard_map/tij,tjk->tik/dot_general | solution.py:14
  44.3 0.0 copy-start.4
  44.3 17.5 %copy.20 = f32[256,128,128]{2,1,0:T(8,128)} copy(f32[256,128,128]{1,2,0:T(8,128)} %select_bitcast_fusion.2) | data formatting | bytes 33554432 | tf_op jit(solution)/shard_map/jit(_where)/select_n | solution.py:17
  61.8 0.0 copy-done.4
  61.8 0.2 broadcast.48.clone.1
  62.0 33.2 %scatter_fusion = f32[32,128,128]{2,1,0:T(8,128)S(1)} fusion(f32[32,128,128]{2,1,0:T(8,128)S(1)} %broadcast.48.clone.1, s32[256]{0:T(256)S(1)} %bitcast.29, f32[256,128,128]{2,1,0:T(8,128)} %copy.20), kind=kCustom, calls=%fused_computation.4 | custom fusion | flops 4194304 | bytes 50332672 | tf_op jit(solution)/shard_map/scatter-add | solution.py:20
  95.2 0.0 copy-start.1
  95.2 1.3 copy-done.1
  96.6 0.0 reduce-scatter.3.cloned.1.call-update
  96.6 0.0 reduce-scatter.5.cloned.1.call-start
  96.6 36.2 %reduce-scatter.3.cloned.1.call-done = f32[512,128]{1,0:T(8,128)} async-done(((f32[4096,128]{1,0:T(8,128)}), f32[512,128]{1,0:T(8,128)}) %reduce-scatter.3.cloned.1.call-update) | async-done | bytes 262160 | tf_op jit(solution)/shard_map/reduce_scatter | solution.py:42
  132.8 1.1 multiply_convert_fusion.1
  133.9 10.6 %all_gather.10 = bf16[2048,128]{1,0:T(8,128)(2,1)S(1)} all-gather(bf16[512,128]{1,0:T(8,128)(2,1)S(1)} %multiply_convert_fusion.1), channel_id=1, replica_groups=mesh['row'=4,'col'=8] {'row'}, dimensions={0}, use_global_device_ids=true | all-gather | bytes 655360 | tf_op jit(solution)/shard_map/all_gather | solution.py:38
  144.5 8.6 %gather_fusion.2 = bf16[256,128,128]{2,1,0:T(8,128)(2,1)} fusion(bf16[16,128,128]{2,1,0:T(8,128)(2,1)S(1)} %bitcast.28, s32[1024]{0:T(1024)S(1)} %pad_clamp_fusion.1), kind=kCustom, calls=%fused_computation.1.clone | custom fusion | bytes 16778240 | tf_op jit(solution)/shard_map/jit(_take)/gather | solution.py:13
  153.1 13.9 %select_bitcast_fusion.1 = f32[256,128,128]{1,2,0:T(8,128)} fusion(bf16[1,1,256,128,128]{4,3,2,1,0:T(8,128)(2,1)} %param.16, bf16[256,128,128]{2,1,0:T(8,128)(2,1)} %gather_fusion.2, pred[256]{0:T(512)(128)(4,1)S(1)} %get-tuple-element.10, pred[256]{0:T(512)(128)(4,1)S(1)} %get-tuple-element.11), kind=kOutput, calls=%fused_computation.8 | convolution fusion | flops 1082130432 | bytes 33554944 | tf_op jit(solution)/shard_map/tij,tjk->tik/dot_general | solution.py:14
  167.0 17.5 %copy.22 = f32[256,128,128]{2,1,0:T(8,128)} copy(f32[256,128,128]{1,2,0:T(8,128)} %select_bitcast_fusion.1) | data formatting | bytes 33554432 | tf_op jit(solution)/shard_map/jit(_where)/select_n | solution.py:17
  184.4 0.2 broadcast.48.clone
  184.7 33.2 %scatter_fusion.1 = f32[32,128,128]{2,1,0:T(8,128)S(1)} fusion(f32[32,128,128]{2,1,0:T(8,128)S(1)} %broadcast.48.clone, s32[256]{0:T(256)S(1)} %bitcast.30, f32[256,128,128]{2,1,0:T(8,128)} %copy.22), kind=kCustom, calls=%fused_computation.5 | custom fusion | flops 4194304 | bytes 50332672 | tf_op jit(solution)/shard_map/scatter-add | solution.py:20
  217.9 0.0 copy-start.2
  217.9 1.3 copy-done.2
  219.2 0.0 reduce-scatter.5.cloned.1.call-update
  219.3 0.0 all-reduce.2.cloned.1.call-start
  219.3 33.1 %reduce-scatter.5.cloned.1.call-done = f32[512,128]{1,0:T(8,128)} async-done(((f32[4096,128]{1,0:T(8,128)}), f32[512,128]{1,0:T(8,128)}) %reduce-scatter.5.cloned.1.call-update) | async-done | bytes 262160 | tf_op jit(solution)/shard_map/reduce_scatter | solution.py:42
  252.4 1.1 multiply_convert_fusion
  253.5 10.4 %all_gather.11 = bf16[2048,128]{1,0:T(8,128)(2,1)S(1)} all-gather(bf16[512,128]{1,0:T(8,128)(2,1)S(1)} %multiply_convert_fusion), channel_id=1, replica_groups=mesh['row'=4,'col'=8] {'row'}, dimensions={0}, use_global_device_ids=true | all-gather | bytes 655360 | tf_op jit(solution)/shard_map/all_gather | solution.py:38
  263.9 8.6 %gather_fusion.3 = bf16[256,128,128]{2,1,0:T(8,128)(2,1)} fusion(bf16[16,128,128]{2,1,0:T(8,128)(2,1)S(1)} %bitcast.27, s32[1024]{0:T(1024)S(1)} %pad_clamp_fusion.1), kind=kCustom, calls=%fused_computation.2.clone | custom fusion | bytes 16778240 | tf_op jit(solution)/shard_map/jit(_take)/gather | solution.py:13
  272.5 13.9 %select_bitcast_fusion = f32[256,128,128]{1,2,0:T(8,128)} fusion(bf16[1,1,256,128,128]{4,3,2,1,0:T(8,128)(2,1)} %param.16, bf16[256,128,128]{2,1,0:T(8,128)(2,1)} %gather_fusion.3, pred[256]{0:T(512)(128)(4,1)S(1)} %get-tuple-element.10, pred[256]{0:T(512)(128)(4,1)S(1)} %get-tuple-element.11), kind=kOutput, calls=%fused_computation.7 | convolution fusion | flops 1082130432 | bytes 33554944 | tf_op jit(solution)/shard_map/tij,tjk->tik/dot_general | solution.py:14
  286.4 17.5 %copy.24 = f32[256,128,128]{2,1,0:T(8,128)} copy(f32[256,128,128]{1,2,0:T(8,128)} %select_bitcast_fusion) | data formatting | bytes 33554432 | tf_op jit(solution)/shard_map/jit(_where)/select_n | solution.py:17
  303.8 0.2 broadcast.48
  304.1 0.0 copy-start.3
  304.1 0.0 copy-start.5
  304.1 0.0 copy-start.6
  304.1 33.2 %scatter_fusion.2 = f32[32,128,128]{2,1,0:T(8,128)S(1)} fusion(f32[32,128,128]{2,1,0:T(8,128)S(1)} %broadcast.48, s32[256]{0:T(256)S(1)} %bitcast.31, f32[256,128,128]{2,1,0:T(8,128)} %copy.24), kind=kCustom, calls=%fused_computation.6 | custom fusion | flops 4194304 | bytes 50332672 | tf_op jit(solution)/shard_map/scatter-add | solution.py:20
  337.3 0.0 copy-start
  337.3 1.3 copy-done
  338.6 0.0 all-reduce.2.cloned.1.call-update
  338.6 0.0 copy-done.3
  338.7 0.0 copy-done.5
  338.7 0.0 copy-done.6
  338.7 0.1 select_reduce_fusion
  338.8 62.3 %all-reduce.2.cloned.1.call-done = f32[4096,128]{1,0:T(8,128)} async-done(((f32[4096,128]{1,0:T(8,128)}), f32[4096,128]{1,0:T(8,128)}) %all-reduce.2.cloned.1.call-update) | async-done | bytes 2097168 | tf_op jit(solution)/shard_map/psum | solution.py:45
  401.0 2.3 gather_fusion
  403.4 0.2 multiply_reduce_fusion
  403.5 0.8 multiply_multiply_fusion
  (5 shorter events, 0.0 us)
Async XLA Ops:
  6.5 126.3 %reduce-scatter.3.cloned.1.call-start = ((), (), s32[]{:S(2)}) async-start(), calls=%async_computation.2 | async-start | bytes 2359296 | tf_op jit(solution)/shard_map/reduce_scatter | solution.py:42
  44.3 17.5 %copy-start.4 = (s32[1,1,256]{2,1,0:T(1,128)S(1)}, s32[1,1,256]{2,1,0:T(1,128)}, u32[]{:S(2)}) copy-start(s32[1,1,256]{2,1,0:T(1,128)} %param.13) | copy-start | bytes 3076
  95.2 1.4 copy-start.1
  96.6 155.8 %reduce-scatter.5.cloned.1.call-start = ((), (), s32[]{:S(2)}) async-start(), calls=%async_computation.3 | async-start | bytes 2359296 | tf_op jit(solution)/shard_map/reduce_scatter | solution.py:42
  217.9 1.4 copy-start.2
  219.3 181.8 %all-reduce.2.cloned.1.call-start = ((), (), s32[]{:S(2)}) async-start(), calls=%async_computation.4 | async-start | bytes 4194304 | tf_op jit(solution)/shard_map/psum | solution.py:45
  304.1 34.6 %copy-start.3 = (s32[256]{0:T(256)S(1)}, s32[256]{0:T(256)}, u32[]{:S(2)}) copy-start(s32[256]{0:T(256)} %param.17) | copy-start | bytes 3076
  304.1 34.6 %copy-start.5 = (s32[256]{0:T(256)S(1)}, s32[256]{0:T(256)}, u32[]{:S(2)}) copy-start(s32[256]{0:T(256)} %param.18) | copy-start | bytes 3076
  304.1 34.6 %copy-start.6 = (f32[16]{0:T(128)S(1)}, f32[16]{0:T(128)}, u32[]{:S(2)}) copy-start(f32[16]{0:T(128)} %param.19) | copy-start | bytes 196
  337.3 1.3 copy-start
Sparse Core Ops, SparseCore 0:
  96.7 36.0 reduce-scatter.2
  219.4 32.9 reduce-scatter.4
  338.8 62.2 all-reduce.1
where the time goes:
time: 414 us; the launch traced here: 411 us
  waiting for transfers between devices  132 us (32%)
  other arithmetic  106 us (26%)
  local copies, waits for them, and re-layouts  85.1 us (21%)
  matrix products  41.7 us (10%)
  blocking collectives  32.5 us (8%)
  between operations  13.9 us (3%)
    scatter-add x3, other arithmetic, tile_products(): sums = jax.ops.segment_sum(prod, targets, num_segments=row_tiles)  99.6 us
    reduce_scatter x2, waiting for transfers between devices, local(): lax.psum_scatter(spread(state), 'col', scatter_dimension=0, tiled=True)  69.3 us
    psum x1, waiting for transfers between devices, local(): block = lax.psum(partial_value, 'col')  62.3 us
    select_n x3, local copies, waits for them, and re-layouts, tile_products(): prod = jnp.where(live[:, None, None], prod, jnp.float32(0.0))  52.4 us
    dot_general x3, matrix products, tile_products(): jnp.einsum('tij,tjk->tik', weights, picked, preferred_element_type=jnp.fl...  41.7 us
    all_gather x3, blocking collectives, spread(): gathered = lax.all_gather(current, 'row', axis=0, tiled=True)  32.5 us
    gather x3, local copies, waits for them, and re-layouts, tile_products(): picked = jnp.take(col_tiles, tile_col, axis=0)  25.8 us
  transfers between devices with their start and end apart: 3, of which 3 were waited for; matrix products, arithmetic and copies ran while one was open for 0% of the time, Pallas kernels for 0%

commit v1 on v0

v1 whole, which is shorter than its diff:
```python
import functools

import jax
import jax.numpy as jnp
from jax import lax
from jax.experimental import pallas as pl
from jax.experimental.pallas import tpu as pltpu
from jax.sharding import PartitionSpec as P

HOPS = 3
GROUP = 4
SHIFT = 256
MIB = 1024 * 1024


def iota(shape, dim):
    return lax.broadcasted_iota(jnp.int32, shape, dim)


def to_column(row):
    n = row.shape[1]
    return jnp.sum(jnp.where(iota((n, n), 0) == iota((n, n), 1), row, 0.0), axis=1, keepdims=True)


def to_row(column):
    n = column.shape[0]
    return jnp.sum(jnp.where(iota((n, n), 0) == iota((n, n), 1), column, 0.0), axis=0, keepdims=True)


def plan_kernel(row_tiles, per_group, zero_tile, info_ref, tile_row_ref, tile_col_ref, plan_ref):
    slots = tile_row_ref.shape[1]
    length = plan_ref.shape[1]
    count, my_row, my_col = info_ref[0], info_ref[1], info_ref[2]
    half = row_tiles // 2
    row = tile_row_ref[...]
    rel = (row // per_group) ^ my_col
    order = (1 - rel % 2) * half + (rel // 2) * per_group + row % per_group
    order = jnp.where(iota((1, slots), 1) < count, order, row_tiles).astype(jnp.float32)
    col = tile_col_ref[...]
    source = ((col // per_group) ^ my_row) * per_group + col % per_group
    entry = (iota((1, slots), 1) * SHIFT + source).astype(jnp.float32)
    order_c = to_column(order)
    entry_c = to_column(entry)
    same = jnp.where((order_c == order) & (iota((slots, slots), 1) < iota((slots, slots), 0)), 1.0, 0.0)
    within = jnp.sum(same, axis=1, keepdims=True)
    tiles_r = iota((row_tiles, slots), 0).astype(jnp.float32)
    held = jnp.sum(jnp.where(tiles_r == order, 1.0, 0.0), axis=1, keepdims=True).astype(jnp.int32)
    steps = jnp.maximum((held + GROUP - 1) // GROUP, 1).astype(jnp.float32)
    square = (row_tiles, row_tiles)
    first_c = jnp.sum(jnp.where(iota(square, 1) < iota(square, 0), to_row(steps), 0.0), axis=1, keepdims=True)
    first_r = to_row(first_c)
    lanes = iota((slots, row_tiles), 1).astype(jnp.float32)
    start = jnp.sum(jnp.where(order_c == lanes, first_r, 0.0), axis=1, keepdims=True)
    place = jnp.where(order_c < row_tiles, GROUP * start + within, -1.0)
    hit = place == iota((slots, length), 1).astype(jnp.float32)
    listed = jnp.sum(jnp.where(hit, entry_c - zero_tile, 0.0), axis=0, keepdims=True) + zero_tile
    ends = first_c + steps
    step_no = iota((row_tiles, length), 1).astype(jnp.float32)
    owner = jnp.sum(jnp.where(ends <= step_no, 1.0, 0.0), axis=0, keepdims=True)
    odd_steps = jnp.sum(jnp.where(iota((row_tiles, 1), 0) == half, first_c, 0.0))
    all_steps = jnp.sum(steps)
    lane = iota((1, length), 1)
    sizes = jnp.where(lane == 0, odd_steps, jnp.where(lane == 1, all_steps, 0.0))
    plan_ref[0:1, :] = listed.astype(jnp.int32)
    plan_ref[1:2, :] = owner.astype(jnp.int32)
    plan_ref[2:3, :] = sizes.astype(jnp.int32)
    plan_ref[3:8, :] = jnp.zeros((5, length), jnp.int32)


def fill_state(pieces, state):
    at = 0
    for piece in pieces:
        state[at : at + piece.shape[0], :] = piece[...]
        at += piece.shape[0]
    state[at:, :] = jnp.zeros((state.shape[0] - at, state.shape[1]), state.dtype)


def multiply(plan_ref, weights_ref, state, total, first, last, base):
    tile = weights_ref.shape[1]

    def step(s, carry):
        left, right = [], []
        for j in range(GROUP):
            entry = plan_ref[0, s * GROUP + j]
            left.append(weights_ref[entry // SHIFT])
            right.append(state[pl.ds(pl.multiple_of((entry % SHIFT) * tile, tile), tile), :])
        prod = jnp.dot(
            jnp.concatenate(left, axis=1),
            jnp.concatenate(right, axis=0),
            preferred_element_type=jnp.float32,
        )
        at = pl.ds(pl.multiple_of((plan_ref[1, s] - base) * tile, tile), tile)
        total[at, :] += prod
        return carry

    lax.fori_loop(first, last, step, 0)


def half_kernel(pieces, part, plan_ref, *refs):
    state_refs, weights_ref, total, state = refs[:pieces], refs[pieces], refs[pieces + 1], refs[pieces + 2]
    half = total.shape[0] // weights_ref.shape[1]
    fill_state(state_refs, state)
    total[...] = jnp.zeros_like(total)
    first = plan_ref[2, 0] if part else 0
    last = plan_ref[2, 1] if part else plan_ref[2, 0]
    multiply(plan_ref, weights_ref, state, total, first, last, half * part)


def pick_kernel(pieces, plan_ref, place_ref, *refs):
    state_refs, weights_ref = refs[:pieces], refs[pieces]
    odd_ref, even_ref, state, total = refs[pieces + 1 :]
    fill_state(state_refs, state)
    total[...] = jnp.zeros_like(total)
    multiply(plan_ref, weights_ref, state, total, 0, plan_ref[2, 1], 0)
    rows = odd_ref.shape[0]
    for part, out in ((0, odd_ref), (1, even_ref)):

        def some(i, carry, part=part, out=out):
            for j in range(8):
                at = i * 8 + j
                out[pl.ds(at, 1), :] = total[pl.ds(place_ref[part, at], 1), :]
            return carry

        lax.fori_loop(0, rows // 8, some, 0)


VMEM_SPEC = pl.BlockSpec(memory_space=pltpu.VMEM)


def local(
    embed, degree, tile_row, tile_col, tile_count, tile_values, new_rows, new_bucket, bucket_norm
):
    rows_here, width = embed.shape
    ncols, nrows = lax.axis_size("col"), lax.axis_size("row")
    my_col, my_row = lax.axis_index("col"), lax.axis_index("row")
    weights = tile_values[0, 0]
    slots, tile = weights.shape[:2]
    block_rows = ncols * rows_here
    row_tiles = block_rows // tile
    per_group = rows_here // tile
    zero_tile = nrows * per_group
    half_rows = block_rows // 2
    length = -(-(slots + GROUP * row_tiles) // 128) * 128

    def swap(array, axis, size, mask):
        return lax.ppermute(array, axis, [(i, i ^ mask) for i in range(size)])

    near = jnp.stack([new_rows, swap(new_rows, "col", ncols, 1)])
    picks = jnp.concatenate([near] + [swap(near, "col", ncols, 2 * k) for k in range(1, ncols // 2)])
    inside = picks - my_row * block_rows
    rel = (inside // rows_here) ^ my_col
    place = (1 - rel % 2) * half_rows + (rel // 2) * rows_here + inside % rows_here
    place = place.reshape(ncols // 2, 2, -1).transpose(1, 0, 2)[::-1].reshape(2, -1)

    info = jnp.stack([tile_count[0, 0], my_row, my_col])
    plan = pl.pallas_call(
        functools.partial(plan_kernel, row_tiles, per_group, zero_tile),
        out_shape=jax.ShapeDtypeStruct((8, length), jnp.int32),
        in_specs=[pl.BlockSpec(memory_space=pltpu.SMEM), VMEM_SPEC, VMEM_SPEC],
        out_specs=VMEM_SPEC,
        name="plan",
    )(info, tile_row[0], tile_col[0])
    weights = pltpu.with_memory_space_constraint(weights, pltpu.VMEM)

    state_scratch = pltpu.VMEM(((zero_tile + 1) * tile, width), jnp.bfloat16)
    half_cost = pl.CostEstimate(
        flops=slots * tile * tile * width, bytes_accessed=slots * tile * tile, transcendentals=0
    )
    params = pltpu.CompilerParams(vmem_limit_bytes=24 * MIB)

    def products(pieces, part):
        return pl.pallas_call(
            functools.partial(half_kernel, nrows, part),
            out_shape=jax.ShapeDtypeStruct((half_rows, width), jnp.float32),
            grid_spec=pltpu.PrefetchScalarGridSpec(
                num_scalar_prefetch=1,
                grid=(),
                in_specs=[VMEM_SPEC] * (nrows + 1),
                out_specs=VMEM_SPEC,
                scratch_shapes=[state_scratch],
            ),
            compiler_params=params,
            cost_estimate=half_cost,
            name=("odd", "even")[part],
        )(plan, *pieces, weights)

    def picked_products(pieces):
        shape = jax.ShapeDtypeStruct((place.shape[1], width), jnp.float32)
        return pl.pallas_call(
            functools.partial(pick_kernel, nrows),
            out_shape=(shape, shape),
            grid_spec=pltpu.PrefetchScalarGridSpec(
                num_scalar_prefetch=2,
                grid=(),
                in_specs=[VMEM_SPEC] * (nrows + 1),
                out_specs=(VMEM_SPEC, VMEM_SPEC),
                scratch_shapes=[state_scratch, pltpu.VMEM((block_rows, width), jnp.float32)],
            ),
            compiler_params=params,
            cost_estimate=half_cost,
            name="last",
        )(plan, place, *pieces, weights)

    def spread(state):
        return [state] + [swap(state, "row", nrows, k) for k in range(1, nrows)]

    def collect(odd, even):
        rows = even.shape[0] // (ncols // 2)
        other = swap(odd, "col", ncols, 1)
        own = even[:rows] + other[:rows]
        for k in range(1, ncols // 2):
            at = slice(k * rows, (k + 1) * rows)
            sent = (even[at] + other[at]).astype(jnp.bfloat16)
            own = own + swap(sent, "col", ncols, 2 * k).astype(jnp.float32)
        return own

    scale = lax.rsqrt(degree.astype(jnp.float32))
    state = (scale[:, None] * embed.astype(jnp.float32)).astype(jnp.bfloat16)
    for hop in range(HOPS - 1):
        pieces = spread(state)
        summed = collect(products(pieces, 0), products(pieces, 1))
        state = ((scale * scale)[:, None] * summed).astype(jnp.bfloat16)
    picked = collect(*picked_products(spread(state)))
    buckets = jnp.arange(bucket_norm.shape[0], dtype=jnp.int32)
    target = jnp.sum(
        jnp.where(new_bucket[:, None] == buckets[None, :], bucket_norm[None, :], jnp.float32(0.0)),
        axis=1,
    )
    return (
        target[:, None]
        * picked
        * lax.rsqrt(jnp.sum(picked * picked, axis=1, keepdims=True) + 1e-06)
    )


def solution(mesh):
    in_specs = (
        P(("row", "col"), None),
        P(("row", "col")),
        P("row", "col", None),
        P("row", "col", None),
        P("row", "col"),
        P("row", "col", None, None, None),
        P(("row", "col")),
        P(("row", "col")),
        P(),
    )
    out_specs = P(("row", "col"), None)
    return jax.shard_map(local, mesh=mesh, in_specs=in_specs, out_specs=out_specs, check_vma=False)
```

time: 414 us -> 140 us (0.34)
  other arithmetic: 106 us -> 6.05 us
  waiting for transfers between devices: 132 us -> 40.3 us
  local copies, waits for them, and re-layouts: 85.1 us -> 11 us
  Pallas kernels: 0 us -> 50.3 us
  matrix products: 41.7 us -> 0 us
  blocking collectives: 32.5 us -> 0 us
  starting transfers between devices: 0.09 us -> 30.7 us
  between operations: 13.9 us -> 0.88 us
    scatter-add x3 -> x0, other arithmetic: 99.6 us -> none  [tile_products(): sums = jax.ops.segment_sum(prod, targets, num_segments=row_tiles)]
    reduce_scatter x2 -> x0, waiting for transfers between devices: 69.3 us -> none  [local(): lax.psum_scatter(spread(state), 'col', scatter_dimension=0, tiled=True)]
    psum x1 -> x0, waiting for transfers between devices: 62.3 us -> none  [local(): block = lax.psum(partial_value, 'col')]
    select_n x3 -> x0, local copies, waits for them, and re-layouts: 52.4 us -> none  [tile_products(): prod = jnp.where(live[:, None, None], prod, jnp.float32(0.0))]
    pallas_call x0 -> x6, Pallas kernels: none -> 50.3 us  [the longest x4 29.3 us: products(): pl.pallas_call(functools.partial(half_kernel, nrows, part), out_shape=jax...]
    dot_general x3 -> x0, matrix products: 41.7 us -> none  [tile_products(): jnp.einsum('tij,tjk->tik', weights, picked, preferred_element_type=jnp.fl...]
    ppermute x0 -> x25, waiting for transfers between devices: none -> 40.3 us  [swap(): return lax.ppermute(array, axis, [(i, i ^ mask) for i in range(size)])]
    all_gather x3 -> x0, blocking collectives: 32.5 us -> none  [spread(): gathered = lax.all_gather(current, 'row', axis=0, tiled=True)]
  transfers between devices with their start and end apart: 3 -> 25, of which waited for: 3 -> 17; matrix products, arithmetic and copies ran while one was open for 0% -> 1% of each run, Pallas kernels for 0% -> 12%
where the time goes in v1:
time: 140 us; the launch traced here: 139 us
  Pallas kernels  50.3 us (36%)
  waiting for transfers between devices  40.3 us (29%)
  starting transfers between devices  30.7 us (22%)
  local copies, waits for them, and re-layouts  11 us (8%)
  other arithmetic  6.05 us (4%)
    ppermute x25, waiting for transfers between devices, swap(): return lax.ppermute(array, axis, [(i, i ^ mask) for i in range(size)])  40.3 us
    ppermute x25, starting transfers between devices, swap(): return lax.ppermute(array, axis, [(i, i ^ mask) for i in range(size)])  30.7 us
    pallas_call x4, Pallas kernels, products(): pl.pallas_call(functools.partial(half_kernel, nrows, part), out_shape=jax...  29.3 us
    pallas_call x1, Pallas kernels, picked_products(): pl.pallas_call(functools.partial(pick_kernel, nrows), out_shape=(shape, s...  19.3 us
    unnamed x20, local copies, waits for them, and re-layouts  10.9 us
  transfers between devices with their start and end apart: 25, of which 17 were waited for; matrix products, arithmetic and copies ran while one was open for 1% of the time, Pallas kernels for 12%

profile of v1, /device:TPU:0, one launch (start us, length us, event | category | flops | bytes accessed | tf_op | source)
XLA Modules:
  0.0 139.2 jit_solution(16076629805677566864)
XLA Ops:
  0.0 0.7 fusion.25
  0.7 1.0 multiply_convert_fusion.refs_0_
  1.7 3.0 %collective-permute-start.4 = (bf16[512,128]{1,0:T(8,128)(2,1)S(1)}, bf16[512,128]{1,0:T(8,128)(2,1)S(1)}, u32[]{:S(2)}, u32[]{:S(2)}) collective-permute-start(bf16[512,128]{1,0:T(8,128)(2,1)S(1)} %multiply_convert_fusion.refs_0_), channel_id=1, source_target_pairs={{0,8},{8,0},{16,24},{24,16},{1,9},{9,1},{17,25},{25,17},{2,10},{10... | collective-permute-start | bytes 393224 | tf_op jit(solution)/shard_map/ppermute | solution.py:146
  4.7 1.5 %collective-permute-start.5 = (bf16[512,128]{1,0:T(8,128)(2,1)S(1)}, bf16[512,128]{1,0:T(8,128)(2,1)S(1)}, u32[]{:S(2)}, u32[]{:S(2)}) collective-permute-start(bf16[512,128]{1,0:T(8,128)(2,1)S(1)} %multiply_convert_fusion.refs_0_), channel_id=1, source_target_pairs={{0,16},{8,24},{16,0},{24,8},{1,17},{9,25},{17,1},{25,9},{2,18},{10... | collective-permute-start | bytes 393224 | tf_op jit(solution)/shard_map/ppermute | solution.py:146
  6.3 0.0 collective-permute-start.6
  6.9 0.7 pad_add_fusion.1.info_ref
  7.6 1.7 %plan.1.plan_ref = s32[8,384]{1,0:T(8,128)} custom-call(s32[3]{0:T(128)} %pad_add_fusion.1.info_ref, s32[1,256]{1,0:T(1,128)} %bitcast.24, s32[1,256]{1,0:T(1,128)} %bitcast.25), custom_call_target="tpu_custom_call" | custom-call | tf_op jit(solution)/shard_map/plan/pallas_call | solution.py:156
  9.3 3.2 %collective-permute-done.5.refs_2_ = bf16[512,128]{1,0:T(8,128)(2,1)S(1)} collective-permute-done((bf16[512,128]{1,0:T(8,128)(2,1)S(1)}, bf16[512,128]{1,0:T(8,128)(2,1)S(1)}, u32[]{:S(2)}, u32[]{:S(2)}) %collective-permute-start.5) | collective-permute-done | bytes 131104 | tf_op jit(solution)/shard_map/ppermute | solution.py:146
  12.5 3.4 %copy-done = bf16[1,1,256,128,128]{4,3,2,1,0:T(8,128)(2,1)S(1)} copy-done((bf16[1,1,256,128,128]{4,3,2,1,0:T(8,128)(2,1)S(1)}, bf16[1,1,256,128,128]{4,3,2,1,0:T(8,128)(2,1)}, u32[]{:S(2)}) %copy-start) | copy-done | bytes 8388632
  15.9 0.7 copy-done.3
  16.6 7.2 %odd.2 = f32[2048,128]{1,0:T(8,128)S(1)} custom-call(s32[8,384]{1,0:T(8,128)S(1)} %copy-done.3, bf16[512,128]{1,0:T(8,128)(2,1)S(1)} %multiply_convert_fusion.refs_0_, bf16[512,128]{1,0:T(8,128)(2,1)S(1)} %collective-permute-done.4.refs_1_, bf16[512,128]{1,0:T(8,128)(2,1)S(1)} %collective-permute-done.5.refs_2_, ...), custom_call_target="tpu_custom_call" | custom-call | flops 536870912 | bytes 4194304 | tf_op jit(solution)/shard_map/odd/pallas_call | solution.py:172
  23.8 0.0 slice-start.1
  23.9 0.1 collective-permute-start.7
  23.9 7.4 %even.2 = f32[2048,128]{1,0:T(8,128)S(1)} custom-call(s32[8,384]{1,0:T(8,128)S(1)} %copy-done.3, bf16[512,128]{1,0:T(8,128)(2,1)S(1)} %multiply_convert_fusion.refs_0_, bf16[512,128]{1,0:T(8,128)(2,1)S(1)} %collective-permute-done.4.refs_1_, bf16[512,128]{1,0:T(8,128)(2,1)S(1)} %collective-permute-done.5.refs_2_, ...), custom_call_target="tpu_custom_call" | custom-call | flops 536870912 | bytes 4194304 | tf_op jit(solution)/shard_map/even/pallas_call | solution.py:172
  31.4 0.0 copy-start.5
  31.4 0.0 copy-start.4
  31.4 0.1 fusion.10
  31.5 4.2 %collective-permute-start.10 = (bf16[512,128]{1,0:T(8,128)(2,1)S(1)}, bf16[512,128]{1,0:T(8,128)(2,1)S(1)}, u32[]{:S(2)}, u32[]{:S(2)}) collective-permute-start(bf16[512,128]{1,0:T(8,128)(2,1)S(1)} %get-tuple-element.15), channel_id=1, source_target_pairs={{0,6},{1,7},{2,4},{3,5},{4,2},{5,3},{6,0},{7,1},{8,14},{9,15},{10,... | collective-permute-start | bytes 393224 | tf_op jit(solution)/shard_map/ppermute | solution.py:146
  35.8 0.6 collective-permute-start.8
  36.4 3.7 %collective-permute-done.10 = bf16[512,128]{1,0:T(8,128)(2,1)S(1)} collective-permute-done((bf16[512,128]{1,0:T(8,128)(2,1)S(1)}, bf16[512,128]{1,0:T(8,128)(2,1)S(1)}, u32[]{:S(2)}, u32[]{:S(2)}) %collective-permute-start.10) | collective-permute-done | bytes 131104 | tf_op jit(solution)/shard_map/ppermute | solution.py:146
  40.1 4.9 %collective-permute-done.9 = bf16[512,128]{1,0:T(8,128)(2,1)S(1)} collective-permute-done((bf16[512,128]{1,0:T(8,128)(2,1)S(1)}, bf16[512,128]{1,0:T(8,128)(2,1)S(1)}, u32[]{:S(2)}, u32[]{:S(2)}) %collective-permute-start.9) | collective-permute-done | bytes 131104 | tf_op jit(solution)/shard_map/ppermute | solution.py:146
  45.1 0.1 fusion.15.refs_0_
  45.2 0.1 collective-permute-start.11
  45.3 2.2 %collective-permute-start.12 = (bf16[512,128]{1,0:T(8,128)(2,1)S(1)}, bf16[512,128]{1,0:T(8,128)(2,1)S(1)}, u32[]{:S(2)}, u32[]{:S(2)}) collective-permute-start(bf16[512,128]{1,0:T(8,128)(2,1)S(1)} %fusion.15.refs_0_), channel_id=1, source_target_pairs={{0,16},{8,24},{16,0},{24,8},{1,17},{9,25},{17,1},{25,9},{2,18},{10... | collective-permute-start | bytes 393224 | tf_op jit(solution)/shard_map/ppermute | solution.py:146
  47.5 1.4 collective-permute-start.13
  48.9 2.2 %collective-permute-done.11.refs_1_ = bf16[512,128]{1,0:T(8,128)(2,1)S(1)} collective-permute-done((bf16[512,128]{1,0:T(8,128)(2,1)S(1)}, bf16[512,128]{1,0:T(8,128)(2,1)S(1)}, u32[]{:S(2)}, u32[]{:S(2)}) %collective-permute-start.11) | collective-permute-done | bytes 131104 | tf_op jit(solution)/shard_map/ppermute | solution.py:146
  51.0 2.0 %collective-permute-done.12.refs_2_ = bf16[512,128]{1,0:T(8,128)(2,1)S(1)} collective-permute-done((bf16[512,128]{1,0:T(8,128)(2,1)S(1)}, bf16[512,128]{1,0:T(8,128)(2,1)S(1)}, u32[]{:S(2)}, u32[]{:S(2)}) %collective-permute-start.12) | collective-permute-done | bytes 131104 | tf_op jit(solution)/shard_map/ppermute | solution.py:146
  53.0 1.8 %collective-permute-done.13.refs_3_ = bf16[512,128]{1,0:T(8,128)(2,1)S(1)} collective-permute-done((bf16[512,128]{1,0:T(8,128)(2,1)S(1)}, bf16[512,128]{1,0:T(8,128)(2,1)S(1)}, u32[]{:S(2)}, u32[]{:S(2)}) %collective-permute-start.13) | collective-permute-done | bytes 131104 | tf_op jit(solution)/shard_map/ppermute | solution.py:146
  54.9 7.2 %odd.3 = f32[2048,128]{1,0:T(8,128)S(1)} custom-call(s32[8,384]{1,0:T(8,128)S(1)} %copy-done.3, bf16[512,128]{1,0:T(8,128)(2,1)S(1)} %fusion.15.refs_0_, bf16[512,128]{1,0:T(8,128)(2,1)S(1)} %collective-permute-done.11.refs_1_, bf16[512,128]{1,0:T(8,128)(2,1)S(1)} %collective-permute-done.12.refs_2_, bf16[512,128]{1,0:T(8,128)(2,1)S(1)} %collective-permute-done.13.refs_3_, ...), custom_call_target="tpu_custom_call" | custom-call | flops 536870912 | bytes 4194304 | tf_op jit(solution)/shard_map/odd/pallas_call | solution.py:172
  62.1 0.1 collective-permute-start.14
  62.2 0.5 collective-permute-start
  62.7 1.8 %collective-permute-done = s32[256]{0:T(256)S(1)} collective-permute-done((s32[256]{0:T(256)S(1)}, s32[256]{0:T(256)S(1)}, u32[]{:S(2)}, u32[]{:S(2)}) %collective-permute-start) | collective-permute-done | bytes 1056 | tf_op jit(solution)/shard_map/ppermute | solution.py:146
  64.5 2.2 %collective-permute-start.2 = (s32[2,256]{1,0:T(2,128)S(1)}, s32[2,256]{1,0:T(2,128)S(1)}, u32[]{:S(2)}, u32[]{:S(2)}) collective-permute-start(s32[2,256]{1,0:T(2,128)S(1)} %pad_add_fusion), channel_id=1, source_target_pairs={{0,4},{1,5},{2,6},{3,7},{4,0},{5,1},{6,2},{7,3},{8,12},{9,13},{10,... | collective-permute-start | bytes 6152 | tf_op jit(solution)/shard_map/ppermute | solution.py:146
  66.6 2.2 %collective-permute-start.3 = (s32[2,256]{1,0:T(2,128)S(1)}, s32[2,256]{1,0:T(2,128)S(1)}, u32[]{:S(2)}, u32[]{:S(2)}) collective-permute-start(s32[2,256]{1,0:T(2,128)S(1)} %pad_add_fusion), channel_id=1, source_target_pairs={{0,6},{1,7},{2,4},{3,5},{4,2},{5,3},{6,0},{7,1},{8,14},{9,15},{10,... | collective-permute-start | bytes 6152 | tf_op jit(solution)/shard_map/ppermute | solution.py:146
  68.9 0.2 collective-permute-done.2
  69.0 3.0 %collective-permute-done.3 = s32[2,256]{1,0:T(2,128)S(1)} collective-permute-done((s32[2,256]{1,0:T(2,128)S(1)}, s32[2,256]{1,0:T(2,128)S(1)}, u32[]{:S(2)}, u32[]{:S(2)}) %collective-permute-start.3) | collective-permute-done | bytes 2080 | tf_op jit(solution)/shard_map/ppermute | solution.py:146
  72.0 0.0 copy-start.1
  72.1 3.4 %copy-done.1 = bf16[1,1,256,128,128]{4,3,2,1,0:T(8,128)(2,1)S(1)} copy-done((bf16[1,1,256,128,128]{4,3,2,1,0:T(8,128)(2,1)S(1)}, bf16[1,1,256,128,128]{4,3,2,1,0:T(8,128)(2,1)}, u32[]{:S(2)}) %copy-start.1) | copy-done | bytes 8388632
  75.4 7.4 %even.3 = f32[2048,128]{1,0:T(8,128)S(1)} custom-call(s32[8,384]{1,0:T(8,128)S(1)} %copy-done.4, bf16[512,128]{1,0:T(8,128)(2,1)S(1)} %fusion.15.refs_0_, bf16[512,128]{1,0:T(8,128)(2,1)S(1)} %collective-permute-done.11.refs_1_, bf16[512,128]{1,0:T(8,128)(2,1)S(1)} %collective-permute-done.12.refs_2_, bf16[512,128]{1,0:T(8,128)(2,1)S(1)} %collective-permute-done.13.refs_3_, ...), custom_call_target="tpu_custom_call" | custom-call | flops 536870912 | bytes 4194304 | tf_op jit(solution)/shard_map/even/pallas_call | solution.py:172
  82.9 1.2 fusion.2
  84.1 2.9 %collective-permute-start.17 = (bf16[512,128]{1,0:T(8,128)(2,1)S(1)}, bf16[512,128]{1,0:T(8,128)(2,1)S(1)}, u32[]{:S(2)}, u32[]{:S(2)}) collective-permute-start(bf16[512,128]{1,0:T(8,128)(2,1)S(1)} %get-tuple-element.12), channel_id=1, source_target_pairs={{0,6},{1,7},{2,4},{3,5},{4,2},{5,3},{6,0},{7,1},{8,14},{9,15},{10,... | collective-permute-start | bytes 393224 | tf_op jit(solution)/shard_map/ppermute | solution.py:146
  87.0 1.6 %collective-permute-start.15 = (bf16[512,128]{1,0:T(8,128)(2,1)S(1)}, bf16[512,128]{1,0:T(8,128)(2,1)S(1)}, u32[]{:S(2)}, u32[]{:S(2)}) collective-permute-start(bf16[512,128]{1,0:T(8,128)(2,1)S(1)} %get-tuple-element.11), channel_id=1, source_target_pairs={{0,2},{1,3},{2,0},{3,1},{4,6},{5,7},{6,4},{7,5},{8,10},{9,11},{10,... | collective-permute-start | bytes 393224 | tf_op jit(solution)/shard_map/ppermute | solution.py:146
  88.6 2.5 %collective-permute-done.17 = bf16[512,128]{1,0:T(8,128)(2,1)S(1)} collective-permute-done((bf16[512,128]{1,0:T(8,128)(2,1)S(1)}, bf16[512,128]{1,0:T(8,128)(2,1)S(1)}, u32[]{:S(2)}, u32[]{:S(2)}) %collective-permute-start.17) | collective-permute-done | bytes 131104 | tf_op jit(solution)/shard_map/ppermute | solution.py:146
  91.1 3.1 %collective-permute-done.16 = bf16[512,128]{1,0:T(8,128)(2,1)S(1)} collective-permute-done((bf16[512,128]{1,0:T(8,128)(2,1)S(1)}, bf16[512,128]{1,0:T(8,128)(2,1)S(1)}, u32[]{:S(2)}, u32[]{:S(2)}) %collective-permute-start.16) | collective-permute-done | bytes 131104 | tf_op jit(solution)/shard_map/ppermute | solution.py:146
  94.1 1.1 fusion.7.refs_0_
  95.2 0.1 collective-permute-start.18
  95.3 2.1 %collective-permute-start.19 = (bf16[512,128]{1,0:T(8,128)(2,1)S(1)}, bf16[512,128]{1,0:T(8,128)(2,1)S(1)}, u32[]{:S(2)}, u32[]{:S(2)}) collective-permute-start(bf16[512,128]{1,0:T(8,128)(2,1)S(1)} %fusion.7.refs_0_), channel_id=1, source_target_pairs={{0,16},{8,24},{16,0},{24,8},{1,17},{9,25},{17,1},{25,9},{2,18},{10... | collective-permute-start | bytes 393224 | tf_op jit(solution)/shard_map/ppermute | solution.py:146
  97.5 1.4 collective-permute-start.20
  98.8 0.1 fusion.24
  98.9 0.1 rev.3
  99.0 2.6 %collective-permute-done.18.refs_1_ = bf16[512,128]{1,0:T(8,128)(2,1)S(1)} collective-permute-done((bf16[512,128]{1,0:T(8,128)(2,1)S(1)}, bf16[512,128]{1,0:T(8,128)(2,1)S(1)}, u32[]{:S(2)}, u32[]{:S(2)}) %collective-permute-start.18) | collective-permute-done | bytes 131104 | tf_op jit(solution)/shard_map/ppermute | solution.py:146
  101.6 0.8 collective-permute-done.19.refs_2_
  102.5 1.8 %collective-permute-done.20.refs_3_ = bf16[512,128]{1,0:T(8,128)(2,1)S(1)} collective-permute-done((bf16[512,128]{1,0:T(8,128)(2,1)S(1)}, bf16[512,128]{1,0:T(8,128)(2,1)S(1)}, u32[]{:S(2)}, u32[]{:S(2)}) %collective-permute-start.20) | collective-permute-done | bytes 131104 | tf_op jit(solution)/shard_map/ppermute | solution.py:146
  104.2 3.4 %copy-done.2 = bf16[1,1,256,128,128]{4,3,2,1,0:T(8,128)(2,1)S(1)} copy-done((bf16[1,1,256,128,128]{4,3,2,1,0:T(8,128)(2,1)S(1)}, bf16[1,1,256,128,128]{4,3,2,1,0:T(8,128)(2,1)}, u32[]{:S(2)}) %copy-start.2) | copy-done | bytes 8388632
  107.6 19.3 %last.1 = (f32[1024,128]{1,0:T(8,128)S(1)}, f32[1024,128]{1,0:T(8,128)S(1)}) custom-call(s32[8,384]{1,0:T(8,128)S(1)} %copy-done.4, s32[2,1024]{1,0:T(2,128)S(1)} %bitcast.19, bf16[512,128]{1,0:T(8,128)(2,1)S(1)} %fusion.7.refs_0_, bf16[512,128]{1,0:T(8,128)(2,1)S(1)} %collective-permute-done.18.refs_1_, ...), custom_call_target="tpu_custom_call" | custom-call | flops 536870912 | bytes 4194304 | tf_op jit(solution)/shard_map/last/pallas_call | solution.py:189
  126.9 0.1 collective-permute-start.21
  127.0 1.9 %collective-permute-done.21 = f32[1024,128]{1,0:T(8,128)S(1)} collective-permute-done((f32[1024,128]{1,0:T(8,128)S(1)}, f32[1024,128]{1,0:T(8,128)S(1)}, u32[]{:S(2)}, u32[]{:S(2)}) %collective-permute-start.21) | collective-permute-done | bytes 524320 | tf_op jit(solution)/shard_map/ppermute | solution.py:146
  128.9 3.0 %collective-permute-start.24 = (bf16[256,128]{1,0:T(8,128)(2,1)S(1)}, bf16[256,128]{1,0:T(8,128)(2,1)S(1)}, u32[]{:S(2)}, u32[]{:S(2)}) collective-permute-start(bf16[256,128]{1,0:T(8,128)(2,1)S(1)} %get-tuple-element.18), channel_id=1, source_target_pairs={{0,6},{1,7},{2,4},{3,5},{4,2},{5,3},{6,0},{7,1},{8,14},{9,15},{10,... | collective-permute-start | bytes 196616 | tf_op jit(solution)/shard_map/ppermute | solution.py:146
  132.0 1.4 %collective-permute-start.22 = (bf16[256,128]{1,0:T(8,128)(2,1)S(1)}, bf16[256,128]{1,0:T(8,128)(2,1)S(1)}, u32[]{:S(2)}, u32[]{:S(2)}) collective-permute-start(bf16[256,128]{1,0:T(8,128)(2,1)S(1)} %get-tuple-element.17), channel_id=1, source_target_pairs={{0,2},{1,3},{2,0},{3,1},{4,6},{5,7},{6,4},{7,5},{8,10},{9,11},{10,... | collective-permute-start | bytes 196616 | tf_op jit(solution)/shard_map/ppermute | solution.py:146
  133.4 0.1 select_reduce_fusion
  133.5 2.3 %collective-permute-done.24 = bf16[256,128]{1,0:T(8,128)(2,1)S(1)} collective-permute-done((bf16[256,128]{1,0:T(8,128)(2,1)S(1)}, bf16[256,128]{1,0:T(8,128)(2,1)S(1)}, u32[]{:S(2)}, u32[]{:S(2)}) %collective-permute-start.24) | collective-permute-done | bytes 65568 | tf_op jit(solution)/shard_map/ppermute | solution.py:146
  135.7 2.5 %collective-permute-done.23 = bf16[256,128]{1,0:T(8,128)(2,1)S(1)} collective-permute-done((bf16[256,128]{1,0:T(8,128)(2,1)S(1)}, bf16[256,128]{1,0:T(8,128)(2,1)S(1)}, u32[]{:S(2)}, u32[]{:S(2)}) %collective-permute-start.23) | collective-permute-done | bytes 65568 | tf_op jit(solution)/shard_map/ppermute | solution.py:146
  138.3 0.1 multiply_reduce_fusion
  138.4 0.8 multiply_multiply_fusion
  (31 shorter events, 0.2 us)
Async XLA Ops:
  1.7 7.6 %collective-permute-start.4 = (bf16[512,128]{1,0:T(8,128)(2,1)S(1)}, bf16[512,128]{1,0:T(8,128)(2,1)S(1)}, u32[]{:S(2)}, u32[]{:S(2)}) collective-permute-start(bf16[512,128]{1,0:T(8,128)(2,1)S(1)} %multiply_convert_fusion.refs_0_), channel_id=1, source_target_pairs={{0,8},{8,0},{16,24},{24,16},{1,9},{9,1},{17,25},{25,17},{2,10},{10... | collective-permute-start | bytes 393224 | tf_op jit(solution)/shard_map/ppermute | solution.py:146
  4.7 7.8 %collective-permute-start.5 = (bf16[512,128]{1,0:T(8,128)(2,1)S(1)}, bf16[512,128]{1,0:T(8,128)(2,1)S(1)}, u32[]{:S(2)}, u32[]{:S(2)}) collective-permute-start(bf16[512,128]{1,0:T(8,128)(2,1)S(1)} %multiply_convert_fusion.refs_0_), channel_id=1, source_target_pairs={{0,16},{8,24},{16,0},{24,8},{1,17},{9,25},{17,1},{25,9},{2,18},{10... | collective-permute-start | bytes 393224 | tf_op jit(solution)/shard_map/ppermute | solution.py:146
  6.3 6.3 %collective-permute-start.6 = (bf16[512,128]{1,0:T(8,128)(2,1)S(1)}, bf16[512,128]{1,0:T(8,128)(2,1)S(1)}, u32[]{:S(2)}, u32[]{:S(2)}) collective-permute-start(bf16[512,128]{1,0:T(8,128)(2,1)S(1)} %multiply_convert_fusion.refs_0_), channel_id=1, source_target_pairs={{0,24},{8,16},{16,8},{24,0},{1,25},{9,17},{17,9},{25,1},{2,26},{10... | collective-permute-start | bytes 393224 | tf_op jit(solution)/shard_map/ppermute | solution.py:146
  12.5 3.4 %copy-start = (bf16[1,1,256,128,128]{4,3,2,1,0:T(8,128)(2,1)S(1)}, bf16[1,1,256,128,128]{4,3,2,1,0:T(8,128)(2,1)}, u32[]{:S(2)}) copy-start(bf16[1,1,256,128,128]{4,3,2,1,0:T(8,128)(2,1)} %param.14) | copy-start | bytes 25165828
  15.9 0.7 copy-start.3
  16.6 38.2 %slice-start = ((s8[8388608]{0:T(1024)(128)(4,1)}), s8[4194304]{0:T(1024)(128)(4,1)S(1)}, s32[]{:S(2)}) async-start(s8[8388608]{0:T(1024)(128)(4,1)} %bitcast.14), calls=%async_computation | async-start | bytes 8388608
  23.8 31.0 %slice-start.1 = ((s8[8388608]{0:T(1024)(128)(4,1)}), s8[4194304]{0:T(1024)(128)(4,1)S(1)}, s32[]{:S(2)}) async-start(s8[8388608]{0:T(1024)(128)(4,1)} %bitcast.14), calls=%async_computation.1 | async-start | bytes 8388608
  23.9 7.5 %collective-permute-start.7 = (f32[2048,128]{1,0:T(8,128)S(1)}, f32[2048,128]{1,0:T(8,128)S(1)}, u32[]{:S(2)}, u32[]{:S(2)}) collective-permute-start(f32[2048,128]{1,0:T(8,128)S(1)} %odd.2), channel_id=1, source_target_pairs={{0,1},{1,0},{2,3},{3,2},{4,5},{5,4},{6,7},{7,6},{8,9},{9,8},{10,11... | collective-permute-start | bytes 3145736 | tf_op jit(solution)/shard_map/ppermute | solution.py:146
  31.4 30.8 %copy-start.5 = (s32[256]{0:T(256)S(1)}, s32[256]{0:T(256)}, u32[]{:S(2)}) copy-start(s32[256]{0:T(256)} %param.15) | copy-start | bytes 3076
  31.4 40.7 %copy-start.4 = (s32[8,384]{1,0:T(8,128)S(1)}, s32[8,384]{1,0:T(8,128)}, u32[]{:S(2)}) copy-start(s32[8,384]{1,0:T(8,128)} %plan.1.plan_ref) | copy-start | bytes 36868
  31.5 8.6 %collective-permute-start.10 = (bf16[512,128]{1,0:T(8,128)(2,1)S(1)}, bf16[512,128]{1,0:T(8,128)(2,1)S(1)}, u32[]{:S(2)}, u32[]{:S(2)}) collective-permute-start(bf16[512,128]{1,0:T(8,128)(2,1)S(1)} %get-tuple-element.15), channel_id=1, source_target_pairs={{0,6},{1,7},{2,4},{3,5},{4,2},{5,3},{6,0},{7,1},{8,14},{9,15},{10,... | collective-permute-start | bytes 393224 | tf_op jit(solution)/shard_map/ppermute | solution.py:146
  35.8 9.3 %collective-permute-start.9 = (bf16[512,128]{1,0:T(8,128)(2,1)S(1)}, bf16[512,128]{1,0:T(8,128)(2,1)S(1)}, u32[]{:S(2)}, u32[]{:S(2)}) collective-permute-start(bf16[512,128]{1,0:T(8,128)(2,1)S(1)} %get-tuple-element.16), channel_id=1, source_target_pairs={{0,4},{1,5},{2,6},{3,7},{4,0},{5,1},{6,2},{7,3},{8,12},{9,13},{10,... | collective-permute-start | bytes 393224 | tf_op jit(solution)/shard_map/ppermute | solution.py:146
  35.8 9.3 %collective-permute-start.8 = (bf16[512,128]{1,0:T(8,128)(2,1)S(1)}, bf16[512,128]{1,0:T(8,128)(2,1)S(1)}, u32[]{:S(2)}, u32[]{:S(2)}) collective-permute-start(bf16[512,128]{1,0:T(8,128)(2,1)S(1)} %get-tuple-element.14), channel_id=1, source_target_pairs={{0,2},{1,3},{2,0},{3,1},{4,6},{5,7},{6,4},{7,5},{8,10},{9,11},{10,... | collective-permute-start | bytes 393224 | tf_op jit(solution)/shard_map/ppermute | solution.py:146
  45.2 5.8 %collective-permute-start.11 = (bf16[512,128]{1,0:T(8,128)(2,1)S(1)}, bf16[512,128]{1,0:T(8,128)(2,1)S(1)}, u32[]{:S(2)}, u32[]{:S(2)}) collective-permute-start(bf16[512,128]{1,0:T(8,128)(2,1)S(1)} %fusion.15.refs_0_), channel_id=1, source_target_pairs={{0,8},{8,0},{16,24},{24,16},{1,9},{9,1},{17,25},{25,17},{2,10},{10... | collective-permute-start | bytes 393224 | tf_op jit(solution)/shard_map/ppermute | solution.py:146
  45.3 7.7 %collective-permute-start.12 = (bf16[512,128]{1,0:T(8,128)(2,1)S(1)}, bf16[512,128]{1,0:T(8,128)(2,1)S(1)}, u32[]{:S(2)}, u32[]{:S(2)}) collective-permute-start(bf16[512,128]{1,0:T(8,128)(2,1)S(1)} %fusion.15.refs_0_), channel_id=1, source_target_pairs={{0,16},{8,24},{16,0},{24,8},{1,17},{9,25},{17,1},{25,9},{2,18},{10... | collective-permute-start | bytes 393224 | tf_op jit(solution)/shard_map/ppermute | solution.py:146
  47.5 7.4 %collective-permute-start.13 = (bf16[512,128]{1,0:T(8,128)(2,1)S(1)}, bf16[512,128]{1,0:T(8,128)(2,1)S(1)}, u32[]{:S(2)}, u32[]{:S(2)}) collective-permute-start(bf16[512,128]{1,0:T(8,128)(2,1)S(1)} %fusion.15.refs_0_), channel_id=1, source_target_pairs={{0,24},{8,16},{16,8},{24,0},{1,25},{9,17},{17,9},{25,1},{2,26},{10... | collective-permute-start | bytes 393224 | tf_op jit(solution)/shard_map/ppermute | solution.py:146
  62.1 20.8 %collective-permute-start.14 = (f32[2048,128]{1,0:T(8,128)S(1)}, f32[2048,128]{1,0:T(8,128)}, u32[]{:S(2)}, u32[]{:S(2)}) collective-permute-start(f32[2048,128]{1,0:T(8,128)S(1)} %odd.3), channel_id=1, source_target_pairs={{0,1},{1,0},{2,3},{3,2},{4,5},{5,4},{6,7},{7,6},{8,9},{9,8},{10,11... | collective-permute-start | bytes 3145736 | tf_op jit(solution)/shard_map/ppermute | solution.py:146
  62.2 2.3 %collective-permute-start = (s32[256]{0:T(256)S(1)}, s32[256]{0:T(256)S(1)}, u32[]{:S(2)}, u32[]{:S(2)}) collective-permute-start(s32[256]{0:T(256)S(1)} %copy-done.5), channel_id=1, source_target_pairs={{0,1},{1,0},{2,3},{3,2},{4,5},{5,4},{6,7},{7,6},{8,9},{9,8},{10,11... | collective-permute-start | bytes 3080 | tf_op jit(solution)/shard_map/ppermute | solution.py:146
  64.5 4.4 %collective-permute-start.1 = (s32[2,256]{1,0:T(2,128)S(1)}, s32[2,256]{1,0:T(2,128)S(1)}, u32[]{:S(2)}, u32[]{:S(2)}) collective-permute-start(s32[2,256]{1,0:T(2,128)S(1)} %pad_add_fusion), channel_id=1, source_target_pairs={{0,2},{1,3},{2,0},{3,1},{4,6},{5,7},{6,4},{7,5},{8,10},{9,11},{10,... | collective-permute-start | bytes 6152 | tf_op jit(solution)/shard_map/ppermute | solution.py:146
  64.5 4.5 %collective-permute-start.2 = (s32[2,256]{1,0:T(2,128)S(1)}, s32[2,256]{1,0:T(2,128)S(1)}, u32[]{:S(2)}, u32[]{:S(2)}) collective-permute-start(s32[2,256]{1,0:T(2,128)S(1)} %pad_add_fusion), channel_id=1, source_target_pairs={{0,4},{1,5},{2,6},{3,7},{4,0},{5,1},{6,2},{7,3},{8,12},{9,13},{10,... | collective-permute-start | bytes 6152 | tf_op jit(solution)/shard_map/ppermute | solution.py:146
  66.6 5.4 %collective-permute-start.3 = (s32[2,256]{1,0:T(2,128)S(1)}, s32[2,256]{1,0:T(2,128)S(1)}, u32[]{:S(2)}, u32[]{:S(2)}) collective-permute-start(s32[2,256]{1,0:T(2,128)S(1)} %pad_add_fusion), channel_id=1, source_target_pairs={{0,6},{1,7},{2,4},{3,5},{4,2},{5,3},{6,0},{7,1},{8,14},{9,15},{10,... | collective-permute-start | bytes 6152 | tf_op jit(solution)/shard_map/ppermute | solution.py:146
  72.0 3.4 %copy-start.1 = (bf16[1,1,256,128,128]{4,3,2,1,0:T(8,128)(2,1)S(1)}, bf16[1,1,256,128,128]{4,3,2,1,0:T(8,128)(2,1)}, u32[]{:S(2)}) copy-start(bf16[1,1,256,128,128]{4,3,2,1,0:T(8,128)(2,1)} %param.14) | copy-start | bytes 25165828
  82.9 50.5 %copy-start.6 = (s32[256]{0:T(256)S(1)}, s32[256]{0:T(256)}, u32[]{:S(2)}) copy-start(s32[256]{0:T(256)} %param.16) | copy-start | bytes 3076
  82.9 50.5 %copy-start.7 = (f32[16]{0:T(128)S(1)}, f32[16]{0:T(128)}, u32[]{:S(2)}) copy-start(f32[16]{0:T(128)} %param.17) | copy-start | bytes 196
  84.1 7.0 %collective-permute-start.17 = (bf16[512,128]{1,0:T(8,128)(2,1)S(1)}, bf16[512,128]{1,0:T(8,128)(2,1)S(1)}, u32[]{:S(2)}, u32[]{:S(2)}) collective-permute-start(bf16[512,128]{1,0:T(8,128)(2,1)S(1)} %get-tuple-element.12), channel_id=1, source_target_pairs={{0,6},{1,7},{2,4},{3,5},{4,2},{5,3},{6,0},{7,1},{8,14},{9,15},{10,... | collective-permute-start | bytes 393224 | tf_op jit(solution)/shard_map/ppermute | solution.py:146
  87.0 7.2 %collective-permute-start.16 = (bf16[512,128]{1,0:T(8,128)(2,1)S(1)}, bf16[512,128]{1,0:T(8,128)(2,1)S(1)}, u32[]{:S(2)}, u32[]{:S(2)}) collective-permute-start(bf16[512,128]{1,0:T(8,128)(2,1)S(1)} %get-tuple-element.13), channel_id=1, source_target_pairs={{0,4},{1,5},{2,6},{3,7},{4,0},{5,1},{6,2},{7,3},{8,12},{9,13},{10,... | collective-permute-start | bytes 393224 | tf_op jit(solution)/shard_map/ppermute | solution.py:146
  87.0 7.2 %collective-permute-start.15 = (bf16[512,128]{1,0:T(8,128)(2,1)S(1)}, bf16[512,128]{1,0:T(8,128)(2,1)S(1)}, u32[]{:S(2)}, u32[]{:S(2)}) collective-permute-start(bf16[512,128]{1,0:T(8,128)(2,1)S(1)} %get-tuple-element.11), channel_id=1, source_target_pairs={{0,2},{1,3},{2,0},{3,1},{4,6},{5,7},{6,4},{7,5},{8,10},{9,11},{10,... | collective-permute-start | bytes 393224 | tf_op jit(solution)/shard_map/ppermute | solution.py:146
  95.2 6.4 %collective-permute-start.18 = (bf16[512,128]{1,0:T(8,128)(2,1)S(1)}, bf16[512,128]{1,0:T(8,128)(2,1)S(1)}, u32[]{:S(2)}, u32[]{:S(2)}) collective-permute-start(bf16[512,128]{1,0:T(8,128)(2,1)S(1)} %fusion.7.refs_0_), channel_id=1, source_target_pairs={{0,8},{8,0},{16,24},{24,16},{1,9},{9,1},{17,25},{25,17},{2,10},{10... | collective-permute-start | bytes 393224 | tf_op jit(solution)/shard_map/ppermute | solution.py:146
  95.3 7.1 %collective-permute-start.19 = (bf16[512,128]{1,0:T(8,128)(2,1)S(1)}, bf16[512,128]{1,0:T(8,128)(2,1)S(1)}, u32[]{:S(2)}, u32[]{:S(2)}) collective-permute-start(bf16[512,128]{1,0:T(8,128)(2,1)S(1)} %fusion.7.refs_0_), channel_id=1, source_target_pairs={{0,16},{8,24},{16,0},{24,8},{1,17},{9,25},{17,1},{25,9},{2,18},{10... | collective-permute-start | bytes 393224 | tf_op jit(solution)/shard_map/ppermute | solution.py:146
  97.5 6.8 %collective-permute-start.20 = (bf16[512,128]{1,0:T(8,128)(2,1)S(1)}, bf16[512,128]{1,0:T(8,128)(2,1)S(1)}, u32[]{:S(2)}, u32[]{:S(2)}) collective-permute-start(bf16[512,128]{1,0:T(8,128)(2,1)S(1)} %fusion.7.refs_0_), channel_id=1, source_target_pairs={{0,24},{8,16},{16,8},{24,0},{1,25},{9,17},{17,9},{25,1},{2,26},{10... | collective-permute-start | bytes 393224 | tf_op jit(solution)/shard_map/ppermute | solution.py:146
  104.2 3.4 %copy-start.2 = (bf16[1,1,256,128,128]{4,3,2,1,0:T(8,128)(2,1)S(1)}, bf16[1,1,256,128,128]{4,3,2,1,0:T(8,128)(2,1)}, u32[]{:S(2)}) copy-start(bf16[1,1,256,128,128]{4,3,2,1,0:T(8,128)(2,1)} %param.14) | copy-start | bytes 25165828
  126.9 2.0 %collective-permute-start.21 = (f32[1024,128]{1,0:T(8,128)S(1)}, f32[1024,128]{1,0:T(8,128)S(1)}, u32[]{:S(2)}, u32[]{:S(2)}) collective-permute-start(f32[1024,128]{1,0:T(8,128)S(1)} %get-tuple-element.8), channel_id=1, source_target_pairs={{0,1},{1,0},{2,3},{3,2},{4,5},{5,4},{6,7},{7,6},{8,9},{9,8},{10,11... | collective-permute-start | bytes 1572872 | tf_op jit(solution)/shard_map/ppermute | solution.py:146
  128.9 6.8 %collective-permute-start.24 = (bf16[256,128]{1,0:T(8,128)(2,1)S(1)}, bf16[256,128]{1,0:T(8,128)(2,1)S(1)}, u32[]{:S(2)}, u32[]{:S(2)}) collective-permute-start(bf16[256,128]{1,0:T(8,128)(2,1)S(1)} %get-tuple-element.18), channel_id=1, source_target_pairs={{0,6},{1,7},{2,4},{3,5},{4,2},{5,3},{6,0},{7,1},{8,14},{9,15},{10,... | collective-permute-start | bytes 196616 | tf_op jit(solution)/shard_map/ppermute | solution.py:146
  132.0 6.3 %collective-permute-start.23 = (bf16[256,128]{1,0:T(8,128)(2,1)S(1)}, bf16[256,128]{1,0:T(8,128)(2,1)S(1)}, u32[]{:S(2)}, u32[]{:S(2)}) collective-permute-start(bf16[256,128]{1,0:T(8,128)(2,1)S(1)} %get-tuple-element.19), channel_id=1, source_target_pairs={{0,4},{1,5},{2,6},{3,7},{4,0},{5,1},{6,2},{7,3},{8,12},{9,13},{10,... | collective-permute-start | bytes 196616 | tf_op jit(solution)/shard_map/ppermute | solution.py:146
  132.0 6.3 %collective-permute-start.22 = (bf16[256,128]{1,0:T(8,128)(2,1)S(1)}, bf16[256,128]{1,0:T(8,128)(2,1)S(1)}, u32[]{:S(2)}, u32[]{:S(2)}) collective-permute-start(bf16[256,128]{1,0:T(8,128)(2,1)S(1)} %get-tuple-element.17), channel_id=1, source_target_pairs={{0,2},{1,3},{2,0},{3,1},{4,6},{5,7},{6,4},{7,5},{8,10},{9,11},{10,... | collective-permute-start | bytes 196616 | tf_op jit(solution)/shard_map/ppermute | solution.py:146

commit v2 on v0

v2 whole, which is shorter than its diff:
```python
import functools

import jax
import jax.numpy as jnp
from jax import lax
from jax.experimental import pallas as pl
from jax.experimental.pallas import tpu as pltpu
from jax.sharding import PartitionSpec as P

HOPS = 3
HALVES = 2
CHUNKS = 2 * HALVES
GROUP = 4
UNROLL = 4
UNPICK = 16
BITS = 8
SHIFT = 1 << BITS
BYTE = 256
LANES = 128
PACK = 16
MIB = 1024 * 1024

VMEM_SPEC = pl.BlockSpec(memory_space=pltpu.VMEM)
SMEM_SPEC = pl.BlockSpec(memory_space=pltpu.SMEM)
HBM_SPEC = pl.BlockSpec(memory_space=pltpu.HBM)
PARAMS = pltpu.CompilerParams(vmem_limit_bytes=16 * MIB)


def iota(shape, dim):
    return lax.broadcasted_iota(jnp.int32, shape, dim)


def to_column(row):
    n = row.shape[1]
    return jnp.sum(jnp.where(iota((n, n), 0) == iota((n, n), 1), row, 0.0), axis=1, keepdims=True)


def to_row(column):
    n = column.shape[0]
    return jnp.sum(jnp.where(iota((n, n), 0) == iota((n, n), 1), column, 0.0), axis=0, keepdims=True)


def plan_kernel(
    row_tiles, per_group, zero_tile, count_ref, tile_row_hbm, tile_col_hbm, weights_hbm,
    plan_ref, weights_ref, tile_row_ref, tile_col_ref, sems,
):
    load = pltpu.make_async_copy(weights_hbm, weights_ref, sems.at[0])
    lists = (
        pltpu.make_async_copy(tile_row_hbm, tile_row_ref, sems.at[1]),
        pltpu.make_async_copy(tile_col_hbm, tile_col_ref, sems.at[2]),
    )
    for copy in lists:
        copy.start()
    load.start()
    for copy in lists:
        copy.wait()
    slots = tile_row_ref.shape[1]
    length = plan_ref.shape[1]
    my_row, my_col = lax.axis_index("row"), lax.axis_index("col")
    chunk_tiles = row_tiles // CHUNKS
    per_half = per_group // HALVES
    row = tile_row_ref[...]
    rel = (row // per_group) ^ my_col
    chunk = (1 - rel % 2) * HALVES + (row % per_group) // per_half
    order = chunk * chunk_tiles + (rel // 2) * per_half + row % per_half
    order = jnp.where(iota((1, slots), 1) < count_ref[0, 0], order, row_tiles).astype(jnp.float32)
    col = tile_col_ref[...]
    source = ((col // per_group) ^ my_row) * per_group + col % per_group
    entry = (iota((1, slots), 1) * SHIFT + source).astype(jnp.float32)
    order_c = to_column(order)
    entry_c = to_column(entry)
    same = jnp.where((order_c == order) & (iota((slots, slots), 1) < iota((slots, slots), 0)), 1.0, 0.0)
    within = jnp.sum(same, axis=1, keepdims=True)
    tiles_r = iota((row_tiles, slots), 0).astype(jnp.float32)
    held = jnp.sum(jnp.where(tiles_r == order, 1.0, 0.0), axis=1, keepdims=True).astype(jnp.int32)
    steps = (held + GROUP - 1) // GROUP
    steps_f = steps.astype(jnp.float32)
    square = (row_tiles, row_tiles)
    first = jnp.sum(jnp.where(iota(square, 1) < iota(square, 0), to_row(steps_f), 0.0), axis=1, keepdims=True)
    tile_no, step_no = iota((row_tiles, 1), 0), iota((1, length), 1)
    raw, begin, ends = jnp.int32(0), jnp.int32(0), []
    limit = jnp.full((1, length), row_tiles - 1, jnp.int32)
    shift = jnp.zeros((row_tiles, 1), jnp.int32)
    for c in range(CHUNKS):
        mine = (tile_no >= c * chunk_tiles) & (tile_no < (c + 1) * chunk_tiles)
        size = jnp.sum(jnp.where(mine, steps_f, 0.0)).astype(jnp.int32)
        shift = shift + jnp.where(mine, begin - raw, 0)
        end = begin + (size + UNROLL - 1) // UNROLL * UNROLL
        limit = jnp.where((step_no >= begin) & (step_no < end), (c + 1) * chunk_tiles - 1, limit)
        raw, begin = raw + size, end
        ends.append(end // UNROLL)
    first = first + shift.astype(jnp.float32)
    lanes = iota((slots, row_tiles), 1).astype(jnp.float32)
    start = jnp.sum(jnp.where(order_c == lanes, to_row(first), 0.0), axis=1, keepdims=True)
    place = jnp.where(order_c < row_tiles, GROUP * start + within, -1.0)
    hit = place == iota((slots, length), 1).astype(jnp.float32)
    listed = jnp.sum(jnp.where(hit, entry_c - zero_tile, 0.0), axis=0, keepdims=True) + zero_tile
    done = (first + steps_f) <= iota((row_tiles, length), 1).astype(jnp.float32)
    owner = jnp.sum(jnp.where(done, 1.0, 0.0), axis=0, keepdims=True).astype(jnp.int32)
    bounds = jnp.zeros((1, length), jnp.int32)
    for c, end in enumerate(ends):
        bounds = jnp.where(step_no == c + 1, end, bounds)
    plan_ref[0:1, :] = listed.astype(jnp.int32)
    plan_ref[1:2, :] = jnp.minimum(owner, limit)
    plan_ref[2:3, :] = bounds
    plan_ref[3:8, :] = jnp.zeros((5, length), jnp.int32)
    load.wait()


def fill_state(pieces, state, halves, tile):
    rows = pieces[0].shape[0]
    devices = (state.shape[0] - tile) // (rows * halves)
    for i, piece in enumerate(pieces):
        half, device = halves - 1 - i // devices, i % devices
        at = (device * halves + half) * rows
        state[at : at + rows, :] = piece[...]
    state[len(pieces) * rows :, :] = jnp.zeros((tile, state.shape[1]), state.dtype)


def multiply(plan_ref, weights_ref, state, total, chunk, chunks, chunk_tiles):
    tile = weights_ref.shape[1]
    total[...] = jnp.zeros_like(total)

    def turn(i, carry):
        prods = []
        for u in range(UNROLL):
            left, right = [], []
            for j in range(GROUP):
                entry = plan_ref[0, (i * UNROLL + u) * GROUP + j]
                left.append(weights_ref[entry >> BITS])
                right.append(state[pl.ds(pl.multiple_of((entry & (SHIFT - 1)) * tile, tile), tile), :])
            prods.append(
                jnp.dot(
                    jnp.concatenate(left, axis=1),
                    jnp.concatenate(right, axis=0),
                    preferred_element_type=jnp.float32,
                )
            )
        for u in range(UNROLL):
            row = plan_ref[1, i * UNROLL + u] - chunk * chunk_tiles
            at = pl.ds(pl.multiple_of(row * tile, tile), tile)
            total[at, :] += prods[u]
        return carry

    lax.fori_loop(plan_ref[2, chunk], plan_ref[2, chunk + chunks], turn, 0)


def odd_kernel(pieces, halves, plan_ref, *refs):
    weights_ref, extra_refs = refs[pieces], refs[pieces + 1 : -3]
    odd_ref, state, total = refs[-3:]
    rows = total.shape[0]
    fill_state(refs[:pieces], state, halves, weights_ref.shape[1])
    multiply(plan_ref, weights_ref, state, total, 0, HALVES, 0)
    odd_ref[0:rows, :] = total[...].astype(odd_ref.dtype)
    for extra in extra_refs:
        odd_ref[rows:, :] = extra[...]


def even0_kernel(plan_ref, state, weights_ref, even_ref):
    multiply(plan_ref, weights_ref, state, even_ref, HALVES, 1, even_ref.shape[0] // weights_ref.shape[1])


def even1_kernel(chips, plan_ref, state, weights_ref, after_ref, other_ref, *refs):
    extra_refs, own_ref, sent_refs, total = refs[: -chips - 1], refs[-chips - 1], refs[-chips:-1], refs[-1]
    rows = total.shape[0]
    multiply(plan_ref, weights_ref, state, total, HALVES + 1, 1, rows // weights_ref.shape[1])
    add_cores(chips, rows, total, other_ref, own_ref, sent_refs)
    for extra in extra_refs:
        size = extra.shape[0]
        far = other_ref[other_ref.shape[0] - size :, :].astype(jnp.float32)
        both = (extra[...].astype(jnp.float32) + pltpu.roll(far, size // 2, 0)).astype(extra.dtype)
        for sent in sent_refs:
            sent[own_ref.shape[0] :, :] = both


def add_cores(chips, offset, even_ref, other_ref, own_ref, sent_refs):
    rows = own_ref.shape[0]
    for k, out in enumerate((own_ref, *sent_refs)):
        other = other_ref[pl.ds(offset + k * rows, rows), :].astype(jnp.float32)
        out[0:rows, :] = (even_ref[pl.ds(k * rows, rows), :] + other).astype(out.dtype)


def merge_kernel(chips, even_ref, other_ref, own_ref, *sent_refs):
    add_cores(chips, 0, even_ref, other_ref, own_ref, sent_refs)


def place_kernel(chips, rows_here, block_rows, id_rows, mine_ref, other_ref, *refs):
    far_refs, place_ref = refs[:-1], refs[-1]
    my_col = lax.axis_index("col")
    half = rows_here // HALVES
    chunk_rows = block_rows // CHUNKS
    extra = mine_ref.shape[0]

    def places(rows):
        ids = (rows[:id_rows] * BYTE + rows[id_rows : 2 * id_rows]).astype(jnp.int32)
        rel = (ids // rows_here) ^ my_col
        chunk = (1 - rel % 2) * HALVES + ids % rows_here // half
        return chunk * chunk_rows + rel // 2 * half + ids % half

    def tail(ref):
        return ref[ref.shape[0] - extra :, :].astype(jnp.float32)

    even, odd = [mine_ref[...].astype(jnp.float32)], [tail(other_ref)]
    for ref in far_refs:
        rows = tail(ref)
        even.append(rows)
        odd.append(pltpu.roll(rows, extra - extra // 2, 0))
    for k in range(chips):
        place_ref[k * id_rows : (k + 1) * id_rows, :] = places(odd[k])
        place_ref[(chips + k) * id_rows : (chips + k + 1) * id_rows, :] = places(even[k])


def pick_rows(place_ref, part, total, picked, out):
    count = picked.shape[0]

    def some(i, carry):
        base = pl.multiple_of(i * UNPICK, UNPICK)
        row = (part * count + base) // LANES
        lane = base % LANES
        for j in range(UNPICK):
            picked[pl.ds(base + j, 1), :] = total[pl.ds(place_ref[row, lane + j], 1), :]
        return carry

    lax.fori_loop(0, count // UNPICK, some, 0)
    if out is not picked:
        out[...] = picked[...].astype(out.dtype)


def last_kernel(pieces, halves, plan_ref, place_ref, *refs):
    weights_ref = refs[pieces]
    odd_ref, total, state, picked = refs[pieces + 1 :]
    fill_state(refs[:pieces], state, halves, weights_ref.shape[1])
    multiply(plan_ref, weights_ref, state, total, 0, CHUNKS, 0)
    pick_rows(place_ref, 0, total, picked, odd_ref)


def pick_kernel(place_ref, total, even_ref):
    pick_rows(place_ref, 1, total, even_ref, even_ref)


def local(
    embed, degree, tile_row, tile_col, tile_count, tile_values, new_rows, new_bucket, bucket_norm
):
    rows_here, width = embed.shape
    ncols, nrows = lax.axis_size("col"), lax.axis_size("row")
    weights = tile_values[0, 0]
    slots, tile = weights.shape[:2]
    chips = ncols // 2
    block_rows = ncols * rows_here
    row_tiles = block_rows // tile
    per_group = rows_here // tile
    half_here = rows_here // HALVES
    chunk_rows = block_rows // CHUNKS
    zero_tile = nrows * per_group
    new_here = new_rows.shape[0]
    id_rows = new_here // LANES
    id_block = -(-4 * id_rows // PACK) * PACK
    length = -(-(slots + GROUP * (row_tiles + CHUNKS * UNROLL)) // LANES) * LANES
    f32, bf16 = jnp.float32, jnp.bfloat16
    array = jax.ShapeDtypeStruct
    in_hbm = lambda x: pltpu.with_memory_space_constraint(x, pltpu.HBM)
    in_vmem = lambda x: pltpu.with_memory_space_constraint(x, pltpu.VMEM)

    def call(kernel, name, out_shape, args, scalars=0, in_specs=None, scratch=(), turns=0.0):
        many = isinstance(out_shape, (list, tuple))
        cost = pl.CostEstimate(
            flops=int(turns * 2 * slots * tile * tile * width),
            bytes_accessed=int(turns * 2 * slots * tile * tile),
            transcendentals=0,
        )
        return pl.pallas_call(
            kernel,
            out_shape=out_shape,
            grid_spec=pltpu.PrefetchScalarGridSpec(
                num_scalar_prefetch=scalars,
                grid=(),
                in_specs=in_specs or [VMEM_SPEC] * (len(args) - scalars),
                out_specs=[VMEM_SPEC] * len(out_shape) if many else VMEM_SPEC,
                scratch_shapes=list(scratch),
            ),
            compiler_params=PARAMS,
            cost_estimate=cost if turns else None,
            name=name,
        )(*args)

    def swap(array, axis, size, mask):
        return lax.ppermute(array, axis, [(i, i ^ mask) for i in range(size)])

    def swap_cores(odd):
        return swap(odd, "col", ncols, 1)

    def spread(state):
        return [state] + [swap(state, "row", nrows, k) for k in range(1, nrows)]

    scale = lax.rsqrt(degree.astype(f32))
    state = (scale[:, None] * embed.astype(f32)).astype(bf16)
    pieces = spread(state)

    plan, weights = call(
        functools.partial(plan_kernel, row_tiles, per_group, zero_tile),
        "plan",
        [array((8, length), jnp.int32), pltpu.VMEM(weights.shape, weights.dtype)],
        (tile_count, in_hbm(tile_row[0]), in_hbm(tile_col[0]), in_hbm(weights)),
        in_specs=[SMEM_SPEC, HBM_SPEC, HBM_SPEC, HBM_SPEC],
        scratch=[
            pltpu.VMEM((1, slots), jnp.int32),
            pltpu.VMEM((1, slots), jnp.int32),
            pltpu.SemaphoreType.DMA((3,)),
        ],
    )
    weights = in_vmem(weights)

    inside = (new_rows - lax.axis_index("row") * block_rows).reshape(id_rows, LANES)
    mine = jnp.concatenate([inside // BYTE, inside % BYTE]).astype(bf16)
    mine = jnp.pad(mine, ((0, id_block - 2 * id_rows), (0, 0)))

    state_shape = ((zero_tile + 1) * tile, width)

    def sums_shape(rows, more=0):
        return [array((rows, width), f32)] + [array((rows + more, width), bf16)] * (chips - 1)

    def send(sent):
        return [swap(part, "col", ncols, 2 * k) for k, part in enumerate(sent, 1)]

    def merge(even, other):
        own, *sent = call(
            functools.partial(merge_kernel, chips), "merge", sums_shape(even.shape[0] // chips), (even, other)
        )
        return own, send(sent)

    def add(own, came):
        for part in came:
            own = own + part[: own.shape[0]].astype(f32)
        return own

    for hop in range(HOPS - 1):
        extra = (mine,) if hop == 0 else ()
        odd, held = call(
            functools.partial(odd_kernel, len(pieces), len(pieces) // nrows),
            "odd",
            [
                array((HALVES * chunk_rows + len(extra) * id_block, width), bf16),
                array(state_shape, bf16),
            ],
            (plan, *pieces, weights, *extra),
            scalars=1,
            scratch=[pltpu.VMEM((HALVES * chunk_rows, width), f32)],
            turns=0.5,
        )
        other = swap_cores(odd)
        even0 = call(
            even0_kernel, "even0", array((chunk_rows, width), f32), (plan, held, weights), scalars=1, turns=0.25
        )
        own0, came0 = merge(even0, other)
        own1, *sent1 = call(
            functools.partial(even1_kernel, chips),
            "even1",
            sums_shape(half_here, len(extra) * id_block),
            (plan, held, weights, own0, other, *extra),
            scalars=1,
            scratch=[pltpu.VMEM((chunk_rows, width), f32)],
            turns=0.25,
        )
        came1 = send(sent1)
        if hop == 0:
            place = call(
                functools.partial(place_kernel, chips, rows_here, block_rows, id_rows),
                "place",
                array((2 * chips * id_rows, LANES), jnp.int32),
                (mine, other, *came1),
            )
        parts = {}
        for half, (own, came) in reversed(tuple(enumerate(((own0, came0), (own1, came1))))):
            here = scale[half * half_here : (half + 1) * half_here]
            parts[half] = spread(((here * here)[:, None] * add(own, came)).astype(bf16))
        pieces = [parts[half][r] for half in reversed(range(HALVES)) for r in range(nrows)]

    odd, total = call(
        functools.partial(last_kernel, len(pieces), len(pieces) // nrows),
        "last",
        [array((chips * new_here, width), bf16), array((block_rows, width), f32)],
        (plan, place, *pieces, weights),
        scalars=2,
        scratch=[pltpu.VMEM(state_shape, bf16), pltpu.VMEM((chips * new_here, width), f32)],
        turns=1.0,
    )
    other = swap_cores(odd)
    even = call(pick_kernel, "pick", array((chips * new_here, width), f32), (place, total), scalars=1, turns=0.2)
    picked = add(*merge(even, other))
    buckets = jnp.arange(bucket_norm.shape[0], dtype=jnp.int32)
    target = jnp.sum(
        jnp.where(new_bucket[:, None] == buckets[None, :], bucket_norm[None, :], jnp.float32(0.0)),
        axis=1,
    )
    return (
        target[:, None]
        * picked
        * lax.rsqrt(jnp.sum(picked * picked, axis=1, keepdims=True) + 1e-06)
    )


def solution(mesh):
    in_specs = (
        P(("row", "col"), None),
        P(("row", "col")),
        P("row", "col", None),
        P("row", "col", None),
        P("row", "col"),
        P("row", "col", None, None, None),
        P(("row", "col")),
        P(("row", "col")),
        P(),
    )
    out_specs = P(("row", "col"), None)
    return jax.shard_map(local, mesh=mesh, in_specs=in_specs, out_specs=out_specs, check_vma=False)
```

time: 414 us -> 95 us (0.23)
  waiting for transfers between devices: 132 us -> 19.1 us
  other arithmetic: 106 us -> 3.86 us
  local copies, waits for them, and re-layouts: 85.1 us -> 0.01 us
  starting transfers between devices: 0.09 us -> 43.2 us
  matrix products: 41.7 us -> 0 us
  blocking collectives: 32.5 us -> 0 us
  Pallas kernels: 0 us -> 27.4 us
  between operations: 13.9 us -> 0.9 us
    scatter-add x3 -> x0, other arithmetic: 99.6 us -> none  [tile_products(): sums = jax.ops.segment_sum(prod, targets, num_segments=row_tiles)]
    reduce_scatter x2 -> x0, waiting for transfers between devices: 69.3 us -> none  [local(): lax.psum_scatter(spread(state), 'col', scatter_dimension=0, tiled=True)]
    psum x1 -> x0, waiting for transfers between devices: 62.3 us -> none  [local(): block = lax.psum(partial_value, 'col')]
    select_n x3 -> x0, local copies, waits for them, and re-layouts: 52.4 us -> none  [tile_products(): prod = jnp.where(live[:, None, None], prod, jnp.float32(0.0))]
    ppermute x0 -> x33, starting transfers between devices: none -> 43.2 us  [swap(): return lax.ppermute(array, axis, [(i, i ^ mask) for i in range(size)])]
    dot_general x3 -> x0, matrix products: 41.7 us -> none  [tile_products(): jnp.einsum('tij,tjk->tik', weights, picked, preferred_element_type=jnp.fl...]
    all_gather x3 -> x0, blocking collectives: 32.5 us -> none  [spread(): gathered = lax.all_gather(current, 'row', axis=0, tiled=True)]
    gather x4 -> x0, local copies, waits for them, and re-layouts: 28.1 us -> none  [the longest x3 25.8 us: tile_products(): picked = jnp.take(col_tiles, tile_col, axis=0)]
  transfers between devices with their start and end apart: 3 -> 33, of which waited for: 3 -> 15; matrix products, arithmetic and copies ran while one was open for 0% -> 1% of each run, Pallas kernels for 0% -> 15%
where the time goes in v2:
time: 95 us; the launch traced here: 94.4 us
  starting transfers between devices  43.2 us (45%)
  Pallas kernels  27.4 us (29%)
  waiting for transfers between devices  19.1 us (20%)
  other arithmetic  3.86 us (4%)
    ppermute x33, starting transfers between devices, swap(): return lax.ppermute(array, axis, [(i, i ^ mask) for i in range(size)])  43.2 us
    pallas_call x13, Pallas kernels, call(): pl.pallas_call(kernel, out_shape=out_shape, grid_spec=pltpu.PrefetchScala...  27.4 us
    ppermute x33, waiting for transfers between devices, swap(): return lax.ppermute(array, axis, [(i, i ^ mask) for i in range(size)])  19.1 us
  transfers between devices with their start and end apart: 33, of which 15 were waited for; matrix products, arithmetic and copies ran while one was open for 1% of the time, Pallas kernels for 15%

profile of v2, /device:TPU:0, one launch (start us, length us, event | category | flops | bytes accessed | tf_op | source)
XLA Modules:
  0.0 94.4 jit_solution(7790544666047901039)
XLA Ops:
  0.0 0.7 convert_rsqrt_fusion
  0.7 1.0 %multiply_convert_fusion.refs_0_ = bf16[512,128]{1,0:T(8,128)(2,1)S(1)} fusion(bf16[512,128]{1,0:T(8,128)(2,1)} %param.9, f32[512]{0:T(512)S(1)} %convert_rsqrt_fusion), kind=kLoop, calls=%fused_computation | loop fusion | flops 196608 | bytes 264192 | tf_op jit(solution)/shard_map/convert_element_type | solution.py:296
  1.7 3.0 %collective-permute-start = (bf16[512,128]{1,0:T(8,128)(2,1)S(1)}, bf16[512,128]{1,0:T(8,128)(2,1)S(1)}, u32[]{:S(2)}, u32[]{:S(2)}) collective-permute-start(bf16[512,128]{1,0:T(8,128)(2,1)S(1)} %multiply_convert_fusion.refs_0_), channel_id=1, source_target_pairs={{0,8},{8,0},{16,24},{24,16},{1,9},{9,1},{17,25},{25,17},{2,10},{10... | collective-permute-start | bytes 393224 | tf_op jit(solution)/shard_map/ppermute | solution.py:287
  4.7 1.5 %collective-permute-start.1 = (bf16[512,128]{1,0:T(8,128)(2,1)S(1)}, bf16[512,128]{1,0:T(8,128)(2,1)S(1)}, u32[]{:S(2)}, u32[]{:S(2)}) collective-permute-start(bf16[512,128]{1,0:T(8,128)(2,1)S(1)} %multiply_convert_fusion.refs_0_), channel_id=1, source_target_pairs={{0,16},{8,24},{16,0},{24,8},{1,17},{9,25},{17,1},{25,9},{2,18},{10... | collective-permute-start | bytes 393224 | tf_op jit(solution)/shard_map/ppermute | solution.py:287
  6.3 0.7 fusion.4
  7.6 3.4 %plan.1 = (s32[8,512]{1,0:T(8,128)S(1)}, bf16[256,128,128]{2,1,0:T(8,128)(2,1)S(1)}) custom-call(s32[1,1]{1,0:T(1,128)S(6)} %copy.10.count_ref, s32[1,256]{1,0:T(1,128)} %bitcast.24, s32[1,256]{1,0:T(1,128)} %bitcast.25, bf16[256,128,128]{2,1,0:T(8,128)(2,1)} %bitcast.23), custom_call_target="tpu_custom_call" | custom-call | tf_op jit(solution)/shard_map/plan/pallas_call | solution.py:271
  11.1 1.4 %collective-permute-done.1.refs_2_ = bf16[512,128]{1,0:T(8,128)(2,1)S(1)} collective-permute-done((bf16[512,128]{1,0:T(8,128)(2,1)S(1)}, bf16[512,128]{1,0:T(8,128)(2,1)S(1)}, u32[]{:S(2)}, u32[]{:S(2)}) %collective-permute-start.1) | collective-permute-done | bytes 131104 | tf_op jit(solution)/shard_map/ppermute | solution.py:287
  12.5 2.7 %odd.2 = (bf16[2064,128]{1,0:T(8,128)(2,1)S(1)}, bf16[2176,128]{1,0:T(8,128)(2,1)S(1)}) custom-call(s32[8,512]{1,0:T(8,128)S(1)} %get-tuple-element.33.plan_ref, bf16[512,128]{1,0:T(8,128)(2,1)S(1)} %multiply_convert_fusion.refs_0_, bf16[512,128]{1,0:T(8,128)(2,1)S(1)} %collective-permute-done.refs_1_, bf16[512,128]{1,0:T(8,128)(2,1)S(1)} %collective-permute-done.1.refs_2_, ...), custom_call_target="tpu_custom_call" | custom-call | flops 536870912 | bytes 4194304 | tf_op jit(solution)/shard_map/odd/pallas_call | solution.py:271
  15.3 0.1 collective-permute-start.3
  15.3 1.7 %even0.2.even_ref = f32[1024,128]{1,0:T(8,128)S(1)} custom-call(s32[8,512]{1,0:T(8,128)S(1)} %get-tuple-element.33.plan_ref, bf16[2176,128]{1,0:T(8,128)(2,1)S(1)} %get-tuple-element.36.state, bf16[256,128,128]{2,1,0:T(8,128)(2,1)S(1)} %get-tuple-element.34.refs_4_.weights_ref.refs_8_), custom_call_target="tpu_custom_call" | custom-call | flops 268435456 | bytes 2097152 | tf_op jit(solution)/shard_map/even0/pallas_call | solution.py:271
  17.1 0.2 collective-permute-done.3.other_ref
  17.3 3.3 %collective-permute-start.10 = (bf16[256,128]{1,0:T(8,128)(2,1)S(1)}, bf16[256,128]{1,0:T(8,128)(2,1)S(1)}, u32[]{:S(2)}, u32[]{:S(2)}) collective-permute-start(bf16[256,128]{1,0:T(8,128)(2,1)S(1)} %get-tuple-element.42), channel_id=1, source_target_pairs={{0,2},{1,3},{2,0},{3,1},{4,6},{5,7},{6,4},{7,5},{8,10},{9,11},{10,... | collective-permute-start | bytes 196616 | tf_op jit(solution)/shard_map/ppermute | solution.py:287
  20.6 2.3 %collective-permute-start.11 = (bf16[256,128]{1,0:T(8,128)(2,1)S(1)}, bf16[256,128]{1,0:T(8,128)(2,1)S(1)}, u32[]{:S(2)}, u32[]{:S(2)}) collective-permute-start(bf16[256,128]{1,0:T(8,128)(2,1)S(1)} %get-tuple-element.43), channel_id=1, source_target_pairs={{0,4},{1,5},{2,6},{3,7},{4,0},{5,1},{6,2},{7,3},{8,12},{9,13},{10,... | collective-permute-start | bytes 196616 | tf_op jit(solution)/shard_map/ppermute | solution.py:287
  22.9 0.1 collective-permute-start.12
  23.0 1.8 %even1.2 = (f32[256,128]{1,0:T(8,128)S(1)}, bf16[272,128]{1,0:T(8,128)(2,1)S(1)}, bf16[272,128]{1,0:T(8,128)(2,1)S(1)}, bf16[272,128]{1,0:T(8,128)(2,1)S(1)}) custom-call(s32[8,512]{1,0:T(8,128)S(1)} %get-tuple-element.33.plan_ref, bf16[2176,128]{1,0:T(8,128)(2,1)S(1)} %get-tuple-element.36.state, ...), custom_call_target="tpu_custom_call" | custom-call | flops 268435456 | bytes 2097152 | tf_op jit(solution)/shard_map/even1/pallas_call | solution.py:271
  24.8 1.4 %collective-permute-start.4 = (bf16[272,128]{1,0:T(8,128)(2,1)S(1)}, bf16[272,128]{1,0:T(8,128)(2,1)S(1)}, u32[]{:S(2)}, u32[]{:S(2)}) collective-permute-start(bf16[272,128]{1,0:T(8,128)(2,1)S(1)} %get-tuple-element.38), channel_id=1, source_target_pairs={{0,2},{1,3},{2,0},{3,1},{4,6},{5,7},{6,4},{7,5},{8,10},{9,11},{10,... | collective-permute-start | bytes 208904 | tf_op jit(solution)/shard_map/ppermute | solution.py:287
  26.2 3.2 %collective-permute-start.5 = (bf16[272,128]{1,0:T(8,128)(2,1)S(1)}, bf16[272,128]{1,0:T(8,128)(2,1)S(1)}, u32[]{:S(2)}, u32[]{:S(2)}) collective-permute-start(bf16[272,128]{1,0:T(8,128)(2,1)S(1)} %get-tuple-element.39), channel_id=1, source_target_pairs={{0,4},{1,5},{2,6},{3,7},{4,0},{5,1},{6,2},{7,3},{8,12},{9,13},{10,... | collective-permute-start | bytes 208904 | tf_op jit(solution)/shard_map/ppermute | solution.py:287
  29.5 0.1 multiply_convert_fusion.3.refs_4_
  29.6 0.3 collective-permute-start.13
  29.8 2.2 %collective-permute-start.14 = (bf16[256,128]{1,0:T(8,128)(2,1)S(1)}, bf16[256,128]{1,0:T(8,128)(2,1)S(1)}, u32[]{:S(2)}, u32[]{:S(2)}) collective-permute-start(bf16[256,128]{1,0:T(8,128)(2,1)S(1)} %multiply_convert_fusion.3.refs_4_), channel_id=1, source_target_pairs={{0,16},{8,24},{16,0},{24,8},{1,17},{9,25},{17,1},{25,9},{2,18},{10... | collective-permute-start | bytes 196616 | tf_op jit(solution)/shard_map/ppermute | solution.py:287
  32.0 1.4 %collective-permute-start.15 = (bf16[256,128]{1,0:T(8,128)(2,1)S(1)}, bf16[256,128]{1,0:T(8,128)(2,1)S(1)}, u32[]{:S(2)}, u32[]{:S(2)}) collective-permute-start(bf16[256,128]{1,0:T(8,128)(2,1)S(1)} %multiply_convert_fusion.3.refs_4_), channel_id=1, source_target_pairs={{0,24},{8,16},{16,8},{24,0},{1,25},{9,17},{17,9},{25,1},{2,26},{10... | collective-permute-start | bytes 196616 | tf_op jit(solution)/shard_map/ppermute | solution.py:287
  33.4 0.7 collective-permute-done.5.refs_1_
  34.2 1.5 %collective-permute-done.6.refs_2_ = bf16[272,128]{1,0:T(8,128)(2,1)S(1)} collective-permute-done((bf16[272,128]{1,0:T(8,128)(2,1)S(1)}, bf16[272,128]{1,0:T(8,128)(2,1)S(1)}, u32[]{:S(2)}, u32[]{:S(2)}) %collective-permute-start.6) | collective-permute-done | bytes 69664 | tf_op jit(solution)/shard_map/ppermute | solution.py:287
  35.7 0.1 multiply_convert_fusion.4.refs_0_
  35.8 0.1 collective-permute-start.7
  35.8 2.3 %collective-permute-start.8 = (bf16[256,128]{1,0:T(8,128)(2,1)S(1)}, bf16[256,128]{1,0:T(8,128)(2,1)S(1)}, u32[]{:S(2)}, u32[]{:S(2)}) collective-permute-start(bf16[256,128]{1,0:T(8,128)(2,1)S(1)} %multiply_convert_fusion.4.refs_0_), channel_id=1, source_target_pairs={{0,16},{8,24},{16,0},{24,8},{1,17},{9,25},{17,1},{25,9},{2,18},{10... | collective-permute-start | bytes 196616 | tf_op jit(solution)/shard_map/ppermute | solution.py:287
  38.2 1.1 %collective-permute-start.9 = (bf16[256,128]{1,0:T(8,128)(2,1)S(1)}, bf16[256,128]{1,0:T(8,128)(2,1)S(1)}, u32[]{:S(2)}, u32[]{:S(2)}) collective-permute-start(bf16[256,128]{1,0:T(8,128)(2,1)S(1)} %multiply_convert_fusion.4.refs_0_), channel_id=1, source_target_pairs={{0,24},{8,16},{16,8},{24,0},{1,25},{9,17},{17,9},{25,1},{2,26},{10... | collective-permute-start | bytes 196616 | tf_op jit(solution)/shard_map/ppermute | solution.py:287
  39.3 0.8 collective-permute-done.7.refs_1_
  40.1 0.7 collective-permute-done.8.refs_2_
  40.8 2.6 %collective-permute-done.9.refs_3_ = bf16[256,128]{1,0:T(8,128)(2,1)S(1)} collective-permute-done((bf16[256,128]{1,0:T(8,128)(2,1)S(1)}, bf16[256,128]{1,0:T(8,128)(2,1)S(1)}, u32[]{:S(2)}, u32[]{:S(2)}) %collective-permute-start.9) | collective-permute-done | bytes 65568 | tf_op jit(solution)/shard_map/ppermute | solution.py:287
  43.3 2.7 %odd.3 = (bf16[2048,128]{1,0:T(8,128)(2,1)S(1)}, bf16[2176,128]{1,0:T(8,128)(2,1)S(1)}) custom-call(s32[8,512]{1,0:T(8,128)S(1)} %get-tuple-element.33.plan_ref, bf16[256,128]{1,0:T(8,128)(2,1)S(1)} %multiply_convert_fusion.4.refs_0_, bf16[256,128]{1,0:T(8,128)(2,1)S(1)} %collective-permute-done.7.refs_1_, ...), custom_call_target="tpu_custom_call" | custom-call | flops 536870912 | bytes 4194304 | tf_op jit(solution)/shard_map/odd/pallas_call | solution.py:271
  46.1 0.1 collective-permute-start.16
  46.2 1.7 %even0.3.even_ref = f32[1024,128]{1,0:T(8,128)S(1)} custom-call(s32[8,512]{1,0:T(8,128)S(1)} %get-tuple-element.33.plan_ref, bf16[2176,128]{1,0:T(8,128)(2,1)S(1)} %get-tuple-element.45.state, bf16[256,128,128]{2,1,0:T(8,128)(2,1)S(1)} %get-tuple-element.34.refs_4_.weights_ref.refs_8_), custom_call_target="tpu_custom_call" | custom-call | flops 268435456 | bytes 2097152 | tf_op jit(solution)/shard_map/even0/pallas_call | solution.py:271
  47.9 0.2 collective-permute-done.16.other_ref
  48.1 1.5 %collective-permute-start.23 = (bf16[256,128]{1,0:T(8,128)(2,1)S(1)}, bf16[256,128]{1,0:T(8,128)(2,1)S(1)}, u32[]{:S(2)}, u32[]{:S(2)}) collective-permute-start(bf16[256,128]{1,0:T(8,128)(2,1)S(1)} %get-tuple-element.52), channel_id=1, source_target_pairs={{0,2},{1,3},{2,0},{3,1},{4,6},{5,7},{6,4},{7,5},{8,10},{9,11},{10,... | collective-permute-start | bytes 196616 | tf_op jit(solution)/shard_map/ppermute | solution.py:287
  49.7 2.1 %collective-permute-start.24 = (bf16[256,128]{1,0:T(8,128)(2,1)S(1)}, bf16[256,128]{1,0:T(8,128)(2,1)S(1)}, u32[]{:S(2)}, u32[]{:S(2)}) collective-permute-start(bf16[256,128]{1,0:T(8,128)(2,1)S(1)} %get-tuple-element.53), channel_id=1, source_target_pairs={{0,4},{1,5},{2,6},{3,7},{4,0},{5,1},{6,2},{7,3},{8,12},{9,13},{10,... | collective-permute-start | bytes 196616 | tf_op jit(solution)/shard_map/ppermute | solution.py:287
  51.8 0.8 collective-permute-start.25
  52.6 1.8 %even1.3 = (f32[256,128]{1,0:T(8,128)S(1)}, bf16[256,128]{1,0:T(8,128)(2,1)S(1)}, bf16[256,128]{1,0:T(8,128)(2,1)S(1)}, bf16[256,128]{1,0:T(8,128)(2,1)S(1)}) custom-call(s32[8,512]{1,0:T(8,128)S(1)} %get-tuple-element.33.plan_ref, bf16[2176,128]{1,0:T(8,128)(2,1)S(1)} %get-tuple-element.45.state, ...), custom_call_target="tpu_custom_call" | custom-call | flops 268435456 | bytes 2097152 | tf_op jit(solution)/shard_map/even1/pallas_call | solution.py:271
  54.4 0.9 collective-permute-start.17
  55.3 3.0 %collective-permute-start.18 = (bf16[256,128]{1,0:T(8,128)(2,1)S(1)}, bf16[256,128]{1,0:T(8,128)(2,1)S(1)}, u32[]{:S(2)}, u32[]{:S(2)}) collective-permute-start(bf16[256,128]{1,0:T(8,128)(2,1)S(1)} %get-tuple-element.50), channel_id=1, source_target_pairs={{0,4},{1,5},{2,6},{3,7},{4,0},{5,1},{6,2},{7,3},{8,12},{9,13},{10,... | collective-permute-start | bytes 196616 | tf_op jit(solution)/shard_map/ppermute | solution.py:287
  58.4 0.5 collective-permute-start.19
  58.9 0.1 multiply_convert_fusion.1.refs_4_
  59.0 0.2 collective-permute-start.26
  59.1 2.2 %collective-permute-start.27 = (bf16[256,128]{1,0:T(8,128)(2,1)S(1)}, bf16[256,128]{1,0:T(8,128)(2,1)S(1)}, u32[]{:S(2)}, u32[]{:S(2)}) collective-permute-start(bf16[256,128]{1,0:T(8,128)(2,1)S(1)} %multiply_convert_fusion.1.refs_4_), channel_id=1, source_target_pairs={{0,16},{8,24},{16,0},{24,8},{1,17},{9,25},{17,1},{25,9},{2,18},{10... | collective-permute-start | bytes 196616 | tf_op jit(solution)/shard_map/ppermute | solution.py:287
  61.4 1.4 %collective-permute-start.28 = (bf16[256,128]{1,0:T(8,128)(2,1)S(1)}, bf16[256,128]{1,0:T(8,128)(2,1)S(1)}, u32[]{:S(2)}, u32[]{:S(2)}) collective-permute-start(bf16[256,128]{1,0:T(8,128)(2,1)S(1)} %multiply_convert_fusion.1.refs_4_), channel_id=1, source_target_pairs={{0,24},{8,16},{16,8},{24,0},{1,25},{9,17},{17,9},{25,1},{2,26},{10... | collective-permute-start | bytes 196616 | tf_op jit(solution)/shard_map/ppermute | solution.py:287
  62.8 0.4 collective-permute-done.18
  63.2 1.4 %collective-permute-done.19 = bf16[256,128]{1,0:T(8,128)(2,1)S(1)} collective-permute-done((bf16[256,128]{1,0:T(8,128)(2,1)S(1)}, bf16[256,128]{1,0:T(8,128)(2,1)S(1)}, u32[]{:S(2)}, u32[]{:S(2)}) %collective-permute-start.19) | collective-permute-done | bytes 65568 | tf_op jit(solution)/shard_map/ppermute | solution.py:287
  64.6 0.1 multiply_convert_fusion.2.refs_0_
  64.7 1.9 %collective-permute-start.21 = (bf16[256,128]{1,0:T(8,128)(2,1)S(1)}, bf16[256,128]{1,0:T(8,128)(2,1)S(1)}, u32[]{:S(2)}, u32[]{:S(2)}) collective-permute-start(bf16[256,128]{1,0:T(8,128)(2,1)S(1)} %multiply_convert_fusion.2.refs_0_), channel_id=1, source_target_pairs={{0,16},{8,24},{16,0},{24,8},{1,17},{9,25},{17,1},{25,9},{2,18},{10... | collective-permute-start | bytes 196616 | tf_op jit(solution)/shard_map/ppermute | solution.py:287
  66.6 1.6 %collective-permute-start.22 = (bf16[256,128]{1,0:T(8,128)(2,1)S(1)}, bf16[256,128]{1,0:T(8,128)(2,1)S(1)}, u32[]{:S(2)}, u32[]{:S(2)}) collective-permute-start(bf16[256,128]{1,0:T(8,128)(2,1)S(1)} %multiply_convert_fusion.2.refs_0_), channel_id=1, source_target_pairs={{0,24},{8,16},{16,8},{24,0},{1,25},{9,17},{17,9},{25,1},{2,26},{10... | collective-permute-start | bytes 196616 | tf_op jit(solution)/shard_map/ppermute | solution.py:287
  68.2 0.1 place.1.place_ref
  68.3 0.7 collective-permute-done.20.refs_1_
  69.0 0.3 collective-permute-done.21.refs_2_
  69.3 2.5 %collective-permute-done.22.refs_3_ = bf16[256,128]{1,0:T(8,128)(2,1)S(1)} collective-permute-done((bf16[256,128]{1,0:T(8,128)(2,1)S(1)}, bf16[256,128]{1,0:T(8,128)(2,1)S(1)}, u32[]{:S(2)}, u32[]{:S(2)}) %collective-permute-start.22) | collective-permute-done | bytes 65568 | tf_op jit(solution)/shard_map/ppermute | solution.py:287
  71.8 7.5 %last.1 = (bf16[1024,128]{1,0:T(8,128)(2,1)S(1)}, f32[4096,128]{1,0:T(8,128)S(1)}) custom-call(s32[8,512]{1,0:T(8,128)S(1)} %get-tuple-element.33.plan_ref, s32[16,128]{1,0:T(8,128)S(1)} %place.1.place_ref, bf16[256,128]{1,0:T(8,128)(2,1)S(1)} %multiply_convert_fusion.2.refs_0_, bf16[256,128]{1,0:T(8,128)(2,1)S(1)} %collective-permute-done.20.refs_1_, ...), custom_call_target="tpu_custom_call" | custom-call | flops 1073741824 | bytes 8388608 | tf_op jit(solution)/shard_map/last/pallas_call | solution.py:271
  79.4 3.6 %pick.1.even_ref = f32[1024,128]{1,0:T(8,128)S(1)} custom-call(s32[16,128]{1,0:T(8,128)S(1)} %place.1.place_ref, f32[4096,128]{1,0:T(8,128)S(1)} %get-tuple-element.55.total), custom_call_target="tpu_custom_call" | custom-call | flops 214748368 | bytes 1677721 | tf_op jit(solution)/shard_map/pick/pallas_call | solution.py:271
  83.1 1.9 %collective-permute-start.30 = (bf16[256,128]{1,0:T(8,128)(2,1)S(1)}, bf16[256,128]{1,0:T(8,128)(2,1)S(1)}, u32[]{:S(2)}, u32[]{:S(2)}) collective-permute-start(bf16[256,128]{1,0:T(8,128)(2,1)S(1)} %get-tuple-element.58), channel_id=1, source_target_pairs={{0,2},{1,3},{2,0},{3,1},{4,6},{5,7},{6,4},{7,5},{8,10},{9,11},{10,... | collective-permute-start | bytes 196616 | tf_op jit(solution)/shard_map/ppermute | solution.py:287
  85.1 2.0 %collective-permute-start.31 = (bf16[256,128]{1,0:T(8,128)(2,1)S(1)}, bf16[256,128]{1,0:T(8,128)(2,1)S(1)}, u32[]{:S(2)}, u32[]{:S(2)}) collective-permute-start(bf16[256,128]{1,0:T(8,128)(2,1)S(1)} %get-tuple-element.59), channel_id=1, source_target_pairs={{0,4},{1,5},{2,6},{3,7},{4,0},{5,1},{6,2},{7,3},{8,12},{9,13},{10,... | collective-permute-start | bytes 196616 | tf_op jit(solution)/shard_map/ppermute | solution.py:287
  87.1 0.5 collective-permute-start.32
  87.6 0.1 select_reduce_fusion
  87.7 0.1 collective-permute-done.30
  87.8 5.7 %collective-permute-done.31 = bf16[256,128]{1,0:T(8,128)(2,1)S(1)} collective-permute-done((bf16[256,128]{1,0:T(8,128)(2,1)S(1)}, bf16[256,128]{1,0:T(8,128)(2,1)S(1)}, u32[]{:S(2)}, u32[]{:S(2)}) %collective-permute-start.31) | collective-permute-done | bytes 65568 | tf_op jit(solution)/shard_map/ppermute | solution.py:287
  93.5 0.1 multiply_reduce_fusion
  93.6 0.8 multiply_multiply_fusion
  (32 shorter events, 0.4 us)
Async XLA Ops:
  1.7 9.4 %collective-permute-start = (bf16[512,128]{1,0:T(8,128)(2,1)S(1)}, bf16[512,128]{1,0:T(8,128)(2,1)S(1)}, u32[]{:S(2)}, u32[]{:S(2)}) collective-permute-start(bf16[512,128]{1,0:T(8,128)(2,1)S(1)} %multiply_convert_fusion.refs_0_), channel_id=1, source_target_pairs={{0,8},{8,0},{16,24},{24,16},{1,9},{9,1},{17,25},{25,17},{2,10},{10... | collective-permute-start | bytes 393224 | tf_op jit(solution)/shard_map/ppermute | solution.py:287
  4.7 7.8 %collective-permute-start.1 = (bf16[512,128]{1,0:T(8,128)(2,1)S(1)}, bf16[512,128]{1,0:T(8,128)(2,1)S(1)}, u32[]{:S(2)}, u32[]{:S(2)}) collective-permute-start(bf16[512,128]{1,0:T(8,128)(2,1)S(1)} %multiply_convert_fusion.refs_0_), channel_id=1, source_target_pairs={{0,16},{8,24},{16,0},{24,8},{1,17},{9,25},{17,1},{25,9},{2,18},{10... | collective-permute-start | bytes 393224 | tf_op jit(solution)/shard_map/ppermute | solution.py:287
  6.3 6.3 %collective-permute-start.2 = (bf16[512,128]{1,0:T(8,128)(2,1)S(1)}, bf16[512,128]{1,0:T(8,128)(2,1)S(1)}, u32[]{:S(2)}, u32[]{:S(2)}) collective-permute-start(bf16[512,128]{1,0:T(8,128)(2,1)S(1)} %multiply_convert_fusion.refs_0_), channel_id=1, source_target_pairs={{0,24},{8,16},{16,8},{24,0},{1,25},{9,17},{17,9},{25,1},{2,26},{10... | collective-permute-start | bytes 393224 | tf_op jit(solution)/shard_map/ppermute | solution.py:287
  15.3 2.0 %collective-permute-start.3 = (bf16[2064,128]{1,0:T(8,128)(2,1)S(1)}, bf16[2064,128]{1,0:T(8,128)(2,1)S(1)}, u32[]{:S(2)}, u32[]{:S(2)}) collective-permute-start(bf16[2064,128]{1,0:T(8,128)(2,1)S(1)} %get-tuple-element.35), channel_id=1, source_target_pairs={{0,1},{1,0},{2,3},{3,2},{4,5},{5,4},{6,7},{7,6},{8,9},{9,8},{10,11... | collective-permute-start | bytes 1585160 | tf_op jit(solution)/shard_map/ppermute | solution.py:287
  17.3 12.1 %collective-permute-start.10 = (bf16[256,128]{1,0:T(8,128)(2,1)S(1)}, bf16[256,128]{1,0:T(8,128)(2,1)S(1)}, u32[]{:S(2)}, u32[]{:S(2)}) collective-permute-start(bf16[256,128]{1,0:T(8,128)(2,1)S(1)} %get-tuple-element.42), channel_id=1, source_target_pairs={{0,2},{1,3},{2,0},{3,1},{4,6},{5,7},{6,4},{7,5},{8,10},{9,11},{10,... | collective-permute-start | bytes 196616 | tf_op jit(solution)/shard_map/ppermute | solution.py:287
  20.6 8.9 %collective-permute-start.11 = (bf16[256,128]{1,0:T(8,128)(2,1)S(1)}, bf16[256,128]{1,0:T(8,128)(2,1)S(1)}, u32[]{:S(2)}, u32[]{:S(2)}) collective-permute-start(bf16[256,128]{1,0:T(8,128)(2,1)S(1)} %get-tuple-element.43), channel_id=1, source_target_pairs={{0,4},{1,5},{2,6},{3,7},{4,0},{5,1},{6,2},{7,3},{8,12},{9,13},{10,... | collective-permute-start | bytes 196616 | tf_op jit(solution)/shard_map/ppermute | solution.py:287
  22.9 6.6 %collective-permute-start.12 = (bf16[256,128]{1,0:T(8,128)(2,1)S(1)}, bf16[256,128]{1,0:T(8,128)(2,1)S(1)}, u32[]{:S(2)}, u32[]{:S(2)}) collective-permute-start(bf16[256,128]{1,0:T(8,128)(2,1)S(1)} %get-tuple-element.44), channel_id=1, source_target_pairs={{0,6},{1,7},{2,4},{3,5},{4,2},{5,3},{6,0},{7,1},{8,14},{9,15},{10,... | collective-permute-start | bytes 196616 | tf_op jit(solution)/shard_map/ppermute | solution.py:287
  24.8 7.2 %collective-permute-start.4 = (bf16[272,128]{1,0:T(8,128)(2,1)S(1)}, bf16[272,128]{1,0:T(8,128)(2,1)S(1)}, u32[]{:S(2)}, u32[]{:S(2)}) collective-permute-start(bf16[272,128]{1,0:T(8,128)(2,1)S(1)} %get-tuple-element.38), channel_id=1, source_target_pairs={{0,2},{1,3},{2,0},{3,1},{4,6},{5,7},{6,4},{7,5},{8,10},{9,11},{10,... | collective-permute-start | bytes 208904 | tf_op jit(solution)/shard_map/ppermute | solution.py:287
  26.2 7.9 %collective-permute-start.5 = (bf16[272,128]{1,0:T(8,128)(2,1)S(1)}, bf16[272,128]{1,0:T(8,128)(2,1)S(1)}, u32[]{:S(2)}, u32[]{:S(2)}) collective-permute-start(bf16[272,128]{1,0:T(8,128)(2,1)S(1)} %get-tuple-element.39), channel_id=1, source_target_pairs={{0,4},{1,5},{2,6},{3,7},{4,0},{5,1},{6,2},{7,3},{8,12},{9,13},{10,... | collective-permute-start | bytes 208904 | tf_op jit(solution)/shard_map/ppermute | solution.py:287
  29.4 6.2 %collective-permute-start.6 = (bf16[272,128]{1,0:T(8,128)(2,1)S(1)}, bf16[272,128]{1,0:T(8,128)(2,1)S(1)}, u32[]{:S(2)}, u32[]{:S(2)}) collective-permute-start(bf16[272,128]{1,0:T(8,128)(2,1)S(1)} %get-tuple-element.40), channel_id=1, source_target_pairs={{0,6},{1,7},{2,4},{3,5},{4,2},{5,3},{6,0},{7,1},{8,14},{9,15},{10,... | collective-permute-start | bytes 208904 | tf_op jit(solution)/shard_map/ppermute | solution.py:287
  29.6 8.6 %collective-permute-start.13 = (bf16[256,128]{1,0:T(8,128)(2,1)S(1)}, bf16[256,128]{1,0:T(8,128)(2,1)S(1)}, u32[]{:S(2)}, u32[]{:S(2)}) collective-permute-start(bf16[256,128]{1,0:T(8,128)(2,1)S(1)} %multiply_convert_fusion.3.refs_4_), channel_id=1, source_target_pairs={{0,8},{8,0},{16,24},{24,16},{1,9},{9,1},{17,25},{25,17},{2,10},{10... | collective-permute-start | bytes 196616 | tf_op jit(solution)/shard_map/ppermute | solution.py:287
  29.8 9.5 %collective-permute-start.14 = (bf16[256,128]{1,0:T(8,128)(2,1)S(1)}, bf16[256,128]{1,0:T(8,128)(2,1)S(1)}, u32[]{:S(2)}, u32[]{:S(2)}) collective-permute-start(bf16[256,128]{1,0:T(8,128)(2,1)S(1)} %multiply_convert_fusion.3.refs_4_), channel_id=1, source_target_pairs={{0,16},{8,24},{16,0},{24,8},{1,17},{9,25},{17,1},{25,9},{2,18},{10... | collective-permute-start | bytes 196616 | tf_op jit(solution)/shard_map/ppermute | solution.py:287
  32.0 7.3 %collective-permute-start.15 = (bf16[256,128]{1,0:T(8,128)(2,1)S(1)}, bf16[256,128]{1,0:T(8,128)(2,1)S(1)}, u32[]{:S(2)}, u32[]{:S(2)}) collective-permute-start(bf16[256,128]{1,0:T(8,128)(2,1)S(1)} %multiply_convert_fusion.3.refs_4_), channel_id=1, source_target_pairs={{0,24},{8,16},{16,8},{24,0},{1,25},{9,17},{17,9},{25,1},{2,26},{10... | collective-permute-start | bytes 196616 | tf_op jit(solution)/shard_map/ppermute | solution.py:287
  35.8 4.3 %collective-permute-start.7 = (bf16[256,128]{1,0:T(8,128)(2,1)S(1)}, bf16[256,128]{1,0:T(8,128)(2,1)S(1)}, u32[]{:S(2)}, u32[]{:S(2)}) collective-permute-start(bf16[256,128]{1,0:T(8,128)(2,1)S(1)} %multiply_convert_fusion.4.refs_0_), channel_id=1, source_target_pairs={{0,8},{8,0},{16,24},{24,16},{1,9},{9,1},{17,25},{25,17},{2,10},{10... | collective-permute-start | bytes 196616 | tf_op jit(solution)/shard_map/ppermute | solution.py:287
  35.8 4.9 %collective-permute-start.8 = (bf16[256,128]{1,0:T(8,128)(2,1)S(1)}, bf16[256,128]{1,0:T(8,128)(2,1)S(1)}, u32[]{:S(2)}, u32[]{:S(2)}) collective-permute-start(bf16[256,128]{1,0:T(8,128)(2,1)S(1)} %multiply_convert_fusion.4.refs_0_), channel_id=1, source_target_pairs={{0,16},{8,24},{16,0},{24,8},{1,17},{9,25},{17,1},{25,9},{2,18},{10... | collective-permute-start | bytes 196616 | tf_op jit(solution)/shard_map/ppermute | solution.py:287
  38.2 5.2 %collective-permute-start.9 = (bf16[256,128]{1,0:T(8,128)(2,1)S(1)}, bf16[256,128]{1,0:T(8,128)(2,1)S(1)}, u32[]{:S(2)}, u32[]{:S(2)}) collective-permute-start(bf16[256,128]{1,0:T(8,128)(2,1)S(1)} %multiply_convert_fusion.4.refs_0_), channel_id=1, source_target_pairs={{0,24},{8,16},{16,8},{24,0},{1,25},{9,17},{17,9},{25,1},{2,26},{10... | collective-permute-start | bytes 196616 | tf_op jit(solution)/shard_map/ppermute | solution.py:287
  46.1 2.0 %collective-permute-start.16 = (bf16[2048,128]{1,0:T(8,128)(2,1)S(1)}, bf16[2048,128]{1,0:T(8,128)(2,1)S(1)}, u32[]{:S(2)}, u32[]{:S(2)}) collective-permute-start(bf16[2048,128]{1,0:T(8,128)(2,1)S(1)} %get-tuple-element.46), channel_id=1, source_target_pairs={{0,1},{1,0},{2,3},{3,2},{4,5},{5,4},{6,7},{7,6},{8,9},{9,8},{10,11... | collective-permute-start | bytes 1572872 | tf_op jit(solution)/shard_map/ppermute | solution.py:287
  48.1 10.3 %collective-permute-start.23 = (bf16[256,128]{1,0:T(8,128)(2,1)S(1)}, bf16[256,128]{1,0:T(8,128)(2,1)S(1)}, u32[]{:S(2)}, u32[]{:S(2)}) collective-permute-start(bf16[256,128]{1,0:T(8,128)(2,1)S(1)} %get-tuple-element.52), channel_id=1, source_target_pairs={{0,2},{1,3},{2,0},{3,1},{4,6},{5,7},{6,4},{7,5},{8,10},{9,11},{10,... | collective-permute-start | bytes 196616 | tf_op jit(solution)/shard_map/ppermute | solution.py:287
  49.7 9.2 %collective-permute-start.24 = (bf16[256,128]{1,0:T(8,128)(2,1)S(1)}, bf16[256,128]{1,0:T(8,128)(2,1)S(1)}, u32[]{:S(2)}, u32[]{:S(2)}) collective-permute-start(bf16[256,128]{1,0:T(8,128)(2,1)S(1)} %get-tuple-element.53), channel_id=1, source_target_pairs={{0,4},{1,5},{2,6},{3,7},{4,0},{5,1},{6,2},{7,3},{8,12},{9,13},{10,... | collective-permute-start | bytes 196616 | tf_op jit(solution)/shard_map/ppermute | solution.py:287
  51.8 7.1 %collective-permute-start.25 = (bf16[256,128]{1,0:T(8,128)(2,1)S(1)}, bf16[256,128]{1,0:T(8,128)(2,1)S(1)}, u32[]{:S(2)}, u32[]{:S(2)}) collective-permute-start(bf16[256,128]{1,0:T(8,128)(2,1)S(1)} %get-tuple-element.54), channel_id=1, source_target_pairs={{0,6},{1,7},{2,4},{3,5},{4,2},{5,3},{6,0},{7,1},{8,14},{9,15},{10,... | collective-permute-start | bytes 196616 | tf_op jit(solution)/shard_map/ppermute | solution.py:287
  54.4 33.2 %copy-start = (s32[256]{0:T(256)S(1)}, s32[256]{0:T(256)}, u32[]{:S(2)}) copy-start(s32[256]{0:T(256)} %param.16) | copy-start | bytes 3076
  54.4 33.2 %copy-start.1 = (f32[16]{0:T(128)S(1)}, f32[16]{0:T(128)}, u32[]{:S(2)}) copy-start(f32[16]{0:T(128)} %param.17) | copy-start | bytes 196
  54.4 7.0 %collective-permute-start.17 = (bf16[256,128]{1,0:T(8,128)(2,1)S(1)}, bf16[256,128]{1,0:T(8,128)(2,1)S(1)}, u32[]{:S(2)}, u32[]{:S(2)}) collective-permute-start(bf16[256,128]{1,0:T(8,128)(2,1)S(1)} %get-tuple-element.49), channel_id=1, source_target_pairs={{0,2},{1,3},{2,0},{3,1},{4,6},{5,7},{6,4},{7,5},{8,10},{9,11},{10,... | collective-permute-start | bytes 196616 | tf_op jit(solution)/shard_map/ppermute | solution.py:287
  55.3 7.8 %collective-permute-start.18 = (bf16[256,128]{1,0:T(8,128)(2,1)S(1)}, bf16[256,128]{1,0:T(8,128)(2,1)S(1)}, u32[]{:S(2)}, u32[]{:S(2)}) collective-permute-start(bf16[256,128]{1,0:T(8,128)(2,1)S(1)} %get-tuple-element.50), channel_id=1, source_target_pairs={{0,4},{1,5},{2,6},{3,7},{4,0},{5,1},{6,2},{7,3},{8,12},{9,13},{10,... | collective-permute-start | bytes 196616 | tf_op jit(solution)/shard_map/ppermute | solution.py:287
  58.4 6.2 %collective-permute-start.19 = (bf16[256,128]{1,0:T(8,128)(2,1)S(1)}, bf16[256,128]{1,0:T(8,128)(2,1)S(1)}, u32[]{:S(2)}, u32[]{:S(2)}) collective-permute-start(bf16[256,128]{1,0:T(8,128)(2,1)S(1)} %get-tuple-element.51), channel_id=1, source_target_pairs={{0,6},{1,7},{2,4},{3,5},{4,2},{5,3},{6,0},{7,1},{8,14},{9,15},{10,... | collective-permute-start | bytes 196616 | tf_op jit(solution)/shard_map/ppermute | solution.py:287
  59.0 7.7 %collective-permute-start.26 = (bf16[256,128]{1,0:T(8,128)(2,1)S(1)}, bf16[256,128]{1,0:T(8,128)(2,1)S(1)}, u32[]{:S(2)}, u32[]{:S(2)}) collective-permute-start(bf16[256,128]{1,0:T(8,128)(2,1)S(1)} %multiply_convert_fusion.1.refs_4_), channel_id=1, source_target_pairs={{0,8},{8,0},{16,24},{24,16},{1,9},{9,1},{17,25},{25,17},{2,10},{10... | collective-permute-start | bytes 196616 | tf_op jit(solution)/shard_map/ppermute | solution.py:287
  59.1 9.2 %collective-permute-start.27 = (bf16[256,128]{1,0:T(8,128)(2,1)S(1)}, bf16[256,128]{1,0:T(8,128)(2,1)S(1)}, u32[]{:S(2)}, u32[]{:S(2)}) collective-permute-start(bf16[256,128]{1,0:T(8,128)(2,1)S(1)} %multiply_convert_fusion.1.refs_4_), channel_id=1, source_target_pairs={{0,16},{8,24},{16,0},{24,8},{1,17},{9,25},{17,1},{25,9},{2,18},{10... | collective-permute-start | bytes 196616 | tf_op jit(solution)/shard_map/ppermute | solution.py:287
  61.4 7.0 %collective-permute-start.28 = (bf16[256,128]{1,0:T(8,128)(2,1)S(1)}, bf16[256,128]{1,0:T(8,128)(2,1)S(1)}, u32[]{:S(2)}, u32[]{:S(2)}) collective-permute-start(bf16[256,128]{1,0:T(8,128)(2,1)S(1)} %multiply_convert_fusion.1.refs_4_), channel_id=1, source_target_pairs={{0,24},{8,16},{16,8},{24,0},{1,25},{9,17},{17,9},{25,1},{2,26},{10... | collective-permute-start | bytes 196616 | tf_op jit(solution)/shard_map/ppermute | solution.py:287
  64.7 4.3 %collective-permute-start.20 = (bf16[256,128]{1,0:T(8,128)(2,1)S(1)}, bf16[256,128]{1,0:T(8,128)(2,1)S(1)}, u32[]{:S(2)}, u32[]{:S(2)}) collective-permute-start(bf16[256,128]{1,0:T(8,128)(2,1)S(1)} %multiply_convert_fusion.2.refs_0_), channel_id=1, source_target_pairs={{0,8},{8,0},{16,24},{24,16},{1,9},{9,1},{17,25},{25,17},{2,10},{10... | collective-permute-start | bytes 196616 | tf_op jit(solution)/shard_map/ppermute | solution.py:287
  64.7 4.5 %collective-permute-start.21 = (bf16[256,128]{1,0:T(8,128)(2,1)S(1)}, bf16[256,128]{1,0:T(8,128)(2,1)S(1)}, u32[]{:S(2)}, u32[]{:S(2)}) collective-permute-start(bf16[256,128]{1,0:T(8,128)(2,1)S(1)} %multiply_convert_fusion.2.refs_0_), channel_id=1, source_target_pairs={{0,16},{8,24},{16,0},{24,8},{1,17},{9,25},{17,1},{25,9},{2,18},{10... | collective-permute-start | bytes 196616 | tf_op jit(solution)/shard_map/ppermute | solution.py:287
  66.6 5.2 %collective-permute-start.22 = (bf16[256,128]{1,0:T(8,128)(2,1)S(1)}, bf16[256,128]{1,0:T(8,128)(2,1)S(1)}, u32[]{:S(2)}, u32[]{:S(2)}) collective-permute-start(bf16[256,128]{1,0:T(8,128)(2,1)S(1)} %multiply_convert_fusion.2.refs_0_), channel_id=1, source_target_pairs={{0,24},{8,16},{16,8},{24,0},{1,25},{9,17},{17,9},{25,1},{2,26},{10... | collective-permute-start | bytes 196616 | tf_op jit(solution)/shard_map/ppermute | solution.py:287
  79.3 3.7 %collective-permute-start.29 = (bf16[1024,128]{1,0:T(8,128)(2,1)S(1)}, bf16[1024,128]{1,0:T(8,128)(2,1)S(1)}, u32[]{:S(2)}, u32[]{:S(2)}) collective-permute-start(bf16[1024,128]{1,0:T(8,128)(2,1)S(1)} %get-tuple-element.56), channel_id=1, source_target_pairs={{0,1},{1,0},{2,3},{3,2},{4,5},{5,4},{6,7},{7,6},{8,9},{9,8},{10,11... | collective-permute-start | bytes 786440 | tf_op jit(solution)/shard_map/ppermute | solution.py:287
  83.1 4.7 %collective-permute-start.30 = (bf16[256,128]{1,0:T(8,128)(2,1)S(1)}, bf16[256,128]{1,0:T(8,128)(2,1)S(1)}, u32[]{:S(2)}, u32[]{:S(2)}) collective-permute-start(bf16[256,128]{1,0:T(8,128)(2,1)S(1)} %get-tuple-element.58), channel_id=1, source_target_pairs={{0,2},{1,3},{2,0},{3,1},{4,6},{5,7},{6,4},{7,5},{8,10},{9,11},{10,... | collective-permute-start | bytes 196616 | tf_op jit(solution)/shard_map/ppermute | solution.py:287
  85.1 8.4 %collective-permute-start.31 = (bf16[256,128]{1,0:T(8,128)(2,1)S(1)}, bf16[256,128]{1,0:T(8,128)(2,1)S(1)}, u32[]{:S(2)}, u32[]{:S(2)}) collective-permute-start(bf16[256,128]{1,0:T(8,128)(2,1)S(1)} %get-tuple-element.59), channel_id=1, source_target_pairs={{0,4},{1,5},{2,6},{3,7},{4,0},{5,1},{6,2},{7,3},{8,12},{9,13},{10,... | collective-permute-start | bytes 196616 | tf_op jit(solution)/shard_map/ppermute | solution.py:287
  87.1 6.4 %collective-permute-start.32 = (bf16[256,128]{1,0:T(8,128)(2,1)S(1)}, bf16[256,128]{1,0:T(8,128)(2,1)S(1)}, u32[]{:S(2)}, u32[]{:S(2)}) collective-permute-start(bf16[256,128]{1,0:T(8,128)(2,1)S(1)} %get-tuple-element.60), channel_id=1, source_target_pairs={{0,6},{1,7},{2,4},{3,5},{4,2},{5,3},{6,0},{7,1},{8,14},{9,15},{10,... | collective-permute-start | bytes 196616 | tf_op jit(solution)/shard_map/ppermute | solution.py:287

commit v3 on v2

--- a/solution.py
+++ b/solution.py
@@ -8,8 +8,7 @@
 from jax.sharding import PartitionSpec as P
 
 HOPS = 3
-HALVES = 2
-CHUNKS = 2 * HALVES
+CHUNKS = 2
 GROUP = 4
 UNROLL = 4
 UNPICK = 16
@@ -56,17 +55,14 @@
         copy.wait()
     slots = tile_row_ref.shape[1]
     length = plan_ref.shape[1]
-    my_row, my_col = lax.axis_index("row"), lax.axis_index("col")
+    my_core = lax.axis_index("col") % 2
     chunk_tiles = row_tiles // CHUNKS
-    per_half = per_group // HALVES
     row = tile_row_ref[...]
-    rel = (row // per_group) ^ my_col
-    chunk = (1 - rel % 2) * HALVES + (row % per_group) // per_half
-    order = chunk * chunk_tiles + (rel // 2) * per_half + row % per_half
+    group = row // per_group
+    chunk = 1 - (group ^ my_core) % 2
+    order = chunk * chunk_tiles + group // 2 * per_group + row % per_group
     order = jnp.where(iota((1, slots), 1) < count_ref[0, 0], order, row_tiles).astype(jnp.float32)
-    col = tile_col_ref[...]
-    source = ((col // per_group) ^ my_row) * per_group + col % per_group
-    entry = (iota((1, slots), 1) * SHIFT + source).astype(jnp.float32)
+    entry = (iota((1, slots), 1) * SHIFT + tile_col_ref[...]).astype(jnp.float32)
     order_c = to_column(order)
     entry_c = to_column(entry)
     same = jnp.where((order_c == order) & (iota((slots, slots), 1) < iota((slots, slots), 0)), 1.0, 0.0)
@@ -107,16 +103,6 @@
     load.wait()
 
 
-def fill_state(pieces, state, halves, tile):
-    rows = pieces[0].shape[0]
-    devices = (state.shape[0] - tile) // (rows * halves)
-    for i, piece in enumerate(pieces):
-        half, device = halves - 1 - i // devices, i % devices
-        at = (device * halves + half) * rows
-        state[at : at + rows, :] = piece[...]
-    state[len(pieces) * rows :, :] = jnp.zeros((tile, state.shape[1]), state.dtype)
-
-
 def multiply(plan_ref, weights_ref, state, total, chunk, chunks, chunk_tiles):
     tile = weights_ref.shape[1]
     total[...] = jnp.zeros_like(total)
@@ -145,69 +131,65 @@
     lax.fori_loop(plan_ref[2, chunk], plan_ref[2, chunk + chunks], turn, 0)
 
 
-def odd_kernel(pieces, halves, plan_ref, *refs):
-    weights_ref, extra_refs = refs[pieces], refs[pieces + 1 : -3]
-    odd_ref, state, total = refs[-3:]
+def fill_state(gathered_ref, state):
+    rows = gathered_ref.shape[0]
+    state[0:rows, :] = gathered_ref[...]
+    state[rows:, :] = jnp.zeros((state.shape[0] - rows, state.shape[1]), state.dtype)
+
+
+def odd_kernel(plan_ref, gathered_ref, weights_ref, *refs):
+    extra_refs, (odd_ref, state, total) = refs[:-3], refs[-3:]
     rows = total.shape[0]
-    fill_state(refs[:pieces], state, halves, weights_ref.shape[1])
-    multiply(plan_ref, weights_ref, state, total, 0, HALVES, 0)
+    fill_state(gathered_ref, state)
+    multiply(plan_ref, weights_ref, state, total, 0, 1, 0)
     odd_ref[0:rows, :] = total[...].astype(odd_ref.dtype)
     for extra in extra_refs:
         odd_ref[rows:, :] = extra[...]
 
 
-def even0_kernel(plan_ref, state, weights_ref, even_ref):
-    multiply(plan_ref, weights_ref, state, even_ref, HALVES, 1, even_ref.shape[0] // weights_ref.shape[1])
-
-
-def even1_kernel(chips, plan_ref, state, weights_ref, after_ref, other_ref, *refs):
-    extra_refs, own_ref, sent_refs, total = refs[: -chips - 1], refs[-chips - 1], refs[-chips:-1], refs[-1]
-    rows = total.shape[0]
-    multiply(plan_ref, weights_ref, state, total, HALVES + 1, 1, rows // weights_ref.shape[1])
-    add_cores(chips, rows, total, other_ref, own_ref, sent_refs)
+def even_kernel(plan_ref, state, weights_ref, even_ref):
+    multiply(plan_ref, weights_ref, state, even_ref, 1, 1, even_ref.shape[0] // weights_ref.shape[1])
+
+
+def merge_kernel(chips, even_ref, other_ref, *refs):
+    extra_refs, sent_ref = refs[:-1], refs[-1]
+    rows, block = even_ref.shape[0] // chips, sent_ref.shape[0] // chips
+    for k in range(chips):
+        part = even_ref[pl.ds(k * rows, rows), :] + other_ref[pl.ds(k * rows, rows), :].astype(jnp.float32)
+        sent_ref[k * block : k * block + rows, :] = part.astype(sent_ref.dtype)
     for extra in extra_refs:
         size = extra.shape[0]
-        far = other_ref[other_ref.shape[0] - size :, :].astype(jnp.float32)
-        both = (extra[...].astype(jnp.float32) + pltpu.roll(far, size // 2, 0)).astype(extra.dtype)
-        for sent in sent_refs:
-            sent[own_ref.shape[0] :, :] = both
-
-
-def add_cores(chips, offset, even_ref, other_ref, own_ref, sent_refs):
-    rows = own_ref.shape[0]
-    for k, out in enumerate((own_ref, *sent_refs)):
-        other = other_ref[pl.ds(offset + k * rows, rows), :].astype(jnp.float32)
-        out[0:rows, :] = (even_ref[pl.ds(k * rows, rows), :] + other).astype(out.dtype)
-
-
-def merge_kernel(chips, even_ref, other_ref, own_ref, *sent_refs):
-    add_cores(chips, 0, even_ref, other_ref, own_ref, sent_refs)
-
-
-def place_kernel(chips, rows_here, block_rows, id_rows, mine_ref, other_ref, *refs):
-    far_refs, place_ref = refs[:-1], refs[-1]
-    my_col = lax.axis_index("col")
-    half = rows_here // HALVES
+        far = other_ref[chips * rows :, :].astype(jnp.float32)
+        both = (extra[...].astype(jnp.float32) + pltpu.roll(far, size // 2, 0)).astype(sent_ref.dtype)
+        for k in range(chips):
+            sent_ref[k * block + rows : (k + 1) * block, :] = both
+
+
+def state_kernel(chips, came_ref, square_ref, state_ref):
+    rows, block = square_ref.shape[0], came_ref.shape[0] // chips
+    total = came_ref[0:rows, :].astype(jnp.float32)
+    for k in range(1, chips):
+        total = total + came_ref[k * block : k * block + rows, :].astype(jnp.float32)
+    state = (square_ref[...] * total).astype(state_ref.dtype)
+    for r in range(state_ref.shape[0] // rows):
+        state_ref[r * rows : (r + 1) * rows, :] = state
+
+
+def place_kernel(chips, rows_here, block_rows, id_rows, extra, came_ref, place_ref):
+    my_core = lax.axis_index("col") % 2
     chunk_rows = block_rows // CHUNKS
-    extra = mine_ref.shape[0]
+    block = came_ref.shape[0] // chips
 
     def places(rows):
         ids = (rows[:id_rows] * BYTE + rows[id_rows : 2 * id_rows]).astype(jnp.int32)
-        rel = (ids // rows_here) ^ my_col
-        chunk = (1 - rel % 2) * HALVES + ids % rows_here // half
-        return chunk * chunk_rows + rel // 2 * half + ids % half
-
-    def tail(ref):
-        return ref[ref.shape[0] - extra :, :].astype(jnp.float32)
-
-    even, odd = [mine_ref[...].astype(jnp.float32)], [tail(other_ref)]
-    for ref in far_refs:
-        rows = tail(ref)
-        even.append(rows)
-        odd.append(pltpu.roll(rows, extra - extra // 2, 0))
+        group = ids // rows_here
+        return (1 - (group ^ my_core) % 2) * chunk_rows + group // 2 * rows_here + ids % rows_here
+
     for k in range(chips):
-        place_ref[k * id_rows : (k + 1) * id_rows, :] = places(odd[k])
-        place_ref[(chips + k) * id_rows : (chips + k + 1) * id_rows, :] = places(even[k])
+        rows = came_ref[(k + 1) * block - extra : (k + 1) * block, :].astype(jnp.float32)
+        odd = pltpu.roll(rows, extra - extra // 2, 0)
+        place_ref[k * id_rows : (k + 1) * id_rows, :] = places(odd)
+        place_ref[(chips + k) * id_rows : (chips + k + 1) * id_rows, :] = places(rows)
 
 
 def pick_rows(place_ref, part, total, picked, out):
@@ -226,10 +208,8 @@
         out[...] = picked[...].astype(out.dtype)
 
 
-def last_kernel(pieces, halves, plan_ref, place_ref, *refs):
-    weights_ref = refs[pieces]
-    odd_ref, total, state, picked = refs[pieces + 1 :]
-    fill_state(refs[:pieces], state, halves, weights_ref.shape[1])
+def last_kernel(plan_ref, place_ref, gathered_ref, weights_ref, odd_ref, total, state, picked):
+    fill_state(gathered_ref, state)
     multiply(plan_ref, weights_ref, state, total, 0, CHUNKS, 0)
     pick_rows(place_ref, 0, total, picked, odd_ref)
 
@@ -249,7 +229,6 @@
     block_rows = ncols * rows_here
     row_tiles = block_rows // tile
     per_group = rows_here // tile
-    half_here = rows_here // HALVES
     chunk_rows = block_rows // CHUNKS
     zero_tile = nrows * per_group
     new_here = new_rows.shape[0]
@@ -283,18 +262,20 @@
             name=name,
         )(*args)
 
-    def swap(array, axis, size, mask):
-        return lax.ppermute(array, axis, [(i, i ^ mask) for i in range(size)])
-
     def swap_cores(odd):
-        return swap(odd, "col", ncols, 1)
-
-    def spread(state):
-        return [state] + [swap(state, "row", nrows, k) for k in range(1, nrows)]
+        return lax.ppermute(odd, "col", [(i, i ^ 1) for i in range(ncols)])
+
+    def to_chips(blocks):
+        cores = [[2 * z + core for z in range(chips)] for core in range(2)]
+        return lax.all_to_all(blocks, "col", 0, 0, axis_index_groups=cores, tiled=True)
+
+    def spread(copies):
+        return lax.all_to_all(copies, "row", 0, 0, tiled=True)
 
     scale = lax.rsqrt(degree.astype(f32))
     state = (scale[:, None] * embed.astype(f32)).astype(bf16)
-    pieces = spread(state)
+    gathered = spread(jnp.tile(state, (nrows, 1)))
+    square = jnp.broadcast_to((scale * scale)[:, None], (rows_here, width))
 
     plan, weights = call(
         functools.partial(plan_kernel, row_tiles, per_group, zero_tile),
@@ -316,77 +297,59 @@
 
     state_shape = ((zero_tile + 1) * tile, width)
 
-    def sums_shape(rows, more=0):
-        return [array((rows, width), f32)] + [array((rows + more, width), bf16)] * (chips - 1)
-
-    def send(sent):
-        return [swap(part, "col", ncols, 2 * k) for k, part in enumerate(sent, 1)]
-
-    def merge(even, other):
-        own, *sent = call(
-            functools.partial(merge_kernel, chips), "merge", sums_shape(even.shape[0] // chips), (even, other)
-        )
-        return own, send(sent)
-
-    def add(own, came):
-        for part in came:
-            own = own + part[: own.shape[0]].astype(f32)
-        return own
+    def collect(even, other, extra=()):
+        more = sum(e.shape[0] for e in extra)
+        sent = call(
+            functools.partial(merge_kernel, chips),
+            "merge",
+            array((even.shape[0] + chips * more, width), bf16),
+            (even, other, *extra),
+        )
+        return to_chips(sent)
 
     for hop in range(HOPS - 1):
         extra = (mine,) if hop == 0 else ()
         odd, held = call(
-            functools.partial(odd_kernel, len(pieces), len(pieces) // nrows),
+            odd_kernel,
             "odd",
-            [
-                array((HALVES * chunk_rows + len(extra) * id_block, width), bf16),
-                array(state_shape, bf16),
-            ],
-            (plan, *pieces, weights, *extra),
-            scalars=1,
-            scratch=[pltpu.VMEM((HALVES * chunk_rows, width), f32)],
-            turns=0.5,
-        )
-        other = swap_cores(odd)
-        even0 = call(
-            even0_kernel, "even0", array((chunk_rows, width), f32), (plan, held, weights), scalars=1, turns=0.25
-        )
-        own0, came0 = merge(even0, other)
-        own1, *sent1 = call(
-            functools.partial(even1_kernel, chips),
-            "even1",
-            sums_shape(half_here, len(extra) * id_block),
-            (plan, held, weights, own0, other, *extra),
+            [array((chunk_rows + len(extra) * id_block, width), bf16), array(state_shape, bf16)],
+            (plan, gathered, weights, *extra),
             scalars=1,
             scratch=[pltpu.VMEM((chunk_rows, width), f32)],
-            turns=0.25,
-        )
-        came1 = send(sent1)
+            turns=0.5,
+        )
+        other = swap_cores(odd)
+        even = call(
+            even_kernel, "even", array((chunk_rows, width), f32), (plan, held, weights), scalars=1, turns=0.5
+        )
+        came = collect(even, other, extra)
         if hop == 0:
             place = call(
-                functools.partial(place_kernel, chips, rows_here, block_rows, id_rows),
+                functools.partial(place_kernel, chips, rows_here, block_rows, id_rows, id_block),
                 "place",
                 array((2 * chips * id_rows, LANES), jnp.int32),
-                (mine, other, *came1),
+                (came,),
             )
-        parts = {}
-        for half, (own, came) in reversed(tuple(enumerate(((own0, came0), (own1, came1))))):
-            here = scale[half * half_here : (half + 1) * half_here]
-            parts[half] = spread(((here * here)[:, None] * add(own, came)).astype(bf16))
-        pieces = [parts[half][r] for half in reversed(range(HALVES)) for r in range(nrows)]
+        copies = call(
+            functools.partial(state_kernel, chips),
+            "state",
+            array((nrows * rows_here, width), bf16),
+            (came, square),
+        )
+        gathered = spread(copies)
 
     odd, total = call(
-        functools.partial(last_kernel, len(pieces), len(pieces) // nrows),
+        last_kernel,
         "last",
         [array((chips * new_here, width), bf16), array((block_rows, width), f32)],
-        (plan, place, *pieces, weights),
+        (plan, place, gathered, weights),
         scalars=2,
         scratch=[pltpu.VMEM(state_shape, bf16), pltpu.VMEM((chips * new_here, width), f32)],
         turns=1.0,
     )
     other = swap_cores(odd)
     even = call(pick_kernel, "pick", array((chips * new_here, width), f32), (place, total), scalars=1, turns=0.2)
-    picked = add(*merge(even, other))
+    picked = jnp.sum(collect(even, other).reshape(chips, new_here, width).astype(f32), axis=0)
     buckets = jnp.arange(bucket_norm.shape[0], dtype=jnp.int32)
     target = jnp.sum(
         jnp.where(new_bucket[:, None] == buckets[None, :], bucket_norm[None, :], jnp.float32(0.0)),

time: 95 us -> 125 us (1.32)
  blocking collectives: 0 us -> 52 us
  starting transfers between devices: 43.2 us -> 13.7 us
  local copies, waits for them, and re-layouts: 0.01 us -> 11 us
  Pallas kernels: 27.4 us -> 24.8 us
    all_to_all x0 -> x3, blocking collectives: none -> 52 us  [the longest x2 39.3 us: to_chips(): lax.all_to_all(blocks, 'col', 0, 0, axis_index_groups=cores, tiled=True)]
    ppermute x33 -> x3, starting transfers between devices: 43.2 us -> 1.24 us  [swap_cores(): return lax.ppermute(odd, 'col', [(i, i ^ 1) for i in range(ncols)])]
    ppermute x33 -> x3, waiting for transfers between devices: 19.1 us -> 0.01 us  [swap_cores(): return lax.ppermute(odd, 'col', [(i, i ^ 1) for i in range(ncols)])]
    all_to_all x0 -> x3, waiting for transfers between devices: none -> 17.9 us  [the longest x1 9.4 us: to_chips(): lax.all_to_all(blocks, 'col', 0, 0, axis_index_groups=cores, tiled=True)]
    all_to_all x0 -> x3, starting transfers between devices: none -> 12.5 us  [the longest x2 9.07 us: spread(): return lax.all_to_all(copies, 'row', 0, 0, tiled=True)]
    unnamed x4 -> x16, local copies, waits for them, and re-layouts: 0.01 us -> 10 us
    pallas_call x13, Pallas kernels: 27.4 us -> 24.8 us  [call(): pl.pallas_call(kernel, out_shape=out_shape, grid_spec=pltpu.PrefetchScala...]
  transfers between devices with their start and end apart: 33 -> 6, of which waited for: 15 -> 3; matrix products, arithmetic and copies ran while one was open for 1% -> 0% of each run, Pallas kernels for 15% -> 10%
where the time goes in v3:
time: 125 us; the launch traced here: 123 us
  blocking collectives  52 us (42%)
  Pallas kernels  24.8 us (20%)
  waiting for transfers between devices  18 us (14%)
  starting transfers between devices  13.7 us (11%)
  local copies, waits for them, and re-layouts  11 us (9%)
  other arithmetic  2.79 us (2%)
    all_to_all x2, blocking collectives, to_chips(): lax.all_to_all(blocks, 'col', 0, 0, axis_index_groups=cores, tiled=True)  39.3 us
    pallas_call x13, Pallas kernels, call(): pl.pallas_call(kernel, out_shape=out_shape, grid_spec=pltpu.PrefetchScala...  24.8 us
    all_to_all x1, blocking collectives, spread(): return lax.all_to_all(copies, 'row', 0, 0, tiled=True)  12.7 us
    unnamed x16, local copies, waits for them, and re-layouts  10 us
    all_to_all x1, waiting for transfers between devices, to_chips(): lax.all_to_all(blocks, 'col', 0, 0, axis_index_groups=cores, tiled=True)  9.4 us
    all_to_all x2, starting transfers between devices, spread(): return lax.all_to_all(copies, 'row', 0, 0, tiled=True)  9.07 us
    all_to_all x2, waiting for transfers between devices, spread(): return lax.all_to_all(copies, 'row', 0, 0, tiled=True)  8.54 us
    all_to_all x1, starting transfers between devices, to_chips(): lax.all_to_all(blocks, 'col', 0, 0, axis_index_groups=cores, tiled=True)  3.4 us
  transfers between devices with their start and end apart: 6, of which 3 were waited for; matrix products, arithmetic and copies ran while one was open for 0% of the time, Pallas kernels for 10%

profile of v3, /device:TPU:0, one launch (start us, length us, event | category | flops | bytes accessed | tf_op | source)
XLA Modules:
  0.0 123.2 jit_solution(5953374122843574524)
XLA Ops:
  0.0 0.0 copy-start.3
  0.0 0.7 fusion.5
  0.7 1.0 multiply_convert_fusion
  1.7 0.9 tile.2
  2.6 5.2 %all-to-all-start = ((bf16[4,512,128]{2,1,0:T(8,128)(2,1)}), bf16[4,512,128]{2,1,0:T(8,128)(2,1)S(1)}, u32[]{:S(2)}, u32[]{:S(2)}) async-start(bf16[4,512,128]{2,1,0:T(8,128)(2,1)} %tile.2), calls=%async_computation | async-start | bytes 1048576 | tf_op jit(solution)/shard_map/all_to_all | solution.py:273
  8.5 3.4 %plan.1 = (s32[8,512]{1,0:T(8,128)S(1)}, bf16[256,128,128]{2,1,0:T(8,128)(2,1)S(1)}) custom-call(s32[1,1]{1,0:T(1,128)S(6)} %copy.10.count_ref, s32[1,256]{1,0:T(1,128)} %bitcast.45, s32[1,256]{1,0:T(1,128)} %bitcast.46, bf16[256,128,128]{2,1,0:T(8,128)(2,1)} %bitcast.44), custom_call_target="tpu_custom_call" | custom-call | tf_op jit(solution)/shard_map/plan/pallas_call | solution.py:250
  11.9 0.0 copy-start
  11.9 3.2 %copy-done = bf16[256,128,128]{2,1,0:T(8,128)(2,1)} copy-done((bf16[256,128,128]{2,1,0:T(8,128)(2,1)}, bf16[256,128,128]{2,1,0:T(8,128)(2,1)S(1)}, u32[]{:S(2)}) %copy-start) | copy-done | bytes 8388632
  15.1 0.0 copy-done.3
  15.2 0.6 all-to-all-done
  15.8 0.0 copy-start.1
  15.8 3.4 %copy-done.1 = bf16[256,128,128]{2,1,0:T(8,128)(2,1)S(1)} copy-done((bf16[256,128,128]{2,1,0:T(8,128)(2,1)S(1)}, bf16[256,128,128]{2,1,0:T(8,128)(2,1)}, u32[]{:S(2)}) %copy-start.1) | copy-done | bytes 8388632
  19.2 2.2 %odd.2 = (bf16[2064,128]{1,0:T(8,128)(2,1)S(1)}, bf16[2176,128]{1,0:T(8,128)(2,1)S(1)}) custom-call(s32[8,512]{1,0:T(8,128)S(1)} %get-tuple-element.13.plan_ref, bf16[2048,128]{1,0:T(8,128)(2,1)S(1)} %bitcast.38, bf16[256,128,128]{2,1,0:T(8,128)(2,1)S(1)} %copy-done.1, bf16[16,128]{1,0:T(8,128)(2,1)S(1)} %fusion.2.refs_0_), custom_call_target="tpu_custom_call" | custom-call | flops 536870912 | bytes 4194304 | tf_op jit(solution)/shard_map/odd/pallas_call | solution.py:250
  21.4 0.0 slice-start
  21.4 0.1 collective-permute-start
  21.5 0.0 slice-start.1
  21.5 2.4 %even.2.even_ref = f32[2048,128]{1,0:T(8,128)S(1)} custom-call(s32[8,512]{1,0:T(8,128)S(1)} %get-tuple-element.13.plan_ref, bf16[2176,128]{1,0:T(8,128)(2,1)S(1)} %get-tuple-element.15.state, bf16[256,128,128]{2,1,0:T(8,128)(2,1)S(1)} %copy-done.1), custom_call_target="tpu_custom_call" | custom-call | flops 536870912 | bytes 4194304 | tf_op jit(solution)/shard_map/even/pallas_call | solution.py:250
  23.9 0.0 collective-permute-done.other_ref
  23.9 0.1 merge.3
  24.0 20.8 %all_to_all.61 = bf16[4,528,128]{2,1,0:T(8,128)(2,1)S(1)} all-to-all(bf16[4,528,128]{2,1,0:T(8,128)(2,1)S(1)} %bitcast.37), channel_id=1, replica_groups={{0,2,4,6},{1,3,5,7},{8,10,12,14},{9,11,13,15},{16,18,20,22},{17,19,21,2..., dimensions={0} | all-to-all | bytes 1081344 | tf_op jit(solution)/shard_map/all_to_all | solution.py:270
  44.7 0.1 broadcast_in_dim.16.square_ref
  44.9 0.1 state.2
  44.9 12.7 %all_to_all.62 = bf16[4,512,128]{2,1,0:T(8,128)(2,1)S(1)} all-to-all(bf16[4,512,128]{2,1,0:T(8,128)(2,1)S(1)} %bitcast.43), channel_id=1, replica_groups=mesh['row'=4,'col'=8] {'row'}, dimensions={0} | all-to-all | bytes 1048576 | tf_op jit(solution)/shard_map/all_to_all | solution.py:273
  57.7 0.0 slice-done
  57.7 0.0 slice-done.1
  57.7 2.2 %odd.3 = (bf16[2048,128]{1,0:T(8,128)(2,1)S(1)}, bf16[2176,128]{1,0:T(8,128)(2,1)S(1)}) custom-call(s32[8,512]{1,0:T(8,128)S(1)} %get-tuple-element.13.plan_ref, bf16[2048,128]{1,0:T(8,128)(2,1)S(1)} %bitcast.40, bf16[256,128,128]{2,1,0:T(8,128)(2,1)S(1)} %bitcast.34), custom_call_target="tpu_custom_call" | custom-call | flops 536870912 | bytes 4194304 | tf_op jit(solution)/shard_map/odd/pallas_call | solution.py:250
  59.9 0.1 collective-permute-start.1
  60.0 2.4 %even.3.even_ref = f32[2048,128]{1,0:T(8,128)S(1)} custom-call(s32[8,512]{1,0:T(8,128)S(1)} %get-tuple-element.13.plan_ref, bf16[2176,128]{1,0:T(8,128)(2,1)S(1)} %get-tuple-element.17.state, bf16[256,128,128]{2,1,0:T(8,128)(2,1)S(1)} %bitcast.34), custom_call_target="tpu_custom_call" | custom-call | flops 536870912 | bytes 4194304 | tf_op jit(solution)/shard_map/even/pallas_call | solution.py:250
  62.3 0.0 collective-permute-done.1.other_ref
  62.3 0.1 merge.4
  62.4 0.0 copy-start.4
  62.4 0.0 copy-start.5
  62.5 18.5 %all_to_all.63 = bf16[4,512,128]{2,1,0:T(8,128)(2,1)S(1)} all-to-all(bf16[4,512,128]{2,1,0:T(8,128)(2,1)S(1)} %bitcast.42), channel_id=1, replica_groups={{0,2,4,6},{1,3,5,7},{8,10,12,14},{9,11,13,15},{16,18,20,22},{17,19,21,2..., dimensions={0} | all-to-all | bytes 1048576 | tf_op jit(solution)/shard_map/all_to_all | solution.py:270
  81.0 0.9 state.3
  81.9 3.9 %all-to-all-start.4 = ((bf16[4,512,128]{2,1,0:T(8,128)(2,1)}), bf16[4,512,128]{2,1,0:T(8,128)(2,1)S(1)}, u32[]{:S(2)}, u32[]{:S(2)}) async-start(bf16[4,512,128]{2,1,0:T(8,128)(2,1)} %bitcast.11), calls=%async_computation.4 | async-start | bytes 1048576 | tf_op jit(solution)/shard_map/all_to_all | solution.py:273
  85.8 0.1 place.1.place_ref
  85.9 7.9 %all-to-all-done.4 = bf16[4,512,128]{2,1,0:T(8,128)(2,1)S(1)} async-done(((bf16[4,512,128]{2,1,0:T(8,128)(2,1)}), bf16[4,512,128]{2,1,0:T(8,128)(2,1)S(1)}, u32[]{:S(2)}, u32[]{:S(2)}) %all-to-all-start.4) | async-done | bytes 524320 | tf_op jit(solution)/shard_map/all_to_all | solution.py:273
  93.8 0.0 copy-start.2
  93.8 3.4 %copy-done.2 = bf16[256,128,128]{2,1,0:T(8,128)(2,1)S(1)} copy-done((bf16[256,128,128]{2,1,0:T(8,128)(2,1)S(1)}, bf16[256,128,128]{2,1,0:T(8,128)(2,1)}, u32[]{:S(2)}) %copy-start.2) | copy-done | bytes 8388632
  97.1 6.6 %last.1 = (bf16[1024,128]{1,0:T(8,128)(2,1)S(1)}, f32[4096,128]{1,0:T(8,128)S(1)}) custom-call(s32[8,512]{1,0:T(8,128)S(1)} %get-tuple-element.13.plan_ref, s32[16,128]{1,0:T(8,128)S(1)} %place.1.place_ref, bf16[2048,128]{1,0:T(8,128)(2,1)S(1)} %bitcast.39, bf16[256,128,128]{2,1,0:T(8,128)(2,1)S(1)} %copy-done.2), custom_call_target="tpu_custom_call" | custom-call | flops 1073741824 | bytes 8388608 | tf_op jit(solution)/shard_map/last/pallas_call | solution.py:250
  103.8 1.1 collective-permute-start.2
  104.9 3.6 %pick.1.even_ref = f32[1024,128]{1,0:T(8,128)S(1)} custom-call(s32[16,128]{1,0:T(8,128)S(1)} %place.1.place_ref, f32[4096,128]{1,0:T(8,128)S(1)} %get-tuple-element.19.total), custom_call_target="tpu_custom_call" | custom-call | flops 214748368 | bytes 1677721 | tf_op jit(solution)/shard_map/pick/pallas_call | solution.py:250
  108.5 0.0 collective-permute-done.2.other_ref
  108.5 0.8 merge.5
  109.3 3.4 %all-to-all-start.5 = ((bf16[4,256,128]{2,1,0:T(8,128)(2,1)}), bf16[4,256,128]{2,1,0:T(8,128)(2,1)S(1)}, u32[]{:S(2)}, u32[]{:S(2)}) async-start(bf16[4,256,128]{2,1,0:T(8,128)(2,1)} %bitcast.13), calls=%async_computation.5 | async-start | bytes 524288 | tf_op jit(solution)/shard_map/all_to_all | solution.py:270
  112.7 0.0 copy-done.4
  112.7 0.0 copy-done.5
  112.7 0.1 select_reduce_fusion
  112.8 9.4 %all-to-all-done.5 = bf16[4,256,128]{2,1,0:T(8,128)(2,1)S(1)} async-done(((bf16[4,256,128]{2,1,0:T(8,128)(2,1)}), bf16[4,256,128]{2,1,0:T(8,128)(2,1)S(1)}, u32[]{:S(2)}, u32[]{:S(2)}) %all-to-all-start.5) | async-done | bytes 262176 | tf_op jit(solution)/shard_map/all_to_all | solution.py:270
  122.3 0.1 multiply_reduce_fusion
  122.4 0.8 multiply_multiply_fusion
  (5 shorter events, 0.1 us)
Async XLA Ops:
  0.0 15.1 %copy-start.3 = (s32[256]{0:T(256)S(1)}, s32[256]{0:T(256)}, u32[]{:S(2)}) copy-start(s32[256]{0:T(256)} %param.15) | copy-start | bytes 3076
  2.6 13.2 %all-to-all-start = ((bf16[4,512,128]{2,1,0:T(8,128)(2,1)}), bf16[4,512,128]{2,1,0:T(8,128)(2,1)S(1)}, u32[]{:S(2)}, u32[]{:S(2)}) async-start(bf16[4,512,128]{2,1,0:T(8,128)(2,1)} %tile.2), calls=%async_computation | async-start | bytes 1048576 | tf_op jit(solution)/shard_map/all_to_all | solution.py:273
  11.9 3.2 %copy-start = (bf16[256,128,128]{2,1,0:T(8,128)(2,1)}, bf16[256,128,128]{2,1,0:T(8,128)(2,1)S(1)}, u32[]{:S(2)}) copy-start(bf16[256,128,128]{2,1,0:T(8,128)(2,1)S(1)} %get-tuple-element.14.weights_ref) | copy-start | bytes 25165828
  15.8 3.4 %copy-start.1 = (bf16[256,128,128]{2,1,0:T(8,128)(2,1)S(1)}, bf16[256,128,128]{2,1,0:T(8,128)(2,1)}, u32[]{:S(2)}) copy-start(bf16[256,128,128]{2,1,0:T(8,128)(2,1)} %copy-done) | copy-start | bytes 25165828
  21.4 36.3 %slice-start = ((s8[8388608]{0:T(1024)(128)(4,1)}), s8[4194304]{0:T(1024)(128)(4,1)S(1)}, s32[]{:S(2)}) async-start(s8[8388608]{0:T(1024)(128)(4,1)} %bitcast.33), calls=%async_computation.6 | async-start | bytes 8388608
  21.4 2.5 %collective-permute-start = (bf16[2064,128]{1,0:T(8,128)(2,1)S(1)}, bf16[2064,128]{1,0:T(8,128)(2,1)S(1)}, u32[]{:S(2)}, u32[]{:S(2)}) collective-permute-start(bf16[2064,128]{1,0:T(8,128)(2,1)S(1)} %get-tuple-element.16), channel_id=1, source_target_pairs={{0,1},{1,0},{2,3},{3,2},{4,5},{5,4},{6,7},{7,6},{8,9},{9,8},{10,11... | collective-permute-start | bytes 1585160 | tf_op jit(solution)/shard_map/ppermute | solution.py:266
  21.5 36.2 %slice-start.1 = ((s8[8388608]{0:T(1024)(128)(4,1)}), s8[4194304]{0:T(1024)(128)(4,1)S(1)}, s32[]{:S(2)}) async-start(s8[8388608]{0:T(1024)(128)(4,1)} %bitcast.33), calls=%async_computation.7 | async-start | bytes 8388608
  59.9 2.4 %collective-permute-start.1 = (bf16[2048,128]{1,0:T(8,128)(2,1)S(1)}, bf16[2048,128]{1,0:T(8,128)(2,1)S(1)}, u32[]{:S(2)}, u32[]{:S(2)}) collective-permute-start(bf16[2048,128]{1,0:T(8,128)(2,1)S(1)} %get-tuple-element.18), channel_id=1, source_target_pairs={{0,1},{1,0},{2,3},{3,2},{4,5},{5,4},{6,7},{7,6},{8,9},{9,8},{10,11... | collective-permute-start | bytes 1572872 | tf_op jit(solution)/shard_map/ppermute | solution.py:266
  62.4 50.3 %copy-start.4 = (s32[256]{0:T(256)S(1)}, s32[256]{0:T(256)}, u32[]{:S(2)}) copy-start(s32[256]{0:T(256)} %param.16) | copy-start | bytes 3076
  62.4 50.3 %copy-start.5 = (f32[16]{0:T(128)S(1)}, f32[16]{0:T(128)}, u32[]{:S(2)}) copy-start(f32[16]{0:T(128)} %param.17) | copy-start | bytes 196
  81.9 11.9 %all-to-all-start.4 = ((bf16[4,512,128]{2,1,0:T(8,128)(2,1)}), bf16[4,512,128]{2,1,0:T(8,128)(2,1)S(1)}, u32[]{:S(2)}, u32[]{:S(2)}) async-start(bf16[4,512,128]{2,1,0:T(8,128)(2,1)} %bitcast.11), calls=%async_computation.4 | async-start | bytes 1048576 | tf_op jit(solution)/shard_map/all_to_all | solution.py:273
  93.8 3.4 %copy-start.2 = (bf16[256,128,128]{2,1,0:T(8,128)(2,1)S(1)}, bf16[256,128,128]{2,1,0:T(8,128)(2,1)}, u32[]{:S(2)}) copy-start(bf16[256,128,128]{2,1,0:T(8,128)(2,1)} %copy-done) | copy-start | bytes 25165828
  103.8 4.7 %collective-permute-start.2 = (bf16[1024,128]{1,0:T(8,128)(2,1)S(1)}, bf16[1024,128]{1,0:T(8,128)(2,1)S(1)}, u32[]{:S(2)}, u32[]{:S(2)}) collective-permute-start(bf16[1024,128]{1,0:T(8,128)(2,1)S(1)} %get-tuple-element.20), channel_id=1, source_target_pairs={{0,1},{1,0},{2,3},{3,2},{4,5},{5,4},{6,7},{7,6},{8,9},{9,8},{10,11... | collective-permute-start | bytes 786440 | tf_op jit(solution)/shard_map/ppermute | solution.py:266
  109.3 12.9 %all-to-all-start.5 = ((bf16[4,256,128]{2,1,0:T(8,128)(2,1)}), bf16[4,256,128]{2,1,0:T(8,128)(2,1)S(1)}, u32[]{:S(2)}, u32[]{:S(2)}) async-start(bf16[4,256,128]{2,1,0:T(8,128)(2,1)} %bitcast.13), calls=%async_computation.5 | async-start | bytes 524288 | tf_op jit(solution)/shard_map/all_to_all | solution.py:270

commit v4 on v2

--- a/solution.py
+++ b/solution.py
@@ -8,8 +8,7 @@
 from jax.sharding import PartitionSpec as P
 
 HOPS = 3
-HALVES = 2
-CHUNKS = 2 * HALVES
+CHUNKS = 4
 GROUP = 4
 UNROLL = 4
 UNPICK = 16
@@ -26,6 +25,10 @@
 PARAMS = pltpu.CompilerParams(vmem_limit_bytes=16 * MIB)
 
 
+def far_first(k, chips):
+    return k ^ (chips // 2)
+
+
 def iota(shape, dim):
     return lax.broadcasted_iota(jnp.int32, shape, dim)
 
@@ -58,11 +61,11 @@
     length = plan_ref.shape[1]
     my_row, my_col = lax.axis_index("row"), lax.axis_index("col")
     chunk_tiles = row_tiles // CHUNKS
-    per_half = per_group // HALVES
     row = tile_row_ref[...]
     rel = (row // per_group) ^ my_col
-    chunk = (1 - rel % 2) * HALVES + (row % per_group) // per_half
-    order = chunk * chunk_tiles + (rel // 2) * per_half + row % per_half
+    chips = 2 * chunk_tiles // per_group
+    place = (1 - rel % 2) * chips + far_first(rel // 2, chips)
+    order = place * per_group + row % per_group
     order = jnp.where(iota((1, slots), 1) < count_ref[0, 0], order, row_tiles).astype(jnp.float32)
     col = tile_col_ref[...]
     source = ((col // per_group) ^ my_row) * per_group + col % per_group
@@ -107,14 +110,29 @@
     load.wait()
 
 
-def fill_state(pieces, state, halves, tile):
+def begin_kernel(degree_hbm, embed_hbm, state_ref, square_ref, degree_ref, embed_ref, sems):
+    copies = (
+        pltpu.make_async_copy(degree_hbm, degree_ref, sems.at[0]),
+        pltpu.make_async_copy(embed_hbm, embed_ref, sems.at[1]),
+    )
+    for copy in copies:
+        copy.start()
+    for copy in copies:
+        copy.wait()
+    lanes = degree_ref.shape[1]
+    for i in range(degree_ref.shape[0]):
+        scale = to_column(lax.rsqrt(degree_ref[i : i + 1, :].astype(jnp.float32)))
+        at = slice(i * lanes, (i + 1) * lanes)
+        state_ref[at, :] = (scale * embed_ref[at, :].astype(jnp.float32)).astype(state_ref.dtype)
+        square_ref[at, :] = jnp.broadcast_to(scale * scale, (lanes, square_ref.shape[1]))
+
+
+def fill_state(pieces, state):
     rows = pieces[0].shape[0]
-    devices = (state.shape[0] - tile) // (rows * halves)
     for i, piece in enumerate(pieces):
-        half, device = halves - 1 - i // devices, i % devices
-        at = (device * halves + half) * rows
-        state[at : at + rows, :] = piece[...]
-    state[len(pieces) * rows :, :] = jnp.zeros((tile, state.shape[1]), state.dtype)
+        state[i * rows : (i + 1) * rows, :] = piece[...]
+    at = len(pieces) * rows
+    state[at:, :] = jnp.zeros((state.shape[0] - at, state.shape[1]), state.dtype)
 
 
 def multiply(plan_ref, weights_ref, state, total, chunk, chunks, chunk_tiles):
@@ -145,57 +163,63 @@
     lax.fori_loop(plan_ref[2, chunk], plan_ref[2, chunk + chunks], turn, 0)
 
 
-def odd_kernel(pieces, halves, plan_ref, *refs):
+def odd_kernel(pieces, plan_ref, *refs):
     weights_ref, extra_refs = refs[pieces], refs[pieces + 1 : -3]
     odd_ref, state, total = refs[-3:]
     rows = total.shape[0]
-    fill_state(refs[:pieces], state, halves, weights_ref.shape[1])
-    multiply(plan_ref, weights_ref, state, total, 0, HALVES, 0)
+    fill_state(refs[:pieces], state)
+    multiply(plan_ref, weights_ref, state, total, 0, 2, 0)
     odd_ref[0:rows, :] = total[...].astype(odd_ref.dtype)
     for extra in extra_refs:
         odd_ref[rows:, :] = extra[...]
 
 
-def even0_kernel(plan_ref, state, weights_ref, even_ref):
-    multiply(plan_ref, weights_ref, state, even_ref, HALVES, 1, even_ref.shape[0] // weights_ref.shape[1])
-
-
-def even1_kernel(chips, plan_ref, state, weights_ref, after_ref, other_ref, *refs):
-    extra_refs, own_ref, sent_refs, total = refs[: -chips - 1], refs[-chips - 1], refs[-chips:-1], refs[-1]
+def add_cores(offset, even_ref, other_ref, extra_refs, out_refs):
+    rows = even_ref.shape[0] // len(out_refs)
+    for i, out in enumerate(out_refs):
+        other = other_ref[offset + i * rows : offset + (i + 1) * rows, :].astype(jnp.float32)
+        out[0:rows, :] = (even_ref[i * rows : (i + 1) * rows, :] + other).astype(out.dtype)
+        for extra in extra_refs:
+            if out.shape[0] > rows:
+                size = extra.shape[0]
+                tail = other_ref[other_ref.shape[0] - size :, :].astype(jnp.float32)
+                both = extra[...].astype(jnp.float32) + pltpu.roll(tail, size // 2, 0)
+                out[rows:, :] = both.astype(out.dtype)
+
+
+def even_far_kernel(plan_ref, state, weights_ref, even_ref):
+    multiply(plan_ref, weights_ref, state, even_ref, 2, 1, even_ref.shape[0] // weights_ref.shape[1])
+
+
+def merge_kernel(outs, even_ref, other_ref, *refs):
+    add_cores(0, even_ref, other_ref, refs[:-outs], refs[-outs:])
+
+
+def even_near_kernel(outs, plan_ref, state, weights_ref, after_ref, other_ref, *refs):
+    extra_refs, out_refs, total = refs[: -outs - 1], refs[-outs - 1 : -1], refs[-1]
     rows = total.shape[0]
-    multiply(plan_ref, weights_ref, state, total, HALVES + 1, 1, rows // weights_ref.shape[1])
-    add_cores(chips, rows, total, other_ref, own_ref, sent_refs)
-    for extra in extra_refs:
-        size = extra.shape[0]
-        far = other_ref[other_ref.shape[0] - size :, :].astype(jnp.float32)
-        both = (extra[...].astype(jnp.float32) + pltpu.roll(far, size // 2, 0)).astype(extra.dtype)
-        for sent in sent_refs:
-            sent[own_ref.shape[0] :, :] = both
-
-
-def add_cores(chips, offset, even_ref, other_ref, own_ref, sent_refs):
-    rows = own_ref.shape[0]
-    for k, out in enumerate((own_ref, *sent_refs)):
-        other = other_ref[pl.ds(offset + k * rows, rows), :].astype(jnp.float32)
-        out[0:rows, :] = (even_ref[pl.ds(k * rows, rows), :] + other).astype(out.dtype)
-
-
-def merge_kernel(chips, even_ref, other_ref, own_ref, *sent_refs):
-    add_cores(chips, 0, even_ref, other_ref, own_ref, sent_refs)
+    multiply(plan_ref, weights_ref, state, total, 3, 1, rows // weights_ref.shape[1])
+    add_cores(rows, total, other_ref, extra_refs, out_refs)
+
+
+def add_kernel(own_ref, *refs):
+    out_ref = refs[-1]
+    rows = out_ref.shape[0]
+    total = own_ref[...]
+    for ref in refs[:-1]:
+        total = total + ref[0:rows, :].astype(jnp.float32)
+    out_ref[...] = total
 
 
 def place_kernel(chips, rows_here, block_rows, id_rows, mine_ref, other_ref, *refs):
     far_refs, place_ref = refs[:-1], refs[-1]
     my_col = lax.axis_index("col")
-    half = rows_here // HALVES
-    chunk_rows = block_rows // CHUNKS
     extra = mine_ref.shape[0]
 
     def places(rows):
         ids = (rows[:id_rows] * BYTE + rows[id_rows : 2 * id_rows]).astype(jnp.int32)
         rel = (ids // rows_here) ^ my_col
-        chunk = (1 - rel % 2) * HALVES + ids % rows_here // half
-        return chunk * chunk_rows + rel // 2 * half + ids % half
+        return ((1 - rel % 2) * chips + far_first(rel // 2, chips)) * rows_here + ids % rows_here
 
     def tail(ref):
         return ref[ref.shape[0] - extra :, :].astype(jnp.float32)
@@ -206,36 +230,43 @@
         even.append(rows)
         odd.append(pltpu.roll(rows, extra - extra // 2, 0))
     for k in range(chips):
-        place_ref[k * id_rows : (k + 1) * id_rows, :] = places(odd[k])
-        place_ref[(chips + k) * id_rows : (chips + k + 1) * id_rows, :] = places(even[k])
-
-
-def pick_rows(place_ref, part, total, picked, out):
-    count = picked.shape[0]
-
+        at = far_first(k, chips) * id_rows
+        place_ref[at : at + id_rows, :] = places(odd[k])
+        at = at + chips * id_rows
+        place_ref[at : at + id_rows, :] = places(even[k])
+
+
+def pick_rows(place_ref, first, total, picked):
     def some(i, carry):
         base = pl.multiple_of(i * UNPICK, UNPICK)
-        row = (part * count + base) // LANES
-        lane = base % LANES
+        row = (first + base) // LANES
+        lane = (first + base) % LANES
+        rows = [total[pl.ds(place_ref[row, lane + j], 1), :] for j in range(UNPICK)]
         for j in range(UNPICK):
-            picked[pl.ds(base + j, 1), :] = total[pl.ds(place_ref[row, lane + j], 1), :]
+            picked[pl.ds(base + j, 1), :] = rows[j]
         return carry
 
-    lax.fori_loop(0, count // UNPICK, some, 0)
-    if out is not picked:
-        out[...] = picked[...].astype(out.dtype)
-
-
-def last_kernel(pieces, halves, plan_ref, place_ref, *refs):
+    lax.fori_loop(0, picked.shape[0] // UNPICK, some, 0)
+
+
+def last_kernel(pieces, plan_ref, place_ref, *refs):
     weights_ref = refs[pieces]
     odd_ref, total, state, picked = refs[pieces + 1 :]
-    fill_state(refs[:pieces], state, halves, weights_ref.shape[1])
+    fill_state(refs[:pieces], state)
     multiply(plan_ref, weights_ref, state, total, 0, CHUNKS, 0)
-    pick_rows(place_ref, 0, total, picked, odd_ref)
-
-
-def pick_kernel(place_ref, total, even_ref):
-    pick_rows(place_ref, 1, total, even_ref, even_ref)
+    pick_rows(place_ref, 0, total, picked)
+    odd_ref[...] = picked[...].astype(odd_ref.dtype)
+
+
+def pick_far_kernel(place_ref, total, even_ref):
+    pick_rows(place_ref, 2 * even_ref.shape[0], total, even_ref)
+
+
+def pick_near_kernel(outs, place_ref, total, after_ref, other_ref, *refs):
+    out_refs, picked = refs[:-1], refs[-1]
+    rows = picked.shape[0]
+    pick_rows(place_ref, 3 * rows, total, picked)
+    add_cores(rows, picked, other_ref, (), out_refs)
 
 
 def local(
@@ -249,7 +280,6 @@
     block_rows = ncols * rows_here
     row_tiles = block_rows // tile
     per_group = rows_here // tile
-    half_here = rows_here // HALVES
     chunk_rows = block_rows // CHUNKS
     zero_tile = nrows * per_group
     new_here = new_rows.shape[0]
@@ -292,8 +322,18 @@
     def spread(state):
         return [state] + [swap(state, "row", nrows, k) for k in range(1, nrows)]
 
-    scale = lax.rsqrt(degree.astype(f32))
-    state = (scale[:, None] * embed.astype(f32)).astype(bf16)
+    state, square = call(
+        begin_kernel,
+        "begin",
+        [array(embed.shape, bf16), array(embed.shape, f32)],
+        (in_hbm(degree.reshape(rows_here // LANES, LANES)), in_hbm(embed)),
+        in_specs=[HBM_SPEC, HBM_SPEC],
+        scratch=[
+            pltpu.VMEM((rows_here // LANES, LANES), jnp.int32),
+            pltpu.VMEM(embed.shape, bf16),
+            pltpu.SemaphoreType.DMA((2,)),
+        ],
+    )
     pieces = spread(state)
 
     plan, weights = call(
@@ -316,67 +356,61 @@
 
     state_shape = ((zero_tile + 1) * tile, width)
 
-    def sums_shape(rows, more=0):
-        return [array((rows, width), f32)] + [array((rows + more, width), bf16)] * (chips - 1)
-
-    def send(sent):
-        return [swap(part, "col", ncols, 2 * k) for k, part in enumerate(sent, 1)]
-
-    def merge(even, other):
-        own, *sent = call(
-            functools.partial(merge_kernel, chips), "merge", sums_shape(even.shape[0] // chips), (even, other)
+    half_chips = chips // 2
+
+    def send(sent, first):
+        return [swap(part, "col", ncols, 2 * (first + i)) for i, part in enumerate(sent)]
+
+    def collect(other, far_part, near_kernel, near_args, near_scalars, rows, turns, extra=()):
+        more = sum(e.shape[0] for e in extra)
+        blocks = [array((rows + more, width), bf16)] * half_chips
+        far = call(functools.partial(merge_kernel, half_chips), "merge", blocks, (far_part, other, *extra))
+        own, *near = call(
+            functools.partial(near_kernel, half_chips),
+            "near",
+            [array((rows, width), f32)] + blocks[1:],
+            (*near_args, far[0], other, *extra),
+            scalars=near_scalars,
+            scratch=[pltpu.VMEM((half_chips * rows, width), f32)],
+            turns=turns,
         )
-        return own, send(sent)
-
-    def add(own, came):
+        came_far, came_near = send(far, half_chips), send(near, 1)
+        return call(add_kernel, "add", array((rows, width), f32), (own, *came_far)), came_near, came_far
+
+    def add(total, came):
         for part in came:
-            own = own + part[: own.shape[0]].astype(f32)
-        return own
+            total = total + part[: total.shape[0]].astype(f32)
+        return total
 
     for hop in range(HOPS - 1):
         extra = (mine,) if hop == 0 else ()
         odd, held = call(
-            functools.partial(odd_kernel, len(pieces), len(pieces) // nrows),
+            functools.partial(odd_kernel, nrows),
             "odd",
-            [
-                array((HALVES * chunk_rows + len(extra) * id_block, width), bf16),
-                array(state_shape, bf16),
-            ],
+            [array((2 * chunk_rows + len(extra) * id_block, width), bf16), array(state_shape, bf16)],
             (plan, *pieces, weights, *extra),
             scalars=1,
-            scratch=[pltpu.VMEM((HALVES * chunk_rows, width), f32)],
+            scratch=[pltpu.VMEM((2 * chunk_rows, width), f32)],
             turns=0.5,
         )
         other = swap_cores(odd)
-        even0 = call(
-            even0_kernel, "even0", array((chunk_rows, width), f32), (plan, held, weights), scalars=1, turns=0.25
+        far_part = call(
+            even_far_kernel, "far", array((chunk_rows, width), f32), (plan, held, weights), scalars=1, turns=0.25
         )
-        own0, came0 = merge(even0, other)
-        own1, *sent1 = call(
-            functools.partial(even1_kernel, chips),
-            "even1",
-            sums_shape(half_here, len(extra) * id_block),
-            (plan, held, weights, own0, other, *extra),
-            scalars=1,
-            scratch=[pltpu.VMEM((chunk_rows, width), f32)],
-            turns=0.25,
+        total, near, far = collect(
+            other, far_part, even_near_kernel, (plan, held, weights), 1, rows_here, 0.25, extra
         )
-        came1 = send(sent1)
         if hop == 0:
             place = call(
                 functools.partial(place_kernel, chips, rows_here, block_rows, id_rows),
                 "place",
                 array((2 * chips * id_rows, LANES), jnp.int32),
-                (mine, other, *came1),
+                (mine, other, *near, *far),
             )
-        parts = {}
-        for half, (own, came) in reversed(tuple(enumerate(((own0, came0), (own1, came1))))):
-            here = scale[half * half_here : (half + 1) * half_here]
-            parts[half] = spread(((here * here)[:, None] * add(own, came)).astype(bf16))
-        pieces = [parts[half][r] for half in reversed(range(HALVES)) for r in range(nrows)]
+        pieces = spread((square * add(total, near)).astype(bf16))
 
     odd, total = call(
-        functools.partial(last_kernel, len(pieces), len(pieces) // nrows),
+        functools.partial(last_kernel, nrows),
         "last",
         [array((chips * new_here, width), bf16), array((block_rows, width), f32)],
         (plan, place, *pieces, weights),
@@ -385,8 +419,11 @@
         turns=1.0,
     )
     other = swap_cores(odd)
-    even = call(pick_kernel, "pick", array((chips * new_here, width), f32), (place, total), scalars=1, turns=0.2)
-    picked = add(*merge(even, other))
+    far_part = call(
+        pick_far_kernel, "pick", array((half_chips * new_here, width), f32), (place, total), scalars=1, turns=0.25
+    )
+    summed, near, _ = collect(other, far_part, pick_near_kernel, (place, total), 1, new_here, 0.25)
+    picked = add(summed, near)
     buckets = jnp.arange(bucket_norm.shape[0], dtype=jnp.int32)
     target = jnp.sum(
         jnp.where(new_bucket[:, None] == buckets[None, :], bucket_norm[None, :], jnp.float32(0.0)),

time: 95 us -> 93.5 us (0.984)
  starting transfers between devices: 43.2 us -> 24.5 us
  waiting for transfers between devices: 19.1 us -> 34.7 us
  Pallas kernels: 27.4 us -> 30.9 us
  other arithmetic: 3.86 us -> 1.81 us
    ppermute x33 -> x21, starting transfers between devices: 43.2 us -> 24.5 us  [swap(): return lax.ppermute(array, axis, [(i, i ^ mask) for i in range(size)])]
    ppermute x33 -> x21, waiting for transfers between devices: 19.1 us -> 34.7 us  [swap(): return lax.ppermute(array, axis, [(i, i ^ mask) for i in range(size)])]
    pallas_call x13 -> x18, Pallas kernels: 27.4 us -> 30.9 us  [call(): pl.pallas_call(kernel, out_shape=out_shape, grid_spec=pltpu.PrefetchScala...]
    convert_element_type x5 -> x2, other arithmetic: 1.46 us -> 0.1 us  [local(): pieces = spread((square * add(total, near)).astype(bf16))]
  transfers between devices with their start and end apart: 33 -> 21, of which waited for: 15 -> 12; matrix products, arithmetic and copies ran while one was open for 1% -> 1% of each run, Pallas kernels for 15% -> 17%
where the time goes in v4:
time: 93.5 us; the launch traced here: 92.8 us
  waiting for transfers between devices  34.7 us (37%)
  Pallas kernels  30.9 us (33%)
  starting transfers between devices  24.5 us (26%)
  other arithmetic  1.81 us (2%)
    ppermute x21, waiting for transfers between devices, swap(): return lax.ppermute(array, axis, [(i, i ^ mask) for i in range(size)])  34.7 us
    pallas_call x18, Pallas kernels, call(): pl.pallas_call(kernel, out_shape=out_shape, grid_spec=pltpu.PrefetchScala...  30.9 us
    ppermute x21, starting transfers between devices, swap(): return lax.ppermute(array, axis, [(i, i ^ mask) for i in range(size)])  24.5 us
  transfers between devices with their start and end apart: 21, of which 12 were waited for; matrix products, arithmetic and copies ran while one was open for 1% of the time, Pallas kernels for 17%

profile of v4, /device:TPU:0, one launch (start us, length us, event | category | flops | bytes accessed | tf_op | source)
XLA Modules:
  0.0 92.8 jit_solution(3742931042903722857)
XLA Ops:
  0.0 1.1 %begin.1 = (bf16[512,128]{1,0:T(8,128)(2,1)S(1)}, f32[512,128]{1,0:T(8,128)S(1)}) custom-call(s32[4,128]{1,0:T(4,128)} %bitcast.25, bf16[512,128]{1,0:T(8,128)(2,1)} %embed_hbm.1), custom_call_target="tpu_custom_call" | custom-call | tf_op jit(solution)/shard_map/begin/pallas_call | solution.py:301
  1.1 3.0 %collective-permute-start = (bf16[512,128]{1,0:T(8,128)(2,1)S(1)}, bf16[512,128]{1,0:T(8,128)(2,1)S(1)}, u32[]{:S(2)}, u32[]{:S(2)}) collective-permute-start(bf16[512,128]{1,0:T(8,128)(2,1)S(1)} %get-tuple-element.28.refs_0_), channel_id=1, source_target_pairs={{0,8},{8,0},{16,24},{24,16},{1,9},{9,1},{17,25},{25,17},{2,10},{10... | collective-permute-start | bytes 393224 | tf_op jit(solution)/shard_map/ppermute | solution.py:317
  4.1 1.5 %collective-permute-start.1 = (bf16[512,128]{1,0:T(8,128)(2,1)S(1)}, bf16[512,128]{1,0:T(8,128)(2,1)S(1)}, u32[]{:S(2)}, u32[]{:S(2)}) collective-permute-start(bf16[512,128]{1,0:T(8,128)(2,1)S(1)} %get-tuple-element.28.refs_0_), channel_id=1, source_target_pairs={{0,16},{8,24},{16,0},{24,8},{1,17},{9,25},{17,1},{25,9},{2,18},{10... | collective-permute-start | bytes 393224 | tf_op jit(solution)/shard_map/ppermute | solution.py:317
  5.6 0.0 collective-permute-start.2
  5.6 0.7 fusion.4
  7.0 3.4 %plan.1 = (s32[8,512]{1,0:T(8,128)S(1)}, bf16[256,128,128]{2,1,0:T(8,128)(2,1)S(1)}) custom-call(s32[1,1]{1,0:T(1,128)S(6)} %copy.10.count_ref, s32[1,256]{1,0:T(1,128)} %bitcast.26, s32[1,256]{1,0:T(1,128)} %bitcast.27, bf16[256,128,128]{2,1,0:T(8,128)(2,1)} %bitcast.24), custom_call_target="tpu_custom_call" | custom-call | tf_op jit(solution)/shard_map/plan/pallas_call | solution.py:301
  10.5 0.0 collective-permute-done.refs_1_
  10.5 1.4 %collective-permute-done.1.refs_2_ = bf16[512,128]{1,0:T(8,128)(2,1)S(1)} collective-permute-done((bf16[512,128]{1,0:T(8,128)(2,1)S(1)}, bf16[512,128]{1,0:T(8,128)(2,1)S(1)}, u32[]{:S(2)}, u32[]{:S(2)}) %collective-permute-start.1) | collective-permute-done | bytes 131104 | tf_op jit(solution)/shard_map/ppermute | solution.py:317
  11.9 0.0 collective-permute-done.2.refs_3_
  11.9 3.0 %odd.2 = (bf16[2064,128]{1,0:T(8,128)(2,1)S(1)}, bf16[2176,128]{1,0:T(8,128)(2,1)S(1)}) custom-call(s32[8,512]{1,0:T(8,128)S(1)} %get-tuple-element.27.plan_ref, bf16[512,128]{1,0:T(8,128)(2,1)S(1)} %get-tuple-element.28.refs_0_, bf16[512,128]{1,0:T(8,128)(2,1)S(1)} %collective-permute-done.refs_1_, bf16[512,128]{1,0:T(8,128)(2,1)S(1)} %collective-permute-done.1.refs_2_, ...), custom_call_target="tpu_custom_call" | custom-call | flops 536870912 | bytes 4194304 | tf_op jit(solution)/shard_map/odd/pallas_call | solution.py:301
  14.9 0.1 collective-permute-start.3
  15.0 2.0 %far.2.even_ref = f32[1024,128]{1,0:T(8,128)S(1)} custom-call(s32[8,512]{1,0:T(8,128)S(1)} %get-tuple-element.27.plan_ref, bf16[2176,128]{1,0:T(8,128)(2,1)S(1)} %get-tuple-element.31.state, bf16[256,128,128]{2,1,0:T(8,128)(2,1)S(1)} %get-tuple-element.29.refs_4_.weights_ref), custom_call_target="tpu_custom_call" | custom-call | flops 268435456 | bytes 2097152 | tf_op jit(solution)/shard_map/far/pallas_call | solution.py:301
  17.1 0.0 collective-permute-done.3.other_ref
  17.1 1.9 %collective-permute-start.5 = (bf16[528,128]{1,0:T(8,128)(2,1)S(1)}, bf16[528,128]{1,0:T(8,128)(2,1)S(1)}, u32[]{:S(2)}, u32[]{:S(2)}) collective-permute-start(bf16[528,128]{1,0:T(8,128)(2,1)S(1)} %get-tuple-element.32.after_ref), channel_id=1, source_target_pairs={{0,4},{1,5},{2,6},{3,7},{4,0},{5,1},{6,2},{7,3},{8,12},{9,13},{10,... | collective-permute-start | bytes 405512 | tf_op jit(solution)/shard_map/ppermute | solution.py:317
  19.0 2.1 %collective-permute-start.6 = (bf16[528,128]{1,0:T(8,128)(2,1)S(1)}, bf16[528,128]{1,0:T(8,128)(2,1)S(1)}, u32[]{:S(2)}, u32[]{:S(2)}) collective-permute-start(bf16[528,128]{1,0:T(8,128)(2,1)S(1)} %get-tuple-element.34), channel_id=1, source_target_pairs={{0,6},{1,7},{2,4},{3,5},{4,2},{5,3},{6,0},{7,1},{8,14},{9,15},{10,... | collective-permute-start | bytes 405512 | tf_op jit(solution)/shard_map/ppermute | solution.py:317
  21.2 1.8 %near.3 = (f32[512,128]{1,0:T(8,128)S(1)}, bf16[528,128]{1,0:T(8,128)(2,1)S(1)}) custom-call(s32[8,512]{1,0:T(8,128)S(1)} %get-tuple-element.27.plan_ref, bf16[2176,128]{1,0:T(8,128)(2,1)S(1)} %get-tuple-element.31.state, bf16[256,128,128]{2,1,0:T(8,128)(2,1)S(1)} %get-tuple-element.29.refs_4_.weights_ref, bf16[528,128]{1,0:T(8,128)(2,1)S(1)} %get-tuple-element.32.after_ref, ...), custom_call_target="tpu_custom_call" | custom-call | flops 268435456 | bytes 2097152 | tf_op jit(solution)/shard_map/near/pallas_call | solution.py:301
  23.0 0.6 collective-permute-start.4
  23.5 6.8 %collective-permute-done.5.refs_1_.refs_0_ = bf16[528,128]{1,0:T(8,128)(2,1)S(1)} collective-permute-done((bf16[528,128]{1,0:T(8,128)(2,1)S(1)}, bf16[528,128]{1,0:T(8,128)(2,1)S(1)}, u32[]{:S(2)}, u32[]{:S(2)}) %collective-permute-start.5) | collective-permute-done | bytes 135200 | tf_op jit(solution)/shard_map/ppermute | solution.py:317
  30.3 0.0 collective-permute-done.6.refs_2_.refs_1_
  30.4 2.1 %collective-permute-done.4.refs_0_ = bf16[528,128]{1,0:T(8,128)(2,1)S(1)} collective-permute-done((bf16[528,128]{1,0:T(8,128)(2,1)S(1)}, bf16[528,128]{1,0:T(8,128)(2,1)S(1)}, u32[]{:S(2)}, u32[]{:S(2)}) %collective-permute-start.4) | collective-permute-done | bytes 135200 | tf_op jit(solution)/shard_map/ppermute | solution.py:317
  32.5 1.9 %collective-permute-start.7 = (bf16[512,128]{1,0:T(8,128)(2,1)S(1)}, bf16[512,128]{1,0:T(8,128)(2,1)S(1)}, u32[]{:S(2)}, u32[]{:S(2)}) collective-permute-start(bf16[512,128]{1,0:T(8,128)(2,1)S(1)} %multiply_convert_fusion.1.refs_0_), channel_id=1, source_target_pairs={{0,8},{8,0},{16,24},{24,16},{1,9},{9,1},{17,25},{25,17},{2,10},{10... | collective-permute-start | bytes 393224 | tf_op jit(solution)/shard_map/ppermute | solution.py:317
  34.4 1.7 %collective-permute-start.8 = (bf16[512,128]{1,0:T(8,128)(2,1)S(1)}, bf16[512,128]{1,0:T(8,128)(2,1)S(1)}, u32[]{:S(2)}, u32[]{:S(2)}) collective-permute-start(bf16[512,128]{1,0:T(8,128)(2,1)S(1)} %multiply_convert_fusion.1.refs_0_), channel_id=1, source_target_pairs={{0,16},{8,24},{16,0},{24,8},{1,17},{9,25},{17,1},{25,9},{2,18},{10... | collective-permute-start | bytes 393224 | tf_op jit(solution)/shard_map/ppermute | solution.py:317
  36.1 0.8 collective-permute-start.9
  36.9 1.3 %collective-permute-done.7.refs_1_ = bf16[512,128]{1,0:T(8,128)(2,1)S(1)} collective-permute-done((bf16[512,128]{1,0:T(8,128)(2,1)S(1)}, bf16[512,128]{1,0:T(8,128)(2,1)S(1)}, u32[]{:S(2)}, u32[]{:S(2)}) %collective-permute-start.7) | collective-permute-done | bytes 131104 | tf_op jit(solution)/shard_map/ppermute | solution.py:317
  38.2 3.3 %collective-permute-done.8.refs_2_ = bf16[512,128]{1,0:T(8,128)(2,1)S(1)} collective-permute-done((bf16[512,128]{1,0:T(8,128)(2,1)S(1)}, bf16[512,128]{1,0:T(8,128)(2,1)S(1)}, u32[]{:S(2)}, u32[]{:S(2)}) %collective-permute-start.8) | collective-permute-done | bytes 131104 | tf_op jit(solution)/shard_map/ppermute | solution.py:317
  41.5 1.6 %collective-permute-done.9.refs_3_ = bf16[512,128]{1,0:T(8,128)(2,1)S(1)} collective-permute-done((bf16[512,128]{1,0:T(8,128)(2,1)S(1)}, bf16[512,128]{1,0:T(8,128)(2,1)S(1)}, u32[]{:S(2)}, u32[]{:S(2)}) %collective-permute-start.9) | collective-permute-done | bytes 131104 | tf_op jit(solution)/shard_map/ppermute | solution.py:317
  43.1 3.0 %odd.3 = (bf16[2048,128]{1,0:T(8,128)(2,1)S(1)}, bf16[2176,128]{1,0:T(8,128)(2,1)S(1)}) custom-call(s32[8,512]{1,0:T(8,128)S(1)} %get-tuple-element.27.plan_ref, bf16[512,128]{1,0:T(8,128)(2,1)S(1)} %multiply_convert_fusion.1.refs_0_, bf16[512,128]{1,0:T(8,128)(2,1)S(1)} %collective-permute-done.7.refs_1_, ...), custom_call_target="tpu_custom_call" | custom-call | flops 536870912 | bytes 4194304 | tf_op jit(solution)/shard_map/odd/pallas_call | solution.py:301
  46.1 0.1 collective-permute-start.10
  46.2 2.0 %far.3.even_ref = f32[1024,128]{1,0:T(8,128)S(1)} custom-call(s32[8,512]{1,0:T(8,128)S(1)} %get-tuple-element.27.plan_ref, bf16[2176,128]{1,0:T(8,128)(2,1)S(1)} %get-tuple-element.37.state, bf16[256,128,128]{2,1,0:T(8,128)(2,1)S(1)} %get-tuple-element.29.refs_4_.weights_ref), custom_call_target="tpu_custom_call" | custom-call | flops 268435456 | bytes 2097152 | tf_op jit(solution)/shard_map/far/pallas_call | solution.py:301
  48.2 0.0 collective-permute-done.10.other_ref
  48.3 0.1 collective-permute-start.11
  48.4 2.3 %collective-permute-start.12 = (bf16[512,128]{1,0:T(8,128)(2,1)S(1)}, bf16[512,128]{1,0:T(8,128)(2,1)S(1)}, u32[]{:S(2)}, u32[]{:S(2)}) collective-permute-start(bf16[512,128]{1,0:T(8,128)(2,1)S(1)} %get-tuple-element.41), channel_id=1, source_target_pairs={{0,6},{1,7},{2,4},{3,5},{4,2},{5,3},{6,0},{7,1},{8,14},{9,15},{10,... | collective-permute-start | bytes 393224 | tf_op jit(solution)/shard_map/ppermute | solution.py:317
  50.7 1.8 %near.4 = (f32[512,128]{1,0:T(8,128)S(1)}, bf16[512,128]{1,0:T(8,128)(2,1)S(1)}) custom-call(s32[8,512]{1,0:T(8,128)S(1)} %get-tuple-element.27.plan_ref, bf16[2176,128]{1,0:T(8,128)(2,1)S(1)} %get-tuple-element.37.state, bf16[256,128,128]{2,1,0:T(8,128)(2,1)S(1)} %get-tuple-element.29.refs_4_.weights_ref, bf16[512,128]{1,0:T(8,128)(2,1)S(1)} %get-tuple-element.39.after_ref, ...), custom_call_target="tpu_custom_call" | custom-call | flops 268435456 | bytes 2097152 | tf_op jit(solution)/shard_map/near/pallas_call | solution.py:301
  52.5 1.2 %collective-permute-start.13 = (bf16[512,128]{1,0:T(8,128)(2,1)S(1)}, bf16[512,128]{1,0:T(8,128)(2,1)S(1)}, u32[]{:S(2)}, u32[]{:S(2)}) collective-permute-start(bf16[512,128]{1,0:T(8,128)(2,1)S(1)} %get-tuple-element.42), channel_id=1, source_target_pairs={{0,2},{1,3},{2,0},{3,1},{4,6},{5,7},{6,4},{7,5},{8,10},{9,11},{10,... | collective-permute-start | bytes 393224 | tf_op jit(solution)/shard_map/ppermute | solution.py:317
  53.7 7.1 %collective-permute-done.11.refs_0_ = bf16[512,128]{1,0:T(8,128)(2,1)S(1)} collective-permute-done((bf16[512,128]{1,0:T(8,128)(2,1)S(1)}, bf16[512,128]{1,0:T(8,128)(2,1)S(1)}, u32[]{:S(2)}, u32[]{:S(2)}) %collective-permute-start.11) | collective-permute-done | bytes 131104 | tf_op jit(solution)/shard_map/ppermute | solution.py:317
  60.8 0.0 collective-permute-done.12.refs_1_
  60.8 0.0 copy-start
  60.8 0.0 copy-start.1
  60.8 2.5 %collective-permute-done.13 = bf16[512,128]{1,0:T(8,128)(2,1)S(1)} collective-permute-done((bf16[512,128]{1,0:T(8,128)(2,1)S(1)}, bf16[512,128]{1,0:T(8,128)(2,1)S(1)}, u32[]{:S(2)}, u32[]{:S(2)}) %collective-permute-start.13) | collective-permute-done | bytes 131104 | tf_op jit(solution)/shard_map/ppermute | solution.py:317
  63.4 1.3 %collective-permute-start.14 = (bf16[512,128]{1,0:T(8,128)(2,1)S(1)}, bf16[512,128]{1,0:T(8,128)(2,1)S(1)}, u32[]{:S(2)}, u32[]{:S(2)}) collective-permute-start(bf16[512,128]{1,0:T(8,128)(2,1)S(1)} %multiply_convert_fusion.refs_0_), channel_id=1, source_target_pairs={{0,8},{8,0},{16,24},{24,16},{1,9},{9,1},{17,25},{25,17},{2,10},{10... | collective-permute-start | bytes 393224 | tf_op jit(solution)/shard_map/ppermute | solution.py:317
  64.6 1.7 %collective-permute-start.15 = (bf16[512,128]{1,0:T(8,128)(2,1)S(1)}, bf16[512,128]{1,0:T(8,128)(2,1)S(1)}, u32[]{:S(2)}, u32[]{:S(2)}) collective-permute-start(bf16[512,128]{1,0:T(8,128)(2,1)S(1)} %multiply_convert_fusion.refs_0_), channel_id=1, source_target_pairs={{0,16},{8,24},{16,0},{24,8},{1,17},{9,25},{17,1},{25,9},{2,18},{10... | collective-permute-start | bytes 393224 | tf_op jit(solution)/shard_map/ppermute | solution.py:317
  66.3 0.6 collective-permute-start.16
  66.9 0.1 place.1.place_ref
  67.0 2.6 %collective-permute-done.14.refs_1_ = bf16[512,128]{1,0:T(8,128)(2,1)S(1)} collective-permute-done((bf16[512,128]{1,0:T(8,128)(2,1)S(1)}, bf16[512,128]{1,0:T(8,128)(2,1)S(1)}, u32[]{:S(2)}, u32[]{:S(2)}) %collective-permute-start.14) | collective-permute-done | bytes 131104 | tf_op jit(solution)/shard_map/ppermute | solution.py:317
  69.6 3.0 %collective-permute-done.15.refs_2_ = bf16[512,128]{1,0:T(8,128)(2,1)S(1)} collective-permute-done((bf16[512,128]{1,0:T(8,128)(2,1)S(1)}, bf16[512,128]{1,0:T(8,128)(2,1)S(1)}, u32[]{:S(2)}, u32[]{:S(2)}) %collective-permute-start.15) | collective-permute-done | bytes 131104 | tf_op jit(solution)/shard_map/ppermute | solution.py:317
  72.6 0.0 collective-permute-done.16.refs_3_
  72.6 8.1 %last.1 = (bf16[1024,128]{1,0:T(8,128)(2,1)S(1)}, f32[4096,128]{1,0:T(8,128)S(1)}) custom-call(s32[8,512]{1,0:T(8,128)S(1)} %get-tuple-element.27.plan_ref, s32[16,128]{1,0:T(8,128)S(1)} %place.1.place_ref, bf16[512,128]{1,0:T(8,128)(2,1)S(1)} %multiply_convert_fusion.refs_0_, bf16[512,128]{1,0:T(8,128)(2,1)S(1)} %collective-permute-done.14.refs_1_, ...), custom_call_target="tpu_custom_call" | custom-call | flops 1073741824 | bytes 8388608 | tf_op jit(solution)/shard_map/last/pallas_call | solution.py:301
  80.8 0.1 collective-permute-start.17
  80.8 2.1 %pick.1.even_ref = f32[512,128]{1,0:T(8,128)S(1)} custom-call(s32[16,128]{1,0:T(8,128)S(1)} %place.1.place_ref, f32[4096,128]{1,0:T(8,128)S(1)} %get-tuple-element.43.total), custom_call_target="tpu_custom_call" | custom-call | flops 268435456 | bytes 2097152 | tf_op jit(solution)/shard_map/pick/pallas_call | solution.py:301
  82.9 0.0 collective-permute-done.17.other_ref
  83.0 0.1 collective-permute-start.18
  83.0 2.2 %collective-permute-start.19 = (bf16[256,128]{1,0:T(8,128)(2,1)S(1)}, bf16[256,128]{1,0:T(8,128)(2,1)S(1)}, u32[]{:S(2)}, u32[]{:S(2)}) collective-permute-start(bf16[256,128]{1,0:T(8,128)(2,1)S(1)} %get-tuple-element.47), channel_id=1, source_target_pairs={{0,6},{1,7},{2,4},{3,5},{4,2},{5,3},{6,0},{7,1},{8,14},{9,15},{10,... | collective-permute-start | bytes 196616 | tf_op jit(solution)/shard_map/ppermute | solution.py:317
  85.2 2.1 %near.5 = (f32[256,128]{1,0:T(8,128)S(1)}, bf16[256,128]{1,0:T(8,128)(2,1)S(1)}) custom-call(s32[16,128]{1,0:T(8,128)S(1)} %place.1.place_ref, f32[4096,128]{1,0:T(8,128)S(1)} %get-tuple-element.43.total, bf16[256,128]{1,0:T(8,128)(2,1)S(1)} %get-tuple-element.45.after_ref, bf16[1024,128]{1,0:T(8,128)(2,1)S(1)} %collective-permute-done.17.other_ref), custom_call_target="tpu_custom_call" | custom-call | flops 268435456 | bytes 2097152 | tf_op jit(solution)/shard_map/near/pallas_call | solution.py:301
  87.4 1.4 %collective-permute-start.20 = (bf16[256,128]{1,0:T(8,128)(2,1)S(1)}, bf16[256,128]{1,0:T(8,128)(2,1)S(1)}, u32[]{:S(2)}, u32[]{:S(2)}) collective-permute-start(bf16[256,128]{1,0:T(8,128)(2,1)S(1)} %get-tuple-element.48), channel_id=1, source_target_pairs={{0,2},{1,3},{2,0},{3,1},{4,6},{5,7},{6,4},{7,5},{8,10},{9,11},{10,... | collective-permute-start | bytes 196616 | tf_op jit(solution)/shard_map/ppermute | solution.py:317
  88.7 0.0 copy-done
  88.7 0.0 copy-done.1
  88.7 0.1 select_reduce_fusion
  88.8 1.7 %collective-permute-done.18.refs_0_ = bf16[256,128]{1,0:T(8,128)(2,1)S(1)} collective-permute-done((bf16[256,128]{1,0:T(8,128)(2,1)S(1)}, bf16[256,128]{1,0:T(8,128)(2,1)S(1)}, u32[]{:S(2)}, u32[]{:S(2)}) %collective-permute-start.18) | collective-permute-done | bytes 65568 | tf_op jit(solution)/shard_map/ppermute | solution.py:317
  90.6 0.0 collective-permute-done.19.refs_1_
  90.6 1.3 %collective-permute-done.20 = bf16[256,128]{1,0:T(8,128)(2,1)S(1)} collective-permute-done((bf16[256,128]{1,0:T(8,128)(2,1)S(1)}, bf16[256,128]{1,0:T(8,128)(2,1)S(1)}, u32[]{:S(2)}, u32[]{:S(2)}) %collective-permute-start.20) | collective-permute-done | bytes 65568 | tf_op jit(solution)/shard_map/ppermute | solution.py:317
  91.9 0.1 multiply_reduce_fusion
  92.0 0.8 multiply_multiply_fusion
  (10 shorter events, 0.4 us)
Async XLA Ops:
  1.1 9.4 %collective-permute-start = (bf16[512,128]{1,0:T(8,128)(2,1)S(1)}, bf16[512,128]{1,0:T(8,128)(2,1)S(1)}, u32[]{:S(2)}, u32[]{:S(2)}) collective-permute-start(bf16[512,128]{1,0:T(8,128)(2,1)S(1)} %get-tuple-element.28.refs_0_), channel_id=1, source_target_pairs={{0,8},{8,0},{16,24},{24,16},{1,9},{9,1},{17,25},{25,17},{2,10},{10... | collective-permute-start | bytes 393224 | tf_op jit(solution)/shard_map/ppermute | solution.py:317
  4.1 7.8 %collective-permute-start.1 = (bf16[512,128]{1,0:T(8,128)(2,1)S(1)}, bf16[512,128]{1,0:T(8,128)(2,1)S(1)}, u32[]{:S(2)}, u32[]{:S(2)}) collective-permute-start(bf16[512,128]{1,0:T(8,128)(2,1)S(1)} %get-tuple-element.28.refs_0_), channel_id=1, source_target_pairs={{0,16},{8,24},{16,0},{24,8},{1,17},{9,25},{17,1},{25,9},{2,18},{10... | collective-permute-start | bytes 393224 | tf_op jit(solution)/shard_map/ppermute | solution.py:317
  5.6 6.3 %collective-permute-start.2 = (bf16[512,128]{1,0:T(8,128)(2,1)S(1)}, bf16[512,128]{1,0:T(8,128)(2,1)S(1)}, u32[]{:S(2)}, u32[]{:S(2)}) collective-permute-start(bf16[512,128]{1,0:T(8,128)(2,1)S(1)} %get-tuple-element.28.refs_0_), channel_id=1, source_target_pairs={{0,24},{8,16},{16,8},{24,0},{1,25},{9,17},{17,9},{25,1},{2,26},{10... | collective-permute-start | bytes 393224 | tf_op jit(solution)/shard_map/ppermute | solution.py:317
  14.9 2.1 %collective-permute-start.3 = (bf16[2064,128]{1,0:T(8,128)(2,1)S(1)}, bf16[2064,128]{1,0:T(8,128)(2,1)S(1)}, u32[]{:S(2)}, u32[]{:S(2)}) collective-permute-start(bf16[2064,128]{1,0:T(8,128)(2,1)S(1)} %get-tuple-element.30), channel_id=1, source_target_pairs={{0,1},{1,0},{2,3},{3,2},{4,5},{5,4},{6,7},{7,6},{8,9},{9,8},{10,11... | collective-permute-start | bytes 1585160 | tf_op jit(solution)/shard_map/ppermute | solution.py:317
  17.1 13.2 %collective-permute-start.5 = (bf16[528,128]{1,0:T(8,128)(2,1)S(1)}, bf16[528,128]{1,0:T(8,128)(2,1)S(1)}, u32[]{:S(2)}, u32[]{:S(2)}) collective-permute-start(bf16[528,128]{1,0:T(8,128)(2,1)S(1)} %get-tuple-element.32.after_ref), channel_id=1, source_target_pairs={{0,4},{1,5},{2,6},{3,7},{4,0},{5,1},{6,2},{7,3},{8,12},{9,13},{10,... | collective-permute-start | bytes 405512 | tf_op jit(solution)/shard_map/ppermute | solution.py:317
  19.0 11.3 %collective-permute-start.6 = (bf16[528,128]{1,0:T(8,128)(2,1)S(1)}, bf16[528,128]{1,0:T(8,128)(2,1)S(1)}, u32[]{:S(2)}, u32[]{:S(2)}) collective-permute-start(bf16[528,128]{1,0:T(8,128)(2,1)S(1)} %get-tuple-element.34), channel_id=1, source_target_pairs={{0,6},{1,7},{2,4},{3,5},{4,2},{5,3},{6,0},{7,1},{8,14},{9,15},{10,... | collective-permute-start | bytes 405512 | tf_op jit(solution)/shard_map/ppermute | solution.py:317
  23.0 9.5 %collective-permute-start.4 = (bf16[528,128]{1,0:T(8,128)(2,1)S(1)}, bf16[528,128]{1,0:T(8,128)(2,1)S(1)}, u32[]{:S(2)}, u32[]{:S(2)}) collective-permute-start(bf16[528,128]{1,0:T(8,128)(2,1)S(1)} %get-tuple-element.33), channel_id=1, source_target_pairs={{0,2},{1,3},{2,0},{3,1},{4,6},{5,7},{6,4},{7,5},{8,10},{9,11},{10,... | collective-permute-start | bytes 405512 | tf_op jit(solution)/shard_map/ppermute | solution.py:317
  32.5 5.7 %collective-permute-start.7 = (bf16[512,128]{1,0:T(8,128)(2,1)S(1)}, bf16[512,128]{1,0:T(8,128)(2,1)S(1)}, u32[]{:S(2)}, u32[]{:S(2)}) collective-permute-start(bf16[512,128]{1,0:T(8,128)(2,1)S(1)} %multiply_convert_fusion.1.refs_0_), channel_id=1, source_target_pairs={{0,8},{8,0},{16,24},{24,16},{1,9},{9,1},{17,25},{25,17},{2,10},{10... | collective-permute-start | bytes 393224 | tf_op jit(solution)/shard_map/ppermute | solution.py:317
  34.4 7.1 %collective-permute-start.8 = (bf16[512,128]{1,0:T(8,128)(2,1)S(1)}, bf16[512,128]{1,0:T(8,128)(2,1)S(1)}, u32[]{:S(2)}, u32[]{:S(2)}) collective-permute-start(bf16[512,128]{1,0:T(8,128)(2,1)S(1)} %multiply_convert_fusion.1.refs_0_), channel_id=1, source_target_pairs={{0,16},{8,24},{16,0},{24,8},{1,17},{9,25},{17,1},{25,9},{2,18},{10... | collective-permute-start | bytes 393224 | tf_op jit(solution)/shard_map/ppermute | solution.py:317
  36.1 7.0 %collective-permute-start.9 = (bf16[512,128]{1,0:T(8,128)(2,1)S(1)}, bf16[512,128]{1,0:T(8,128)(2,1)S(1)}, u32[]{:S(2)}, u32[]{:S(2)}) collective-permute-start(bf16[512,128]{1,0:T(8,128)(2,1)S(1)} %multiply_convert_fusion.1.refs_0_), channel_id=1, source_target_pairs={{0,24},{8,16},{16,8},{24,0},{1,25},{9,17},{17,9},{25,1},{2,26},{10... | collective-permute-start | bytes 393224 | tf_op jit(solution)/shard_map/ppermute | solution.py:317
  46.1 2.1 %collective-permute-start.10 = (bf16[2048,128]{1,0:T(8,128)(2,1)S(1)}, bf16[2048,128]{1,0:T(8,128)(2,1)S(1)}, u32[]{:S(2)}, u32[]{:S(2)}) collective-permute-start(bf16[2048,128]{1,0:T(8,128)(2,1)S(1)} %get-tuple-element.38), channel_id=1, source_target_pairs={{0,1},{1,0},{2,3},{3,2},{4,5},{5,4},{6,7},{7,6},{8,9},{9,8},{10,11... | collective-permute-start | bytes 1572872 | tf_op jit(solution)/shard_map/ppermute | solution.py:317
  48.3 12.5 %collective-permute-start.11 = (bf16[512,128]{1,0:T(8,128)(2,1)S(1)}, bf16[512,128]{1,0:T(8,128)(2,1)S(1)}, u32[]{:S(2)}, u32[]{:S(2)}) collective-permute-start(bf16[512,128]{1,0:T(8,128)(2,1)S(1)} %get-tuple-element.39.after_ref), channel_id=1, source_target_pairs={{0,4},{1,5},{2,6},{3,7},{4,0},{5,1},{6,2},{7,3},{8,12},{9,13},{10,... | collective-permute-start | bytes 393224 | tf_op jit(solution)/shard_map/ppermute | solution.py:317
  48.4 12.4 %collective-permute-start.12 = (bf16[512,128]{1,0:T(8,128)(2,1)S(1)}, bf16[512,128]{1,0:T(8,128)(2,1)S(1)}, u32[]{:S(2)}, u32[]{:S(2)}) collective-permute-start(bf16[512,128]{1,0:T(8,128)(2,1)S(1)} %get-tuple-element.41), channel_id=1, source_target_pairs={{0,6},{1,7},{2,4},{3,5},{4,2},{5,3},{6,0},{7,1},{8,14},{9,15},{10,... | collective-permute-start | bytes 393224 | tf_op jit(solution)/shard_map/ppermute | solution.py:317
  52.5 10.8 %collective-permute-start.13 = (bf16[512,128]{1,0:T(8,128)(2,1)S(1)}, bf16[512,128]{1,0:T(8,128)(2,1)S(1)}, u32[]{:S(2)}, u32[]{:S(2)}) collective-permute-start(bf16[512,128]{1,0:T(8,128)(2,1)S(1)} %get-tuple-element.42), channel_id=1, source_target_pairs={{0,2},{1,3},{2,0},{3,1},{4,6},{5,7},{6,4},{7,5},{8,10},{9,11},{10,... | collective-permute-start | bytes 393224 | tf_op jit(solution)/shard_map/ppermute | solution.py:317
  60.8 27.9 %copy-start = (s32[256]{0:T(256)S(1)}, s32[256]{0:T(256)}, u32[]{:S(2)}) copy-start(s32[256]{0:T(256)} %param.16) | copy-start | bytes 3076
  60.8 27.9 %copy-start.1 = (f32[16]{0:T(128)S(1)}, f32[16]{0:T(128)}, u32[]{:S(2)}) copy-start(f32[16]{0:T(128)} %param.17) | copy-start | bytes 196
  63.4 6.2 %collective-permute-start.14 = (bf16[512,128]{1,0:T(8,128)(2,1)S(1)}, bf16[512,128]{1,0:T(8,128)(2,1)S(1)}, u32[]{:S(2)}, u32[]{:S(2)}) collective-permute-start(bf16[512,128]{1,0:T(8,128)(2,1)S(1)} %multiply_convert_fusion.refs_0_), channel_id=1, source_target_pairs={{0,8},{8,0},{16,24},{24,16},{1,9},{9,1},{17,25},{25,17},{2,10},{10... | collective-permute-start | bytes 393224 | tf_op jit(solution)/shard_map/ppermute | solution.py:317
  64.6 8.0 %collective-permute-start.15 = (bf16[512,128]{1,0:T(8,128)(2,1)S(1)}, bf16[512,128]{1,0:T(8,128)(2,1)S(1)}, u32[]{:S(2)}, u32[]{:S(2)}) collective-permute-start(bf16[512,128]{1,0:T(8,128)(2,1)S(1)} %multiply_convert_fusion.refs_0_), channel_id=1, source_target_pairs={{0,16},{8,24},{16,0},{24,8},{1,17},{9,25},{17,1},{25,9},{2,18},{10... | collective-permute-start | bytes 393224 | tf_op jit(solution)/shard_map/ppermute | solution.py:317
  66.3 6.3 %collective-permute-start.16 = (bf16[512,128]{1,0:T(8,128)(2,1)S(1)}, bf16[512,128]{1,0:T(8,128)(2,1)S(1)}, u32[]{:S(2)}, u32[]{:S(2)}) collective-permute-start(bf16[512,128]{1,0:T(8,128)(2,1)S(1)} %multiply_convert_fusion.refs_0_), channel_id=1, source_target_pairs={{0,24},{8,16},{16,8},{24,0},{1,25},{9,17},{17,9},{25,1},{2,26},{10... | collective-permute-start | bytes 393224 | tf_op jit(solution)/shard_map/ppermute | solution.py:317
  80.8 2.2 %collective-permute-start.17 = (bf16[1024,128]{1,0:T(8,128)(2,1)S(1)}, bf16[1024,128]{1,0:T(8,128)(2,1)S(1)}, u32[]{:S(2)}, u32[]{:S(2)}) collective-permute-start(bf16[1024,128]{1,0:T(8,128)(2,1)S(1)} %get-tuple-element.44), channel_id=1, source_target_pairs={{0,1},{1,0},{2,3},{3,2},{4,5},{5,4},{6,7},{7,6},{8,9},{9,8},{10,11... | collective-permute-start | bytes 786440 | tf_op jit(solution)/shard_map/ppermute | solution.py:317
  83.0 7.6 %collective-permute-start.18 = (bf16[256,128]{1,0:T(8,128)(2,1)S(1)}, bf16[256,128]{1,0:T(8,128)(2,1)S(1)}, u32[]{:S(2)}, u32[]{:S(2)}) collective-permute-start(bf16[256,128]{1,0:T(8,128)(2,1)S(1)} %get-tuple-element.45.after_ref), channel_id=1, source_target_pairs={{0,4},{1,5},{2,6},{3,7},{4,0},{5,1},{6,2},{7,3},{8,12},{9,13},{10,... | collective-permute-start | bytes 196616 | tf_op jit(solution)/shard_map/ppermute | solution.py:317
  83.0 7.5 %collective-permute-start.19 = (bf16[256,128]{1,0:T(8,128)(2,1)S(1)}, bf16[256,128]{1,0:T(8,128)(2,1)S(1)}, u32[]{:S(2)}, u32[]{:S(2)}) collective-permute-start(bf16[256,128]{1,0:T(8,128)(2,1)S(1)} %get-tuple-element.47), channel_id=1, source_target_pairs={{0,6},{1,7},{2,4},{3,5},{4,2},{5,3},{6,0},{7,1},{8,14},{9,15},{10,... | collective-permute-start | bytes 196616 | tf_op jit(solution)/shard_map/ppermute | solution.py:317
  87.4 4.6 %collective-permute-start.20 = (bf16[256,128]{1,0:T(8,128)(2,1)S(1)}, bf16[256,128]{1,0:T(8,128)(2,1)S(1)}, u32[]{:S(2)}, u32[]{:S(2)}) collective-permute-start(bf16[256,128]{1,0:T(8,128)(2,1)S(1)} %get-tuple-element.48), channel_id=1, source_target_pairs={{0,2},{1,3},{2,0},{3,1},{4,6},{5,7},{6,4},{7,5},{8,10},{9,11},{10,... | collective-permute-start | bytes 196616 | tf_op jit(solution)/shard_map/ppermute | solution.py:317

commit v5 on v4

--- a/solution.py
+++ b/solution.py
@@ -25,8 +25,11 @@
 PARAMS = pltpu.CompilerParams(vmem_limit_bytes=16 * MIB)
 
 
-def far_first(k, chips):
-    return k ^ (chips // 2)
+def block_place(k, chips):
+    place, last = 0, chips.bit_length() - 2
+    for j in range(last + 1):
+        place = place + (1 - (k >> j) % 2) * (1 << (last - j))
+    return place
 
 
 def iota(shape, dim):
@@ -64,7 +67,7 @@
     row = tile_row_ref[...]
     rel = (row // per_group) ^ my_col
     chips = 2 * chunk_tiles // per_group
-    place = (1 - rel % 2) * chips + far_first(rel // 2, chips)
+    place = (1 - rel % 2) * chips + block_place(rel // 2, chips)
     order = place * per_group + row % per_group
     order = jnp.where(iota((1, slots), 1) < count_ref[0, 0], order, row_tiles).astype(jnp.float32)
     col = tile_col_ref[...]
@@ -174,76 +177,61 @@
         odd_ref[rows:, :] = extra[...]
 
 
-def add_cores(offset, even_ref, other_ref, extra_refs, out_refs):
-    rows = even_ref.shape[0] // len(out_refs)
-    for i, out in enumerate(out_refs):
-        other = other_ref[offset + i * rows : offset + (i + 1) * rows, :].astype(jnp.float32)
-        out[0:rows, :] = (even_ref[i * rows : (i + 1) * rows, :] + other).astype(out.dtype)
-        for extra in extra_refs:
-            if out.shape[0] > rows:
-                size = extra.shape[0]
-                tail = other_ref[other_ref.shape[0] - size :, :].astype(jnp.float32)
-                both = extra[...].astype(jnp.float32) + pltpu.roll(tail, size // 2, 0)
-                out[rows:, :] = both.astype(out.dtype)
-
-
-def even_far_kernel(plan_ref, state, weights_ref, even_ref):
+def even_sent_kernel(plan_ref, state, weights_ref, even_ref):
     multiply(plan_ref, weights_ref, state, even_ref, 2, 1, even_ref.shape[0] // weights_ref.shape[1])
 
 
-def merge_kernel(outs, even_ref, other_ref, *refs):
-    add_cores(0, even_ref, other_ref, refs[:-outs], refs[-outs:])
-
-
-def even_near_kernel(outs, plan_ref, state, weights_ref, after_ref, other_ref, *refs):
-    extra_refs, out_refs, total = refs[: -outs - 1], refs[-outs - 1 : -1], refs[-1]
-    rows = total.shape[0]
-    multiply(plan_ref, weights_ref, state, total, 3, 1, rows // weights_ref.shape[1])
-    add_cores(rows, total, other_ref, extra_refs, out_refs)
-
-
-def add_kernel(own_ref, *refs):
-    out_ref = refs[-1]
-    rows = out_ref.shape[0]
-    total = own_ref[...]
-    for ref in refs[:-1]:
-        total = total + ref[0:rows, :].astype(jnp.float32)
-    out_ref[...] = total
-
-
-def place_kernel(chips, rows_here, block_rows, id_rows, mine_ref, other_ref, *refs):
-    far_refs, place_ref = refs[:-1], refs[-1]
+def merge_kernel(even_ref, other_ref, *refs):
+    extra_refs, sent_ref = refs[:-1], refs[-1]
+    rows = even_ref.shape[0]
+    sent_ref[0:rows, :] = (even_ref[...] + other_ref[0:rows, :].astype(jnp.float32)).astype(sent_ref.dtype)
+    for extra in extra_refs:
+        size = extra.shape[0]
+        tail = other_ref[2 * rows :, :].astype(jnp.float32)
+        both = extra[...].astype(jnp.float32) + pltpu.roll(tail, size // 4, 0)
+        sent_ref[rows:, :] = both.astype(sent_ref.dtype)
+
+
+def even_kept_kernel(plan_ref, state, weights_ref, after_ref, other_ref, kept_ref):
+    rows = kept_ref.shape[0]
+    multiply(plan_ref, weights_ref, state, kept_ref, 3, 1, rows // weights_ref.shape[1])
+    kept_ref[...] += other_ref[rows : 2 * rows, :].astype(jnp.float32)
+
+
+def round_kernel(ids, kept_ref, before_ref, came_ref, sent_ref, left_ref):
+    rows = left_ref.shape[0]
+    sent_ref[0:rows, :] = (kept_ref[0:rows, :] + came_ref[0:rows, :].astype(jnp.float32)).astype(sent_ref.dtype)
+    left_ref[...] = kept_ref[rows:, :] + came_ref[rows : 2 * rows, :].astype(jnp.float32)
+    if ids:
+        known = [r[2 * rows :, :].astype(jnp.float32)[:ids] for r in (before_ref, came_ref)]
+        sent_ref[rows:, :] = jnp.concatenate(known).astype(sent_ref.dtype)
+
+
+def place_kernel(chips, rows_here, id_rows, sent_ref, came_ref, place_ref):
     my_col = lax.axis_index("col")
-    extra = mine_ref.shape[0]
-
-    def places(rows):
-        ids = (rows[:id_rows] * BYTE + rows[id_rows : 2 * id_rows]).astype(jnp.int32)
-        rel = (ids // rows_here) ^ my_col
-        return ((1 - rel % 2) * chips + far_first(rel // 2, chips)) * rows_here + ids % rows_here
-
-    def tail(ref):
-        return ref[ref.shape[0] - extra :, :].astype(jnp.float32)
-
-    even, odd = [mine_ref[...].astype(jnp.float32)], [tail(other_ref)]
-    for ref in far_refs:
-        rows = tail(ref)
-        even.append(rows)
-        odd.append(pltpu.roll(rows, extra - extra // 2, 0))
+    half = chips // 2
+    step = 4 * id_rows
+    rows = (sent_ref.shape[0] // rows_here) * rows_here
+
     for k in range(chips):
-        at = far_first(k, chips) * id_rows
-        place_ref[at : at + id_rows, :] = places(odd[k])
-        at = at + chips * id_rows
-        place_ref[at : at + id_rows, :] = places(even[k])
+        ref = came_ref if k >= half else sent_ref
+        tail = ref[rows:, :].astype(jnp.float32)[k % half * step : (k % half + 1) * step]
+        for part in range(2):
+            own = tail[(1 - part) * 2 * id_rows :]
+            ids = (own[:id_rows] * BYTE + own[id_rows : 2 * id_rows]).astype(jnp.int32)
+            rel = (ids // rows_here) ^ my_col
+            place = (1 - rel % 2) * chips + block_place(rel // 2, chips)
+            place = place * rows_here + ids % rows_here
+            for r in range(id_rows):
+                at = ((part * chips + block_place(k, chips)) * id_rows + r) * LANES
+                place_ref[0:1, at : at + LANES] = place[r : r + 1, :]
 
 
 def pick_rows(place_ref, first, total, picked):
     def some(i, carry):
-        base = pl.multiple_of(i * UNPICK, UNPICK)
-        row = (first + base) // LANES
-        lane = (first + base) % LANES
-        rows = [total[pl.ds(place_ref[row, lane + j], 1), :] for j in range(UNPICK)]
         for j in range(UNPICK):
-            picked[pl.ds(base + j, 1), :] = rows[j]
+            at = i * UNPICK + j
+            picked[pl.ds(at, 1), :] = total[pl.ds(place_ref[0, first + at], 1), :]
         return carry
 
     lax.fori_loop(0, picked.shape[0] // UNPICK, some, 0)
@@ -258,15 +246,14 @@
     odd_ref[...] = picked[...].astype(odd_ref.dtype)
 
 
-def pick_far_kernel(place_ref, total, even_ref):
+def pick_sent_kernel(place_ref, total, even_ref):
     pick_rows(place_ref, 2 * even_ref.shape[0], total, even_ref)
 
 
-def pick_near_kernel(outs, place_ref, total, after_ref, other_ref, *refs):
-    out_refs, picked = refs[:-1], refs[-1]
-    rows = picked.shape[0]
-    pick_rows(place_ref, 3 * rows, total, picked)
-    add_cores(rows, picked, other_ref, (), out_refs)
+def pick_kept_kernel(place_ref, total, after_ref, other_ref, kept_ref):
+    rows = kept_ref.shape[0]
+    pick_rows(place_ref, 3 * rows, total, kept_ref)
+    kept_ref[...] += other_ref[rows : 2 * rows, :].astype(jnp.float32)
 
 
 def local(
@@ -356,31 +343,27 @@
 
     state_shape = ((zero_tile + 1) * tile, width)
 
-    half_chips = chips // 2
-
-    def send(sent, first):
-        return [swap(part, "col", ncols, 2 * (first + i)) for i, part in enumerate(sent)]
-
-    def collect(other, far_part, near_kernel, near_args, near_scalars, rows, turns, extra=()):
+    def collect(other, even, kept_kernel, kept_args, turns, extra=()):
+        rows = even.shape[0]
         more = sum(e.shape[0] for e in extra)
-        blocks = [array((rows + more, width), bf16)] * half_chips
-        far = call(functools.partial(merge_kernel, half_chips), "merge", blocks, (far_part, other, *extra))
-        own, *near = call(
-            functools.partial(near_kernel, half_chips),
-            "near",
-            [array((rows, width), f32)] + blocks[1:],
-            (*near_args, far[0], other, *extra),
-            scalars=near_scalars,
-            scratch=[pltpu.VMEM((half_chips * rows, width), f32)],
-            turns=turns,
+        sent = call(merge_kernel, "merge", array((rows + more, width), bf16), (even, other, *extra))
+        kept = call(
+            kept_kernel, "kept", array((rows, width), f32), (*kept_args, sent, other), scalars=1, turns=turns
         )
-        came_far, came_near = send(far, half_chips), send(near, 1)
-        return call(add_kernel, "add", array((rows, width), f32), (own, *came_far)), came_near, came_far
-
-    def add(total, came):
-        for part in came:
-            total = total + part[: total.shape[0]].astype(f32)
-        return total
+        apart, ids = 1, 4 * id_rows if extra else 0
+        while True:
+            came = swap(sent, "col", ncols, 2 * apart)
+            apart *= 2
+            if apart == chips:
+                return kept, sent, came
+            rows //= 2
+            sent, kept = call(
+                functools.partial(round_kernel, ids),
+                "round",
+                [array((rows + 2 * ids, width), bf16), array((rows, width), f32)],
+                (kept, sent, came),
+            )
+            ids *= 2
 
     for hop in range(HOPS - 1):
         extra = (mine,) if hop == 0 else ()
@@ -394,20 +377,18 @@
             turns=0.5,
         )
         other = swap_cores(odd)
-        far_part = call(
-            even_far_kernel, "far", array((chunk_rows, width), f32), (plan, held, weights), scalars=1, turns=0.25
+        even = call(
+            even_sent_kernel, "even", array((chunk_rows, width), f32), (plan, held, weights), scalars=1, turns=0.25
         )
-        total, near, far = collect(
-            other, far_part, even_near_kernel, (plan, held, weights), 1, rows_here, 0.25, extra
-        )
+        kept, sent, came = collect(other, even, even_kept_kernel, (plan, held, weights), 0.25, extra)
         if hop == 0:
             place = call(
-                functools.partial(place_kernel, chips, rows_here, block_rows, id_rows),
+                functools.partial(place_kernel, chips, rows_here, id_rows),
                 "place",
-                array((2 * chips * id_rows, LANES), jnp.int32),
-                (mine, other, *near, *far),
+                array((1, ncols * new_here), jnp.int32),
+                (sent, came),
             )
-        pieces = spread((square * add(total, near)).astype(bf16))
+        pieces = spread((square * (kept + came[:rows_here].astype(f32))).astype(bf16))
 
     odd, total = call(
         functools.partial(last_kernel, nrows),
@@ -419,11 +400,11 @@
         turns=1.0,
     )
     other = swap_cores(odd)
-    far_part = call(
-        pick_far_kernel, "pick", array((half_chips * new_here, width), f32), (place, total), scalars=1, turns=0.25
-    )
-    summed, near, _ = collect(other, far_part, pick_near_kernel, (place, total), 1, new_here, 0.25)
-    picked = add(summed, near)
+    even = call(
+        pick_sent_kernel, "pick", array((chips * new_here // 2, width), f32), (place, total), scalars=1, turns=0.25
+    )
+    kept, _, came = collect(other, even, pick_kept_kernel, (place, total), 0.25)
+    picked = kept + came.astype(f32)
     buckets = jnp.arange(bucket_norm.shape[0], dtype=jnp.int32)
     target = jnp.sum(
         jnp.where(new_bucket[:, None] == buckets[None, :], bucket_norm[None, :], jnp.float32(0.0)),

time: 93.5 us -> 97.6 us (1.044)
  waiting for transfers between devices: 34.7 us -> 44.6 us
  Pallas kernels: 30.9 us -> 22.1 us
  starting transfers between devices: 24.5 us -> 27.7 us
    ppermute x21 -> x18, waiting for transfers between devices: 34.7 us -> 44.6 us  [swap(): return lax.ppermute(array, axis, [(i, i ^ mask) for i in range(size)])]
    pallas_call x18, Pallas kernels: 30.9 us -> 22.1 us  [call(): pl.pallas_call(kernel, out_shape=out_shape, grid_spec=pltpu.PrefetchScala...]
    ppermute x21 -> x18, starting transfers between devices: 24.5 us -> 27.7 us  [swap(): return lax.ppermute(array, axis, [(i, i ^ mask) for i in range(size)])]
  transfers between devices with their start and end apart: 21 -> 18, of which waited for: 12 -> 15; matrix products, arithmetic and copies ran while one was open for 1% -> 1% of each run, Pallas kernels for 17% -> 12%
where the time goes in v5:
time: 97.6 us; the launch traced here: 97 us
  waiting for transfers between devices  44.6 us (46%)
  starting transfers between devices  27.7 us (28%)
  Pallas kernels  22.1 us (23%)
  other arithmetic  1.81 us (2%)
    ppermute x18, waiting for transfers between devices, swap(): return lax.ppermute(array, axis, [(i, i ^ mask) for i in range(size)])  44.6 us
    ppermute x18, starting transfers between devices, swap(): return lax.ppermute(array, axis, [(i, i ^ mask) for i in range(size)])  27.7 us
    pallas_call x18, Pallas kernels, call(): pl.pallas_call(kernel, out_shape=out_shape, grid_spec=pltpu.PrefetchScala...  22.1 us
  transfers between devices with their start and end apart: 18, of which 15 were waited for; matrix products, arithmetic and copies ran while one was open for 1% of the time, Pallas kernels for 12%

profile of v5, /device:TPU:0, one launch (start us, length us, event | category | flops | bytes accessed | tf_op | source)
XLA Modules:
  0.0 97.0 jit_solution(17083356460838296921)
XLA Ops:
  0.0 1.1 %begin.1 = (bf16[512,128]{1,0:T(8,128)(2,1)S(1)}, f32[512,128]{1,0:T(8,128)S(1)}) custom-call(s32[4,128]{1,0:T(4,128)} %bitcast.25, bf16[512,128]{1,0:T(8,128)(2,1)} %embed_hbm.1), custom_call_target="tpu_custom_call" | custom-call | tf_op jit(solution)/shard_map/begin/pallas_call | solution.py:288
  1.1 3.0 %collective-permute-start = (bf16[512,128]{1,0:T(8,128)(2,1)S(1)}, bf16[512,128]{1,0:T(8,128)(2,1)S(1)}, u32[]{:S(2)}, u32[]{:S(2)}) collective-permute-start(bf16[512,128]{1,0:T(8,128)(2,1)S(1)} %get-tuple-element.22.refs_0_), channel_id=1, source_target_pairs={{0,8},{8,0},{16,24},{24,16},{1,9},{9,1},{17,25},{25,17},{2,10},{10... | collective-permute-start | bytes 393224 | tf_op jit(solution)/shard_map/ppermute | solution.py:304
  4.1 1.5 %collective-permute-start.1 = (bf16[512,128]{1,0:T(8,128)(2,1)S(1)}, bf16[512,128]{1,0:T(8,128)(2,1)S(1)}, u32[]{:S(2)}, u32[]{:S(2)}) collective-permute-start(bf16[512,128]{1,0:T(8,128)(2,1)S(1)} %get-tuple-element.22.refs_0_), channel_id=1, source_target_pairs={{0,16},{8,24},{16,0},{24,8},{1,17},{9,25},{17,1},{25,9},{2,18},{10... | collective-permute-start | bytes 393224 | tf_op jit(solution)/shard_map/ppermute | solution.py:304
  5.6 0.0 collective-permute-start.2
  5.6 0.7 fusion.4
  7.0 3.4 %plan.1 = (s32[8,512]{1,0:T(8,128)S(1)}, bf16[256,128,128]{2,1,0:T(8,128)(2,1)S(1)}) custom-call(s32[1,1]{1,0:T(1,128)S(6)} %copy.10.count_ref, s32[1,256]{1,0:T(1,128)} %bitcast.26, s32[1,256]{1,0:T(1,128)} %bitcast.27, bf16[256,128,128]{2,1,0:T(8,128)(2,1)} %bitcast.24), custom_call_target="tpu_custom_call" | custom-call | tf_op jit(solution)/shard_map/plan/pallas_call | solution.py:288
  10.5 0.0 collective-permute-done.refs_1_
  10.5 1.4 %collective-permute-done.1.refs_2_ = bf16[512,128]{1,0:T(8,128)(2,1)S(1)} collective-permute-done((bf16[512,128]{1,0:T(8,128)(2,1)S(1)}, bf16[512,128]{1,0:T(8,128)(2,1)S(1)}, u32[]{:S(2)}, u32[]{:S(2)}) %collective-permute-start.1) | collective-permute-done | bytes 131104 | tf_op jit(solution)/shard_map/ppermute | solution.py:304
  11.9 0.0 collective-permute-done.2.refs_3_
  11.9 2.2 %odd.2 = (bf16[2064,128]{1,0:T(8,128)(2,1)S(1)}, bf16[2176,128]{1,0:T(8,128)(2,1)S(1)}) custom-call(s32[8,512]{1,0:T(8,128)S(1)} %get-tuple-element.21.plan_ref, bf16[512,128]{1,0:T(8,128)(2,1)S(1)} %get-tuple-element.22.refs_0_, bf16[512,128]{1,0:T(8,128)(2,1)S(1)} %collective-permute-done.refs_1_, bf16[512,128]{1,0:T(8,128)(2,1)S(1)} %collective-permute-done.1.refs_2_, ...), custom_call_target="tpu_custom_call" | custom-call | flops 536870912 | bytes 4194304 | tf_op jit(solution)/shard_map/odd/pallas_call | solution.py:288
  14.1 0.1 collective-permute-start.3
  14.1 1.4 %even.2.even_ref = f32[1024,128]{1,0:T(8,128)S(1)} custom-call(s32[8,512]{1,0:T(8,128)S(1)} %get-tuple-element.21.plan_ref, bf16[2176,128]{1,0:T(8,128)(2,1)S(1)} %get-tuple-element.24.state, bf16[256,128,128]{2,1,0:T(8,128)(2,1)S(1)} %get-tuple-element.23.refs_4_.weights_ref), custom_call_target="tpu_custom_call" | custom-call | flops 268435456 | bytes 2097152 | tf_op jit(solution)/shard_map/even/pallas_call | solution.py:288
  15.6 0.5 collective-permute-done.3.other_ref
  16.0 0.1 merge.3.after_ref.before_ref
  16.1 3.3 %collective-permute-start.4 = (bf16[1040,128]{1,0:T(8,128)(2,1)S(1)}, bf16[1040,128]{1,0:T(8,128)(2,1)S(1)}, u32[]{:S(2)}, u32[]{:S(2)}) collective-permute-start(bf16[1040,128]{1,0:T(8,128)(2,1)S(1)} %merge.3.after_ref.before_ref), channel_id=1, source_target_pairs={{0,2},{1,3},{2,0},{3,1},{4,6},{5,7},{6,4},{7,5},{8,10},{9,11},{10,... | collective-permute-start | bytes 798728 | tf_op jit(solution)/shard_map/ppermute | solution.py:304
  19.4 1.5 %kept.3.kept_ref = f32[1024,128]{1,0:T(8,128)S(1)} custom-call(s32[8,512]{1,0:T(8,128)S(1)} %get-tuple-element.21.plan_ref, bf16[2176,128]{1,0:T(8,128)(2,1)S(1)} %get-tuple-element.24.state, bf16[256,128,128]{2,1,0:T(8,128)(2,1)S(1)} %get-tuple-element.23.refs_4_.weights_ref, bf16[1040,128]{1,0:T(8,128)(2,1)S(1)} %merge.3.after_ref.before_ref, ...), custom_call_target="tpu_custom_call" | custom-call | flops 268435456 | bytes 2097152 | tf_op jit(solution)/shard_map/kept/pallas_call | solution.py:288
  20.9 5.5 %collective-permute-done.4.came_ref = bf16[1040,128]{1,0:T(8,128)(2,1)S(1)} collective-permute-done((bf16[1040,128]{1,0:T(8,128)(2,1)S(1)}, bf16[1040,128]{1,0:T(8,128)(2,1)S(1)}, u32[]{:S(2)}, u32[]{:S(2)}) %collective-permute-start.4) | collective-permute-done | bytes 266272 | tf_op jit(solution)/shard_map/ppermute | solution.py:304
  26.5 0.1 round.3
  26.5 1.4 %collective-permute-start.5 = (bf16[528,128]{1,0:T(8,128)(2,1)S(1)}, bf16[528,128]{1,0:T(8,128)(2,1)S(1)}, u32[]{:S(2)}, u32[]{:S(2)}) collective-permute-start(bf16[528,128]{1,0:T(8,128)(2,1)S(1)} %get-tuple-element.26.sent_ref), channel_id=1, source_target_pairs={{0,4},{1,5},{2,6},{3,7},{4,0},{5,1},{6,2},{7,3},{8,12},{9,13},{10,... | collective-permute-start | bytes 405512 | tf_op jit(solution)/shard_map/ppermute | solution.py:304
  28.0 7.8 %collective-permute-done.5.came_ref = bf16[528,128]{1,0:T(8,128)(2,1)S(1)} collective-permute-done((bf16[528,128]{1,0:T(8,128)(2,1)S(1)}, bf16[528,128]{1,0:T(8,128)(2,1)S(1)}, u32[]{:S(2)}, u32[]{:S(2)}) %collective-permute-start.5) | collective-permute-done | bytes 135200 | tf_op jit(solution)/shard_map/ppermute | solution.py:304
  35.8 0.1 multiply_convert_fusion.1.refs_0_
  35.9 1.2 %collective-permute-start.6 = (bf16[512,128]{1,0:T(8,128)(2,1)S(1)}, bf16[512,128]{1,0:T(8,128)(2,1)S(1)}, u32[]{:S(2)}, u32[]{:S(2)}) collective-permute-start(bf16[512,128]{1,0:T(8,128)(2,1)S(1)} %multiply_convert_fusion.1.refs_0_), channel_id=1, source_target_pairs={{0,8},{8,0},{16,24},{24,16},{1,9},{9,1},{17,25},{25,17},{2,10},{10... | collective-permute-start | bytes 393224 | tf_op jit(solution)/shard_map/ppermute | solution.py:304
  37.1 0.6 collective-permute-start.7
  37.7 1.7 %collective-permute-start.8 = (bf16[512,128]{1,0:T(8,128)(2,1)S(1)}, bf16[512,128]{1,0:T(8,128)(2,1)S(1)}, u32[]{:S(2)}, u32[]{:S(2)}) collective-permute-start(bf16[512,128]{1,0:T(8,128)(2,1)S(1)} %multiply_convert_fusion.1.refs_0_), channel_id=1, source_target_pairs={{0,24},{8,16},{16,8},{24,0},{1,25},{9,17},{17,9},{25,1},{2,26},{10... | collective-permute-start | bytes 393224 | tf_op jit(solution)/shard_map/ppermute | solution.py:304
  39.4 2.6 %collective-permute-done.6.refs_1_ = bf16[512,128]{1,0:T(8,128)(2,1)S(1)} collective-permute-done((bf16[512,128]{1,0:T(8,128)(2,1)S(1)}, bf16[512,128]{1,0:T(8,128)(2,1)S(1)}, u32[]{:S(2)}, u32[]{:S(2)}) %collective-permute-start.6) | collective-permute-done | bytes 131104 | tf_op jit(solution)/shard_map/ppermute | solution.py:304
  42.0 1.0 %collective-permute-done.7.refs_2_ = bf16[512,128]{1,0:T(8,128)(2,1)S(1)} collective-permute-done((bf16[512,128]{1,0:T(8,128)(2,1)S(1)}, bf16[512,128]{1,0:T(8,128)(2,1)S(1)}, u32[]{:S(2)}, u32[]{:S(2)}) %collective-permute-start.7) | collective-permute-done | bytes 131104 | tf_op jit(solution)/shard_map/ppermute | solution.py:304
  43.0 1.2 %collective-permute-done.8.refs_3_ = bf16[512,128]{1,0:T(8,128)(2,1)S(1)} collective-permute-done((bf16[512,128]{1,0:T(8,128)(2,1)S(1)}, bf16[512,128]{1,0:T(8,128)(2,1)S(1)}, u32[]{:S(2)}, u32[]{:S(2)}) %collective-permute-start.8) | collective-permute-done | bytes 131104 | tf_op jit(solution)/shard_map/ppermute | solution.py:304
  44.3 2.2 %odd.3 = (bf16[2048,128]{1,0:T(8,128)(2,1)S(1)}, bf16[2176,128]{1,0:T(8,128)(2,1)S(1)}) custom-call(s32[8,512]{1,0:T(8,128)S(1)} %get-tuple-element.21.plan_ref, bf16[512,128]{1,0:T(8,128)(2,1)S(1)} %multiply_convert_fusion.1.refs_0_, bf16[512,128]{1,0:T(8,128)(2,1)S(1)} %collective-permute-done.6.refs_1_, ...), custom_call_target="tpu_custom_call" | custom-call | flops 536870912 | bytes 4194304 | tf_op jit(solution)/shard_map/odd/pallas_call | solution.py:288
  46.5 0.1 collective-permute-start.9
  46.5 1.4 %even.3.even_ref = f32[1024,128]{1,0:T(8,128)S(1)} custom-call(s32[8,512]{1,0:T(8,128)S(1)} %get-tuple-element.21.plan_ref, bf16[2176,128]{1,0:T(8,128)(2,1)S(1)} %get-tuple-element.29.state, bf16[256,128,128]{2,1,0:T(8,128)(2,1)S(1)} %get-tuple-element.23.refs_4_.weights_ref), custom_call_target="tpu_custom_call" | custom-call | flops 268435456 | bytes 2097152 | tf_op jit(solution)/shard_map/even/pallas_call | solution.py:288
  48.0 0.5 collective-permute-done.9.other_ref
  48.5 3.2 %collective-permute-start.10 = (bf16[1024,128]{1,0:T(8,128)(2,1)S(1)}, bf16[1024,128]{1,0:T(8,128)(2,1)S(1)}, u32[]{:S(2)}, u32[]{:S(2)}) collective-permute-start(bf16[1024,128]{1,0:T(8,128)(2,1)S(1)} %merge.4.after_ref.before_ref), channel_id=1, source_target_pairs={{0,2},{1,3},{2,0},{3,1},{4,6},{5,7},{6,4},{7,5},{8,10},{9,11},{10,... | collective-permute-start | bytes 786440 | tf_op jit(solution)/shard_map/ppermute | solution.py:304
  51.7 1.5 %kept.4.kept_ref = f32[1024,128]{1,0:T(8,128)S(1)} custom-call(s32[8,512]{1,0:T(8,128)S(1)} %get-tuple-element.21.plan_ref, bf16[2176,128]{1,0:T(8,128)(2,1)S(1)} %get-tuple-element.29.state, bf16[256,128,128]{2,1,0:T(8,128)(2,1)S(1)} %get-tuple-element.23.refs_4_.weights_ref, bf16[1024,128]{1,0:T(8,128)(2,1)S(1)} %merge.4.after_ref.before_ref, ...), custom_call_target="tpu_custom_call" | custom-call | flops 268435456 | bytes 2097152 | tf_op jit(solution)/shard_map/kept/pallas_call | solution.py:288
  53.2 5.5 %collective-permute-done.10.came_ref = bf16[1024,128]{1,0:T(8,128)(2,1)S(1)} collective-permute-done((bf16[1024,128]{1,0:T(8,128)(2,1)S(1)}, bf16[1024,128]{1,0:T(8,128)(2,1)S(1)}, u32[]{:S(2)}, u32[]{:S(2)}) %collective-permute-start.10) | collective-permute-done | bytes 262176 | tf_op jit(solution)/shard_map/ppermute | solution.py:304
  58.7 0.0 copy-start
  58.7 0.0 copy-start.1
  58.7 2.2 %collective-permute-start.11 = (bf16[512,128]{1,0:T(8,128)(2,1)S(1)}, bf16[512,128]{1,0:T(8,128)(2,1)S(1)}, u32[]{:S(2)}, u32[]{:S(2)}) collective-permute-start(bf16[512,128]{1,0:T(8,128)(2,1)S(1)} %get-tuple-element.32), channel_id=1, source_target_pairs={{0,4},{1,5},{2,6},{3,7},{4,0},{5,1},{6,2},{7,3},{8,12},{9,13},{10,... | collective-permute-start | bytes 393224 | tf_op jit(solution)/shard_map/ppermute | solution.py:304
  61.0 6.8 %collective-permute-done.11 = bf16[512,128]{1,0:T(8,128)(2,1)S(1)} collective-permute-done((bf16[512,128]{1,0:T(8,128)(2,1)S(1)}, bf16[512,128]{1,0:T(8,128)(2,1)S(1)}, u32[]{:S(2)}, u32[]{:S(2)}) %collective-permute-start.11) | collective-permute-done | bytes 131104 | tf_op jit(solution)/shard_map/ppermute | solution.py:304
  67.9 1.5 %collective-permute-start.12 = (bf16[512,128]{1,0:T(8,128)(2,1)S(1)}, bf16[512,128]{1,0:T(8,128)(2,1)S(1)}, u32[]{:S(2)}, u32[]{:S(2)}) collective-permute-start(bf16[512,128]{1,0:T(8,128)(2,1)S(1)} %multiply_convert_fusion.refs_0_), channel_id=1, source_target_pairs={{0,8},{8,0},{16,24},{24,16},{1,9},{9,1},{17,25},{25,17},{2,10},{10... | collective-permute-start | bytes 393224 | tf_op jit(solution)/shard_map/ppermute | solution.py:304
  69.4 0.6 collective-permute-start.13
  69.9 1.5 %collective-permute-start.14 = (bf16[512,128]{1,0:T(8,128)(2,1)S(1)}, bf16[512,128]{1,0:T(8,128)(2,1)S(1)}, u32[]{:S(2)}, u32[]{:S(2)}) collective-permute-start(bf16[512,128]{1,0:T(8,128)(2,1)S(1)} %multiply_convert_fusion.refs_0_), channel_id=1, source_target_pairs={{0,24},{8,16},{16,8},{24,0},{1,25},{9,17},{17,9},{25,1},{2,26},{10... | collective-permute-start | bytes 393224 | tf_op jit(solution)/shard_map/ppermute | solution.py:304
  71.4 0.1 place.1.place_ref
  71.5 1.8 %collective-permute-done.12.refs_1_ = bf16[512,128]{1,0:T(8,128)(2,1)S(1)} collective-permute-done((bf16[512,128]{1,0:T(8,128)(2,1)S(1)}, bf16[512,128]{1,0:T(8,128)(2,1)S(1)}, u32[]{:S(2)}, u32[]{:S(2)}) %collective-permute-start.12) | collective-permute-done | bytes 131104 | tf_op jit(solution)/shard_map/ppermute | solution.py:304
  73.3 3.6 %collective-permute-done.13.refs_2_ = bf16[512,128]{1,0:T(8,128)(2,1)S(1)} collective-permute-done((bf16[512,128]{1,0:T(8,128)(2,1)S(1)}, bf16[512,128]{1,0:T(8,128)(2,1)S(1)}, u32[]{:S(2)}, u32[]{:S(2)}) %collective-permute-start.13) | collective-permute-done | bytes 131104 | tf_op jit(solution)/shard_map/ppermute | solution.py:304
  76.9 0.0 collective-permute-done.14.refs_3_
  76.9 4.6 %last.1 = (bf16[1024,128]{1,0:T(8,128)(2,1)S(1)}, f32[4096,128]{1,0:T(8,128)S(1)}) custom-call(s32[8,512]{1,0:T(8,128)S(1)} %get-tuple-element.21.plan_ref, s32[1,2048]{1,0:T(1,128)S(1)} %place.1.place_ref, bf16[512,128]{1,0:T(8,128)(2,1)S(1)} %multiply_convert_fusion.refs_0_, bf16[512,128]{1,0:T(8,128)(2,1)S(1)} %collective-permute-done.12.refs_1_, ...), custom_call_target="tpu_custom_call" | custom-call | flops 1073741824 | bytes 8388608 | tf_op jit(solution)/shard_map/last/pallas_call | solution.py:288
  81.5 0.1 collective-permute-start.15
  81.6 1.2 %pick.1.even_ref = f32[512,128]{1,0:T(8,128)S(1)} custom-call(s32[1,2048]{1,0:T(1,128)S(1)} %place.1.place_ref, f32[4096,128]{1,0:T(8,128)S(1)} %get-tuple-element.33.total), custom_call_target="tpu_custom_call" | custom-call | flops 268435456 | bytes 2097152 | tf_op jit(solution)/shard_map/pick/pallas_call | solution.py:288
  82.8 0.3 collective-permute-done.15.other_ref
  83.1 3.5 %collective-permute-start.16 = (bf16[512,128]{1,0:T(8,128)(2,1)S(1)}, bf16[512,128]{1,0:T(8,128)(2,1)S(1)}, u32[]{:S(2)}, u32[]{:S(2)}) collective-permute-start(bf16[512,128]{1,0:T(8,128)(2,1)S(1)} %merge.5.after_ref.before_ref), channel_id=1, source_target_pairs={{0,2},{1,3},{2,0},{3,1},{4,6},{5,7},{6,4},{7,5},{8,10},{9,11},{10,... | collective-permute-start | bytes 393224 | tf_op jit(solution)/shard_map/ppermute | solution.py:304
  86.7 1.2 %kept.5.kept_ref = f32[512,128]{1,0:T(8,128)S(1)} custom-call(s32[1,2048]{1,0:T(1,128)S(1)} %place.1.place_ref, f32[4096,128]{1,0:T(8,128)S(1)} %get-tuple-element.33.total, bf16[512,128]{1,0:T(8,128)(2,1)S(1)} %merge.5.after_ref.before_ref, bf16[1024,128]{1,0:T(8,128)(2,1)S(1)} %collective-permute-done.15.other_ref), custom_call_target="tpu_custom_call" | custom-call | flops 268435456 | bytes 2097152 | tf_op jit(solution)/shard_map/kept/pallas_call | solution.py:288
  87.9 2.6 %collective-permute-done.16.came_ref = bf16[512,128]{1,0:T(8,128)(2,1)S(1)} collective-permute-done((bf16[512,128]{1,0:T(8,128)(2,1)S(1)}, bf16[512,128]{1,0:T(8,128)(2,1)S(1)}, u32[]{:S(2)}, u32[]{:S(2)}) %collective-permute-start.16) | collective-permute-done | bytes 131104 | tf_op jit(solution)/shard_map/ppermute | solution.py:304
  90.6 2.1 %collective-permute-start.17 = (bf16[256,128]{1,0:T(8,128)(2,1)S(1)}, bf16[256,128]{1,0:T(8,128)(2,1)S(1)}, u32[]{:S(2)}, u32[]{:S(2)}) collective-permute-start(bf16[256,128]{1,0:T(8,128)(2,1)S(1)} %get-tuple-element.36), channel_id=1, source_target_pairs={{0,4},{1,5},{2,6},{3,7},{4,0},{5,1},{6,2},{7,3},{8,12},{9,13},{10,... | collective-permute-start | bytes 196616 | tf_op jit(solution)/shard_map/ppermute | solution.py:304
  92.7 0.0 copy-done
  92.7 0.0 copy-done.1
  92.7 0.1 select_reduce_fusion
  92.8 3.3 %collective-permute-done.17 = bf16[256,128]{1,0:T(8,128)(2,1)S(1)} collective-permute-done((bf16[256,128]{1,0:T(8,128)(2,1)S(1)}, bf16[256,128]{1,0:T(8,128)(2,1)S(1)}, u32[]{:S(2)}, u32[]{:S(2)}) %collective-permute-start.17) | collective-permute-done | bytes 65568 | tf_op jit(solution)/shard_map/ppermute | solution.py:304
  96.1 0.1 multiply_reduce_fusion
  96.2 0.8 multiply_multiply_fusion
  (7 shorter events, 0.2 us)
Async XLA Ops:
  1.1 9.4 %collective-permute-start = (bf16[512,128]{1,0:T(8,128)(2,1)S(1)}, bf16[512,128]{1,0:T(8,128)(2,1)S(1)}, u32[]{:S(2)}, u32[]{:S(2)}) collective-permute-start(bf16[512,128]{1,0:T(8,128)(2,1)S(1)} %get-tuple-element.22.refs_0_), channel_id=1, source_target_pairs={{0,8},{8,0},{16,24},{24,16},{1,9},{9,1},{17,25},{25,17},{2,10},{10... | collective-permute-start | bytes 393224 | tf_op jit(solution)/shard_map/ppermute | solution.py:304
  4.1 7.8 %collective-permute-start.1 = (bf16[512,128]{1,0:T(8,128)(2,1)S(1)}, bf16[512,128]{1,0:T(8,128)(2,1)S(1)}, u32[]{:S(2)}, u32[]{:S(2)}) collective-permute-start(bf16[512,128]{1,0:T(8,128)(2,1)S(1)} %get-tuple-element.22.refs_0_), channel_id=1, source_target_pairs={{0,16},{8,24},{16,0},{24,8},{1,17},{9,25},{17,1},{25,9},{2,18},{10... | collective-permute-start | bytes 393224 | tf_op jit(solution)/shard_map/ppermute | solution.py:304
  5.6 6.3 %collective-permute-start.2 = (bf16[512,128]{1,0:T(8,128)(2,1)S(1)}, bf16[512,128]{1,0:T(8,128)(2,1)S(1)}, u32[]{:S(2)}, u32[]{:S(2)}) collective-permute-start(bf16[512,128]{1,0:T(8,128)(2,1)S(1)} %get-tuple-element.22.refs_0_), channel_id=1, source_target_pairs={{0,24},{8,16},{16,8},{24,0},{1,25},{9,17},{17,9},{25,1},{2,26},{10... | collective-permute-start | bytes 393224 | tf_op jit(solution)/shard_map/ppermute | solution.py:304
  14.1 2.0 %collective-permute-start.3 = (bf16[2064,128]{1,0:T(8,128)(2,1)S(1)}, bf16[2064,128]{1,0:T(8,128)(2,1)S(1)}, u32[]{:S(2)}, u32[]{:S(2)}) collective-permute-start(bf16[2064,128]{1,0:T(8,128)(2,1)S(1)} %get-tuple-element.25), channel_id=1, source_target_pairs={{0,1},{1,0},{2,3},{3,2},{4,5},{5,4},{6,7},{7,6},{8,9},{9,8},{10,11... | collective-permute-start | bytes 1585160 | tf_op jit(solution)/shard_map/ppermute | solution.py:304
  16.1 10.4 %collective-permute-start.4 = (bf16[1040,128]{1,0:T(8,128)(2,1)S(1)}, bf16[1040,128]{1,0:T(8,128)(2,1)S(1)}, u32[]{:S(2)}, u32[]{:S(2)}) collective-permute-start(bf16[1040,128]{1,0:T(8,128)(2,1)S(1)} %merge.3.after_ref.before_ref), channel_id=1, source_target_pairs={{0,2},{1,3},{2,0},{3,1},{4,6},{5,7},{6,4},{7,5},{8,10},{9,11},{10,... | collective-permute-start | bytes 798728 | tf_op jit(solution)/shard_map/ppermute | solution.py:304
  26.5 9.3 %collective-permute-start.5 = (bf16[528,128]{1,0:T(8,128)(2,1)S(1)}, bf16[528,128]{1,0:T(8,128)(2,1)S(1)}, u32[]{:S(2)}, u32[]{:S(2)}) collective-permute-start(bf16[528,128]{1,0:T(8,128)(2,1)S(1)} %get-tuple-element.26.sent_ref), channel_id=1, source_target_pairs={{0,4},{1,5},{2,6},{3,7},{4,0},{5,1},{6,2},{7,3},{8,12},{9,13},{10,... | collective-permute-start | bytes 405512 | tf_op jit(solution)/shard_map/ppermute | solution.py:304
  35.9 6.1 %collective-permute-start.6 = (bf16[512,128]{1,0:T(8,128)(2,1)S(1)}, bf16[512,128]{1,0:T(8,128)(2,1)S(1)}, u32[]{:S(2)}, u32[]{:S(2)}) collective-permute-start(bf16[512,128]{1,0:T(8,128)(2,1)S(1)} %multiply_convert_fusion.1.refs_0_), channel_id=1, source_target_pairs={{0,8},{8,0},{16,24},{24,16},{1,9},{9,1},{17,25},{25,17},{2,10},{10... | collective-permute-start | bytes 393224 | tf_op jit(solution)/shard_map/ppermute | solution.py:304
  37.1 6.0 %collective-permute-start.7 = (bf16[512,128]{1,0:T(8,128)(2,1)S(1)}, bf16[512,128]{1,0:T(8,128)(2,1)S(1)}, u32[]{:S(2)}, u32[]{:S(2)}) collective-permute-start(bf16[512,128]{1,0:T(8,128)(2,1)S(1)} %multiply_convert_fusion.1.refs_0_), channel_id=1, source_target_pairs={{0,16},{8,24},{16,0},{24,8},{1,17},{9,25},{17,1},{25,9},{2,18},{10... | collective-permute-start | bytes 393224 | tf_op jit(solution)/shard_map/ppermute | solution.py:304
  37.7 6.6 %collective-permute-start.8 = (bf16[512,128]{1,0:T(8,128)(2,1)S(1)}, bf16[512,128]{1,0:T(8,128)(2,1)S(1)}, u32[]{:S(2)}, u32[]{:S(2)}) collective-permute-start(bf16[512,128]{1,0:T(8,128)(2,1)S(1)} %multiply_convert_fusion.1.refs_0_), channel_id=1, source_target_pairs={{0,24},{8,16},{16,8},{24,0},{1,25},{9,17},{17,9},{25,1},{2,26},{10... | collective-permute-start | bytes 393224 | tf_op jit(solution)/shard_map/ppermute | solution.py:304
  46.5 2.0 %collective-permute-start.9 = (bf16[2048,128]{1,0:T(8,128)(2,1)S(1)}, bf16[2048,128]{1,0:T(8,128)(2,1)S(1)}, u32[]{:S(2)}, u32[]{:S(2)}) collective-permute-start(bf16[2048,128]{1,0:T(8,128)(2,1)S(1)} %get-tuple-element.30), channel_id=1, source_target_pairs={{0,1},{1,0},{2,3},{3,2},{4,5},{5,4},{6,7},{7,6},{8,9},{9,8},{10,11... | collective-permute-start | bytes 1572872 | tf_op jit(solution)/shard_map/ppermute | solution.py:304
  48.5 10.2 %collective-permute-start.10 = (bf16[1024,128]{1,0:T(8,128)(2,1)S(1)}, bf16[1024,128]{1,0:T(8,128)(2,1)S(1)}, u32[]{:S(2)}, u32[]{:S(2)}) collective-permute-start(bf16[1024,128]{1,0:T(8,128)(2,1)S(1)} %merge.4.after_ref.before_ref), channel_id=1, source_target_pairs={{0,2},{1,3},{2,0},{3,1},{4,6},{5,7},{6,4},{7,5},{8,10},{9,11},{10,... | collective-permute-start | bytes 786440 | tf_op jit(solution)/shard_map/ppermute | solution.py:304
  58.7 34.0 %copy-start = (s32[256]{0:T(256)S(1)}, s32[256]{0:T(256)}, u32[]{:S(2)}) copy-start(s32[256]{0:T(256)} %param.16) | copy-start | bytes 3076
  58.7 34.0 %copy-start.1 = (f32[16]{0:T(128)S(1)}, f32[16]{0:T(128)}, u32[]{:S(2)}) copy-start(f32[16]{0:T(128)} %param.17) | copy-start | bytes 196
  58.7 9.1 %collective-permute-start.11 = (bf16[512,128]{1,0:T(8,128)(2,1)S(1)}, bf16[512,128]{1,0:T(8,128)(2,1)S(1)}, u32[]{:S(2)}, u32[]{:S(2)}) collective-permute-start(bf16[512,128]{1,0:T(8,128)(2,1)S(1)} %get-tuple-element.32), channel_id=1, source_target_pairs={{0,4},{1,5},{2,6},{3,7},{4,0},{5,1},{6,2},{7,3},{8,12},{9,13},{10,... | collective-permute-start | bytes 393224 | tf_op jit(solution)/shard_map/ppermute | solution.py:304
  67.9 5.5 %collective-permute-start.12 = (bf16[512,128]{1,0:T(8,128)(2,1)S(1)}, bf16[512,128]{1,0:T(8,128)(2,1)S(1)}, u32[]{:S(2)}, u32[]{:S(2)}) collective-permute-start(bf16[512,128]{1,0:T(8,128)(2,1)S(1)} %multiply_convert_fusion.refs_0_), channel_id=1, source_target_pairs={{0,8},{8,0},{16,24},{24,16},{1,9},{9,1},{17,25},{25,17},{2,10},{10... | collective-permute-start | bytes 393224 | tf_op jit(solution)/shard_map/ppermute | solution.py:304
  69.4 7.5 %collective-permute-start.13 = (bf16[512,128]{1,0:T(8,128)(2,1)S(1)}, bf16[512,128]{1,0:T(8,128)(2,1)S(1)}, u32[]{:S(2)}, u32[]{:S(2)}) collective-permute-start(bf16[512,128]{1,0:T(8,128)(2,1)S(1)} %multiply_convert_fusion.refs_0_), channel_id=1, source_target_pairs={{0,16},{8,24},{16,0},{24,8},{1,17},{9,25},{17,1},{25,9},{2,18},{10... | collective-permute-start | bytes 393224 | tf_op jit(solution)/shard_map/ppermute | solution.py:304
  69.9 7.0 %collective-permute-start.14 = (bf16[512,128]{1,0:T(8,128)(2,1)S(1)}, bf16[512,128]{1,0:T(8,128)(2,1)S(1)}, u32[]{:S(2)}, u32[]{:S(2)}) collective-permute-start(bf16[512,128]{1,0:T(8,128)(2,1)S(1)} %multiply_convert_fusion.refs_0_), channel_id=1, source_target_pairs={{0,24},{8,16},{16,8},{24,0},{1,25},{9,17},{17,9},{25,1},{2,26},{10... | collective-permute-start | bytes 393224 | tf_op jit(solution)/shard_map/ppermute | solution.py:304
  81.5 1.6 %collective-permute-start.15 = (bf16[1024,128]{1,0:T(8,128)(2,1)S(1)}, bf16[1024,128]{1,0:T(8,128)(2,1)S(1)}, u32[]{:S(2)}, u32[]{:S(2)}) collective-permute-start(bf16[1024,128]{1,0:T(8,128)(2,1)S(1)} %get-tuple-element.34), channel_id=1, source_target_pairs={{0,1},{1,0},{2,3},{3,2},{4,5},{5,4},{6,7},{7,6},{8,9},{9,8},{10,11... | collective-permute-start | bytes 786440 | tf_op jit(solution)/shard_map/ppermute | solution.py:304
  83.1 7.4 %collective-permute-start.16 = (bf16[512,128]{1,0:T(8,128)(2,1)S(1)}, bf16[512,128]{1,0:T(8,128)(2,1)S(1)}, u32[]{:S(2)}, u32[]{:S(2)}) collective-permute-start(bf16[512,128]{1,0:T(8,128)(2,1)S(1)} %merge.5.after_ref.before_ref), channel_id=1, source_target_pairs={{0,2},{1,3},{2,0},{3,1},{4,6},{5,7},{6,4},{7,5},{8,10},{9,11},{10,... | collective-permute-start | bytes 393224 | tf_op jit(solution)/shard_map/ppermute | solution.py:304
  90.6 5.5 %collective-permute-start.17 = (bf16[256,128]{1,0:T(8,128)(2,1)S(1)}, bf16[256,128]{1,0:T(8,128)(2,1)S(1)}, u32[]{:S(2)}, u32[]{:S(2)}) collective-permute-start(bf16[256,128]{1,0:T(8,128)(2,1)S(1)} %get-tuple-element.36), channel_id=1, source_target_pairs={{0,4},{1,5},{2,6},{3,7},{4,0},{5,1},{6,2},{7,3},{8,12},{9,13},{10,... | collective-permute-start | bytes 196616 | tf_op jit(solution)/shard_map/ppermute | solution.py:304

commit v6 on v2

--- a/solution.py
+++ b/solution.py
@@ -107,6 +107,27 @@
     load.wait()
 
 
+def begin_kernel(degree_hbm, embed_hbm, state_ref, *refs):
+    square_refs, (degree_ref, embed_ref, sems) = refs[:HALVES], refs[HALVES:]
+    half = embed_ref.shape[0] // HALVES
+    copies = (
+        pltpu.make_async_copy(degree_hbm, degree_ref, sems.at[0]),
+        pltpu.make_async_copy(embed_hbm, embed_ref, sems.at[1]),
+    )
+    for copy in copies:
+        copy.start()
+    for copy in copies:
+        copy.wait()
+    lanes = degree_ref.shape[1]
+    for i in range(degree_ref.shape[0]):
+        scale = to_column(lax.rsqrt(degree_ref[i : i + 1, :].astype(jnp.float32)))
+        at = slice(i * lanes, (i + 1) * lanes)
+        state_ref[at, :] = (scale * embed_ref[at, :].astype(jnp.float32)).astype(state_ref.dtype)
+        inside = i * lanes % half
+        square = jnp.broadcast_to(scale * scale, (lanes, embed_ref.shape[1]))
+        square_refs[i * lanes // half][inside : inside + lanes, :] = square
+
+
 def fill_state(pieces, state, halves, tile):
     rows = pieces[0].shape[0]
     devices = (state.shape[0] - tile) // (rows * halves)
@@ -184,6 +205,14 @@
     add_cores(chips, 0, even_ref, other_ref, own_ref, sent_refs)
 
 
+def state_kernel(parts, square_ref, own_ref, *refs):
+    state_ref = refs[-1]
+    total = own_ref[...]
+    for ref in refs[:parts]:
+        total = total + ref[0 : total.shape[0], :].astype(jnp.float32)
+    state_ref[...] = (square_ref[...] * total).astype(state_ref.dtype)
+
+
 def place_kernel(chips, rows_here, block_rows, id_rows, mine_ref, other_ref, *refs):
     far_refs, place_ref = refs[:-1], refs[-1]
     my_col = lax.axis_index("col")
@@ -206,24 +235,20 @@
         even.append(rows)
         odd.append(pltpu.roll(rows, extra - extra // 2, 0))
     for k in range(chips):
-        place_ref[k * id_rows : (k + 1) * id_rows, :] = places(odd[k])
-        place_ref[(chips + k) * id_rows : (chips + k + 1) * id_rows, :] = places(even[k])
-
-
-def pick_rows(place_ref, part, total, picked, out):
-    count = picked.shape[0]
-
+        for part, rows in enumerate((places(odd[k]), places(even[k]))):
+            for r in range(id_rows):
+                at = ((part * chips + k) * id_rows + r) * LANES
+                place_ref[0:1, at : at + LANES] = rows[r : r + 1, :]
+
+
+def pick_rows(place_ref, first, total, picked):
     def some(i, carry):
-        base = pl.multiple_of(i * UNPICK, UNPICK)
-        row = (part * count + base) // LANES
-        lane = base % LANES
         for j in range(UNPICK):
-            picked[pl.ds(base + j, 1), :] = total[pl.ds(place_ref[row, lane + j], 1), :]
+            at = i * UNPICK + j
+            picked[pl.ds(at, 1), :] = total[pl.ds(place_ref[0, first + at], 1), :]
         return carry
 
-    lax.fori_loop(0, count // UNPICK, some, 0)
-    if out is not picked:
-        out[...] = picked[...].astype(out.dtype)
+    lax.fori_loop(0, picked.shape[0] // UNPICK, some, 0)
 
 
 def last_kernel(pieces, halves, plan_ref, place_ref, *refs):
@@ -231,11 +256,12 @@
     odd_ref, total, state, picked = refs[pieces + 1 :]
     fill_state(refs[:pieces], state, halves, weights_ref.shape[1])
     multiply(plan_ref, weights_ref, state, total, 0, CHUNKS, 0)
-    pick_rows(place_ref, 0, total, picked, odd_ref)
+    pick_rows(place_ref, 0, total, picked)
+    odd_ref[...] = picked[...].astype(odd_ref.dtype)
 
 
 def pick_kernel(place_ref, total, even_ref):
-    pick_rows(place_ref, 1, total, even_ref, even_ref)
+    pick_rows(place_ref, even_ref.shape[0], total, even_ref)
 
 
 def local(
@@ -292,8 +318,18 @@
     def spread(state):
         return [state] + [swap(state, "row", nrows, k) for k in range(1, nrows)]
 
-    scale = lax.rsqrt(degree.astype(f32))
-    state = (scale[:, None] * embed.astype(f32)).astype(bf16)
+    state, *squares = call(
+        begin_kernel,
+        "begin",
+        [array(embed.shape, bf16)] + [array((half_here, width), f32)] * HALVES,
+        (in_hbm(degree.reshape(rows_here // LANES, LANES)), in_hbm(embed)),
+        in_specs=[HBM_SPEC, HBM_SPEC],
+        scratch=[
+            pltpu.VMEM((rows_here // LANES, LANES), jnp.int32),
+            pltpu.VMEM(embed.shape, bf16),
+            pltpu.SemaphoreType.DMA((2,)),
+        ],
+    )
     pieces = spread(state)
 
     plan, weights = call(
@@ -334,7 +370,7 @@
         return own
 
     for hop in range(HOPS - 1):
-        extra = (mine,) if hop == 0 else ()
+        extra = (mine,)
         odd, held = call(
             functools.partial(odd_kernel, len(pieces), len(pieces) // nrows),
             "odd",
@@ -366,13 +402,19 @@
             place = call(
                 functools.partial(place_kernel, chips, rows_here, block_rows, id_rows),
                 "place",
-                array((2 * chips * id_rows, LANES), jnp.int32),
+                array((1, ncols * new_here), jnp.int32),
                 (mine, other, *came1),
             )
-        parts = {}
-        for half, (own, came) in reversed(tuple(enumerate(((own0, came0), (own1, came1))))):
-            here = scale[half * half_here : (half + 1) * half_here]
-            parts[half] = spread(((here * here)[:, None] * add(own, came)).astype(bf16))
+        parts, after = [], ()
+        for square, own, came in zip(squares, (own0, own1), (came0, came1)):
+            half_state = call(
+                functools.partial(state_kernel, len(came)),
+                "state",
+                array(square.shape, bf16),
+                (square, own, *came, *after),
+            )
+            parts.append(spread(half_state))
+            after = (half_state,)
         pieces = [parts[half][r] for half in reversed(range(HALVES)) for r in range(nrows)]
 
     odd, total = call(

time: 95 us -> 90.4 us (0.952); the launches traced: 94.4 us -> 90.8 us
  starting transfers between devices: 43.2 us -> 48.6 us
  Pallas kernels: 27.4 us -> 22.5 us
  other arithmetic: 3.86 us -> 1.71 us
  waiting for transfers between devices: 19.1 us -> 17.2 us
    ppermute x33, starting transfers between devices: 43.2 us -> 48.6 us  [swap(): return lax.ppermute(array, axis, [(i, i ^ mask) for i in range(size)])]
    pallas_call x13 -> x18, Pallas kernels: 27.4 us -> 22.5 us  [call(): pl.pallas_call(kernel, out_shape=out_shape, grid_spec=pltpu.PrefetchScala...]
    ppermute x33, waiting for transfers between devices: 19.1 us -> 17.2 us  [swap(): return lax.ppermute(array, axis, [(i, i ^ mask) for i in range(size)])]
    convert_element_type x5 -> x0, other arithmetic: 1.46 us -> none  [the longest x1 1.04 us: local(): state = (scale[:, None] * embed.astype(f32)).astype(bf16)]
  transfers between devices with their start and end apart: 33 -> 33, of which waited for: 15 -> 14; matrix products, arithmetic and copies ran while one was open for 1% -> 1% of each run, Pallas kernels for 15% -> 13%
where the time goes in v6:
time: 90.4 us; the launch traced here: 90.8 us
  starting transfers between devices  48.6 us (54%)
  Pallas kernels  22.5 us (25%)
  waiting for transfers between devices  17.2 us (19%)
  other arithmetic  1.71 us (2%)
    ppermute x33, starting transfers between devices, swap(): return lax.ppermute(array, axis, [(i, i ^ mask) for i in range(size)])  48.6 us
    pallas_call x18, Pallas kernels, call(): pl.pallas_call(kernel, out_shape=out_shape, grid_spec=pltpu.PrefetchScala...  22.5 us
    ppermute x33, waiting for transfers between devices, swap(): return lax.ppermute(array, axis, [(i, i ^ mask) for i in range(size)])  17.2 us
  transfers between devices with their start and end apart: 33, of which 14 were waited for; matrix products, arithmetic and copies ran while one was open for 1% of the time, Pallas kernels for 13%

profile of v6, /device:TPU:0, one launch (start us, length us, event | category | flops | bytes accessed | tf_op | source)
XLA Modules:
  0.0 90.8 jit_solution(8702050888760479791)
XLA Ops:
  0.0 1.1 %begin.1 = (bf16[512,128]{1,0:T(8,128)(2,1)S(1)}, f32[256,128]{1,0:T(8,128)S(1)}, f32[256,128]{1,0:T(8,128)S(1)}) custom-call(s32[4,128]{1,0:T(4,128)} %bitcast.25, bf16[512,128]{1,0:T(8,128)(2,1)} %embed_hbm.1), custom_call_target="tpu_custom_call" | custom-call | tf_op jit(solution)/shard_map/begin/pallas_call | solution.py:297
  1.1 3.0 %collective-permute-start = (bf16[512,128]{1,0:T(8,128)(2,1)S(1)}, bf16[512,128]{1,0:T(8,128)(2,1)S(1)}, u32[]{:S(2)}, u32[]{:S(2)}) collective-permute-start(bf16[512,128]{1,0:T(8,128)(2,1)S(1)} %get-tuple-element.37.refs_0_), channel_id=1, source_target_pairs={{0,8},{8,0},{16,24},{24,16},{1,9},{9,1},{17,25},{25,17},{2,10},{10... | collective-permute-start | bytes 393224 | tf_op jit(solution)/shard_map/ppermute | solution.py:313
  4.1 1.5 %collective-permute-start.1 = (bf16[512,128]{1,0:T(8,128)(2,1)S(1)}, bf16[512,128]{1,0:T(8,128)(2,1)S(1)}, u32[]{:S(2)}, u32[]{:S(2)}) collective-permute-start(bf16[512,128]{1,0:T(8,128)(2,1)S(1)} %get-tuple-element.37.refs_0_), channel_id=1, source_target_pairs={{0,16},{8,24},{16,0},{24,8},{1,17},{9,25},{17,1},{25,9},{2,18},{10... | collective-permute-start | bytes 393224 | tf_op jit(solution)/shard_map/ppermute | solution.py:313
  5.6 0.0 collective-permute-start.2
  5.6 0.7 fusion.4
  7.0 3.4 %plan.1 = (s32[8,512]{1,0:T(8,128)S(1)}, bf16[256,128,128]{2,1,0:T(8,128)(2,1)S(1)}) custom-call(s32[1,1]{1,0:T(1,128)S(6)} %copy.10.count_ref, s32[1,256]{1,0:T(1,128)} %bitcast.26, s32[1,256]{1,0:T(1,128)} %bitcast.27, bf16[256,128,128]{2,1,0:T(8,128)(2,1)} %bitcast.24), custom_call_target="tpu_custom_call" | custom-call | tf_op jit(solution)/shard_map/plan/pallas_call | solution.py:297
  10.5 0.0 collective-permute-done.refs_1_
  10.5 1.4 %collective-permute-done.1.refs_2_ = bf16[512,128]{1,0:T(8,128)(2,1)S(1)} collective-permute-done((bf16[512,128]{1,0:T(8,128)(2,1)S(1)}, bf16[512,128]{1,0:T(8,128)(2,1)S(1)}, u32[]{:S(2)}, u32[]{:S(2)}) %collective-permute-start.1) | collective-permute-done | bytes 131104 | tf_op jit(solution)/shard_map/ppermute | solution.py:313
  11.9 0.0 collective-permute-done.2.refs_3_
  11.9 2.2 %odd.2 = (bf16[2064,128]{1,0:T(8,128)(2,1)S(1)}, bf16[2176,128]{1,0:T(8,128)(2,1)S(1)}) custom-call(s32[8,512]{1,0:T(8,128)S(1)} %get-tuple-element.36.plan_ref, bf16[512,128]{1,0:T(8,128)(2,1)S(1)} %get-tuple-element.37.refs_0_, bf16[512,128]{1,0:T(8,128)(2,1)S(1)} %collective-permute-done.refs_1_, bf16[512,128]{1,0:T(8,128)(2,1)S(1)} %collective-permute-done.1.refs_2_, ...), custom_call_target="tpu_custom_call" | custom-call | flops 536870912 | bytes 4194304 | tf_op jit(solution)/shard_map/odd/pallas_call | solution.py:297
  14.1 0.1 collective-permute-start.3
  14.1 1.7 %even0.2.even_ref = f32[1024,128]{1,0:T(8,128)S(1)} custom-call(s32[8,512]{1,0:T(8,128)S(1)} %get-tuple-element.36.plan_ref, bf16[2176,128]{1,0:T(8,128)(2,1)S(1)} %get-tuple-element.40.state, bf16[256,128,128]{2,1,0:T(8,128)(2,1)S(1)} %get-tuple-element.38.refs_4_.weights_ref.refs_8_), custom_call_target="tpu_custom_call" | custom-call | flops 268435456 | bytes 2097152 | tf_op jit(solution)/shard_map/even0/pallas_call | solution.py:297
  15.9 0.2 collective-permute-done.3.other_ref
  16.0 0.1 merge.3
  16.1 3.3 %collective-permute-start.7 = (bf16[256,128]{1,0:T(8,128)(2,1)S(1)}, bf16[256,128]{1,0:T(8,128)(2,1)S(1)}, u32[]{:S(2)}, u32[]{:S(2)}) collective-permute-start(bf16[256,128]{1,0:T(8,128)(2,1)S(1)} %get-tuple-element.48), channel_id=1, source_target_pairs={{0,2},{1,3},{2,0},{3,1},{4,6},{5,7},{6,4},{7,5},{8,10},{9,11},{10,... | collective-permute-start | bytes 196616 | tf_op jit(solution)/shard_map/ppermute | solution.py:313
  19.4 3.5 %collective-permute-start.8 = (bf16[256,128]{1,0:T(8,128)(2,1)S(1)}, bf16[256,128]{1,0:T(8,128)(2,1)S(1)}, u32[]{:S(2)}, u32[]{:S(2)}) collective-permute-start(bf16[256,128]{1,0:T(8,128)(2,1)S(1)} %get-tuple-element.49), channel_id=1, source_target_pairs={{0,4},{1,5},{2,6},{3,7},{4,0},{5,1},{6,2},{7,3},{8,12},{9,13},{10,... | collective-permute-start | bytes 196616 | tf_op jit(solution)/shard_map/ppermute | solution.py:313
  22.9 1.5 %even1.2 = (f32[256,128]{1,0:T(8,128)S(1)}, bf16[272,128]{1,0:T(8,128)(2,1)S(1)}, bf16[272,128]{1,0:T(8,128)(2,1)S(1)}, bf16[272,128]{1,0:T(8,128)(2,1)S(1)}) custom-call(s32[8,512]{1,0:T(8,128)S(1)} %get-tuple-element.36.plan_ref, bf16[2176,128]{1,0:T(8,128)(2,1)S(1)} %get-tuple-element.40.state, ...), custom_call_target="tpu_custom_call" | custom-call | flops 268435456 | bytes 2097152 | tf_op jit(solution)/shard_map/even1/pallas_call | solution.py:297
  24.4 1.5 %collective-permute-start.4 = (bf16[272,128]{1,0:T(8,128)(2,1)S(1)}, bf16[272,128]{1,0:T(8,128)(2,1)S(1)}, u32[]{:S(2)}, u32[]{:S(2)}) collective-permute-start(bf16[272,128]{1,0:T(8,128)(2,1)S(1)} %get-tuple-element.42), channel_id=1, source_target_pairs={{0,2},{1,3},{2,0},{3,1},{4,6},{5,7},{6,4},{7,5},{8,10},{9,11},{10,... | collective-permute-start | bytes 208904 | tf_op jit(solution)/shard_map/ppermute | solution.py:313
  26.0 3.8 %collective-permute-start.5 = (bf16[272,128]{1,0:T(8,128)(2,1)S(1)}, bf16[272,128]{1,0:T(8,128)(2,1)S(1)}, u32[]{:S(2)}, u32[]{:S(2)}) collective-permute-start(bf16[272,128]{1,0:T(8,128)(2,1)S(1)} %get-tuple-element.43), channel_id=1, source_target_pairs={{0,4},{1,5},{2,6},{3,7},{4,0},{5,1},{6,2},{7,3},{8,12},{9,13},{10,... | collective-permute-start | bytes 208904 | tf_op jit(solution)/shard_map/ppermute | solution.py:313
  29.8 0.0 collective-permute-done.9.refs_2_
  29.9 0.1 collective-permute-start.13
  29.9 1.3 %collective-permute-start.14 = (bf16[256,128]{1,0:T(8,128)(2,1)S(1)}, bf16[256,128]{1,0:T(8,128)(2,1)S(1)}, u32[]{:S(2)}, u32[]{:S(2)}) collective-permute-start(bf16[256,128]{1,0:T(8,128)(2,1)S(1)} %state.4.refs_3_.refs_4_), channel_id=1, source_target_pairs={{0,16},{8,24},{16,0},{24,8},{1,17},{9,25},{17,1},{25,9},{2,18},{10... | collective-permute-start | bytes 196616 | tf_op jit(solution)/shard_map/ppermute | solution.py:313
  31.3 2.1 %collective-permute-start.15 = (bf16[256,128]{1,0:T(8,128)(2,1)S(1)}, bf16[256,128]{1,0:T(8,128)(2,1)S(1)}, u32[]{:S(2)}, u32[]{:S(2)}) collective-permute-start(bf16[256,128]{1,0:T(8,128)(2,1)S(1)} %state.4.refs_3_.refs_4_), channel_id=1, source_target_pairs={{0,24},{8,16},{16,8},{24,0},{1,25},{9,17},{17,9},{25,1},{2,26},{10... | collective-permute-start | bytes 196616 | tf_op jit(solution)/shard_map/ppermute | solution.py:313
  33.4 0.1 collective-permute-done.5.refs_1_
  33.5 2.4 %collective-permute-done.6.refs_2_ = bf16[272,128]{1,0:T(8,128)(2,1)S(1)} collective-permute-done((bf16[272,128]{1,0:T(8,128)(2,1)S(1)}, bf16[272,128]{1,0:T(8,128)(2,1)S(1)}, u32[]{:S(2)}, u32[]{:S(2)}) %collective-permute-start.6) | collective-permute-done | bytes 69664 | tf_op jit(solution)/shard_map/ppermute | solution.py:313
  35.9 0.2 collective-permute-start.10
  36.1 3.4 %collective-permute-start.12 = (bf16[256,128]{1,0:T(8,128)(2,1)S(1)}, bf16[256,128]{1,0:T(8,128)(2,1)S(1)}, u32[]{:S(2)}, u32[]{:S(2)}) collective-permute-start(bf16[256,128]{1,0:T(8,128)(2,1)S(1)} %state.5.refs_0_), channel_id=1, source_target_pairs={{0,24},{8,16},{16,8},{24,0},{1,25},{9,17},{17,9},{25,1},{2,26},{10... | collective-permute-start | bytes 196616 | tf_op jit(solution)/shard_map/ppermute | solution.py:313
  39.5 0.8 collective-permute-done.10.refs_1_
  40.3 0.1 collective-permute-done.11.refs_2_
  40.4 1.3 %collective-permute-done.12.refs_3_ = bf16[256,128]{1,0:T(8,128)(2,1)S(1)} collective-permute-done((bf16[256,128]{1,0:T(8,128)(2,1)S(1)}, bf16[256,128]{1,0:T(8,128)(2,1)S(1)}, u32[]{:S(2)}, u32[]{:S(2)}) %collective-permute-start.12) | collective-permute-done | bytes 65568 | tf_op jit(solution)/shard_map/ppermute | solution.py:313
  41.7 2.2 %odd.3 = (bf16[2064,128]{1,0:T(8,128)(2,1)S(1)}, bf16[2176,128]{1,0:T(8,128)(2,1)S(1)}) custom-call(s32[8,512]{1,0:T(8,128)S(1)} %get-tuple-element.36.plan_ref, bf16[256,128]{1,0:T(8,128)(2,1)S(1)} %state.5.refs_0_, bf16[256,128]{1,0:T(8,128)(2,1)S(1)} %collective-permute-done.10.refs_1_, bf16[256,128]{1,0:T(8,128)(2,1)S(1)} %collective-permute-done.11.refs_2_, ...), custom_call_target="tpu_custom_call" | custom-call | flops 536870912 | bytes 4194304 | tf_op jit(solution)/shard_map/odd/pallas_call | solution.py:297
  43.9 0.1 collective-permute-start.16
  44.0 1.7 %even0.3.even_ref = f32[1024,128]{1,0:T(8,128)S(1)} custom-call(s32[8,512]{1,0:T(8,128)S(1)} %get-tuple-element.36.plan_ref, bf16[2176,128]{1,0:T(8,128)(2,1)S(1)} %get-tuple-element.51.state, bf16[256,128,128]{2,1,0:T(8,128)(2,1)S(1)} %get-tuple-element.38.refs_4_.weights_ref.refs_8_), custom_call_target="tpu_custom_call" | custom-call | flops 268435456 | bytes 2097152 | tf_op jit(solution)/shard_map/even0/pallas_call | solution.py:297
  45.8 0.2 collective-permute-done.16.other_ref
  45.9 0.1 merge.4
  46.0 2.6 %collective-permute-start.20 = (bf16[256,128]{1,0:T(8,128)(2,1)S(1)}, bf16[256,128]{1,0:T(8,128)(2,1)S(1)}, u32[]{:S(2)}, u32[]{:S(2)}) collective-permute-start(bf16[256,128]{1,0:T(8,128)(2,1)S(1)} %get-tuple-element.58), channel_id=1, source_target_pairs={{0,2},{1,3},{2,0},{3,1},{4,6},{5,7},{6,4},{7,5},{8,10},{9,11},{10,... | collective-permute-start | bytes 196616 | tf_op jit(solution)/shard_map/ppermute | solution.py:313
  48.6 2.6 %collective-permute-start.21 = (bf16[256,128]{1,0:T(8,128)(2,1)S(1)}, bf16[256,128]{1,0:T(8,128)(2,1)S(1)}, u32[]{:S(2)}, u32[]{:S(2)}) collective-permute-start(bf16[256,128]{1,0:T(8,128)(2,1)S(1)} %get-tuple-element.59), channel_id=1, source_target_pairs={{0,4},{1,5},{2,6},{3,7},{4,0},{5,1},{6,2},{7,3},{8,12},{9,13},{10,... | collective-permute-start | bytes 196616 | tf_op jit(solution)/shard_map/ppermute | solution.py:313
  51.3 1.5 %even1.3 = (f32[256,128]{1,0:T(8,128)S(1)}, bf16[272,128]{1,0:T(8,128)(2,1)S(1)}, bf16[272,128]{1,0:T(8,128)(2,1)S(1)}, bf16[272,128]{1,0:T(8,128)(2,1)S(1)}) custom-call(s32[8,512]{1,0:T(8,128)S(1)} %get-tuple-element.36.plan_ref, bf16[2176,128]{1,0:T(8,128)(2,1)S(1)} %get-tuple-element.51.state, ...), custom_call_target="tpu_custom_call" | custom-call | flops 268435456 | bytes 2097152 | tf_op jit(solution)/shard_map/even1/pallas_call | solution.py:297
  52.8 0.0 copy-start
  52.8 0.0 copy-start.1
  52.8 1.8 %collective-permute-start.17 = (bf16[272,128]{1,0:T(8,128)(2,1)S(1)}, bf16[272,128]{1,0:T(8,128)(2,1)S(1)}, u32[]{:S(2)}, u32[]{:S(2)}) collective-permute-start(bf16[272,128]{1,0:T(8,128)(2,1)S(1)} %get-tuple-element.55), channel_id=1, source_target_pairs={{0,2},{1,3},{2,0},{3,1},{4,6},{5,7},{6,4},{7,5},{8,10},{9,11},{10,... | collective-permute-start | bytes 208904 | tf_op jit(solution)/shard_map/ppermute | solution.py:313
  54.6 3.5 %collective-permute-start.18 = (bf16[272,128]{1,0:T(8,128)(2,1)S(1)}, bf16[272,128]{1,0:T(8,128)(2,1)S(1)}, u32[]{:S(2)}, u32[]{:S(2)}) collective-permute-start(bf16[272,128]{1,0:T(8,128)(2,1)S(1)} %get-tuple-element.56), channel_id=1, source_target_pairs={{0,4},{1,5},{2,6},{3,7},{4,0},{5,1},{6,2},{7,3},{8,12},{9,13},{10,... | collective-permute-start | bytes 208904 | tf_op jit(solution)/shard_map/ppermute | solution.py:313
  58.2 0.8 collective-permute-start.26
  59.0 2.7 %collective-permute-start.27 = (bf16[256,128]{1,0:T(8,128)(2,1)S(1)}, bf16[256,128]{1,0:T(8,128)(2,1)S(1)}, u32[]{:S(2)}, u32[]{:S(2)}) collective-permute-start(bf16[256,128]{1,0:T(8,128)(2,1)S(1)} %state.6.refs_3_.refs_4_), channel_id=1, source_target_pairs={{0,16},{8,24},{16,0},{24,8},{1,17},{9,25},{17,1},{25,9},{2,18},{10... | collective-permute-start | bytes 196616 | tf_op jit(solution)/shard_map/ppermute | solution.py:313
  61.7 0.5 collective-permute-start.28
  62.2 2.1 %collective-permute-done.19.refs_2_ = bf16[272,128]{1,0:T(8,128)(2,1)S(1)} collective-permute-done((bf16[272,128]{1,0:T(8,128)(2,1)S(1)}, bf16[272,128]{1,0:T(8,128)(2,1)S(1)}, u32[]{:S(2)}, u32[]{:S(2)}) %collective-permute-start.19) | collective-permute-done | bytes 69664 | tf_op jit(solution)/shard_map/ppermute | solution.py:313
  64.3 0.4 collective-permute-start.23
  64.7 1.0 %collective-permute-start.24 = (bf16[256,128]{1,0:T(8,128)(2,1)S(1)}, bf16[256,128]{1,0:T(8,128)(2,1)S(1)}, u32[]{:S(2)}, u32[]{:S(2)}) collective-permute-start(bf16[256,128]{1,0:T(8,128)(2,1)S(1)} %state.7.refs_0_), channel_id=1, source_target_pairs={{0,16},{8,24},{16,0},{24,8},{1,17},{9,25},{17,1},{25,9},{2,18},{10... | collective-permute-start | bytes 196616 | tf_op jit(solution)/shard_map/ppermute | solution.py:313
  65.8 2.1 %collective-permute-start.25 = (bf16[256,128]{1,0:T(8,128)(2,1)S(1)}, bf16[256,128]{1,0:T(8,128)(2,1)S(1)}, u32[]{:S(2)}, u32[]{:S(2)}) collective-permute-start(bf16[256,128]{1,0:T(8,128)(2,1)S(1)} %state.7.refs_0_), channel_id=1, source_target_pairs={{0,24},{8,16},{16,8},{24,0},{1,25},{9,17},{17,9},{25,1},{2,26},{10... | collective-permute-start | bytes 196616 | tf_op jit(solution)/shard_map/ppermute | solution.py:313
  67.9 0.1 place.1.place_ref
  68.0 0.6 collective-permute-done.23.refs_1_
  68.6 0.4 collective-permute-done.24.refs_2_
  69.0 1.9 %collective-permute-done.25.refs_3_ = bf16[256,128]{1,0:T(8,128)(2,1)S(1)} collective-permute-done((bf16[256,128]{1,0:T(8,128)(2,1)S(1)}, bf16[256,128]{1,0:T(8,128)(2,1)S(1)}, u32[]{:S(2)}, u32[]{:S(2)}) %collective-permute-start.25) | collective-permute-done | bytes 65568 | tf_op jit(solution)/shard_map/ppermute | solution.py:313
  70.9 4.9 %last.1 = (bf16[1024,128]{1,0:T(8,128)(2,1)S(1)}, f32[4096,128]{1,0:T(8,128)S(1)}) custom-call(s32[8,512]{1,0:T(8,128)S(1)} %get-tuple-element.36.plan_ref, s32[1,2048]{1,0:T(1,128)S(1)} %place.1.place_ref, bf16[256,128]{1,0:T(8,128)(2,1)S(1)} %state.7.refs_0_, bf16[256,128]{1,0:T(8,128)(2,1)S(1)} %collective-permute-done.23.refs_1_, ...), custom_call_target="tpu_custom_call" | custom-call | flops 1073741824 | bytes 8388608 | tf_op jit(solution)/shard_map/last/pallas_call | solution.py:297
  75.8 0.1 collective-permute-start.29
  75.9 1.7 %pick.1.even_ref = f32[1024,128]{1,0:T(8,128)S(1)} custom-call(s32[1,2048]{1,0:T(1,128)S(1)} %place.1.place_ref, f32[4096,128]{1,0:T(8,128)S(1)} %get-tuple-element.61.total), custom_call_target="tpu_custom_call" | custom-call | flops 214748368 | bytes 1677721 | tf_op jit(solution)/shard_map/pick/pallas_call | solution.py:297
  77.7 0.1 merge.5
  77.7 5.8 %collective-permute-start.32 = (bf16[256,128]{1,0:T(8,128)(2,1)S(1)}, bf16[256,128]{1,0:T(8,128)(2,1)S(1)}, u32[]{:S(2)}, u32[]{:S(2)}) collective-permute-start(bf16[256,128]{1,0:T(8,128)(2,1)S(1)} %get-tuple-element.66), channel_id=1, source_target_pairs={{0,6},{1,7},{2,4},{3,5},{4,2},{5,3},{6,0},{7,1},{8,14},{9,15},{10,... | collective-permute-start | bytes 196616 | tf_op jit(solution)/shard_map/ppermute | solution.py:313
  83.5 0.6 collective-permute-start.30
  84.2 0.1 select_reduce_fusion
  84.2 2.3 %collective-permute-done.32 = bf16[256,128]{1,0:T(8,128)(2,1)S(1)} collective-permute-done((bf16[256,128]{1,0:T(8,128)(2,1)S(1)}, bf16[256,128]{1,0:T(8,128)(2,1)S(1)}, u32[]{:S(2)}, u32[]{:S(2)}) %collective-permute-start.32) | collective-permute-done | bytes 65568 | tf_op jit(solution)/shard_map/ppermute | solution.py:313
  86.6 3.4 %collective-permute-done.31 = bf16[256,128]{1,0:T(8,128)(2,1)S(1)} collective-permute-done((bf16[256,128]{1,0:T(8,128)(2,1)S(1)}, bf16[256,128]{1,0:T(8,128)(2,1)S(1)}, u32[]{:S(2)}, u32[]{:S(2)}) %collective-permute-start.31) | collective-permute-done | bytes 65568 | tf_op jit(solution)/shard_map/ppermute | solution.py:313
  89.9 0.1 multiply_reduce_fusion
  90.0 0.8 multiply_multiply_fusion
  (30 shorter events, 0.3 us)
Async XLA Ops:
  1.1 9.4 %collective-permute-start = (bf16[512,128]{1,0:T(8,128)(2,1)S(1)}, bf16[512,128]{1,0:T(8,128)(2,1)S(1)}, u32[]{:S(2)}, u32[]{:S(2)}) collective-permute-start(bf16[512,128]{1,0:T(8,128)(2,1)S(1)} %get-tuple-element.37.refs_0_), channel_id=1, source_target_pairs={{0,8},{8,0},{16,24},{24,16},{1,9},{9,1},{17,25},{25,17},{2,10},{10... | collective-permute-start | bytes 393224 | tf_op jit(solution)/shard_map/ppermute | solution.py:313
  4.1 7.8 %collective-permute-start.1 = (bf16[512,128]{1,0:T(8,128)(2,1)S(1)}, bf16[512,128]{1,0:T(8,128)(2,1)S(1)}, u32[]{:S(2)}, u32[]{:S(2)}) collective-permute-start(bf16[512,128]{1,0:T(8,128)(2,1)S(1)} %get-tuple-element.37.refs_0_), channel_id=1, source_target_pairs={{0,16},{8,24},{16,0},{24,8},{1,17},{9,25},{17,1},{25,9},{2,18},{10... | collective-permute-start | bytes 393224 | tf_op jit(solution)/shard_map/ppermute | solution.py:313
  5.6 6.3 %collective-permute-start.2 = (bf16[512,128]{1,0:T(8,128)(2,1)S(1)}, bf16[512,128]{1,0:T(8,128)(2,1)S(1)}, u32[]{:S(2)}, u32[]{:S(2)}) collective-permute-start(bf16[512,128]{1,0:T(8,128)(2,1)S(1)} %get-tuple-element.37.refs_0_), channel_id=1, source_target_pairs={{0,24},{8,16},{16,8},{24,0},{1,25},{9,17},{17,9},{25,1},{2,26},{10... | collective-permute-start | bytes 393224 | tf_op jit(solution)/shard_map/ppermute | solution.py:313
  14.1 2.0 %collective-permute-start.3 = (bf16[2064,128]{1,0:T(8,128)(2,1)S(1)}, bf16[2064,128]{1,0:T(8,128)(2,1)S(1)}, u32[]{:S(2)}, u32[]{:S(2)}) collective-permute-start(bf16[2064,128]{1,0:T(8,128)(2,1)S(1)} %get-tuple-element.39), channel_id=1, source_target_pairs={{0,1},{1,0},{2,3},{3,2},{4,5},{5,4},{6,7},{7,6},{8,9},{9,8},{10,11... | collective-permute-start | bytes 1585160 | tf_op jit(solution)/shard_map/ppermute | solution.py:313
  16.1 13.7 %collective-permute-start.7 = (bf16[256,128]{1,0:T(8,128)(2,1)S(1)}, bf16[256,128]{1,0:T(8,128)(2,1)S(1)}, u32[]{:S(2)}, u32[]{:S(2)}) collective-permute-start(bf16[256,128]{1,0:T(8,128)(2,1)S(1)} %get-tuple-element.48), channel_id=1, source_target_pairs={{0,2},{1,3},{2,0},{3,1},{4,6},{5,7},{6,4},{7,5},{8,10},{9,11},{10,... | collective-permute-start | bytes 196616 | tf_op jit(solution)/shard_map/ppermute | solution.py:313
  19.4 10.4 %collective-permute-start.8 = (bf16[256,128]{1,0:T(8,128)(2,1)S(1)}, bf16[256,128]{1,0:T(8,128)(2,1)S(1)}, u32[]{:S(2)}, u32[]{:S(2)}) collective-permute-start(bf16[256,128]{1,0:T(8,128)(2,1)S(1)} %get-tuple-element.49), channel_id=1, source_target_pairs={{0,4},{1,5},{2,6},{3,7},{4,0},{5,1},{6,2},{7,3},{8,12},{9,13},{10,... | collective-permute-start | bytes 196616 | tf_op jit(solution)/shard_map/ppermute | solution.py:313
  22.9 6.9 %collective-permute-start.9 = (bf16[256,128]{1,0:T(8,128)(2,1)S(1)}, bf16[256,128]{1,0:T(8,128)(2,1)S(1)}, u32[]{:S(2)}, u32[]{:S(2)}) collective-permute-start(bf16[256,128]{1,0:T(8,128)(2,1)S(1)} %get-tuple-element.50), channel_id=1, source_target_pairs={{0,6},{1,7},{2,4},{3,5},{4,2},{5,3},{6,0},{7,1},{8,14},{9,15},{10,... | collective-permute-start | bytes 196616 | tf_op jit(solution)/shard_map/ppermute | solution.py:313
  24.4 6.8 %collective-permute-start.4 = (bf16[272,128]{1,0:T(8,128)(2,1)S(1)}, bf16[272,128]{1,0:T(8,128)(2,1)S(1)}, u32[]{:S(2)}, u32[]{:S(2)}) collective-permute-start(bf16[272,128]{1,0:T(8,128)(2,1)S(1)} %get-tuple-element.42), channel_id=1, source_target_pairs={{0,2},{1,3},{2,0},{3,1},{4,6},{5,7},{6,4},{7,5},{8,10},{9,11},{10,... | collective-permute-start | bytes 208904 | tf_op jit(solution)/shard_map/ppermute | solution.py:313
  26.0 7.5 %collective-permute-start.5 = (bf16[272,128]{1,0:T(8,128)(2,1)S(1)}, bf16[272,128]{1,0:T(8,128)(2,1)S(1)}, u32[]{:S(2)}, u32[]{:S(2)}) collective-permute-start(bf16[272,128]{1,0:T(8,128)(2,1)S(1)} %get-tuple-element.43), channel_id=1, source_target_pairs={{0,4},{1,5},{2,6},{3,7},{4,0},{5,1},{6,2},{7,3},{8,12},{9,13},{10,... | collective-permute-start | bytes 208904 | tf_op jit(solution)/shard_map/ppermute | solution.py:313
  29.8 6.1 %collective-permute-start.6 = (bf16[272,128]{1,0:T(8,128)(2,1)S(1)}, bf16[272,128]{1,0:T(8,128)(2,1)S(1)}, u32[]{:S(2)}, u32[]{:S(2)}) collective-permute-start(bf16[272,128]{1,0:T(8,128)(2,1)S(1)} %get-tuple-element.44), channel_id=1, source_target_pairs={{0,6},{1,7},{2,4},{3,5},{4,2},{5,3},{6,0},{7,1},{8,14},{9,15},{10,... | collective-permute-start | bytes 208904 | tf_op jit(solution)/shard_map/ppermute | solution.py:313
  29.9 6.3 %collective-permute-start.13 = (bf16[256,128]{1,0:T(8,128)(2,1)S(1)}, bf16[256,128]{1,0:T(8,128)(2,1)S(1)}, u32[]{:S(2)}, u32[]{:S(2)}) collective-permute-start(bf16[256,128]{1,0:T(8,128)(2,1)S(1)} %state.4.refs_3_.refs_4_), channel_id=1, source_target_pairs={{0,8},{8,0},{16,24},{24,16},{1,9},{9,1},{17,25},{25,17},{2,10},{10... | collective-permute-start | bytes 196616 | tf_op jit(solution)/shard_map/ppermute | solution.py:313
  29.9 9.6 %collective-permute-start.14 = (bf16[256,128]{1,0:T(8,128)(2,1)S(1)}, bf16[256,128]{1,0:T(8,128)(2,1)S(1)}, u32[]{:S(2)}, u32[]{:S(2)}) collective-permute-start(bf16[256,128]{1,0:T(8,128)(2,1)S(1)} %state.4.refs_3_.refs_4_), channel_id=1, source_target_pairs={{0,16},{8,24},{16,0},{24,8},{1,17},{9,25},{17,1},{25,9},{2,18},{10... | collective-permute-start | bytes 196616 | tf_op jit(solution)/shard_map/ppermute | solution.py:313
  31.3 8.2 %collective-permute-start.15 = (bf16[256,128]{1,0:T(8,128)(2,1)S(1)}, bf16[256,128]{1,0:T(8,128)(2,1)S(1)}, u32[]{:S(2)}, u32[]{:S(2)}) collective-permute-start(bf16[256,128]{1,0:T(8,128)(2,1)S(1)} %state.4.refs_3_.refs_4_), channel_id=1, source_target_pairs={{0,24},{8,16},{16,8},{24,0},{1,25},{9,17},{17,9},{25,1},{2,26},{10... | collective-permute-start | bytes 196616 | tf_op jit(solution)/shard_map/ppermute | solution.py:313
  35.9 4.3 %collective-permute-start.10 = (bf16[256,128]{1,0:T(8,128)(2,1)S(1)}, bf16[256,128]{1,0:T(8,128)(2,1)S(1)}, u32[]{:S(2)}, u32[]{:S(2)}) collective-permute-start(bf16[256,128]{1,0:T(8,128)(2,1)S(1)} %state.5.refs_0_), channel_id=1, source_target_pairs={{0,8},{8,0},{16,24},{24,16},{1,9},{9,1},{17,25},{25,17},{2,10},{10... | collective-permute-start | bytes 196616 | tf_op jit(solution)/shard_map/ppermute | solution.py:313
  36.1 4.3 %collective-permute-start.11 = (bf16[256,128]{1,0:T(8,128)(2,1)S(1)}, bf16[256,128]{1,0:T(8,128)(2,1)S(1)}, u32[]{:S(2)}, u32[]{:S(2)}) collective-permute-start(bf16[256,128]{1,0:T(8,128)(2,1)S(1)} %state.5.refs_0_), channel_id=1, source_target_pairs={{0,16},{8,24},{16,0},{24,8},{1,17},{9,25},{17,1},{25,9},{2,18},{10... | collective-permute-start | bytes 196616 | tf_op jit(solution)/shard_map/ppermute | solution.py:313
  36.1 5.6 %collective-permute-start.12 = (bf16[256,128]{1,0:T(8,128)(2,1)S(1)}, bf16[256,128]{1,0:T(8,128)(2,1)S(1)}, u32[]{:S(2)}, u32[]{:S(2)}) collective-permute-start(bf16[256,128]{1,0:T(8,128)(2,1)S(1)} %state.5.refs_0_), channel_id=1, source_target_pairs={{0,24},{8,16},{16,8},{24,0},{1,25},{9,17},{17,9},{25,1},{2,26},{10... | collective-permute-start | bytes 196616 | tf_op jit(solution)/shard_map/ppermute | solution.py:313
  43.9 2.0 %collective-permute-start.16 = (bf16[2064,128]{1,0:T(8,128)(2,1)S(1)}, bf16[2064,128]{1,0:T(8,128)(2,1)S(1)}, u32[]{:S(2)}, u32[]{:S(2)}) collective-permute-start(bf16[2064,128]{1,0:T(8,128)(2,1)S(1)} %get-tuple-element.52), channel_id=1, source_target_pairs={{0,1},{1,0},{2,3},{3,2},{4,5},{5,4},{6,7},{7,6},{8,9},{9,8},{10,11... | collective-permute-start | bytes 1585160 | tf_op jit(solution)/shard_map/ppermute | solution.py:313
  46.0 12.2 %collective-permute-start.20 = (bf16[256,128]{1,0:T(8,128)(2,1)S(1)}, bf16[256,128]{1,0:T(8,128)(2,1)S(1)}, u32[]{:S(2)}, u32[]{:S(2)}) collective-permute-start(bf16[256,128]{1,0:T(8,128)(2,1)S(1)} %get-tuple-element.58), channel_id=1, source_target_pairs={{0,2},{1,3},{2,0},{3,1},{4,6},{5,7},{6,4},{7,5},{8,10},{9,11},{10,... | collective-permute-start | bytes 196616 | tf_op jit(solution)/shard_map/ppermute | solution.py:313
  48.6 9.5 %collective-permute-start.21 = (bf16[256,128]{1,0:T(8,128)(2,1)S(1)}, bf16[256,128]{1,0:T(8,128)(2,1)S(1)}, u32[]{:S(2)}, u32[]{:S(2)}) collective-permute-start(bf16[256,128]{1,0:T(8,128)(2,1)S(1)} %get-tuple-element.59), channel_id=1, source_target_pairs={{0,4},{1,5},{2,6},{3,7},{4,0},{5,1},{6,2},{7,3},{8,12},{9,13},{10,... | collective-permute-start | bytes 196616 | tf_op jit(solution)/shard_map/ppermute | solution.py:313
  51.3 6.9 %collective-permute-start.22 = (bf16[256,128]{1,0:T(8,128)(2,1)S(1)}, bf16[256,128]{1,0:T(8,128)(2,1)S(1)}, u32[]{:S(2)}, u32[]{:S(2)}) collective-permute-start(bf16[256,128]{1,0:T(8,128)(2,1)S(1)} %get-tuple-element.60), channel_id=1, source_target_pairs={{0,6},{1,7},{2,4},{3,5},{4,2},{5,3},{6,0},{7,1},{8,14},{9,15},{10,... | collective-permute-start | bytes 196616 | tf_op jit(solution)/shard_map/ppermute | solution.py:313
  52.8 31.4 %copy-start = (s32[256]{0:T(256)S(1)}, s32[256]{0:T(256)}, u32[]{:S(2)}) copy-start(s32[256]{0:T(256)} %param.16) | copy-start | bytes 3076
  52.8 31.4 %copy-start.1 = (f32[16]{0:T(128)S(1)}, f32[16]{0:T(128)}, u32[]{:S(2)}) copy-start(f32[16]{0:T(128)} %param.17) | copy-start | bytes 196
  52.8 8.9 %collective-permute-start.17 = (bf16[272,128]{1,0:T(8,128)(2,1)S(1)}, bf16[272,128]{1,0:T(8,128)(2,1)S(1)}, u32[]{:S(2)}, u32[]{:S(2)}) collective-permute-start(bf16[272,128]{1,0:T(8,128)(2,1)S(1)} %get-tuple-element.55), channel_id=1, source_target_pairs={{0,2},{1,3},{2,0},{3,1},{4,6},{5,7},{6,4},{7,5},{8,10},{9,11},{10,... | collective-permute-start | bytes 208904 | tf_op jit(solution)/shard_map/ppermute | solution.py:313
  54.6 7.6 %collective-permute-start.18 = (bf16[272,128]{1,0:T(8,128)(2,1)S(1)}, bf16[272,128]{1,0:T(8,128)(2,1)S(1)}, u32[]{:S(2)}, u32[]{:S(2)}) collective-permute-start(bf16[272,128]{1,0:T(8,128)(2,1)S(1)} %get-tuple-element.56), channel_id=1, source_target_pairs={{0,4},{1,5},{2,6},{3,7},{4,0},{5,1},{6,2},{7,3},{8,12},{9,13},{10,... | collective-permute-start | bytes 208904 | tf_op jit(solution)/shard_map/ppermute | solution.py:313
  58.1 6.1 %collective-permute-start.19 = (bf16[272,128]{1,0:T(8,128)(2,1)S(1)}, bf16[272,128]{1,0:T(8,128)(2,1)S(1)}, u32[]{:S(2)}, u32[]{:S(2)}) collective-permute-start(bf16[272,128]{1,0:T(8,128)(2,1)S(1)} %get-tuple-element.57), channel_id=1, source_target_pairs={{0,6},{1,7},{2,4},{3,5},{4,2},{5,3},{6,0},{7,1},{8,14},{9,15},{10,... | collective-permute-start | bytes 208904 | tf_op jit(solution)/shard_map/ppermute | solution.py:313
  58.2 7.5 %collective-permute-start.26 = (bf16[256,128]{1,0:T(8,128)(2,1)S(1)}, bf16[256,128]{1,0:T(8,128)(2,1)S(1)}, u32[]{:S(2)}, u32[]{:S(2)}) collective-permute-start(bf16[256,128]{1,0:T(8,128)(2,1)S(1)} %state.6.refs_3_.refs_4_), channel_id=1, source_target_pairs={{0,8},{8,0},{16,24},{24,16},{1,9},{9,1},{17,25},{25,17},{2,10},{10... | collective-permute-start | bytes 196616 | tf_op jit(solution)/shard_map/ppermute | solution.py:313
  59.0 9.0 %collective-permute-start.27 = (bf16[256,128]{1,0:T(8,128)(2,1)S(1)}, bf16[256,128]{1,0:T(8,128)(2,1)S(1)}, u32[]{:S(2)}, u32[]{:S(2)}) collective-permute-start(bf16[256,128]{1,0:T(8,128)(2,1)S(1)} %state.6.refs_3_.refs_4_), channel_id=1, source_target_pairs={{0,16},{8,24},{16,0},{24,8},{1,17},{9,25},{17,1},{25,9},{2,18},{10... | collective-permute-start | bytes 196616 | tf_op jit(solution)/shard_map/ppermute | solution.py:313
  61.7 6.3 %collective-permute-start.28 = (bf16[256,128]{1,0:T(8,128)(2,1)S(1)}, bf16[256,128]{1,0:T(8,128)(2,1)S(1)}, u32[]{:S(2)}, u32[]{:S(2)}) collective-permute-start(bf16[256,128]{1,0:T(8,128)(2,1)S(1)} %state.6.refs_3_.refs_4_), channel_id=1, source_target_pairs={{0,24},{8,16},{16,8},{24,0},{1,25},{9,17},{17,9},{25,1},{2,26},{10... | collective-permute-start | bytes 196616 | tf_op jit(solution)/shard_map/ppermute | solution.py:313
  64.3 4.3 %collective-permute-start.23 = (bf16[256,128]{1,0:T(8,128)(2,1)S(1)}, bf16[256,128]{1,0:T(8,128)(2,1)S(1)}, u32[]{:S(2)}, u32[]{:S(2)}) collective-permute-start(bf16[256,128]{1,0:T(8,128)(2,1)S(1)} %state.7.refs_0_), channel_id=1, source_target_pairs={{0,8},{8,0},{16,24},{24,16},{1,9},{9,1},{17,25},{25,17},{2,10},{10... | collective-permute-start | bytes 196616 | tf_op jit(solution)/shard_map/ppermute | solution.py:313
  64.7 4.3 %collective-permute-start.24 = (bf16[256,128]{1,0:T(8,128)(2,1)S(1)}, bf16[256,128]{1,0:T(8,128)(2,1)S(1)}, u32[]{:S(2)}, u32[]{:S(2)}) collective-permute-start(bf16[256,128]{1,0:T(8,128)(2,1)S(1)} %state.7.refs_0_), channel_id=1, source_target_pairs={{0,16},{8,24},{16,0},{24,8},{1,17},{9,25},{17,1},{25,9},{2,18},{10... | collective-permute-start | bytes 196616 | tf_op jit(solution)/shard_map/ppermute | solution.py:313
  65.8 5.2 %collective-permute-start.25 = (bf16[256,128]{1,0:T(8,128)(2,1)S(1)}, bf16[256,128]{1,0:T(8,128)(2,1)S(1)}, u32[]{:S(2)}, u32[]{:S(2)}) collective-permute-start(bf16[256,128]{1,0:T(8,128)(2,1)S(1)} %state.7.refs_0_), channel_id=1, source_target_pairs={{0,24},{8,16},{16,8},{24,0},{1,25},{9,17},{17,9},{25,1},{2,26},{10... | collective-permute-start | bytes 196616 | tf_op jit(solution)/shard_map/ppermute | solution.py:313
  75.8 1.8 %collective-permute-start.29 = (bf16[1024,128]{1,0:T(8,128)(2,1)S(1)}, bf16[1024,128]{1,0:T(8,128)(2,1)S(1)}, u32[]{:S(2)}, u32[]{:S(2)}) collective-permute-start(bf16[1024,128]{1,0:T(8,128)(2,1)S(1)} %get-tuple-element.62), channel_id=1, source_target_pairs={{0,1},{1,0},{2,3},{3,2},{4,5},{5,4},{6,7},{7,6},{8,9},{9,8},{10,11... | collective-permute-start | bytes 786440 | tf_op jit(solution)/shard_map/ppermute | solution.py:313
  77.7 8.8 %collective-permute-start.32 = (bf16[256,128]{1,0:T(8,128)(2,1)S(1)}, bf16[256,128]{1,0:T(8,128)(2,1)S(1)}, u32[]{:S(2)}, u32[]{:S(2)}) collective-permute-start(bf16[256,128]{1,0:T(8,128)(2,1)S(1)} %get-tuple-element.66), channel_id=1, source_target_pairs={{0,6},{1,7},{2,4},{3,5},{4,2},{5,3},{6,0},{7,1},{8,14},{9,15},{10,... | collective-permute-start | bytes 196616 | tf_op jit(solution)/shard_map/ppermute | solution.py:313
  83.5 6.4 %collective-permute-start.31 = (bf16[256,128]{1,0:T(8,128)(2,1)S(1)}, bf16[256,128]{1,0:T(8,128)(2,1)S(1)}, u32[]{:S(2)}, u32[]{:S(2)}) collective-permute-start(bf16[256,128]{1,0:T(8,128)(2,1)S(1)} %get-tuple-element.65), channel_id=1, source_target_pairs={{0,4},{1,5},{2,6},{3,7},{4,0},{5,1},{6,2},{7,3},{8,12},{9,13},{10,... | collective-permute-start | bytes 196616 | tf_op jit(solution)/shard_map/ppermute | solution.py:313
  83.5 6.4 %collective-permute-start.30 = (bf16[256,128]{1,0:T(8,128)(2,1)S(1)}, bf16[256,128]{1,0:T(8,128)(2,1)S(1)}, u32[]{:S(2)}, u32[]{:S(2)}) collective-permute-start(bf16[256,128]{1,0:T(8,128)(2,1)S(1)} %get-tuple-element.64), channel_id=1, source_target_pairs={{0,2},{1,3},{2,0},{3,1},{4,6},{5,7},{6,4},{7,5},{8,10},{9,11},{10,... | collective-permute-start | bytes 196616 | tf_op jit(solution)/shard_map/ppermute | solution.py:313

commit v7 on v6

--- a/solution.py
+++ b/solution.py
@@ -11,7 +11,7 @@
 HALVES = 2
 CHUNKS = 2 * HALVES
 GROUP = 4
-UNROLL = 4
+UNROLL = 8
 UNPICK = 16
 BITS = 8
 SHIFT = 1 << BITS
@@ -85,7 +85,9 @@
         mine = (tile_no >= c * chunk_tiles) & (tile_no < (c + 1) * chunk_tiles)
         size = jnp.sum(jnp.where(mine, steps_f, 0.0)).astype(jnp.int32)
         shift = shift + jnp.where(mine, begin - raw, 0)
-        end = begin + (size + UNROLL - 1) // UNROLL * UNROLL
+        end = begin + size
+        if c > 0:
+            end = (end + UNROLL - 1) // UNROLL * UNROLL
         limit = jnp.where((step_no >= begin) & (step_no < end), (c + 1) * chunk_tiles - 1, limit)
         raw, begin = raw + size, end
         ends.append(end // UNROLL)

time: 90.4 us -> 87.7 us (0.970)
  starting transfers between devices: 48.6 us -> 43.9 us
  Pallas kernels: 22.5 us -> 23.8 us
    ppermute x33, starting transfers between devices: 48.6 us -> 43.9 us  [swap(): return lax.ppermute(array, axis, [(i, i ^ mask) for i in range(size)])]
    pallas_call x18, Pallas kernels: 22.5 us -> 23.8 us  [call(): pl.pallas_call(kernel, out_shape=out_shape, grid_spec=pltpu.PrefetchScala...]
  transfers between devices with their start and end apart: 33 -> 33, of which waited for: 14 -> 16; matrix products, arithmetic and copies ran while one was open for 1% -> 1% of each run, Pallas kernels for 13% -> 14%
where the time goes in v7:
time: 87.7 us; the launch traced here: 87.8 us
  starting transfers between devices  43.9 us (50%)
  Pallas kernels  23.8 us (27%)
  waiting for transfers between devices  17.5 us (20%)
  other arithmetic  1.71 us (2%)
    ppermute x33, starting transfers between devices, swap(): return lax.ppermute(array, axis, [(i, i ^ mask) for i in range(size)])  43.9 us
    pallas_call x18, Pallas kernels, call(): pl.pallas_call(kernel, out_shape=out_shape, grid_spec=pltpu.PrefetchScala...  23.8 us
    ppermute x33, waiting for transfers between devices, swap(): return lax.ppermute(array, axis, [(i, i ^ mask) for i in range(size)])  17.5 us
  transfers between devices with their start and end apart: 33, of which 16 were waited for; matrix products, arithmetic and copies ran while one was open for 1% of the time, Pallas kernels for 14%

profile of v7, /device:TPU:0, one launch (start us, length us, event | category | flops | bytes accessed | tf_op | source)
XLA Modules:
  0.0 87.8 jit_solution(13877031080159019257)
XLA Ops:
  0.0 1.1 %begin.1 = (bf16[512,128]{1,0:T(8,128)(2,1)S(1)}, f32[256,128]{1,0:T(8,128)S(1)}, f32[256,128]{1,0:T(8,128)S(1)}) custom-call(s32[4,128]{1,0:T(4,128)} %bitcast.25, bf16[512,128]{1,0:T(8,128)(2,1)} %embed_hbm.1), custom_call_target="tpu_custom_call" | custom-call | tf_op jit(solution)/shard_map/begin/pallas_call | solution.py:299
  1.1 3.0 %collective-permute-start = (bf16[512,128]{1,0:T(8,128)(2,1)S(1)}, bf16[512,128]{1,0:T(8,128)(2,1)S(1)}, u32[]{:S(2)}, u32[]{:S(2)}) collective-permute-start(bf16[512,128]{1,0:T(8,128)(2,1)S(1)} %get-tuple-element.37.refs_0_), channel_id=1, source_target_pairs={{0,8},{8,0},{16,24},{24,16},{1,9},{9,1},{17,25},{25,17},{2,10},{10... | collective-permute-start | bytes 393224 | tf_op jit(solution)/shard_map/ppermute | solution.py:315
  4.1 1.5 %collective-permute-start.1 = (bf16[512,128]{1,0:T(8,128)(2,1)S(1)}, bf16[512,128]{1,0:T(8,128)(2,1)S(1)}, u32[]{:S(2)}, u32[]{:S(2)}) collective-permute-start(bf16[512,128]{1,0:T(8,128)(2,1)S(1)} %get-tuple-element.37.refs_0_), channel_id=1, source_target_pairs={{0,16},{8,24},{16,0},{24,8},{1,17},{9,25},{17,1},{25,9},{2,18},{10... | collective-permute-start | bytes 393224 | tf_op jit(solution)/shard_map/ppermute | solution.py:315
  5.6 0.0 collective-permute-start.2
  5.6 0.7 fusion.4
  7.0 3.4 %plan.1 = (s32[8,512]{1,0:T(8,128)S(1)}, bf16[256,128,128]{2,1,0:T(8,128)(2,1)S(1)}) custom-call(s32[1,1]{1,0:T(1,128)S(6)} %copy.10.count_ref, s32[1,256]{1,0:T(1,128)} %bitcast.26, s32[1,256]{1,0:T(1,128)} %bitcast.27, bf16[256,128,128]{2,1,0:T(8,128)(2,1)} %bitcast.24), custom_call_target="tpu_custom_call" | custom-call | tf_op jit(solution)/shard_map/plan/pallas_call | solution.py:299
  10.5 1.4 %collective-permute-done.1.refs_2_ = bf16[512,128]{1,0:T(8,128)(2,1)S(1)} collective-permute-done((bf16[512,128]{1,0:T(8,128)(2,1)S(1)}, bf16[512,128]{1,0:T(8,128)(2,1)S(1)}, u32[]{:S(2)}, u32[]{:S(2)}) %collective-permute-start.1) | collective-permute-done | bytes 131104 | tf_op jit(solution)/shard_map/ppermute | solution.py:315
  11.9 2.3 %odd.2 = (bf16[2064,128]{1,0:T(8,128)(2,1)S(1)}, bf16[2176,128]{1,0:T(8,128)(2,1)S(1)}) custom-call(s32[8,512]{1,0:T(8,128)S(1)} %get-tuple-element.36.plan_ref, bf16[512,128]{1,0:T(8,128)(2,1)S(1)} %get-tuple-element.37.refs_0_, bf16[512,128]{1,0:T(8,128)(2,1)S(1)} %collective-permute-done.refs_1_, bf16[512,128]{1,0:T(8,128)(2,1)S(1)} %collective-permute-done.1.refs_2_, ...), custom_call_target="tpu_custom_call" | custom-call | flops 536870912 | bytes 4194304 | tf_op jit(solution)/shard_map/odd/pallas_call | solution.py:299
  14.2 0.1 collective-permute-start.3
  14.3 1.7 %even0.2.even_ref = f32[1024,128]{1,0:T(8,128)S(1)} custom-call(s32[8,512]{1,0:T(8,128)S(1)} %get-tuple-element.36.plan_ref, bf16[2176,128]{1,0:T(8,128)(2,1)S(1)} %get-tuple-element.40.state, bf16[256,128,128]{2,1,0:T(8,128)(2,1)S(1)} %get-tuple-element.38.refs_4_.weights_ref.refs_8_), custom_call_target="tpu_custom_call" | custom-call | flops 268435456 | bytes 2097152 | tf_op jit(solution)/shard_map/even0/pallas_call | solution.py:299
  16.0 0.1 collective-permute-done.3.other_ref
  16.2 0.1 merge.3
  16.2 2.4 %collective-permute-start.7 = (bf16[256,128]{1,0:T(8,128)(2,1)S(1)}, bf16[256,128]{1,0:T(8,128)(2,1)S(1)}, u32[]{:S(2)}, u32[]{:S(2)}) collective-permute-start(bf16[256,128]{1,0:T(8,128)(2,1)S(1)} %get-tuple-element.48), channel_id=1, source_target_pairs={{0,2},{1,3},{2,0},{3,1},{4,6},{5,7},{6,4},{7,5},{8,10},{9,11},{10,... | collective-permute-start | bytes 196616 | tf_op jit(solution)/shard_map/ppermute | solution.py:315
  18.7 2.6 %collective-permute-start.8 = (bf16[256,128]{1,0:T(8,128)(2,1)S(1)}, bf16[256,128]{1,0:T(8,128)(2,1)S(1)}, u32[]{:S(2)}, u32[]{:S(2)}) collective-permute-start(bf16[256,128]{1,0:T(8,128)(2,1)S(1)} %get-tuple-element.49), channel_id=1, source_target_pairs={{0,4},{1,5},{2,6},{3,7},{4,0},{5,1},{6,2},{7,3},{8,12},{9,13},{10,... | collective-permute-start | bytes 196616 | tf_op jit(solution)/shard_map/ppermute | solution.py:315
  21.2 1.8 %even1.2 = (f32[256,128]{1,0:T(8,128)S(1)}, bf16[272,128]{1,0:T(8,128)(2,1)S(1)}, bf16[272,128]{1,0:T(8,128)(2,1)S(1)}, bf16[272,128]{1,0:T(8,128)(2,1)S(1)}) custom-call(s32[8,512]{1,0:T(8,128)S(1)} %get-tuple-element.36.plan_ref, bf16[2176,128]{1,0:T(8,128)(2,1)S(1)} %get-tuple-element.40.state, ...), custom_call_target="tpu_custom_call" | custom-call | flops 268435456 | bytes 2097152 | tf_op jit(solution)/shard_map/even1/pallas_call | solution.py:299
  23.0 1.4 %collective-permute-start.4 = (bf16[272,128]{1,0:T(8,128)(2,1)S(1)}, bf16[272,128]{1,0:T(8,128)(2,1)S(1)}, u32[]{:S(2)}, u32[]{:S(2)}) collective-permute-start(bf16[272,128]{1,0:T(8,128)(2,1)S(1)} %get-tuple-element.42), channel_id=1, source_target_pairs={{0,2},{1,3},{2,0},{3,1},{4,6},{5,7},{6,4},{7,5},{8,10},{9,11},{10,... | collective-permute-start | bytes 208904 | tf_op jit(solution)/shard_map/ppermute | solution.py:315
  24.5 3.0 %collective-permute-start.5 = (bf16[272,128]{1,0:T(8,128)(2,1)S(1)}, bf16[272,128]{1,0:T(8,128)(2,1)S(1)}, u32[]{:S(2)}, u32[]{:S(2)}) collective-permute-start(bf16[272,128]{1,0:T(8,128)(2,1)S(1)} %get-tuple-element.43), channel_id=1, source_target_pairs={{0,4},{1,5},{2,6},{3,7},{4,0},{5,1},{6,2},{7,3},{8,12},{9,13},{10,... | collective-permute-start | bytes 208904 | tf_op jit(solution)/shard_map/ppermute | solution.py:315
  27.5 0.2 collective-permute-done.9.refs_2_
  27.8 2.2 %collective-permute-start.13 = (bf16[256,128]{1,0:T(8,128)(2,1)S(1)}, bf16[256,128]{1,0:T(8,128)(2,1)S(1)}, u32[]{:S(2)}, u32[]{:S(2)}) collective-permute-start(bf16[256,128]{1,0:T(8,128)(2,1)S(1)} %state.4.refs_3_.refs_4_), channel_id=1, source_target_pairs={{0,8},{8,0},{16,24},{24,16},{1,9},{9,1},{17,25},{25,17},{2,10},{10... | collective-permute-start | bytes 196616 | tf_op jit(solution)/shard_map/ppermute | solution.py:315
  30.0 0.2 collective-permute-start.14
  30.2 1.3 %collective-permute-start.15 = (bf16[256,128]{1,0:T(8,128)(2,1)S(1)}, bf16[256,128]{1,0:T(8,128)(2,1)S(1)}, u32[]{:S(2)}, u32[]{:S(2)}) collective-permute-start(bf16[256,128]{1,0:T(8,128)(2,1)S(1)} %state.4.refs_3_.refs_4_), channel_id=1, source_target_pairs={{0,24},{8,16},{16,8},{24,0},{1,25},{9,17},{17,9},{25,1},{2,26},{10... | collective-permute-start | bytes 196616 | tf_op jit(solution)/shard_map/ppermute | solution.py:315
  31.5 0.6 collective-permute-done.5.refs_1_
  32.1 1.5 %collective-permute-done.6.refs_2_ = bf16[272,128]{1,0:T(8,128)(2,1)S(1)} collective-permute-done((bf16[272,128]{1,0:T(8,128)(2,1)S(1)}, bf16[272,128]{1,0:T(8,128)(2,1)S(1)}, u32[]{:S(2)}, u32[]{:S(2)}) %collective-permute-start.6) | collective-permute-done | bytes 69664 | tf_op jit(solution)/shard_map/ppermute | solution.py:315
  33.7 0.3 collective-permute-start.10
  34.0 2.4 %collective-permute-start.11 = (bf16[256,128]{1,0:T(8,128)(2,1)S(1)}, bf16[256,128]{1,0:T(8,128)(2,1)S(1)}, u32[]{:S(2)}, u32[]{:S(2)}) collective-permute-start(bf16[256,128]{1,0:T(8,128)(2,1)S(1)} %state.5.refs_0_), channel_id=1, source_target_pairs={{0,16},{8,24},{16,0},{24,8},{1,17},{9,25},{17,1},{25,9},{2,18},{10... | collective-permute-start | bytes 196616 | tf_op jit(solution)/shard_map/ppermute | solution.py:315
  36.4 1.2 %collective-permute-start.12 = (bf16[256,128]{1,0:T(8,128)(2,1)S(1)}, bf16[256,128]{1,0:T(8,128)(2,1)S(1)}, u32[]{:S(2)}, u32[]{:S(2)}) collective-permute-start(bf16[256,128]{1,0:T(8,128)(2,1)S(1)} %state.5.refs_0_), channel_id=1, source_target_pairs={{0,24},{8,16},{16,8},{24,0},{1,25},{9,17},{17,9},{25,1},{2,26},{10... | collective-permute-start | bytes 196616 | tf_op jit(solution)/shard_map/ppermute | solution.py:315
  37.6 0.4 collective-permute-done.10.refs_1_
  38.0 1.1 %collective-permute-done.11.refs_2_ = bf16[256,128]{1,0:T(8,128)(2,1)S(1)} collective-permute-done((bf16[256,128]{1,0:T(8,128)(2,1)S(1)}, bf16[256,128]{1,0:T(8,128)(2,1)S(1)}, u32[]{:S(2)}, u32[]{:S(2)}) %collective-permute-start.11) | collective-permute-done | bytes 65568 | tf_op jit(solution)/shard_map/ppermute | solution.py:315
  39.1 2.4 %collective-permute-done.12.refs_3_ = bf16[256,128]{1,0:T(8,128)(2,1)S(1)} collective-permute-done((bf16[256,128]{1,0:T(8,128)(2,1)S(1)}, bf16[256,128]{1,0:T(8,128)(2,1)S(1)}, u32[]{:S(2)}, u32[]{:S(2)}) %collective-permute-start.12) | collective-permute-done | bytes 65568 | tf_op jit(solution)/shard_map/ppermute | solution.py:315
  41.5 2.3 %odd.3 = (bf16[2064,128]{1,0:T(8,128)(2,1)S(1)}, bf16[2176,128]{1,0:T(8,128)(2,1)S(1)}) custom-call(s32[8,512]{1,0:T(8,128)S(1)} %get-tuple-element.36.plan_ref, bf16[256,128]{1,0:T(8,128)(2,1)S(1)} %state.5.refs_0_, bf16[256,128]{1,0:T(8,128)(2,1)S(1)} %collective-permute-done.10.refs_1_, bf16[256,128]{1,0:T(8,128)(2,1)S(1)} %collective-permute-done.11.refs_2_, ...), custom_call_target="tpu_custom_call" | custom-call | flops 536870912 | bytes 4194304 | tf_op jit(solution)/shard_map/odd/pallas_call | solution.py:299
  43.8 0.1 collective-permute-start.16
  43.9 1.7 %even0.3.even_ref = f32[1024,128]{1,0:T(8,128)S(1)} custom-call(s32[8,512]{1,0:T(8,128)S(1)} %get-tuple-element.36.plan_ref, bf16[2176,128]{1,0:T(8,128)(2,1)S(1)} %get-tuple-element.51.state, bf16[256,128,128]{2,1,0:T(8,128)(2,1)S(1)} %get-tuple-element.38.refs_4_.weights_ref.refs_8_), custom_call_target="tpu_custom_call" | custom-call | flops 268435456 | bytes 2097152 | tf_op jit(solution)/shard_map/even0/pallas_call | solution.py:299
  45.7 0.2 collective-permute-done.16.other_ref
  45.8 0.1 merge.4
  45.9 1.9 %collective-permute-start.20 = (bf16[256,128]{1,0:T(8,128)(2,1)S(1)}, bf16[256,128]{1,0:T(8,128)(2,1)S(1)}, u32[]{:S(2)}, u32[]{:S(2)}) collective-permute-start(bf16[256,128]{1,0:T(8,128)(2,1)S(1)} %get-tuple-element.58), channel_id=1, source_target_pairs={{0,2},{1,3},{2,0},{3,1},{4,6},{5,7},{6,4},{7,5},{8,10},{9,11},{10,... | collective-permute-start | bytes 196616 | tf_op jit(solution)/shard_map/ppermute | solution.py:315
  47.7 1.7 %collective-permute-start.21 = (bf16[256,128]{1,0:T(8,128)(2,1)S(1)}, bf16[256,128]{1,0:T(8,128)(2,1)S(1)}, u32[]{:S(2)}, u32[]{:S(2)}) collective-permute-start(bf16[256,128]{1,0:T(8,128)(2,1)S(1)} %get-tuple-element.59), channel_id=1, source_target_pairs={{0,4},{1,5},{2,6},{3,7},{4,0},{5,1},{6,2},{7,3},{8,12},{9,13},{10,... | collective-permute-start | bytes 196616 | tf_op jit(solution)/shard_map/ppermute | solution.py:315
  49.4 1.0 %collective-permute-start.22 = (bf16[256,128]{1,0:T(8,128)(2,1)S(1)}, bf16[256,128]{1,0:T(8,128)(2,1)S(1)}, u32[]{:S(2)}, u32[]{:S(2)}) collective-permute-start(bf16[256,128]{1,0:T(8,128)(2,1)S(1)} %get-tuple-element.60), channel_id=1, source_target_pairs={{0,6},{1,7},{2,4},{3,5},{4,2},{5,3},{6,0},{7,1},{8,14},{9,15},{10,... | collective-permute-start | bytes 196616 | tf_op jit(solution)/shard_map/ppermute | solution.py:315
  50.4 1.8 %even1.3 = (f32[256,128]{1,0:T(8,128)S(1)}, bf16[272,128]{1,0:T(8,128)(2,1)S(1)}, bf16[272,128]{1,0:T(8,128)(2,1)S(1)}, bf16[272,128]{1,0:T(8,128)(2,1)S(1)}) custom-call(s32[8,512]{1,0:T(8,128)S(1)} %get-tuple-element.36.plan_ref, bf16[2176,128]{1,0:T(8,128)(2,1)S(1)} %get-tuple-element.51.state, ...), custom_call_target="tpu_custom_call" | custom-call | flops 268435456 | bytes 2097152 | tf_op jit(solution)/shard_map/even1/pallas_call | solution.py:299
  52.2 0.0 copy-start.1
  52.2 1.4 %collective-permute-start.17 = (bf16[272,128]{1,0:T(8,128)(2,1)S(1)}, bf16[272,128]{1,0:T(8,128)(2,1)S(1)}, u32[]{:S(2)}, u32[]{:S(2)}) collective-permute-start(bf16[272,128]{1,0:T(8,128)(2,1)S(1)} %get-tuple-element.55), channel_id=1, source_target_pairs={{0,2},{1,3},{2,0},{3,1},{4,6},{5,7},{6,4},{7,5},{8,10},{9,11},{10,... | collective-permute-start | bytes 208904 | tf_op jit(solution)/shard_map/ppermute | solution.py:315
  53.6 2.1 %collective-permute-start.18 = (bf16[272,128]{1,0:T(8,128)(2,1)S(1)}, bf16[272,128]{1,0:T(8,128)(2,1)S(1)}, u32[]{:S(2)}, u32[]{:S(2)}) collective-permute-start(bf16[272,128]{1,0:T(8,128)(2,1)S(1)} %get-tuple-element.56), channel_id=1, source_target_pairs={{0,4},{1,5},{2,6},{3,7},{4,0},{5,1},{6,2},{7,3},{8,12},{9,13},{10,... | collective-permute-start | bytes 208904 | tf_op jit(solution)/shard_map/ppermute | solution.py:315
  55.7 0.9 %collective-permute-start.19 = (bf16[272,128]{1,0:T(8,128)(2,1)S(1)}, bf16[272,128]{1,0:T(8,128)(2,1)S(1)}, u32[]{:S(2)}, u32[]{:S(2)}) collective-permute-start(bf16[272,128]{1,0:T(8,128)(2,1)S(1)} %get-tuple-element.57), channel_id=1, source_target_pairs={{0,6},{1,7},{2,4},{3,5},{4,2},{5,3},{6,0},{7,1},{8,14},{9,15},{10,... | collective-permute-start | bytes 208904 | tf_op jit(solution)/shard_map/ppermute | solution.py:315
  56.7 3.5 %collective-permute-start.26 = (bf16[256,128]{1,0:T(8,128)(2,1)S(1)}, bf16[256,128]{1,0:T(8,128)(2,1)S(1)}, u32[]{:S(2)}, u32[]{:S(2)}) collective-permute-start(bf16[256,128]{1,0:T(8,128)(2,1)S(1)} %state.6.refs_3_.refs_4_), channel_id=1, source_target_pairs={{0,8},{8,0},{16,24},{24,16},{1,9},{9,1},{17,25},{25,17},{2,10},{10... | collective-permute-start | bytes 196616 | tf_op jit(solution)/shard_map/ppermute | solution.py:315
  60.2 1.5 %collective-permute-start.28 = (bf16[256,128]{1,0:T(8,128)(2,1)S(1)}, bf16[256,128]{1,0:T(8,128)(2,1)S(1)}, u32[]{:S(2)}, u32[]{:S(2)}) collective-permute-start(bf16[256,128]{1,0:T(8,128)(2,1)S(1)} %state.6.refs_3_.refs_4_), channel_id=1, source_target_pairs={{0,24},{8,16},{16,8},{24,0},{1,25},{9,17},{17,9},{25,1},{2,26},{10... | collective-permute-start | bytes 196616 | tf_op jit(solution)/shard_map/ppermute | solution.py:315
  61.8 0.1 collective-permute-done.19.refs_2_
  62.0 1.9 %collective-permute-start.23 = (bf16[256,128]{1,0:T(8,128)(2,1)S(1)}, bf16[256,128]{1,0:T(8,128)(2,1)S(1)}, u32[]{:S(2)}, u32[]{:S(2)}) collective-permute-start(bf16[256,128]{1,0:T(8,128)(2,1)S(1)} %state.7.refs_0_), channel_id=1, source_target_pairs={{0,8},{8,0},{16,24},{24,16},{1,9},{9,1},{17,25},{25,17},{2,10},{10... | collective-permute-start | bytes 196616 | tf_op jit(solution)/shard_map/ppermute | solution.py:315
  63.8 1.7 %collective-permute-start.25 = (bf16[256,128]{1,0:T(8,128)(2,1)S(1)}, bf16[256,128]{1,0:T(8,128)(2,1)S(1)}, u32[]{:S(2)}, u32[]{:S(2)}) collective-permute-start(bf16[256,128]{1,0:T(8,128)(2,1)S(1)} %state.7.refs_0_), channel_id=1, source_target_pairs={{0,24},{8,16},{16,8},{24,0},{1,25},{9,17},{17,9},{25,1},{2,26},{10... | collective-permute-start | bytes 196616 | tf_op jit(solution)/shard_map/ppermute | solution.py:315
  65.5 0.1 place.1.place_ref
  65.6 0.2 collective-permute-done.28.refs_7_
  65.8 0.8 collective-permute-done.23.refs_1_
  66.7 1.4 %collective-permute-done.24.refs_2_ = bf16[256,128]{1,0:T(8,128)(2,1)S(1)} collective-permute-done((bf16[256,128]{1,0:T(8,128)(2,1)S(1)}, bf16[256,128]{1,0:T(8,128)(2,1)S(1)}, u32[]{:S(2)}, u32[]{:S(2)}) %collective-permute-start.24) | collective-permute-done | bytes 65568 | tf_op jit(solution)/shard_map/ppermute | solution.py:315
  68.1 0.9 %collective-permute-done.25.refs_3_ = bf16[256,128]{1,0:T(8,128)(2,1)S(1)} collective-permute-done((bf16[256,128]{1,0:T(8,128)(2,1)S(1)}, bf16[256,128]{1,0:T(8,128)(2,1)S(1)}, u32[]{:S(2)}, u32[]{:S(2)}) %collective-permute-start.25) | collective-permute-done | bytes 65568 | tf_op jit(solution)/shard_map/ppermute | solution.py:315
  69.0 5.4 %last.1 = (bf16[1024,128]{1,0:T(8,128)(2,1)S(1)}, f32[4096,128]{1,0:T(8,128)S(1)}) custom-call(s32[8,512]{1,0:T(8,128)S(1)} %get-tuple-element.36.plan_ref, s32[1,2048]{1,0:T(1,128)S(1)} %place.1.place_ref, bf16[256,128]{1,0:T(8,128)(2,1)S(1)} %state.7.refs_0_, bf16[256,128]{1,0:T(8,128)(2,1)S(1)} %collective-permute-done.23.refs_1_, ...), custom_call_target="tpu_custom_call" | custom-call | flops 1073741824 | bytes 8388608 | tf_op jit(solution)/shard_map/last/pallas_call | solution.py:299
  74.4 0.1 collective-permute-start.29
  74.5 1.7 %pick.1.even_ref = f32[1024,128]{1,0:T(8,128)S(1)} custom-call(s32[1,2048]{1,0:T(1,128)S(1)} %place.1.place_ref, f32[4096,128]{1,0:T(8,128)S(1)} %get-tuple-element.61.total), custom_call_target="tpu_custom_call" | custom-call | flops 214748368 | bytes 1677721 | tf_op jit(solution)/shard_map/pick/pallas_call | solution.py:299
  76.3 0.1 merge.5
  76.3 3.4 %collective-permute-start.32 = (bf16[256,128]{1,0:T(8,128)(2,1)S(1)}, bf16[256,128]{1,0:T(8,128)(2,1)S(1)}, u32[]{:S(2)}, u32[]{:S(2)}) collective-permute-start(bf16[256,128]{1,0:T(8,128)(2,1)S(1)} %get-tuple-element.66), channel_id=1, source_target_pairs={{0,6},{1,7},{2,4},{3,5},{4,2},{5,3},{6,0},{7,1},{8,14},{9,15},{10,... | collective-permute-start | bytes 196616 | tf_op jit(solution)/shard_map/ppermute | solution.py:315
  79.8 0.6 collective-permute-start.31
  80.4 0.4 collective-permute-start.30
  80.8 0.1 select_reduce_fusion
  80.9 2.2 %collective-permute-done.32 = bf16[256,128]{1,0:T(8,128)(2,1)S(1)} collective-permute-done((bf16[256,128]{1,0:T(8,128)(2,1)S(1)}, bf16[256,128]{1,0:T(8,128)(2,1)S(1)}, u32[]{:S(2)}, u32[]{:S(2)}) %collective-permute-start.32) | collective-permute-done | bytes 65568 | tf_op jit(solution)/shard_map/ppermute | solution.py:315
  83.0 3.8 %collective-permute-done.31 = bf16[256,128]{1,0:T(8,128)(2,1)S(1)} collective-permute-done((bf16[256,128]{1,0:T(8,128)(2,1)S(1)}, bf16[256,128]{1,0:T(8,128)(2,1)S(1)}, u32[]{:S(2)}, u32[]{:S(2)}) %collective-permute-start.31) | collective-permute-done | bytes 65568 | tf_op jit(solution)/shard_map/ppermute | solution.py:315
  86.9 0.1 multiply_reduce_fusion
  87.0 0.8 multiply_multiply_fusion
  (30 shorter events, 0.3 us)
Async XLA Ops:
  1.1 9.4 %collective-permute-start = (bf16[512,128]{1,0:T(8,128)(2,1)S(1)}, bf16[512,128]{1,0:T(8,128)(2,1)S(1)}, u32[]{:S(2)}, u32[]{:S(2)}) collective-permute-start(bf16[512,128]{1,0:T(8,128)(2,1)S(1)} %get-tuple-element.37.refs_0_), channel_id=1, source_target_pairs={{0,8},{8,0},{16,24},{24,16},{1,9},{9,1},{17,25},{25,17},{2,10},{10... | collective-permute-start | bytes 393224 | tf_op jit(solution)/shard_map/ppermute | solution.py:315
  4.1 7.8 %collective-permute-start.1 = (bf16[512,128]{1,0:T(8,128)(2,1)S(1)}, bf16[512,128]{1,0:T(8,128)(2,1)S(1)}, u32[]{:S(2)}, u32[]{:S(2)}) collective-permute-start(bf16[512,128]{1,0:T(8,128)(2,1)S(1)} %get-tuple-element.37.refs_0_), channel_id=1, source_target_pairs={{0,16},{8,24},{16,0},{24,8},{1,17},{9,25},{17,1},{25,9},{2,18},{10... | collective-permute-start | bytes 393224 | tf_op jit(solution)/shard_map/ppermute | solution.py:315
  5.6 6.3 %collective-permute-start.2 = (bf16[512,128]{1,0:T(8,128)(2,1)S(1)}, bf16[512,128]{1,0:T(8,128)(2,1)S(1)}, u32[]{:S(2)}, u32[]{:S(2)}) collective-permute-start(bf16[512,128]{1,0:T(8,128)(2,1)S(1)} %get-tuple-element.37.refs_0_), channel_id=1, source_target_pairs={{0,24},{8,16},{16,8},{24,0},{1,25},{9,17},{17,9},{25,1},{2,26},{10... | collective-permute-start | bytes 393224 | tf_op jit(solution)/shard_map/ppermute | solution.py:315
  14.2 2.0 %collective-permute-start.3 = (bf16[2064,128]{1,0:T(8,128)(2,1)S(1)}, bf16[2064,128]{1,0:T(8,128)(2,1)S(1)}, u32[]{:S(2)}, u32[]{:S(2)}) collective-permute-start(bf16[2064,128]{1,0:T(8,128)(2,1)S(1)} %get-tuple-element.39), channel_id=1, source_target_pairs={{0,1},{1,0},{2,3},{3,2},{4,5},{5,4},{6,7},{7,6},{8,9},{9,8},{10,11... | collective-permute-start | bytes 1585160 | tf_op jit(solution)/shard_map/ppermute | solution.py:315
  16.2 11.3 %collective-permute-start.7 = (bf16[256,128]{1,0:T(8,128)(2,1)S(1)}, bf16[256,128]{1,0:T(8,128)(2,1)S(1)}, u32[]{:S(2)}, u32[]{:S(2)}) collective-permute-start(bf16[256,128]{1,0:T(8,128)(2,1)S(1)} %get-tuple-element.48), channel_id=1, source_target_pairs={{0,2},{1,3},{2,0},{3,1},{4,6},{5,7},{6,4},{7,5},{8,10},{9,11},{10,... | collective-permute-start | bytes 196616 | tf_op jit(solution)/shard_map/ppermute | solution.py:315
  18.7 8.9 %collective-permute-start.8 = (bf16[256,128]{1,0:T(8,128)(2,1)S(1)}, bf16[256,128]{1,0:T(8,128)(2,1)S(1)}, u32[]{:S(2)}, u32[]{:S(2)}) collective-permute-start(bf16[256,128]{1,0:T(8,128)(2,1)S(1)} %get-tuple-element.49), channel_id=1, source_target_pairs={{0,4},{1,5},{2,6},{3,7},{4,0},{5,1},{6,2},{7,3},{8,12},{9,13},{10,... | collective-permute-start | bytes 196616 | tf_op jit(solution)/shard_map/ppermute | solution.py:315
  21.2 6.5 %collective-permute-start.9 = (bf16[256,128]{1,0:T(8,128)(2,1)S(1)}, bf16[256,128]{1,0:T(8,128)(2,1)S(1)}, u32[]{:S(2)}, u32[]{:S(2)}) collective-permute-start(bf16[256,128]{1,0:T(8,128)(2,1)S(1)} %get-tuple-element.50), channel_id=1, source_target_pairs={{0,6},{1,7},{2,4},{3,5},{4,2},{5,3},{6,0},{7,1},{8,14},{9,15},{10,... | collective-permute-start | bytes 196616 | tf_op jit(solution)/shard_map/ppermute | solution.py:315
  23.0 7.1 %collective-permute-start.4 = (bf16[272,128]{1,0:T(8,128)(2,1)S(1)}, bf16[272,128]{1,0:T(8,128)(2,1)S(1)}, u32[]{:S(2)}, u32[]{:S(2)}) collective-permute-start(bf16[272,128]{1,0:T(8,128)(2,1)S(1)} %get-tuple-element.42), channel_id=1, source_target_pairs={{0,2},{1,3},{2,0},{3,1},{4,6},{5,7},{6,4},{7,5},{8,10},{9,11},{10,... | collective-permute-start | bytes 208904 | tf_op jit(solution)/shard_map/ppermute | solution.py:315
  24.5 7.6 %collective-permute-start.5 = (bf16[272,128]{1,0:T(8,128)(2,1)S(1)}, bf16[272,128]{1,0:T(8,128)(2,1)S(1)}, u32[]{:S(2)}, u32[]{:S(2)}) collective-permute-start(bf16[272,128]{1,0:T(8,128)(2,1)S(1)} %get-tuple-element.43), channel_id=1, source_target_pairs={{0,4},{1,5},{2,6},{3,7},{4,0},{5,1},{6,2},{7,3},{8,12},{9,13},{10,... | collective-permute-start | bytes 208904 | tf_op jit(solution)/shard_map/ppermute | solution.py:315
  27.5 6.1 %collective-permute-start.6 = (bf16[272,128]{1,0:T(8,128)(2,1)S(1)}, bf16[272,128]{1,0:T(8,128)(2,1)S(1)}, u32[]{:S(2)}, u32[]{:S(2)}) collective-permute-start(bf16[272,128]{1,0:T(8,128)(2,1)S(1)} %get-tuple-element.44), channel_id=1, source_target_pairs={{0,6},{1,7},{2,4},{3,5},{4,2},{5,3},{6,0},{7,1},{8,14},{9,15},{10,... | collective-permute-start | bytes 208904 | tf_op jit(solution)/shard_map/ppermute | solution.py:315
  27.8 8.6 %collective-permute-start.13 = (bf16[256,128]{1,0:T(8,128)(2,1)S(1)}, bf16[256,128]{1,0:T(8,128)(2,1)S(1)}, u32[]{:S(2)}, u32[]{:S(2)}) collective-permute-start(bf16[256,128]{1,0:T(8,128)(2,1)S(1)} %state.4.refs_3_.refs_4_), channel_id=1, source_target_pairs={{0,8},{8,0},{16,24},{24,16},{1,9},{9,1},{17,25},{25,17},{2,10},{10... | collective-permute-start | bytes 196616 | tf_op jit(solution)/shard_map/ppermute | solution.py:315
  30.0 7.6 %collective-permute-start.14 = (bf16[256,128]{1,0:T(8,128)(2,1)S(1)}, bf16[256,128]{1,0:T(8,128)(2,1)S(1)}, u32[]{:S(2)}, u32[]{:S(2)}) collective-permute-start(bf16[256,128]{1,0:T(8,128)(2,1)S(1)} %state.4.refs_3_.refs_4_), channel_id=1, source_target_pairs={{0,16},{8,24},{16,0},{24,8},{1,17},{9,25},{17,1},{25,9},{2,18},{10... | collective-permute-start | bytes 196616 | tf_op jit(solution)/shard_map/ppermute | solution.py:315
  30.2 7.4 %collective-permute-start.15 = (bf16[256,128]{1,0:T(8,128)(2,1)S(1)}, bf16[256,128]{1,0:T(8,128)(2,1)S(1)}, u32[]{:S(2)}, u32[]{:S(2)}) collective-permute-start(bf16[256,128]{1,0:T(8,128)(2,1)S(1)} %state.4.refs_3_.refs_4_), channel_id=1, source_target_pairs={{0,24},{8,16},{16,8},{24,0},{1,25},{9,17},{17,9},{25,1},{2,26},{10... | collective-permute-start | bytes 196616 | tf_op jit(solution)/shard_map/ppermute | solution.py:315
  33.7 4.3 %collective-permute-start.10 = (bf16[256,128]{1,0:T(8,128)(2,1)S(1)}, bf16[256,128]{1,0:T(8,128)(2,1)S(1)}, u32[]{:S(2)}, u32[]{:S(2)}) collective-permute-start(bf16[256,128]{1,0:T(8,128)(2,1)S(1)} %state.5.refs_0_), channel_id=1, source_target_pairs={{0,8},{8,0},{16,24},{24,16},{1,9},{9,1},{17,25},{25,17},{2,10},{10... | collective-permute-start | bytes 196616 | tf_op jit(solution)/shard_map/ppermute | solution.py:315
  34.0 5.1 %collective-permute-start.11 = (bf16[256,128]{1,0:T(8,128)(2,1)S(1)}, bf16[256,128]{1,0:T(8,128)(2,1)S(1)}, u32[]{:S(2)}, u32[]{:S(2)}) collective-permute-start(bf16[256,128]{1,0:T(8,128)(2,1)S(1)} %state.5.refs_0_), channel_id=1, source_target_pairs={{0,16},{8,24},{16,0},{24,8},{1,17},{9,25},{17,1},{25,9},{2,18},{10... | collective-permute-start | bytes 196616 | tf_op jit(solution)/shard_map/ppermute | solution.py:315
  36.4 5.2 %collective-permute-start.12 = (bf16[256,128]{1,0:T(8,128)(2,1)S(1)}, bf16[256,128]{1,0:T(8,128)(2,1)S(1)}, u32[]{:S(2)}, u32[]{:S(2)}) collective-permute-start(bf16[256,128]{1,0:T(8,128)(2,1)S(1)} %state.5.refs_0_), channel_id=1, source_target_pairs={{0,24},{8,16},{16,8},{24,0},{1,25},{9,17},{17,9},{25,1},{2,26},{10... | collective-permute-start | bytes 196616 | tf_op jit(solution)/shard_map/ppermute | solution.py:315
  43.8 2.0 %collective-permute-start.16 = (bf16[2064,128]{1,0:T(8,128)(2,1)S(1)}, bf16[2064,128]{1,0:T(8,128)(2,1)S(1)}, u32[]{:S(2)}, u32[]{:S(2)}) collective-permute-start(bf16[2064,128]{1,0:T(8,128)(2,1)S(1)} %get-tuple-element.52), channel_id=1, source_target_pairs={{0,1},{1,0},{2,3},{3,2},{4,5},{5,4},{6,7},{7,6},{8,9},{9,8},{10,11... | collective-permute-start | bytes 1585160 | tf_op jit(solution)/shard_map/ppermute | solution.py:315
  45.9 9.8 %collective-permute-start.20 = (bf16[256,128]{1,0:T(8,128)(2,1)S(1)}, bf16[256,128]{1,0:T(8,128)(2,1)S(1)}, u32[]{:S(2)}, u32[]{:S(2)}) collective-permute-start(bf16[256,128]{1,0:T(8,128)(2,1)S(1)} %get-tuple-element.58), channel_id=1, source_target_pairs={{0,2},{1,3},{2,0},{3,1},{4,6},{5,7},{6,4},{7,5},{8,10},{9,11},{10,... | collective-permute-start | bytes 196616 | tf_op jit(solution)/shard_map/ppermute | solution.py:315
  47.7 8.9 %collective-permute-start.21 = (bf16[256,128]{1,0:T(8,128)(2,1)S(1)}, bf16[256,128]{1,0:T(8,128)(2,1)S(1)}, u32[]{:S(2)}, u32[]{:S(2)}) collective-permute-start(bf16[256,128]{1,0:T(8,128)(2,1)S(1)} %get-tuple-element.59), channel_id=1, source_target_pairs={{0,4},{1,5},{2,6},{3,7},{4,0},{5,1},{6,2},{7,3},{8,12},{9,13},{10,... | collective-permute-start | bytes 196616 | tf_op jit(solution)/shard_map/ppermute | solution.py:315
  49.4 7.2 %collective-permute-start.22 = (bf16[256,128]{1,0:T(8,128)(2,1)S(1)}, bf16[256,128]{1,0:T(8,128)(2,1)S(1)}, u32[]{:S(2)}, u32[]{:S(2)}) collective-permute-start(bf16[256,128]{1,0:T(8,128)(2,1)S(1)} %get-tuple-element.60), channel_id=1, source_target_pairs={{0,6},{1,7},{2,4},{3,5},{4,2},{5,3},{6,0},{7,1},{8,14},{9,15},{10,... | collective-permute-start | bytes 196616 | tf_op jit(solution)/shard_map/ppermute | solution.py:315
  52.2 28.6 %copy-start = (s32[256]{0:T(256)S(1)}, s32[256]{0:T(256)}, u32[]{:S(2)}) copy-start(s32[256]{0:T(256)} %param.16) | copy-start | bytes 3076
  52.2 28.6 %copy-start.1 = (f32[16]{0:T(128)S(1)}, f32[16]{0:T(128)}, u32[]{:S(2)}) copy-start(f32[16]{0:T(128)} %param.17) | copy-start | bytes 196
  52.2 8.0 %collective-permute-start.17 = (bf16[272,128]{1,0:T(8,128)(2,1)S(1)}, bf16[272,128]{1,0:T(8,128)(2,1)S(1)}, u32[]{:S(2)}, u32[]{:S(2)}) collective-permute-start(bf16[272,128]{1,0:T(8,128)(2,1)S(1)} %get-tuple-element.55), channel_id=1, source_target_pairs={{0,2},{1,3},{2,0},{3,1},{4,6},{5,7},{6,4},{7,5},{8,10},{9,11},{10,... | collective-permute-start | bytes 208904 | tf_op jit(solution)/shard_map/ppermute | solution.py:315
  53.6 8.2 %collective-permute-start.18 = (bf16[272,128]{1,0:T(8,128)(2,1)S(1)}, bf16[272,128]{1,0:T(8,128)(2,1)S(1)}, u32[]{:S(2)}, u32[]{:S(2)}) collective-permute-start(bf16[272,128]{1,0:T(8,128)(2,1)S(1)} %get-tuple-element.56), channel_id=1, source_target_pairs={{0,4},{1,5},{2,6},{3,7},{4,0},{5,1},{6,2},{7,3},{8,12},{9,13},{10,... | collective-permute-start | bytes 208904 | tf_op jit(solution)/shard_map/ppermute | solution.py:315
  55.7 6.2 %collective-permute-start.19 = (bf16[272,128]{1,0:T(8,128)(2,1)S(1)}, bf16[272,128]{1,0:T(8,128)(2,1)S(1)}, u32[]{:S(2)}, u32[]{:S(2)}) collective-permute-start(bf16[272,128]{1,0:T(8,128)(2,1)S(1)} %get-tuple-element.57), channel_id=1, source_target_pairs={{0,6},{1,7},{2,4},{3,5},{4,2},{5,3},{6,0},{7,1},{8,14},{9,15},{10,... | collective-permute-start | bytes 208904 | tf_op jit(solution)/shard_map/ppermute | solution.py:315
  56.7 7.1 %collective-permute-start.26 = (bf16[256,128]{1,0:T(8,128)(2,1)S(1)}, bf16[256,128]{1,0:T(8,128)(2,1)S(1)}, u32[]{:S(2)}, u32[]{:S(2)}) collective-permute-start(bf16[256,128]{1,0:T(8,128)(2,1)S(1)} %state.6.refs_3_.refs_4_), channel_id=1, source_target_pairs={{0,8},{8,0},{16,24},{24,16},{1,9},{9,1},{17,25},{25,17},{2,10},{10... | collective-permute-start | bytes 196616 | tf_op jit(solution)/shard_map/ppermute | solution.py:315
  60.2 5.4 %collective-permute-start.27 = (bf16[256,128]{1,0:T(8,128)(2,1)S(1)}, bf16[256,128]{1,0:T(8,128)(2,1)S(1)}, u32[]{:S(2)}, u32[]{:S(2)}) collective-permute-start(bf16[256,128]{1,0:T(8,128)(2,1)S(1)} %state.6.refs_3_.refs_4_), channel_id=1, source_target_pairs={{0,16},{8,24},{16,0},{24,8},{1,17},{9,25},{17,1},{25,9},{2,18},{10... | collective-permute-start | bytes 196616 | tf_op jit(solution)/shard_map/ppermute | solution.py:315
  60.2 5.6 %collective-permute-start.28 = (bf16[256,128]{1,0:T(8,128)(2,1)S(1)}, bf16[256,128]{1,0:T(8,128)(2,1)S(1)}, u32[]{:S(2)}, u32[]{:S(2)}) collective-permute-start(bf16[256,128]{1,0:T(8,128)(2,1)S(1)} %state.6.refs_3_.refs_4_), channel_id=1, source_target_pairs={{0,24},{8,16},{16,8},{24,0},{1,25},{9,17},{17,9},{25,1},{2,26},{10... | collective-permute-start | bytes 196616 | tf_op jit(solution)/shard_map/ppermute | solution.py:315
  62.0 4.7 %collective-permute-start.23 = (bf16[256,128]{1,0:T(8,128)(2,1)S(1)}, bf16[256,128]{1,0:T(8,128)(2,1)S(1)}, u32[]{:S(2)}, u32[]{:S(2)}) collective-permute-start(bf16[256,128]{1,0:T(8,128)(2,1)S(1)} %state.7.refs_0_), channel_id=1, source_target_pairs={{0,8},{8,0},{16,24},{24,16},{1,9},{9,1},{17,25},{25,17},{2,10},{10... | collective-permute-start | bytes 196616 | tf_op jit(solution)/shard_map/ppermute | solution.py:315
  63.8 4.3 %collective-permute-start.24 = (bf16[256,128]{1,0:T(8,128)(2,1)S(1)}, bf16[256,128]{1,0:T(8,128)(2,1)S(1)}, u32[]{:S(2)}, u32[]{:S(2)}) collective-permute-start(bf16[256,128]{1,0:T(8,128)(2,1)S(1)} %state.7.refs_0_), channel_id=1, source_target_pairs={{0,16},{8,24},{16,0},{24,8},{1,17},{9,25},{17,1},{25,9},{2,18},{10... | collective-permute-start | bytes 196616 | tf_op jit(solution)/shard_map/ppermute | solution.py:315
  63.8 5.2 %collective-permute-start.25 = (bf16[256,128]{1,0:T(8,128)(2,1)S(1)}, bf16[256,128]{1,0:T(8,128)(2,1)S(1)}, u32[]{:S(2)}, u32[]{:S(2)}) collective-permute-start(bf16[256,128]{1,0:T(8,128)(2,1)S(1)} %state.7.refs_0_), channel_id=1, source_target_pairs={{0,24},{8,16},{16,8},{24,0},{1,25},{9,17},{17,9},{25,1},{2,26},{10... | collective-permute-start | bytes 196616 | tf_op jit(solution)/shard_map/ppermute | solution.py:315
  74.4 1.8 %collective-permute-start.29 = (bf16[1024,128]{1,0:T(8,128)(2,1)S(1)}, bf16[1024,128]{1,0:T(8,128)(2,1)S(1)}, u32[]{:S(2)}, u32[]{:S(2)}) collective-permute-start(bf16[1024,128]{1,0:T(8,128)(2,1)S(1)} %get-tuple-element.62), channel_id=1, source_target_pairs={{0,1},{1,0},{2,3},{3,2},{4,5},{5,4},{6,7},{7,6},{8,9},{9,8},{10,11... | collective-permute-start | bytes 786440 | tf_op jit(solution)/shard_map/ppermute | solution.py:315
  76.3 6.7 %collective-permute-start.32 = (bf16[256,128]{1,0:T(8,128)(2,1)S(1)}, bf16[256,128]{1,0:T(8,128)(2,1)S(1)}, u32[]{:S(2)}, u32[]{:S(2)}) collective-permute-start(bf16[256,128]{1,0:T(8,128)(2,1)S(1)} %get-tuple-element.66), channel_id=1, source_target_pairs={{0,6},{1,7},{2,4},{3,5},{4,2},{5,3},{6,0},{7,1},{8,14},{9,15},{10,... | collective-permute-start | bytes 196616 | tf_op jit(solution)/shard_map/ppermute | solution.py:315
  79.8 7.1 %collective-permute-start.31 = (bf16[256,128]{1,0:T(8,128)(2,1)S(1)}, bf16[256,128]{1,0:T(8,128)(2,1)S(1)}, u32[]{:S(2)}, u32[]{:S(2)}) collective-permute-start(bf16[256,128]{1,0:T(8,128)(2,1)S(1)} %get-tuple-element.65), channel_id=1, source_target_pairs={{0,4},{1,5},{2,6},{3,7},{4,0},{5,1},{6,2},{7,3},{8,12},{9,13},{10,... | collective-permute-start | bytes 196616 | tf_op jit(solution)/shard_map/ppermute | solution.py:315
  80.4 6.5 %collective-permute-start.30 = (bf16[256,128]{1,0:T(8,128)(2,1)S(1)}, bf16[256,128]{1,0:T(8,128)(2,1)S(1)}, u32[]{:S(2)}, u32[]{:S(2)}) collective-permute-start(bf16[256,128]{1,0:T(8,128)(2,1)S(1)} %get-tuple-element.64), channel_id=1, source_target_pairs={{0,2},{1,3},{2,0},{3,1},{4,6},{5,7},{6,4},{7,5},{8,10},{9,11},{10,... | collective-permute-start | bytes 196616 | tf_op jit(solution)/shard_map/ppermute | solution.py:315

commit v8 on v7

--- a/solution.py
+++ b/solution.py
@@ -26,6 +26,18 @@
 PARAMS = pltpu.CompilerParams(vmem_limit_bytes=16 * MIB)
 
 
+def chip_slot(k, core, chips):
+    return jnp.where(core == 0, k, (chips - k) % chips)
+
+
+def row_slot(k, core, nrows):
+    return jnp.where(core == 0, k, k // 2 + k % 2 * (nrows // 2))
+
+
+def row_mask(slot, core, nrows):
+    return slot if core == 0 else slot * 2 % nrows + slot * 2 // nrows
+
+
 def iota(shape, dim):
     return lax.broadcasted_iota(jnp.int32, shape, dim)
 
@@ -41,7 +53,7 @@
 
 
 def plan_kernel(
-    row_tiles, per_group, zero_tile, count_ref, tile_row_hbm, tile_col_hbm, weights_hbm,
+    row_tiles, per_group, nrows, count_ref, tile_row_hbm, tile_col_hbm, weights_hbm,
     plan_ref, weights_ref, tile_row_ref, tile_col_ref, sems,
 ):
     load = pltpu.make_async_copy(weights_hbm, weights_ref, sems.at[0])
@@ -57,15 +69,17 @@
     slots = tile_row_ref.shape[1]
     length = plan_ref.shape[1]
     my_row, my_col = lax.axis_index("row"), lax.axis_index("col")
+    zero_tile = nrows * per_group
     chunk_tiles = row_tiles // CHUNKS
     per_half = per_group // HALVES
     row = tile_row_ref[...]
     rel = (row // per_group) ^ my_col
     chunk = (1 - rel % 2) * HALVES + (row % per_group) // per_half
-    order = chunk * chunk_tiles + (rel // 2) * per_half + row % per_half
+    slot = chip_slot(rel // 2, (my_col + rel) % 2, chunk_tiles // per_half)
+    order = chunk * chunk_tiles + slot * per_half + row % per_half
     order = jnp.where(iota((1, slots), 1) < count_ref[0, 0], order, row_tiles).astype(jnp.float32)
     col = tile_col_ref[...]
-    source = ((col // per_group) ^ my_row) * per_group + col % per_group
+    source = row_slot((col // per_group) ^ my_row, my_col % 2, nrows) * per_group + col % per_group
     entry = (iota((1, slots), 1) * SHIFT + source).astype(jnp.float32)
     order_c = to_column(order)
     entry_c = to_column(entry)
@@ -226,7 +240,8 @@
         ids = (rows[:id_rows] * BYTE + rows[id_rows : 2 * id_rows]).astype(jnp.int32)
         rel = (ids // rows_here) ^ my_col
         chunk = (1 - rel % 2) * HALVES + ids % rows_here // half
-        return chunk * chunk_rows + rel // 2 * half + ids % half
+        slot = chip_slot(rel // 2, (my_col + rel) % 2, chips)
+        return chunk * chunk_rows + slot * half + ids % half
 
     def tail(ref):
         return ref[ref.shape[0] - extra :, :].astype(jnp.float32)
@@ -237,9 +252,9 @@
         even.append(rows)
         odd.append(pltpu.roll(rows, extra - extra // 2, 0))
     for k in range(chips):
-        for part, rows in enumerate((places(odd[k]), places(even[k]))):
+        for place, rows in (((chips - k) % chips, places(odd[k])), (chips + k, places(even[k]))):
             for r in range(id_rows):
-                at = ((part * chips + k) * id_rows + r) * LANES
+                at = (place * id_rows + r) * LANES
                 place_ref[0:1, at : at + LANES] = rows[r : r + 1, :]
 
 
@@ -311,14 +326,25 @@
             name=name,
         )(*args)
 
-    def swap(array, axis, size, mask):
-        return lax.ppermute(array, axis, [(i, i ^ mask) for i in range(size)])
-
     def swap_cores(odd):
-        return swap(odd, "col", ncols, 1)
+        return lax.ppermute(odd, "col", [(i, i ^ 1) for i in range(ncols)])
+
+    def send(sent):
+        came = []
+        for slot, part in enumerate(sent, 1):
+            masks = (2 * slot, 2 * (chips - slot))
+            came.append(lax.ppermute(part, "col", [(i, i ^ masks[i % 2]) for i in range(ncols)]))
+        return came
 
     def spread(state):
-        return [state] + [swap(state, "row", nrows, k) for k in range(1, nrows)]
+        pieces = [state]
+        for slot in range(1, nrows):
+            masks = [row_mask(slot, core, nrows) for core in range(2)]
+            pairs = [
+                (r * ncols + c, (r ^ masks[c % 2]) * ncols + c) for r in range(nrows) for c in range(ncols)
+            ]
+            pieces.append(lax.ppermute(state, ("row", "col"), pairs))
+        return pieces
 
     state, *squares = call(
         begin_kernel,
@@ -335,7 +361,7 @@
     pieces = spread(state)
 
     plan, weights = call(
-        functools.partial(plan_kernel, row_tiles, per_group, zero_tile),
+        functools.partial(plan_kernel, row_tiles, per_group, nrows),
         "plan",
         [array((8, length), jnp.int32), pltpu.VMEM(weights.shape, weights.dtype)],
         (tile_count, in_hbm(tile_row[0]), in_hbm(tile_col[0]), in_hbm(weights)),
@@ -356,9 +382,6 @@
 
     def sums_shape(rows, more=0):
         return [array((rows, width), f32)] + [array((rows + more, width), bf16)] * (chips - 1)
-
-    def send(sent):
-        return [swap(part, "col", ncols, 2 * k) for k, part in enumerate(sent, 1)]
 
     def merge(even, other):
         own, *sent = call(

time: 87.7 us -> 86.6 us (0.987); the launches traced: 87.8 us -> 85.8 us
  starting transfers between devices: 43.9 us -> 41.8 us
    ppermute x33, starting transfers between devices: 43.9 us -> 41.8 us  [the longest x15 22.3 us: send(): lax.ppermute(part, 'col', [(i, i ^ masks[i % 2]) for i in range(ncols)])]
  transfers between devices with their start and end apart: 33 -> 33, of which waited for: 16 -> 14; matrix products, arithmetic and copies ran while one was open for 1% -> 1% of each run, Pallas kernels for 14% -> 15%
where the time goes in v8:
time: 86.6 us; the launch traced here: 85.8 us
  starting transfers between devices  41.8 us (48%)
  Pallas kernels  23.9 us (28%)
  waiting for transfers between devices  17.6 us (20%)
  other arithmetic  1.71 us (2%)
  between operations  0.88 us (1%)
    pallas_call x18, Pallas kernels, call(): pl.pallas_call(kernel, out_shape=out_shape, grid_spec=pltpu.PrefetchScala...  23.9 us
    ppermute x15, starting transfers between devices, send(): lax.ppermute(part, 'col', [(i, i ^ masks[i % 2]) for i in range(ncols)])  22.3 us
    ppermute x15, starting transfers between devices, spread(): pieces.append(lax.ppermute(state, ('row', 'col'), pairs))  19.3 us
    ppermute x15, waiting for transfers between devices, spread(): pieces.append(lax.ppermute(state, ('row', 'col'), pairs))  9.89 us
    ppermute x15, waiting for transfers between devices, send(): lax.ppermute(part, 'col', [(i, i ^ masks[i % 2]) for i in range(ncols)])  7.38 us
  transfers between devices with their start and end apart: 33, of which 14 were waited for; matrix products, arithmetic and copies ran while one was open for 1% of the time, Pallas kernels for 15%

profile of v8, /device:TPU:0, one launch (start us, length us, event | category | flops | bytes accessed | tf_op | source)
XLA Modules:
  0.0 85.8 jit_solution(7771561983325790627)
XLA Ops:
  0.0 1.1 %begin.1 = (bf16[512,128]{1,0:T(8,128)(2,1)S(1)}, f32[256,128]{1,0:T(8,128)S(1)}, f32[256,128]{1,0:T(8,128)S(1)}) custom-call(s32[4,128]{1,0:T(4,128)} %bitcast.25, bf16[512,128]{1,0:T(8,128)(2,1)} %embed_hbm.1), custom_call_target="tpu_custom_call" | custom-call | tf_op jit(solution)/shard_map/begin/pallas_call | solution.py:314
  1.1 3.0 %collective-permute-start = (bf16[512,128]{1,0:T(8,128)(2,1)S(1)}, bf16[512,128]{1,0:T(8,128)(2,1)S(1)}, u32[]{:S(2)}, u32[]{:S(2)}) collective-permute-start(bf16[512,128]{1,0:T(8,128)(2,1)S(1)} %get-tuple-element.37.refs_0_), channel_id=1, source_target_pairs={{0,8},{1,17},{2,10},{3,19},{4,12},{5,21},{6,14},{7,23},{8,0},{9,25... | collective-permute-start | bytes 393224 | tf_op jit(solution)/shard_map/ppermute | solution.py:346
  4.1 1.5 %collective-permute-start.1 = (bf16[512,128]{1,0:T(8,128)(2,1)S(1)}, bf16[512,128]{1,0:T(8,128)(2,1)S(1)}, u32[]{:S(2)}, u32[]{:S(2)}) collective-permute-start(bf16[512,128]{1,0:T(8,128)(2,1)S(1)} %get-tuple-element.37.refs_0_), channel_id=1, source_target_pairs={{0,16},{1,9},{2,18},{3,11},{4,20},{5,13},{6,22},{7,15},{8,24},{9,1... | collective-permute-start | bytes 393224 | tf_op jit(solution)/shard_map/ppermute | solution.py:346
  5.6 0.0 collective-permute-start.2
  5.6 0.7 fusion.4
  7.0 3.4 %plan.1 = (s32[8,512]{1,0:T(8,128)S(1)}, bf16[256,128,128]{2,1,0:T(8,128)(2,1)S(1)}) custom-call(s32[1,1]{1,0:T(1,128)S(6)} %copy.10.count_ref, s32[1,256]{1,0:T(1,128)} %bitcast.26, s32[1,256]{1,0:T(1,128)} %bitcast.27, bf16[256,128,128]{2,1,0:T(8,128)(2,1)} %bitcast.24), custom_call_target="tpu_custom_call" | custom-call | tf_op jit(solution)/shard_map/plan/pallas_call | solution.py:314
  10.5 1.4 %collective-permute-done.1.refs_2_ = bf16[512,128]{1,0:T(8,128)(2,1)S(1)} collective-permute-done((bf16[512,128]{1,0:T(8,128)(2,1)S(1)}, bf16[512,128]{1,0:T(8,128)(2,1)S(1)}, u32[]{:S(2)}, u32[]{:S(2)}) %collective-permute-start.1) | collective-permute-done | bytes 131104 | tf_op jit(solution)/shard_map/ppermute | solution.py:346
  11.9 2.3 %odd.2 = (bf16[2064,128]{1,0:T(8,128)(2,1)S(1)}, bf16[2176,128]{1,0:T(8,128)(2,1)S(1)}) custom-call(s32[8,512]{1,0:T(8,128)S(1)} %get-tuple-element.36.plan_ref, bf16[512,128]{1,0:T(8,128)(2,1)S(1)} %get-tuple-element.37.refs_0_, bf16[512,128]{1,0:T(8,128)(2,1)S(1)} %collective-permute-done.refs_1_, bf16[512,128]{1,0:T(8,128)(2,1)S(1)} %collective-permute-done.1.refs_2_, ...), custom_call_target="tpu_custom_call" | custom-call | flops 536870912 | bytes 4194304 | tf_op jit(solution)/shard_map/odd/pallas_call | solution.py:314
  14.2 0.1 collective-permute-start.3
  14.3 1.7 %even0.2.even_ref = f32[1024,128]{1,0:T(8,128)S(1)} custom-call(s32[8,512]{1,0:T(8,128)S(1)} %get-tuple-element.36.plan_ref, bf16[2176,128]{1,0:T(8,128)(2,1)S(1)} %get-tuple-element.40.state, bf16[256,128,128]{2,1,0:T(8,128)(2,1)S(1)} %get-tuple-element.38.refs_4_.weights_ref.refs_8_), custom_call_target="tpu_custom_call" | custom-call | flops 268435456 | bytes 2097152 | tf_op jit(solution)/shard_map/even0/pallas_call | solution.py:314
  16.0 0.1 collective-permute-done.3.other_ref
  16.2 0.1 merge.3
  16.2 1.6 %collective-permute-start.7 = (bf16[256,128]{1,0:T(8,128)(2,1)S(1)}, bf16[256,128]{1,0:T(8,128)(2,1)S(1)}, u32[]{:S(2)}, u32[]{:S(2)}) collective-permute-start(bf16[256,128]{1,0:T(8,128)(2,1)S(1)} %get-tuple-element.48), channel_id=1, source_target_pairs={{0,2},{1,7},{2,0},{3,5},{4,6},{5,3},{6,4},{7,1},{8,10},{9,15},{10,... | collective-permute-start | bytes 196616 | tf_op jit(solution)/shard_map/ppermute | solution.py:336
  17.9 2.6 %collective-permute-start.8 = (bf16[256,128]{1,0:T(8,128)(2,1)S(1)}, bf16[256,128]{1,0:T(8,128)(2,1)S(1)}, u32[]{:S(2)}, u32[]{:S(2)}) collective-permute-start(bf16[256,128]{1,0:T(8,128)(2,1)S(1)} %get-tuple-element.49), channel_id=1, source_target_pairs={{0,4},{1,5},{2,6},{3,7},{4,0},{5,1},{6,2},{7,3},{8,12},{9,13},{10,... | collective-permute-start | bytes 196616 | tf_op jit(solution)/shard_map/ppermute | solution.py:336
  20.5 0.2 collective-permute-start.9
  20.7 1.8 %even1.2 = (f32[256,128]{1,0:T(8,128)S(1)}, bf16[272,128]{1,0:T(8,128)(2,1)S(1)}, bf16[272,128]{1,0:T(8,128)(2,1)S(1)}, bf16[272,128]{1,0:T(8,128)(2,1)S(1)}) custom-call(s32[8,512]{1,0:T(8,128)S(1)} %get-tuple-element.36.plan_ref, bf16[2176,128]{1,0:T(8,128)(2,1)S(1)} %get-tuple-element.40.state, ...), custom_call_target="tpu_custom_call" | custom-call | flops 268435456 | bytes 2097152 | tf_op jit(solution)/shard_map/even1/pallas_call | solution.py:314
  22.5 0.7 collective-permute-start.4
  23.2 3.5 %collective-permute-start.5 = (bf16[272,128]{1,0:T(8,128)(2,1)S(1)}, bf16[272,128]{1,0:T(8,128)(2,1)S(1)}, u32[]{:S(2)}, u32[]{:S(2)}) collective-permute-start(bf16[272,128]{1,0:T(8,128)(2,1)S(1)} %get-tuple-element.43), channel_id=1, source_target_pairs={{0,4},{1,5},{2,6},{3,7},{4,0},{5,1},{6,2},{7,3},{8,12},{9,13},{10,... | collective-permute-start | bytes 208904 | tf_op jit(solution)/shard_map/ppermute | solution.py:336
  26.7 0.2 collective-permute-start.6
  27.0 0.1 collective-permute-done.9.refs_2_
  27.1 1.9 %collective-permute-start.13 = (bf16[256,128]{1,0:T(8,128)(2,1)S(1)}, bf16[256,128]{1,0:T(8,128)(2,1)S(1)}, u32[]{:S(2)}, u32[]{:S(2)}) collective-permute-start(bf16[256,128]{1,0:T(8,128)(2,1)S(1)} %state.4.refs_3_.refs_4_), channel_id=1, source_target_pairs={{0,8},{1,17},{2,10},{3,19},{4,12},{5,21},{6,14},{7,23},{8,0},{9,25... | collective-permute-start | bytes 196616 | tf_op jit(solution)/shard_map/ppermute | solution.py:346
  29.0 2.2 %collective-permute-start.14 = (bf16[256,128]{1,0:T(8,128)(2,1)S(1)}, bf16[256,128]{1,0:T(8,128)(2,1)S(1)}, u32[]{:S(2)}, u32[]{:S(2)}) collective-permute-start(bf16[256,128]{1,0:T(8,128)(2,1)S(1)} %state.4.refs_3_.refs_4_), channel_id=1, source_target_pairs={{0,16},{1,9},{2,18},{3,11},{4,20},{5,13},{6,22},{7,15},{8,24},{9,1... | collective-permute-start | bytes 196616 | tf_op jit(solution)/shard_map/ppermute | solution.py:346
  31.2 1.6 %collective-permute-done.6.refs_2_ = bf16[272,128]{1,0:T(8,128)(2,1)S(1)} collective-permute-done((bf16[272,128]{1,0:T(8,128)(2,1)S(1)}, bf16[272,128]{1,0:T(8,128)(2,1)S(1)}, u32[]{:S(2)}, u32[]{:S(2)}) %collective-permute-start.6) | collective-permute-done | bytes 69664 | tf_op jit(solution)/shard_map/ppermute | solution.py:336
  32.9 1.4 %collective-permute-start.10 = (bf16[256,128]{1,0:T(8,128)(2,1)S(1)}, bf16[256,128]{1,0:T(8,128)(2,1)S(1)}, u32[]{:S(2)}, u32[]{:S(2)}) collective-permute-start(bf16[256,128]{1,0:T(8,128)(2,1)S(1)} %state.5.refs_0_), channel_id=1, source_target_pairs={{0,8},{1,17},{2,10},{3,19},{4,12},{5,21},{6,14},{7,23},{8,0},{9,25... | collective-permute-start | bytes 196616 | tf_op jit(solution)/shard_map/ppermute | solution.py:346
  34.3 2.0 %collective-permute-start.11 = (bf16[256,128]{1,0:T(8,128)(2,1)S(1)}, bf16[256,128]{1,0:T(8,128)(2,1)S(1)}, u32[]{:S(2)}, u32[]{:S(2)}) collective-permute-start(bf16[256,128]{1,0:T(8,128)(2,1)S(1)} %state.5.refs_0_), channel_id=1, source_target_pairs={{0,16},{1,9},{2,18},{3,11},{4,20},{5,13},{6,22},{7,15},{8,24},{9,1... | collective-permute-start | bytes 196616 | tf_op jit(solution)/shard_map/ppermute | solution.py:346
  36.3 0.2 collective-permute-start.12
  36.5 1.0 %collective-permute-done.10.refs_1_ = bf16[256,128]{1,0:T(8,128)(2,1)S(1)} collective-permute-done((bf16[256,128]{1,0:T(8,128)(2,1)S(1)}, bf16[256,128]{1,0:T(8,128)(2,1)S(1)}, u32[]{:S(2)}, u32[]{:S(2)}) %collective-permute-start.10) | collective-permute-done | bytes 65568 | tf_op jit(solution)/shard_map/ppermute | solution.py:346
  37.5 1.7 %collective-permute-done.11.refs_2_ = bf16[256,128]{1,0:T(8,128)(2,1)S(1)} collective-permute-done((bf16[256,128]{1,0:T(8,128)(2,1)S(1)}, bf16[256,128]{1,0:T(8,128)(2,1)S(1)}, u32[]{:S(2)}, u32[]{:S(2)}) %collective-permute-start.11) | collective-permute-done | bytes 65568 | tf_op jit(solution)/shard_map/ppermute | solution.py:346
  39.2 2.2 %collective-permute-done.12.refs_3_ = bf16[256,128]{1,0:T(8,128)(2,1)S(1)} collective-permute-done((bf16[256,128]{1,0:T(8,128)(2,1)S(1)}, bf16[256,128]{1,0:T(8,128)(2,1)S(1)}, u32[]{:S(2)}, u32[]{:S(2)}) %collective-permute-start.12) | collective-permute-done | bytes 65568 | tf_op jit(solution)/shard_map/ppermute | solution.py:346
  41.4 2.3 %odd.3 = (bf16[2064,128]{1,0:T(8,128)(2,1)S(1)}, bf16[2176,128]{1,0:T(8,128)(2,1)S(1)}) custom-call(s32[8,512]{1,0:T(8,128)S(1)} %get-tuple-element.36.plan_ref, bf16[256,128]{1,0:T(8,128)(2,1)S(1)} %state.5.refs_0_, bf16[256,128]{1,0:T(8,128)(2,1)S(1)} %collective-permute-done.10.refs_1_, bf16[256,128]{1,0:T(8,128)(2,1)S(1)} %collective-permute-done.11.refs_2_, ...), custom_call_target="tpu_custom_call" | custom-call | flops 536870912 | bytes 4194304 | tf_op jit(solution)/shard_map/odd/pallas_call | solution.py:314
  43.8 0.1 collective-permute-start.16
  43.8 1.7 %even0.3.even_ref = f32[1024,128]{1,0:T(8,128)S(1)} custom-call(s32[8,512]{1,0:T(8,128)S(1)} %get-tuple-element.36.plan_ref, bf16[2176,128]{1,0:T(8,128)(2,1)S(1)} %get-tuple-element.51.state, bf16[256,128,128]{2,1,0:T(8,128)(2,1)S(1)} %get-tuple-element.38.refs_4_.weights_ref.refs_8_), custom_call_target="tpu_custom_call" | custom-call | flops 268435456 | bytes 2097152 | tf_op jit(solution)/shard_map/even0/pallas_call | solution.py:314
  45.6 0.1 collective-permute-done.16.other_ref
  45.7 0.1 merge.4
  45.8 0.8 collective-permute-start.20
  46.6 1.4 %collective-permute-start.21 = (bf16[256,128]{1,0:T(8,128)(2,1)S(1)}, bf16[256,128]{1,0:T(8,128)(2,1)S(1)}, u32[]{:S(2)}, u32[]{:S(2)}) collective-permute-start(bf16[256,128]{1,0:T(8,128)(2,1)S(1)} %get-tuple-element.59), channel_id=1, source_target_pairs={{0,4},{1,5},{2,6},{3,7},{4,0},{5,1},{6,2},{7,3},{8,12},{9,13},{10,... | collective-permute-start | bytes 196616 | tf_op jit(solution)/shard_map/ppermute | solution.py:336
  48.1 2.2 %collective-permute-start.22 = (bf16[256,128]{1,0:T(8,128)(2,1)S(1)}, bf16[256,128]{1,0:T(8,128)(2,1)S(1)}, u32[]{:S(2)}, u32[]{:S(2)}) collective-permute-start(bf16[256,128]{1,0:T(8,128)(2,1)S(1)} %get-tuple-element.60), channel_id=1, source_target_pairs={{0,6},{1,3},{2,4},{3,1},{4,2},{5,7},{6,0},{7,5},{8,14},{9,11},{10,... | collective-permute-start | bytes 196616 | tf_op jit(solution)/shard_map/ppermute | solution.py:336
  50.3 1.8 %even1.3 = (f32[256,128]{1,0:T(8,128)S(1)}, bf16[272,128]{1,0:T(8,128)(2,1)S(1)}, bf16[272,128]{1,0:T(8,128)(2,1)S(1)}, bf16[272,128]{1,0:T(8,128)(2,1)S(1)}) custom-call(s32[8,512]{1,0:T(8,128)S(1)} %get-tuple-element.36.plan_ref, bf16[2176,128]{1,0:T(8,128)(2,1)S(1)} %get-tuple-element.51.state, ...), custom_call_target="tpu_custom_call" | custom-call | flops 268435456 | bytes 2097152 | tf_op jit(solution)/shard_map/even1/pallas_call | solution.py:314
  52.1 0.1 collective-permute-start.17
  52.2 2.2 %collective-permute-start.18 = (bf16[272,128]{1,0:T(8,128)(2,1)S(1)}, bf16[272,128]{1,0:T(8,128)(2,1)S(1)}, u32[]{:S(2)}, u32[]{:S(2)}) collective-permute-start(bf16[272,128]{1,0:T(8,128)(2,1)S(1)} %get-tuple-element.56), channel_id=1, source_target_pairs={{0,4},{1,5},{2,6},{3,7},{4,0},{5,1},{6,2},{7,3},{8,12},{9,13},{10,... | collective-permute-start | bytes 208904 | tf_op jit(solution)/shard_map/ppermute | solution.py:336
  54.4 2.2 %collective-permute-start.19 = (bf16[272,128]{1,0:T(8,128)(2,1)S(1)}, bf16[272,128]{1,0:T(8,128)(2,1)S(1)}, u32[]{:S(2)}, u32[]{:S(2)}) collective-permute-start(bf16[272,128]{1,0:T(8,128)(2,1)S(1)} %get-tuple-element.57), channel_id=1, source_target_pairs={{0,6},{1,3},{2,4},{3,1},{4,2},{5,7},{6,0},{7,5},{8,14},{9,11},{10,... | collective-permute-start | bytes 208904 | tf_op jit(solution)/shard_map/ppermute | solution.py:336
  56.6 0.9 %collective-permute-start.26 = (bf16[256,128]{1,0:T(8,128)(2,1)S(1)}, bf16[256,128]{1,0:T(8,128)(2,1)S(1)}, u32[]{:S(2)}, u32[]{:S(2)}) collective-permute-start(bf16[256,128]{1,0:T(8,128)(2,1)S(1)} %state.6.refs_3_.refs_4_), channel_id=1, source_target_pairs={{0,8},{1,17},{2,10},{3,19},{4,12},{5,21},{6,14},{7,23},{8,0},{9,25... | collective-permute-start | bytes 196616 | tf_op jit(solution)/shard_map/ppermute | solution.py:346
  57.5 1.3 %collective-permute-start.27 = (bf16[256,128]{1,0:T(8,128)(2,1)S(1)}, bf16[256,128]{1,0:T(8,128)(2,1)S(1)}, u32[]{:S(2)}, u32[]{:S(2)}) collective-permute-start(bf16[256,128]{1,0:T(8,128)(2,1)S(1)} %state.6.refs_3_.refs_4_), channel_id=1, source_target_pairs={{0,16},{1,9},{2,18},{3,11},{4,20},{5,13},{6,22},{7,15},{8,24},{9,1... | collective-permute-start | bytes 196616 | tf_op jit(solution)/shard_map/ppermute | solution.py:346
  58.8 1.3 %collective-permute-start.28 = (bf16[256,128]{1,0:T(8,128)(2,1)S(1)}, bf16[256,128]{1,0:T(8,128)(2,1)S(1)}, u32[]{:S(2)}, u32[]{:S(2)}) collective-permute-start(bf16[256,128]{1,0:T(8,128)(2,1)S(1)} %state.6.refs_3_.refs_4_), channel_id=1, source_target_pairs={{0,24},{1,25},{2,26},{3,27},{4,28},{5,29},{6,30},{7,31},{8,16},{9,... | collective-permute-start | bytes 196616 | tf_op jit(solution)/shard_map/ppermute | solution.py:346
  60.2 0.6 collective-permute-done.18.refs_1_
  60.9 1.3 %collective-permute-start.23 = (bf16[256,128]{1,0:T(8,128)(2,1)S(1)}, bf16[256,128]{1,0:T(8,128)(2,1)S(1)}, u32[]{:S(2)}, u32[]{:S(2)}) collective-permute-start(bf16[256,128]{1,0:T(8,128)(2,1)S(1)} %state.7.refs_0_), channel_id=1, source_target_pairs={{0,8},{1,17},{2,10},{3,19},{4,12},{5,21},{6,14},{7,23},{8,0},{9,25... | collective-permute-start | bytes 196616 | tf_op jit(solution)/shard_map/ppermute | solution.py:346
  62.1 0.7 collective-permute-start.24
  62.9 1.5 %collective-permute-start.25 = (bf16[256,128]{1,0:T(8,128)(2,1)S(1)}, bf16[256,128]{1,0:T(8,128)(2,1)S(1)}, u32[]{:S(2)}, u32[]{:S(2)}) collective-permute-start(bf16[256,128]{1,0:T(8,128)(2,1)S(1)} %state.7.refs_0_), channel_id=1, source_target_pairs={{0,24},{1,25},{2,26},{3,27},{4,28},{5,29},{6,30},{7,31},{8,16},{9,... | collective-permute-start | bytes 196616 | tf_op jit(solution)/shard_map/ppermute | solution.py:346
  64.4 0.1 place.1.place_ref
  64.6 0.9 %collective-permute-done.23.refs_1_ = bf16[256,128]{1,0:T(8,128)(2,1)S(1)} collective-permute-done((bf16[256,128]{1,0:T(8,128)(2,1)S(1)}, bf16[256,128]{1,0:T(8,128)(2,1)S(1)}, u32[]{:S(2)}, u32[]{:S(2)}) %collective-permute-start.23) | collective-permute-done | bytes 65568 | tf_op jit(solution)/shard_map/ppermute | solution.py:346
  65.5 1.6 %collective-permute-done.24.refs_2_ = bf16[256,128]{1,0:T(8,128)(2,1)S(1)} collective-permute-done((bf16[256,128]{1,0:T(8,128)(2,1)S(1)}, bf16[256,128]{1,0:T(8,128)(2,1)S(1)}, u32[]{:S(2)}, u32[]{:S(2)}) %collective-permute-start.24) | collective-permute-done | bytes 65568 | tf_op jit(solution)/shard_map/ppermute | solution.py:346
  67.1 0.9 %collective-permute-done.25.refs_3_ = bf16[256,128]{1,0:T(8,128)(2,1)S(1)} collective-permute-done((bf16[256,128]{1,0:T(8,128)(2,1)S(1)}, bf16[256,128]{1,0:T(8,128)(2,1)S(1)}, u32[]{:S(2)}, u32[]{:S(2)}) %collective-permute-start.25) | collective-permute-done | bytes 65568 | tf_op jit(solution)/shard_map/ppermute | solution.py:346
  68.0 5.4 %last.1 = (bf16[1024,128]{1,0:T(8,128)(2,1)S(1)}, f32[4096,128]{1,0:T(8,128)S(1)}) custom-call(s32[8,512]{1,0:T(8,128)S(1)} %get-tuple-element.36.plan_ref, s32[1,2048]{1,0:T(1,128)S(1)} %place.1.place_ref, bf16[256,128]{1,0:T(8,128)(2,1)S(1)} %state.7.refs_0_, bf16[256,128]{1,0:T(8,128)(2,1)S(1)} %collective-permute-done.23.refs_1_, ...), custom_call_target="tpu_custom_call" | custom-call | flops 1073741824 | bytes 8388608 | tf_op jit(solution)/shard_map/last/pallas_call | solution.py:314
  73.4 0.1 collective-permute-start.29
  73.5 1.7 %pick.1.even_ref = f32[1024,128]{1,0:T(8,128)S(1)} custom-call(s32[1,2048]{1,0:T(1,128)S(1)} %place.1.place_ref, f32[4096,128]{1,0:T(8,128)S(1)} %get-tuple-element.61.total), custom_call_target="tpu_custom_call" | custom-call | flops 214748368 | bytes 1677721 | tf_op jit(solution)/shard_map/pick/pallas_call | solution.py:314
  75.3 0.1 merge.5
  75.4 2.2 %collective-permute-start.32 = (bf16[256,128]{1,0:T(8,128)(2,1)S(1)}, bf16[256,128]{1,0:T(8,128)(2,1)S(1)}, u32[]{:S(2)}, u32[]{:S(2)}) collective-permute-start(bf16[256,128]{1,0:T(8,128)(2,1)S(1)} %get-tuple-element.66), channel_id=1, source_target_pairs={{0,6},{1,3},{2,4},{3,1},{4,2},{5,7},{6,0},{7,5},{8,14},{9,11},{10,... | collective-permute-start | bytes 196616 | tf_op jit(solution)/shard_map/ppermute | solution.py:336
  77.6 0.6 collective-permute-start.31
  78.2 1.6 %collective-permute-start.30 = (bf16[256,128]{1,0:T(8,128)(2,1)S(1)}, bf16[256,128]{1,0:T(8,128)(2,1)S(1)}, u32[]{:S(2)}, u32[]{:S(2)}) collective-permute-start(bf16[256,128]{1,0:T(8,128)(2,1)S(1)} %get-tuple-element.64), channel_id=1, source_target_pairs={{0,2},{1,7},{2,0},{3,5},{4,6},{5,3},{6,4},{7,1},{8,10},{9,15},{10,... | collective-permute-start | bytes 196616 | tf_op jit(solution)/shard_map/ppermute | solution.py:336
  79.8 0.1 select_reduce_fusion
  79.9 2.3 %collective-permute-done.32 = bf16[256,128]{1,0:T(8,128)(2,1)S(1)} collective-permute-done((bf16[256,128]{1,0:T(8,128)(2,1)S(1)}, bf16[256,128]{1,0:T(8,128)(2,1)S(1)}, u32[]{:S(2)}, u32[]{:S(2)}) %collective-permute-start.32) | collective-permute-done | bytes 65568 | tf_op jit(solution)/shard_map/ppermute | solution.py:336
  82.2 2.7 %collective-permute-done.31 = bf16[256,128]{1,0:T(8,128)(2,1)S(1)} collective-permute-done((bf16[256,128]{1,0:T(8,128)(2,1)S(1)}, bf16[256,128]{1,0:T(8,128)(2,1)S(1)}, u32[]{:S(2)}, u32[]{:S(2)}) %collective-permute-start.31) | collective-permute-done | bytes 65568 | tf_op jit(solution)/shard_map/ppermute | solution.py:336
  84.9 0.1 multiply_reduce_fusion
  85.0 0.8 multiply_multiply_fusion
  (30 shorter events, 0.3 us)
Async XLA Ops:
  1.1 9.4 %collective-permute-start = (bf16[512,128]{1,0:T(8,128)(2,1)S(1)}, bf16[512,128]{1,0:T(8,128)(2,1)S(1)}, u32[]{:S(2)}, u32[]{:S(2)}) collective-permute-start(bf16[512,128]{1,0:T(8,128)(2,1)S(1)} %get-tuple-element.37.refs_0_), channel_id=1, source_target_pairs={{0,8},{1,17},{2,10},{3,19},{4,12},{5,21},{6,14},{7,23},{8,0},{9,25... | collective-permute-start | bytes 393224 | tf_op jit(solution)/shard_map/ppermute | solution.py:346
  4.1 7.8 %collective-permute-start.1 = (bf16[512,128]{1,0:T(8,128)(2,1)S(1)}, bf16[512,128]{1,0:T(8,128)(2,1)S(1)}, u32[]{:S(2)}, u32[]{:S(2)}) collective-permute-start(bf16[512,128]{1,0:T(8,128)(2,1)S(1)} %get-tuple-element.37.refs_0_), channel_id=1, source_target_pairs={{0,16},{1,9},{2,18},{3,11},{4,20},{5,13},{6,22},{7,15},{8,24},{9,1... | collective-permute-start | bytes 393224 | tf_op jit(solution)/shard_map/ppermute | solution.py:346
  5.6 6.3 %collective-permute-start.2 = (bf16[512,128]{1,0:T(8,128)(2,1)S(1)}, bf16[512,128]{1,0:T(8,128)(2,1)S(1)}, u32[]{:S(2)}, u32[]{:S(2)}) collective-permute-start(bf16[512,128]{1,0:T(8,128)(2,1)S(1)} %get-tuple-element.37.refs_0_), channel_id=1, source_target_pairs={{0,24},{1,25},{2,26},{3,27},{4,28},{5,29},{6,30},{7,31},{8,16},{9,... | collective-permute-start | bytes 393224 | tf_op jit(solution)/shard_map/ppermute | solution.py:346
  14.2 2.0 %collective-permute-start.3 = (bf16[2064,128]{1,0:T(8,128)(2,1)S(1)}, bf16[2064,128]{1,0:T(8,128)(2,1)S(1)}, u32[]{:S(2)}, u32[]{:S(2)}) collective-permute-start(bf16[2064,128]{1,0:T(8,128)(2,1)S(1)} %get-tuple-element.39), channel_id=1, source_target_pairs={{0,1},{1,0},{2,3},{3,2},{4,5},{5,4},{6,7},{7,6},{8,9},{9,8},{10,11... | collective-permute-start | bytes 1585160 | tf_op jit(solution)/shard_map/ppermute | solution.py:330
  16.2 10.5 %collective-permute-start.7 = (bf16[256,128]{1,0:T(8,128)(2,1)S(1)}, bf16[256,128]{1,0:T(8,128)(2,1)S(1)}, u32[]{:S(2)}, u32[]{:S(2)}) collective-permute-start(bf16[256,128]{1,0:T(8,128)(2,1)S(1)} %get-tuple-element.48), channel_id=1, source_target_pairs={{0,2},{1,7},{2,0},{3,5},{4,6},{5,3},{6,4},{7,1},{8,10},{9,15},{10,... | collective-permute-start | bytes 196616 | tf_op jit(solution)/shard_map/ppermute | solution.py:336
  17.9 9.1 %collective-permute-start.8 = (bf16[256,128]{1,0:T(8,128)(2,1)S(1)}, bf16[256,128]{1,0:T(8,128)(2,1)S(1)}, u32[]{:S(2)}, u32[]{:S(2)}) collective-permute-start(bf16[256,128]{1,0:T(8,128)(2,1)S(1)} %get-tuple-element.49), channel_id=1, source_target_pairs={{0,4},{1,5},{2,6},{3,7},{4,0},{5,1},{6,2},{7,3},{8,12},{9,13},{10,... | collective-permute-start | bytes 196616 | tf_op jit(solution)/shard_map/ppermute | solution.py:336
  20.5 6.6 %collective-permute-start.9 = (bf16[256,128]{1,0:T(8,128)(2,1)S(1)}, bf16[256,128]{1,0:T(8,128)(2,1)S(1)}, u32[]{:S(2)}, u32[]{:S(2)}) collective-permute-start(bf16[256,128]{1,0:T(8,128)(2,1)S(1)} %get-tuple-element.50), channel_id=1, source_target_pairs={{0,6},{1,3},{2,4},{3,1},{4,2},{5,7},{6,0},{7,5},{8,14},{9,11},{10,... | collective-permute-start | bytes 196616 | tf_op jit(solution)/shard_map/ppermute | solution.py:336
  22.5 8.7 %collective-permute-start.4 = (bf16[272,128]{1,0:T(8,128)(2,1)S(1)}, bf16[272,128]{1,0:T(8,128)(2,1)S(1)}, u32[]{:S(2)}, u32[]{:S(2)}) collective-permute-start(bf16[272,128]{1,0:T(8,128)(2,1)S(1)} %get-tuple-element.42), channel_id=1, source_target_pairs={{0,2},{1,7},{2,0},{3,5},{4,6},{5,3},{6,4},{7,1},{8,10},{9,15},{10,... | collective-permute-start | bytes 208904 | tf_op jit(solution)/shard_map/ppermute | solution.py:336
  23.2 7.9 %collective-permute-start.5 = (bf16[272,128]{1,0:T(8,128)(2,1)S(1)}, bf16[272,128]{1,0:T(8,128)(2,1)S(1)}, u32[]{:S(2)}, u32[]{:S(2)}) collective-permute-start(bf16[272,128]{1,0:T(8,128)(2,1)S(1)} %get-tuple-element.43), channel_id=1, source_target_pairs={{0,4},{1,5},{2,6},{3,7},{4,0},{5,1},{6,2},{7,3},{8,12},{9,13},{10,... | collective-permute-start | bytes 208904 | tf_op jit(solution)/shard_map/ppermute | solution.py:336
  26.7 6.1 %collective-permute-start.6 = (bf16[272,128]{1,0:T(8,128)(2,1)S(1)}, bf16[272,128]{1,0:T(8,128)(2,1)S(1)}, u32[]{:S(2)}, u32[]{:S(2)}) collective-permute-start(bf16[272,128]{1,0:T(8,128)(2,1)S(1)} %get-tuple-element.44), channel_id=1, source_target_pairs={{0,6},{1,3},{2,4},{3,1},{4,2},{5,7},{6,0},{7,5},{8,14},{9,11},{10,... | collective-permute-start | bytes 208904 | tf_op jit(solution)/shard_map/ppermute | solution.py:336
  27.1 9.2 %collective-permute-start.13 = (bf16[256,128]{1,0:T(8,128)(2,1)S(1)}, bf16[256,128]{1,0:T(8,128)(2,1)S(1)}, u32[]{:S(2)}, u32[]{:S(2)}) collective-permute-start(bf16[256,128]{1,0:T(8,128)(2,1)S(1)} %state.4.refs_3_.refs_4_), channel_id=1, source_target_pairs={{0,8},{1,17},{2,10},{3,19},{4,12},{5,21},{6,14},{7,23},{8,0},{9,25... | collective-permute-start | bytes 196616 | tf_op jit(solution)/shard_map/ppermute | solution.py:346
  29.0 7.5 %collective-permute-start.14 = (bf16[256,128]{1,0:T(8,128)(2,1)S(1)}, bf16[256,128]{1,0:T(8,128)(2,1)S(1)}, u32[]{:S(2)}, u32[]{:S(2)}) collective-permute-start(bf16[256,128]{1,0:T(8,128)(2,1)S(1)} %state.4.refs_3_.refs_4_), channel_id=1, source_target_pairs={{0,16},{1,9},{2,18},{3,11},{4,20},{5,13},{6,22},{7,15},{8,24},{9,1... | collective-permute-start | bytes 196616 | tf_op jit(solution)/shard_map/ppermute | solution.py:346
  31.2 5.3 %collective-permute-start.15 = (bf16[256,128]{1,0:T(8,128)(2,1)S(1)}, bf16[256,128]{1,0:T(8,128)(2,1)S(1)}, u32[]{:S(2)}, u32[]{:S(2)}) collective-permute-start(bf16[256,128]{1,0:T(8,128)(2,1)S(1)} %state.4.refs_3_.refs_4_), channel_id=1, source_target_pairs={{0,24},{1,25},{2,26},{3,27},{4,28},{5,29},{6,30},{7,31},{8,16},{9,... | collective-permute-start | bytes 196616 | tf_op jit(solution)/shard_map/ppermute | solution.py:346
  32.9 4.6 %collective-permute-start.10 = (bf16[256,128]{1,0:T(8,128)(2,1)S(1)}, bf16[256,128]{1,0:T(8,128)(2,1)S(1)}, u32[]{:S(2)}, u32[]{:S(2)}) collective-permute-start(bf16[256,128]{1,0:T(8,128)(2,1)S(1)} %state.5.refs_0_), channel_id=1, source_target_pairs={{0,8},{1,17},{2,10},{3,19},{4,12},{5,21},{6,14},{7,23},{8,0},{9,25... | collective-permute-start | bytes 196616 | tf_op jit(solution)/shard_map/ppermute | solution.py:346
  34.3 5.0 %collective-permute-start.11 = (bf16[256,128]{1,0:T(8,128)(2,1)S(1)}, bf16[256,128]{1,0:T(8,128)(2,1)S(1)}, u32[]{:S(2)}, u32[]{:S(2)}) collective-permute-start(bf16[256,128]{1,0:T(8,128)(2,1)S(1)} %state.5.refs_0_), channel_id=1, source_target_pairs={{0,16},{1,9},{2,18},{3,11},{4,20},{5,13},{6,22},{7,15},{8,24},{9,1... | collective-permute-start | bytes 196616 | tf_op jit(solution)/shard_map/ppermute | solution.py:346
  36.3 5.2 %collective-permute-start.12 = (bf16[256,128]{1,0:T(8,128)(2,1)S(1)}, bf16[256,128]{1,0:T(8,128)(2,1)S(1)}, u32[]{:S(2)}, u32[]{:S(2)}) collective-permute-start(bf16[256,128]{1,0:T(8,128)(2,1)S(1)} %state.5.refs_0_), channel_id=1, source_target_pairs={{0,24},{1,25},{2,26},{3,27},{4,28},{5,29},{6,30},{7,31},{8,16},{9,... | collective-permute-start | bytes 196616 | tf_op jit(solution)/shard_map/ppermute | solution.py:346
  43.8 2.0 %collective-permute-start.16 = (bf16[2064,128]{1,0:T(8,128)(2,1)S(1)}, bf16[2064,128]{1,0:T(8,128)(2,1)S(1)}, u32[]{:S(2)}, u32[]{:S(2)}) collective-permute-start(bf16[2064,128]{1,0:T(8,128)(2,1)S(1)} %get-tuple-element.52), channel_id=1, source_target_pairs={{0,1},{1,0},{2,3},{3,2},{4,5},{5,4},{6,7},{7,6},{8,9},{9,8},{10,11... | collective-permute-start | bytes 1585160 | tf_op jit(solution)/shard_map/ppermute | solution.py:330
  45.8 8.5 %collective-permute-start.20 = (bf16[256,128]{1,0:T(8,128)(2,1)S(1)}, bf16[256,128]{1,0:T(8,128)(2,1)S(1)}, u32[]{:S(2)}, u32[]{:S(2)}) collective-permute-start(bf16[256,128]{1,0:T(8,128)(2,1)S(1)} %get-tuple-element.58), channel_id=1, source_target_pairs={{0,2},{1,7},{2,0},{3,5},{4,6},{5,3},{6,4},{7,1},{8,10},{9,15},{10,... | collective-permute-start | bytes 196616 | tf_op jit(solution)/shard_map/ppermute | solution.py:336
  46.6 9.9 %collective-permute-start.21 = (bf16[256,128]{1,0:T(8,128)(2,1)S(1)}, bf16[256,128]{1,0:T(8,128)(2,1)S(1)}, u32[]{:S(2)}, u32[]{:S(2)}) collective-permute-start(bf16[256,128]{1,0:T(8,128)(2,1)S(1)} %get-tuple-element.59), channel_id=1, source_target_pairs={{0,4},{1,5},{2,6},{3,7},{4,0},{5,1},{6,2},{7,3},{8,12},{9,13},{10,... | collective-permute-start | bytes 196616 | tf_op jit(solution)/shard_map/ppermute | solution.py:336
  48.1 8.5 %collective-permute-start.22 = (bf16[256,128]{1,0:T(8,128)(2,1)S(1)}, bf16[256,128]{1,0:T(8,128)(2,1)S(1)}, u32[]{:S(2)}, u32[]{:S(2)}) collective-permute-start(bf16[256,128]{1,0:T(8,128)(2,1)S(1)} %get-tuple-element.60), channel_id=1, source_target_pairs={{0,6},{1,3},{2,4},{3,1},{4,2},{5,7},{6,0},{7,5},{8,14},{9,11},{10,... | collective-permute-start | bytes 196616 | tf_op jit(solution)/shard_map/ppermute | solution.py:336
  52.1 27.8 %copy-start = (s32[256]{0:T(256)S(1)}, s32[256]{0:T(256)}, u32[]{:S(2)}) copy-start(s32[256]{0:T(256)} %param.16) | copy-start | bytes 3076
  52.1 27.7 %copy-start.1 = (f32[16]{0:T(128)S(1)}, f32[16]{0:T(128)}, u32[]{:S(2)}) copy-start(f32[16]{0:T(128)} %param.17) | copy-start | bytes 196
  52.1 6.7 %collective-permute-start.17 = (bf16[272,128]{1,0:T(8,128)(2,1)S(1)}, bf16[272,128]{1,0:T(8,128)(2,1)S(1)}, u32[]{:S(2)}, u32[]{:S(2)}) collective-permute-start(bf16[272,128]{1,0:T(8,128)(2,1)S(1)} %get-tuple-element.55), channel_id=1, source_target_pairs={{0,2},{1,7},{2,0},{3,5},{4,6},{5,3},{6,4},{7,1},{8,10},{9,15},{10,... | collective-permute-start | bytes 208904 | tf_op jit(solution)/shard_map/ppermute | solution.py:336
  52.2 8.6 %collective-permute-start.18 = (bf16[272,128]{1,0:T(8,128)(2,1)S(1)}, bf16[272,128]{1,0:T(8,128)(2,1)S(1)}, u32[]{:S(2)}, u32[]{:S(2)}) collective-permute-start(bf16[272,128]{1,0:T(8,128)(2,1)S(1)} %get-tuple-element.56), channel_id=1, source_target_pairs={{0,4},{1,5},{2,6},{3,7},{4,0},{5,1},{6,2},{7,3},{8,12},{9,13},{10,... | collective-permute-start | bytes 208904 | tf_op jit(solution)/shard_map/ppermute | solution.py:336
  54.4 6.5 %collective-permute-start.19 = (bf16[272,128]{1,0:T(8,128)(2,1)S(1)}, bf16[272,128]{1,0:T(8,128)(2,1)S(1)}, u32[]{:S(2)}, u32[]{:S(2)}) collective-permute-start(bf16[272,128]{1,0:T(8,128)(2,1)S(1)} %get-tuple-element.57), channel_id=1, source_target_pairs={{0,6},{1,3},{2,4},{3,1},{4,2},{5,7},{6,0},{7,5},{8,14},{9,11},{10,... | collective-permute-start | bytes 208904 | tf_op jit(solution)/shard_map/ppermute | solution.py:336
  56.6 6.3 %collective-permute-start.26 = (bf16[256,128]{1,0:T(8,128)(2,1)S(1)}, bf16[256,128]{1,0:T(8,128)(2,1)S(1)}, u32[]{:S(2)}, u32[]{:S(2)}) collective-permute-start(bf16[256,128]{1,0:T(8,128)(2,1)S(1)} %state.6.refs_3_.refs_4_), channel_id=1, source_target_pairs={{0,8},{1,17},{2,10},{3,19},{4,12},{5,21},{6,14},{7,23},{8,0},{9,25... | collective-permute-start | bytes 196616 | tf_op jit(solution)/shard_map/ppermute | solution.py:346
  57.5 7.0 %collective-permute-start.27 = (bf16[256,128]{1,0:T(8,128)(2,1)S(1)}, bf16[256,128]{1,0:T(8,128)(2,1)S(1)}, u32[]{:S(2)}, u32[]{:S(2)}) collective-permute-start(bf16[256,128]{1,0:T(8,128)(2,1)S(1)} %state.6.refs_3_.refs_4_), channel_id=1, source_target_pairs={{0,16},{1,9},{2,18},{3,11},{4,20},{5,13},{6,22},{7,15},{8,24},{9,1... | collective-permute-start | bytes 196616 | tf_op jit(solution)/shard_map/ppermute | solution.py:346
  58.8 5.7 %collective-permute-start.28 = (bf16[256,128]{1,0:T(8,128)(2,1)S(1)}, bf16[256,128]{1,0:T(8,128)(2,1)S(1)}, u32[]{:S(2)}, u32[]{:S(2)}) collective-permute-start(bf16[256,128]{1,0:T(8,128)(2,1)S(1)} %state.6.refs_3_.refs_4_), channel_id=1, source_target_pairs={{0,24},{1,25},{2,26},{3,27},{4,28},{5,29},{6,30},{7,31},{8,16},{9,... | collective-permute-start | bytes 196616 | tf_op jit(solution)/shard_map/ppermute | solution.py:346
  60.9 4.6 %collective-permute-start.23 = (bf16[256,128]{1,0:T(8,128)(2,1)S(1)}, bf16[256,128]{1,0:T(8,128)(2,1)S(1)}, u32[]{:S(2)}, u32[]{:S(2)}) collective-permute-start(bf16[256,128]{1,0:T(8,128)(2,1)S(1)} %state.7.refs_0_), channel_id=1, source_target_pairs={{0,8},{1,17},{2,10},{3,19},{4,12},{5,21},{6,14},{7,23},{8,0},{9,25... | collective-permute-start | bytes 196616 | tf_op jit(solution)/shard_map/ppermute | solution.py:346
  62.1 5.0 %collective-permute-start.24 = (bf16[256,128]{1,0:T(8,128)(2,1)S(1)}, bf16[256,128]{1,0:T(8,128)(2,1)S(1)}, u32[]{:S(2)}, u32[]{:S(2)}) collective-permute-start(bf16[256,128]{1,0:T(8,128)(2,1)S(1)} %state.7.refs_0_), channel_id=1, source_target_pairs={{0,16},{1,9},{2,18},{3,11},{4,20},{5,13},{6,22},{7,15},{8,24},{9,1... | collective-permute-start | bytes 196616 | tf_op jit(solution)/shard_map/ppermute | solution.py:346
  62.9 5.2 %collective-permute-start.25 = (bf16[256,128]{1,0:T(8,128)(2,1)S(1)}, bf16[256,128]{1,0:T(8,128)(2,1)S(1)}, u32[]{:S(2)}, u32[]{:S(2)}) collective-permute-start(bf16[256,128]{1,0:T(8,128)(2,1)S(1)} %state.7.refs_0_), channel_id=1, source_target_pairs={{0,24},{1,25},{2,26},{3,27},{4,28},{5,29},{6,30},{7,31},{8,16},{9,... | collective-permute-start | bytes 196616 | tf_op jit(solution)/shard_map/ppermute | solution.py:346
  73.4 1.8 %collective-permute-start.29 = (bf16[1024,128]{1,0:T(8,128)(2,1)S(1)}, bf16[1024,128]{1,0:T(8,128)(2,1)S(1)}, u32[]{:S(2)}, u32[]{:S(2)}) collective-permute-start(bf16[1024,128]{1,0:T(8,128)(2,1)S(1)} %get-tuple-element.62), channel_id=1, source_target_pairs={{0,1},{1,0},{2,3},{3,2},{4,5},{5,4},{6,7},{7,6},{8,9},{9,8},{10,11... | collective-permute-start | bytes 786440 | tf_op jit(solution)/shard_map/ppermute | solution.py:330
  75.4 6.8 %collective-permute-start.32 = (bf16[256,128]{1,0:T(8,128)(2,1)S(1)}, bf16[256,128]{1,0:T(8,128)(2,1)S(1)}, u32[]{:S(2)}, u32[]{:S(2)}) collective-permute-start(bf16[256,128]{1,0:T(8,128)(2,1)S(1)} %get-tuple-element.66), channel_id=1, source_target_pairs={{0,6},{1,3},{2,4},{3,1},{4,2},{5,7},{6,0},{7,5},{8,14},{9,11},{10,... | collective-permute-start | bytes 196616 | tf_op jit(solution)/shard_map/ppermute | solution.py:336
  77.6 7.3 %collective-permute-start.31 = (bf16[256,128]{1,0:T(8,128)(2,1)S(1)}, bf16[256,128]{1,0:T(8,128)(2,1)S(1)}, u32[]{:S(2)}, u32[]{:S(2)}) collective-permute-start(bf16[256,128]{1,0:T(8,128)(2,1)S(1)} %get-tuple-element.65), channel_id=1, source_target_pairs={{0,4},{1,5},{2,6},{3,7},{4,0},{5,1},{6,2},{7,3},{8,12},{9,13},{10,... | collective-permute-start | bytes 196616 | tf_op jit(solution)/shard_map/ppermute | solution.py:336
  78.2 6.7 %collective-permute-start.30 = (bf16[256,128]{1,0:T(8,128)(2,1)S(1)}, bf16[256,128]{1,0:T(8,128)(2,1)S(1)}, u32[]{:S(2)}, u32[]{:S(2)}) collective-permute-start(bf16[256,128]{1,0:T(8,128)(2,1)S(1)} %get-tuple-element.64), channel_id=1, source_target_pairs={{0,2},{1,7},{2,0},{3,5},{4,6},{5,3},{6,4},{7,1},{8,10},{9,15},{10,... | collective-permute-start | bytes 196616 | tf_op jit(solution)/shard_map/ppermute | solution.py:336

commit v9 on v8

--- a/solution.py
+++ b/solution.py
@@ -146,12 +146,16 @@
 
 def fill_state(pieces, state, halves, tile):
     rows = pieces[0].shape[0]
-    devices = (state.shape[0] - tile) // (rows * halves)
-    for i, piece in enumerate(pieces):
-        half, device = halves - 1 - i // devices, i % devices
-        at = (device * halves + half) * rows
-        state[at : at + rows, :] = piece[...]
-    state[len(pieces) * rows :, :] = jnp.zeros((tile, state.shape[1]), state.dtype)
+    each = len(pieces) // halves
+    for i in range(halves):
+        slot = 0
+        for piece in pieces[i * each : (i + 1) * each]:
+            for j in range(piece.shape[0] // rows):
+                at = (slot * halves + halves - 1 - i) * rows
+                state[at : at + rows, :] = piece[j * rows : (j + 1) * rows, :]
+                slot += 1
+    filled = state.shape[0] - tile
+    state[filled:, :] = jnp.zeros((tile, state.shape[1]), state.dtype)
 
 
 def multiply(plan_ref, weights_ref, state, total, chunk, chunks, chunk_tiles):
@@ -336,15 +340,19 @@
             came.append(lax.ppermute(part, "col", [(i, i ^ masks[i % 2]) for i in range(ncols)]))
         return came
 
+    row_bits = nrows.bit_length() - 1
+
+    def swap_rows(sent, slot):
+        masks = [row_mask(slot, core, nrows) for core in range(2)]
+        pairs = [(r * ncols + c, (r ^ masks[c % 2]) * ncols + c) for r in range(nrows) for c in range(ncols)]
+        return lax.ppermute(sent, ("row", "col"), pairs)
+
     def spread(state):
-        pieces = [state]
-        for slot in range(1, nrows):
-            masks = [row_mask(slot, core, nrows) for core in range(2)]
-            pairs = [
-                (r * ncols + c, (r ^ masks[c % 2]) * ncols + c) for r in range(nrows) for c in range(ncols)
-            ]
-            pieces.append(lax.ppermute(state, ("row", "col"), pairs))
-        return pieces
+        held = [state]
+        while 1 << (len(held) - 1) < nrows:
+            sent = jnp.concatenate(held) if len(held) > 1 else state
+            held.append(swap_rows(sent, 1 << (len(held) - 1)))
+        return held
 
     state, *squares = call(
         begin_kernel,
@@ -358,7 +366,7 @@
             pltpu.SemaphoreType.DMA((2,)),
         ],
     )
-    pieces = spread(state)
+    pieces = [state] + [swap_rows(state, slot) for slot in range(1, nrows)]
 
     plan, weights = call(
         functools.partial(plan_kernel, row_tiles, per_group, nrows),
@@ -397,7 +405,7 @@
     for hop in range(HOPS - 1):
         extra = (mine,)
         odd, held = call(
-            functools.partial(odd_kernel, len(pieces), len(pieces) // nrows),
+            functools.partial(odd_kernel, len(pieces), HALVES if hop else 1),
             "odd",
             [
                 array((HALVES * chunk_rows + len(extra) * id_block, width), bf16),
@@ -440,10 +448,10 @@
             )
             parts.append(spread(half_state))
             after = (half_state,)
-        pieces = [parts[half][r] for half in reversed(range(HALVES)) for r in range(nrows)]
+        pieces = [piece for half in reversed(range(HALVES)) for piece in parts[half]]
 
     odd, total = call(
-        functools.partial(last_kernel, len(pieces), len(pieces) // nrows),
+        functools.partial(last_kernel, len(pieces), HALVES),
         "last",
         [array((chips * new_here, width), bf16), array((block_rows, width), f32)],
         (plan, place, *pieces, weights),

time: 86.6 us -> 93 us (1.074)
  waiting for transfers between devices: 17.6 us -> 22.7 us
  Pallas kernels: 23.9 us -> 25.2 us
    ppermute x15, waiting for transfers between devices: 7.38 us -> 10 us  [send(): lax.ppermute(part, 'col', [(i, i ^ masks[i % 2]) for i in range(ncols)])]
    ppermute x15 -> x11, waiting for transfers between devices: 9.89 us -> 12.4 us  [swap_rows(): return lax.ppermute(sent, ('row', 'col'), pairs)]
    pallas_call x18, Pallas kernels: 23.9 us -> 25.2 us  [call(): pl.pallas_call(kernel, out_shape=out_shape, grid_spec=pltpu.PrefetchScala...]
    ppermute x15 -> x11, starting transfers between devices: 19.3 us -> 19 us  [swap_rows(): return lax.ppermute(sent, ('row', 'col'), pairs)]
  transfers between devices with their start and end apart: 33 -> 29, of which waited for: 14 -> 15; matrix products, arithmetic and copies ran while one was open for 1% -> 1% of each run, Pallas kernels for 15% -> 14%
where the time goes in v9:
time: 93 us; the launch traced here: 92 us
  starting transfers between devices  41.5 us (45%)
  Pallas kernels  25.2 us (27%)
  waiting for transfers between devices  22.7 us (24%)
  other arithmetic  1.75 us (2%)
    pallas_call x18, Pallas kernels, call(): pl.pallas_call(kernel, out_shape=out_shape, grid_spec=pltpu.PrefetchScala...  25.2 us
    ppermute x15, starting transfers between devices, send(): lax.ppermute(part, 'col', [(i, i ^ masks[i % 2]) for i in range(ncols)])  22.2 us
    ppermute x11, starting transfers between devices, swap_rows(): return lax.ppermute(sent, ('row', 'col'), pairs)  19 us
    ppermute x11, waiting for transfers between devices, swap_rows(): return lax.ppermute(sent, ('row', 'col'), pairs)  12.4 us
    ppermute x15, waiting for transfers between devices, send(): lax.ppermute(part, 'col', [(i, i ^ masks[i % 2]) for i in range(ncols)])  10 us
  transfers between devices with their start and end apart: 29, of which 15 were waited for; matrix products, arithmetic and copies ran while one was open for 1% of the time, Pallas kernels for 14%

profile of v9, /device:TPU:0, one launch (start us, length us, event | category | flops | bytes accessed | tf_op | source)
XLA Modules:
  0.0 92.0 jit_solution(5592164006816224846)
XLA Ops:
  0.0 1.1 %begin.1 = (bf16[512,128]{1,0:T(8,128)(2,1)S(1)}, f32[256,128]{1,0:T(8,128)S(1)}, f32[256,128]{1,0:T(8,128)S(1)}) custom-call(s32[4,128]{1,0:T(4,128)} %bitcast.25, bf16[512,128]{1,0:T(8,128)(2,1)} %embed_hbm.1), custom_call_target="tpu_custom_call" | custom-call | tf_op jit(solution)/shard_map/begin/pallas_call | solution.py:318
  1.1 3.0 %collective-permute-start = (bf16[512,128]{1,0:T(8,128)(2,1)S(1)}, bf16[512,128]{1,0:T(8,128)(2,1)S(1)}, u32[]{:S(2)}, u32[]{:S(2)}) collective-permute-start(bf16[512,128]{1,0:T(8,128)(2,1)S(1)} %get-tuple-element.37.refs_0_), channel_id=1, source_target_pairs={{0,8},{1,17},{2,10},{3,19},{4,12},{5,21},{6,14},{7,23},{8,0},{9,25... | collective-permute-start | bytes 393224 | tf_op jit(solution)/shard_map/ppermute | solution.py:348
  4.1 1.5 %collective-permute-start.1 = (bf16[512,128]{1,0:T(8,128)(2,1)S(1)}, bf16[512,128]{1,0:T(8,128)(2,1)S(1)}, u32[]{:S(2)}, u32[]{:S(2)}) collective-permute-start(bf16[512,128]{1,0:T(8,128)(2,1)S(1)} %get-tuple-element.37.refs_0_), channel_id=1, source_target_pairs={{0,16},{1,9},{2,18},{3,11},{4,20},{5,13},{6,22},{7,15},{8,24},{9,1... | collective-permute-start | bytes 393224 | tf_op jit(solution)/shard_map/ppermute | solution.py:348
  5.6 0.0 collective-permute-start.2
  5.6 0.7 fusion.4
  7.0 3.4 %plan.1 = (s32[8,512]{1,0:T(8,128)S(1)}, bf16[256,128,128]{2,1,0:T(8,128)(2,1)S(1)}) custom-call(s32[1,1]{1,0:T(1,128)S(6)} %copy.10.count_ref, s32[1,256]{1,0:T(1,128)} %bitcast.26, s32[1,256]{1,0:T(1,128)} %bitcast.27, bf16[256,128,128]{2,1,0:T(8,128)(2,1)} %bitcast.24), custom_call_target="tpu_custom_call" | custom-call | tf_op jit(solution)/shard_map/plan/pallas_call | solution.py:318
  10.5 1.4 %collective-permute-done.1.refs_2_ = bf16[512,128]{1,0:T(8,128)(2,1)S(1)} collective-permute-done((bf16[512,128]{1,0:T(8,128)(2,1)S(1)}, bf16[512,128]{1,0:T(8,128)(2,1)S(1)}, u32[]{:S(2)}, u32[]{:S(2)}) %collective-permute-start.1) | collective-permute-done | bytes 131104 | tf_op jit(solution)/shard_map/ppermute | solution.py:348
  11.9 2.8 %odd.2 = (bf16[2064,128]{1,0:T(8,128)(2,1)S(1)}, bf16[2176,128]{1,0:T(8,128)(2,1)S(1)}) custom-call(s32[8,512]{1,0:T(8,128)S(1)} %get-tuple-element.36.plan_ref, bf16[512,128]{1,0:T(8,128)(2,1)S(1)} %get-tuple-element.37.refs_0_, bf16[512,128]{1,0:T(8,128)(2,1)S(1)} %collective-permute-done.refs_1_, bf16[512,128]{1,0:T(8,128)(2,1)S(1)} %collective-permute-done.1.refs_2_, ...), custom_call_target="tpu_custom_call" | custom-call | flops 536870912 | bytes 4194304 | tf_op jit(solution)/shard_map/odd/pallas_call | solution.py:318
  14.7 0.1 collective-permute-start.3
  14.7 1.7 %even0.2.even_ref = f32[1024,128]{1,0:T(8,128)S(1)} custom-call(s32[8,512]{1,0:T(8,128)S(1)} %get-tuple-element.36.plan_ref, bf16[2176,128]{1,0:T(8,128)(2,1)S(1)} %get-tuple-element.40.state, bf16[256,128,128]{2,1,0:T(8,128)(2,1)S(1)} %get-tuple-element.38.refs_4_.weights_ref.refs_6_), custom_call_target="tpu_custom_call" | custom-call | flops 268435456 | bytes 2097152 | tf_op jit(solution)/shard_map/even0/pallas_call | solution.py:318
  16.5 0.1 collective-permute-done.3.other_ref
  16.6 0.1 merge.3
  16.7 1.6 %collective-permute-start.7 = (bf16[256,128]{1,0:T(8,128)(2,1)S(1)}, bf16[256,128]{1,0:T(8,128)(2,1)S(1)}, u32[]{:S(2)}, u32[]{:S(2)}) collective-permute-start(bf16[256,128]{1,0:T(8,128)(2,1)S(1)} %get-tuple-element.48), channel_id=1, source_target_pairs={{0,2},{1,7},{2,0},{3,5},{4,6},{5,3},{6,4},{7,1},{8,10},{9,15},{10,... | collective-permute-start | bytes 196616 | tf_op jit(solution)/shard_map/ppermute | solution.py:340
  18.3 2.6 %collective-permute-start.8 = (bf16[256,128]{1,0:T(8,128)(2,1)S(1)}, bf16[256,128]{1,0:T(8,128)(2,1)S(1)}, u32[]{:S(2)}, u32[]{:S(2)}) collective-permute-start(bf16[256,128]{1,0:T(8,128)(2,1)S(1)} %get-tuple-element.49), channel_id=1, source_target_pairs={{0,4},{1,5},{2,6},{3,7},{4,0},{5,1},{6,2},{7,3},{8,12},{9,13},{10,... | collective-permute-start | bytes 196616 | tf_op jit(solution)/shard_map/ppermute | solution.py:340
  20.9 0.2 collective-permute-start.9
  21.2 1.8 %even1.2 = (f32[256,128]{1,0:T(8,128)S(1)}, bf16[272,128]{1,0:T(8,128)(2,1)S(1)}, bf16[272,128]{1,0:T(8,128)(2,1)S(1)}, bf16[272,128]{1,0:T(8,128)(2,1)S(1)}) custom-call(s32[8,512]{1,0:T(8,128)S(1)} %get-tuple-element.36.plan_ref, bf16[2176,128]{1,0:T(8,128)(2,1)S(1)} %get-tuple-element.40.state, ...), custom_call_target="tpu_custom_call" | custom-call | flops 268435456 | bytes 2097152 | tf_op jit(solution)/shard_map/even1/pallas_call | solution.py:318
  22.9 0.7 collective-permute-start.4
  23.7 3.5 %collective-permute-start.5 = (bf16[272,128]{1,0:T(8,128)(2,1)S(1)}, bf16[272,128]{1,0:T(8,128)(2,1)S(1)}, u32[]{:S(2)}, u32[]{:S(2)}) collective-permute-start(bf16[272,128]{1,0:T(8,128)(2,1)S(1)} %get-tuple-element.43), channel_id=1, source_target_pairs={{0,4},{1,5},{2,6},{3,7},{4,0},{5,1},{6,2},{7,3},{8,12},{9,13},{10,... | collective-permute-start | bytes 208904 | tf_op jit(solution)/shard_map/ppermute | solution.py:340
  27.2 0.2 collective-permute-start.6
  27.5 2.5 %collective-permute-start.12 = (bf16[256,128]{1,0:T(8,128)(2,1)S(1)}, bf16[256,128]{1,0:T(8,128)(2,1)S(1)}, u32[]{:S(2)}, u32[]{:S(2)}) collective-permute-start(bf16[256,128]{1,0:T(8,128)(2,1)S(1)} %state.4.refs_3_), channel_id=1, source_target_pairs={{0,8},{1,17},{2,10},{3,19},{4,12},{5,21},{6,14},{7,23},{8,0},{9,25... | collective-permute-start | bytes 196616 | tf_op jit(solution)/shard_map/ppermute | solution.py:348
  30.0 1.1 %collective-permute-done.5.refs_1_ = bf16[272,128]{1,0:T(8,128)(2,1)S(1)} collective-permute-done((bf16[272,128]{1,0:T(8,128)(2,1)S(1)}, bf16[272,128]{1,0:T(8,128)(2,1)S(1)}, u32[]{:S(2)}, u32[]{:S(2)}) %collective-permute-start.5) | collective-permute-done | bytes 69664 | tf_op jit(solution)/shard_map/ppermute | solution.py:340
  31.1 2.2 %collective-permute-done.6.refs_2_ = bf16[272,128]{1,0:T(8,128)(2,1)S(1)} collective-permute-done((bf16[272,128]{1,0:T(8,128)(2,1)S(1)}, bf16[272,128]{1,0:T(8,128)(2,1)S(1)}, u32[]{:S(2)}, u32[]{:S(2)}) %collective-permute-start.6) | collective-permute-done | bytes 69664 | tf_op jit(solution)/shard_map/ppermute | solution.py:340
  33.3 2.7 %collective-permute-start.10 = (bf16[256,128]{1,0:T(8,128)(2,1)S(1)}, bf16[256,128]{1,0:T(8,128)(2,1)S(1)}, u32[]{:S(2)}, u32[]{:S(2)}) collective-permute-start(bf16[256,128]{1,0:T(8,128)(2,1)S(1)} %state.5.refs_0_), channel_id=1, source_target_pairs={{0,8},{1,17},{2,10},{3,19},{4,12},{5,21},{6,14},{7,23},{8,0},{9,25... | collective-permute-start | bytes 196616 | tf_op jit(solution)/shard_map/ppermute | solution.py:348
  36.1 1.5 %collective-permute-start.13 = (bf16[512,128]{1,0:T(8,128)(2,1)S(1)}, bf16[512,128]{1,0:T(8,128)(2,1)S(1)}, u32[]{:S(2)}, u32[]{:S(2)}) collective-permute-start(bf16[512,128]{1,0:T(8,128)(2,1)S(1)} %pad_maximum_fusion.1), channel_id=1, source_target_pairs={{0,16},{1,9},{2,18},{3,11},{4,20},{5,13},{6,22},{7,15},{8,24},{9,1... | collective-permute-start | bytes 393224 | tf_op jit(solution)/shard_map/ppermute | solution.py:348
  37.6 1.5 %collective-permute-done.10.refs_1_ = bf16[256,128]{1,0:T(8,128)(2,1)S(1)} collective-permute-done((bf16[256,128]{1,0:T(8,128)(2,1)S(1)}, bf16[256,128]{1,0:T(8,128)(2,1)S(1)}, u32[]{:S(2)}, u32[]{:S(2)}) %collective-permute-start.10) | collective-permute-done | bytes 65568 | tf_op jit(solution)/shard_map/ppermute | solution.py:348
  39.0 1.3 %collective-permute-start.11 = (bf16[512,128]{1,0:T(8,128)(2,1)S(1)}, bf16[512,128]{1,0:T(8,128)(2,1)S(1)}, u32[]{:S(2)}, u32[]{:S(2)}) collective-permute-start(bf16[512,128]{1,0:T(8,128)(2,1)S(1)} %pad_maximum_fusion), channel_id=1, source_target_pairs={{0,16},{1,9},{2,18},{3,11},{4,20},{5,13},{6,22},{7,15},{8,24},{9,1... | collective-permute-start | bytes 393224 | tf_op jit(solution)/shard_map/ppermute | solution.py:348
  40.3 0.8 collective-permute-done.13.refs_5_
  41.1 2.9 %collective-permute-done.11.refs_2_ = bf16[512,128]{1,0:T(8,128)(2,1)S(1)} collective-permute-done((bf16[512,128]{1,0:T(8,128)(2,1)S(1)}, bf16[512,128]{1,0:T(8,128)(2,1)S(1)}, u32[]{:S(2)}, u32[]{:S(2)}) %collective-permute-start.11) | collective-permute-done | bytes 131104 | tf_op jit(solution)/shard_map/ppermute | solution.py:348
  44.1 2.8 %odd.3 = (bf16[2064,128]{1,0:T(8,128)(2,1)S(1)}, bf16[2176,128]{1,0:T(8,128)(2,1)S(1)}) custom-call(s32[8,512]{1,0:T(8,128)S(1)} %get-tuple-element.36.plan_ref, bf16[256,128]{1,0:T(8,128)(2,1)S(1)} %state.5.refs_0_, bf16[256,128]{1,0:T(8,128)(2,1)S(1)} %collective-permute-done.10.refs_1_, bf16[512,128]{1,0:T(8,128)(2,1)S(1)} %collective-permute-done.11.refs_2_, ...), custom_call_target="tpu_custom_call" | custom-call | flops 536870912 | bytes 4194304 | tf_op jit(solution)/shard_map/odd/pallas_call | solution.py:318
  46.8 0.1 collective-permute-start.14
  46.9 1.7 %even0.3.even_ref = f32[1024,128]{1,0:T(8,128)S(1)} custom-call(s32[8,512]{1,0:T(8,128)S(1)} %get-tuple-element.36.plan_ref, bf16[2176,128]{1,0:T(8,128)(2,1)S(1)} %get-tuple-element.51.state, bf16[256,128,128]{2,1,0:T(8,128)(2,1)S(1)} %get-tuple-element.38.refs_4_.weights_ref.refs_6_), custom_call_target="tpu_custom_call" | custom-call | flops 268435456 | bytes 2097152 | tf_op jit(solution)/shard_map/even0/pallas_call | solution.py:318
  48.7 0.2 collective-permute-done.14.other_ref
  48.8 0.1 merge.4
  48.9 0.1 collective-permute-start.18
  49.0 1.2 %collective-permute-start.19 = (bf16[256,128]{1,0:T(8,128)(2,1)S(1)}, bf16[256,128]{1,0:T(8,128)(2,1)S(1)}, u32[]{:S(2)}, u32[]{:S(2)}) collective-permute-start(bf16[256,128]{1,0:T(8,128)(2,1)S(1)} %get-tuple-element.59), channel_id=1, source_target_pairs={{0,4},{1,5},{2,6},{3,7},{4,0},{5,1},{6,2},{7,3},{8,12},{9,13},{10,... | collective-permute-start | bytes 196616 | tf_op jit(solution)/shard_map/ppermute | solution.py:340
  50.2 3.1 %collective-permute-start.20 = (bf16[256,128]{1,0:T(8,128)(2,1)S(1)}, bf16[256,128]{1,0:T(8,128)(2,1)S(1)}, u32[]{:S(2)}, u32[]{:S(2)}) collective-permute-start(bf16[256,128]{1,0:T(8,128)(2,1)S(1)} %get-tuple-element.60), channel_id=1, source_target_pairs={{0,6},{1,3},{2,4},{3,1},{4,2},{5,7},{6,0},{7,5},{8,14},{9,11},{10,... | collective-permute-start | bytes 196616 | tf_op jit(solution)/shard_map/ppermute | solution.py:340
  53.3 1.8 %even1.3 = (f32[256,128]{1,0:T(8,128)S(1)}, bf16[272,128]{1,0:T(8,128)(2,1)S(1)}, bf16[272,128]{1,0:T(8,128)(2,1)S(1)}, bf16[272,128]{1,0:T(8,128)(2,1)S(1)}) custom-call(s32[8,512]{1,0:T(8,128)S(1)} %get-tuple-element.36.plan_ref, bf16[2176,128]{1,0:T(8,128)(2,1)S(1)} %get-tuple-element.51.state, ...), custom_call_target="tpu_custom_call" | custom-call | flops 268435456 | bytes 2097152 | tf_op jit(solution)/shard_map/even1/pallas_call | solution.py:318
  55.1 0.0 copy-start
  55.1 0.0 copy-start.1
  55.2 0.1 collective-permute-start.15
  55.2 1.3 %collective-permute-start.16 = (bf16[272,128]{1,0:T(8,128)(2,1)S(1)}, bf16[272,128]{1,0:T(8,128)(2,1)S(1)}, u32[]{:S(2)}, u32[]{:S(2)}) collective-permute-start(bf16[272,128]{1,0:T(8,128)(2,1)S(1)} %get-tuple-element.56), channel_id=1, source_target_pairs={{0,4},{1,5},{2,6},{3,7},{4,0},{5,1},{6,2},{7,3},{8,12},{9,13},{10,... | collective-permute-start | bytes 208904 | tf_op jit(solution)/shard_map/ppermute | solution.py:340
  56.5 3.1 %collective-permute-start.17 = (bf16[272,128]{1,0:T(8,128)(2,1)S(1)}, bf16[272,128]{1,0:T(8,128)(2,1)S(1)}, u32[]{:S(2)}, u32[]{:S(2)}) collective-permute-start(bf16[272,128]{1,0:T(8,128)(2,1)S(1)} %get-tuple-element.57), channel_id=1, source_target_pairs={{0,6},{1,3},{2,4},{3,1},{4,2},{5,7},{6,0},{7,5},{8,14},{9,11},{10,... | collective-permute-start | bytes 208904 | tf_op jit(solution)/shard_map/ppermute | solution.py:340
  59.7 2.1 %collective-permute-start.23 = (bf16[256,128]{1,0:T(8,128)(2,1)S(1)}, bf16[256,128]{1,0:T(8,128)(2,1)S(1)}, u32[]{:S(2)}, u32[]{:S(2)}) collective-permute-start(bf16[256,128]{1,0:T(8,128)(2,1)S(1)} %state.6.refs_3_), channel_id=1, source_target_pairs={{0,8},{1,17},{2,10},{3,19},{4,12},{5,21},{6,14},{7,23},{8,0},{9,25... | collective-permute-start | bytes 196616 | tf_op jit(solution)/shard_map/ppermute | solution.py:348
  61.8 0.2 collective-permute-done.15.refs_0_
  61.9 1.4 %collective-permute-done.16.refs_1_ = bf16[272,128]{1,0:T(8,128)(2,1)S(1)} collective-permute-done((bf16[272,128]{1,0:T(8,128)(2,1)S(1)}, bf16[272,128]{1,0:T(8,128)(2,1)S(1)}, u32[]{:S(2)}, u32[]{:S(2)}) %collective-permute-start.16) | collective-permute-done | bytes 69664 | tf_op jit(solution)/shard_map/ppermute | solution.py:340
  63.4 2.3 %collective-permute-start.21 = (bf16[256,128]{1,0:T(8,128)(2,1)S(1)}, bf16[256,128]{1,0:T(8,128)(2,1)S(1)}, u32[]{:S(2)}, u32[]{:S(2)}) collective-permute-start(bf16[256,128]{1,0:T(8,128)(2,1)S(1)} %state.7.refs_0_), channel_id=1, source_target_pairs={{0,8},{1,17},{2,10},{3,19},{4,12},{5,21},{6,14},{7,23},{8,0},{9,25... | collective-permute-start | bytes 196616 | tf_op jit(solution)/shard_map/ppermute | solution.py:348
  65.8 1.0 %collective-permute-start.24 = (bf16[512,128]{1,0:T(8,128)(2,1)S(1)}, bf16[512,128]{1,0:T(8,128)(2,1)S(1)}, u32[]{:S(2)}, u32[]{:S(2)}) collective-permute-start(bf16[512,128]{1,0:T(8,128)(2,1)S(1)} %pad_maximum_fusion.3), channel_id=1, source_target_pairs={{0,16},{1,9},{2,18},{3,11},{4,20},{5,13},{6,22},{7,15},{8,24},{9,1... | collective-permute-start | bytes 393224 | tf_op jit(solution)/shard_map/ppermute | solution.py:348
  66.8 1.9 %collective-permute-done.21.refs_1_ = bf16[256,128]{1,0:T(8,128)(2,1)S(1)} collective-permute-done((bf16[256,128]{1,0:T(8,128)(2,1)S(1)}, bf16[256,128]{1,0:T(8,128)(2,1)S(1)}, u32[]{:S(2)}, u32[]{:S(2)}) %collective-permute-start.21) | collective-permute-done | bytes 65568 | tf_op jit(solution)/shard_map/ppermute | solution.py:348
  68.7 1.0 %collective-permute-start.22 = (bf16[512,128]{1,0:T(8,128)(2,1)S(1)}, bf16[512,128]{1,0:T(8,128)(2,1)S(1)}, u32[]{:S(2)}, u32[]{:S(2)}) collective-permute-start(bf16[512,128]{1,0:T(8,128)(2,1)S(1)} %pad_maximum_fusion.2), channel_id=1, source_target_pairs={{0,16},{1,9},{2,18},{3,11},{4,20},{5,13},{6,22},{7,15},{8,24},{9,1... | collective-permute-start | bytes 393224 | tf_op jit(solution)/shard_map/ppermute | solution.py:348
  69.7 0.1 place.1.place_ref
  69.8 1.0 %collective-permute-done.24.refs_5_ = bf16[512,128]{1,0:T(8,128)(2,1)S(1)} collective-permute-done((bf16[512,128]{1,0:T(8,128)(2,1)S(1)}, bf16[512,128]{1,0:T(8,128)(2,1)S(1)}, u32[]{:S(2)}, u32[]{:S(2)}) %collective-permute-start.24) | collective-permute-done | bytes 131104 | tf_op jit(solution)/shard_map/ppermute | solution.py:348
  70.8 2.9 %collective-permute-done.22.refs_2_ = bf16[512,128]{1,0:T(8,128)(2,1)S(1)} collective-permute-done((bf16[512,128]{1,0:T(8,128)(2,1)S(1)}, bf16[512,128]{1,0:T(8,128)(2,1)S(1)}, u32[]{:S(2)}, u32[]{:S(2)}) %collective-permute-start.22) | collective-permute-done | bytes 131104 | tf_op jit(solution)/shard_map/ppermute | solution.py:348
  73.7 5.8 %last.1 = (bf16[1024,128]{1,0:T(8,128)(2,1)S(1)}, f32[4096,128]{1,0:T(8,128)S(1)}) custom-call(s32[8,512]{1,0:T(8,128)S(1)} %get-tuple-element.36.plan_ref, s32[1,2048]{1,0:T(1,128)S(1)} %place.1.place_ref, bf16[256,128]{1,0:T(8,128)(2,1)S(1)} %state.7.refs_0_, bf16[256,128]{1,0:T(8,128)(2,1)S(1)} %collective-permute-done.21.refs_1_, ...), custom_call_target="tpu_custom_call" | custom-call | flops 1073741824 | bytes 8388608 | tf_op jit(solution)/shard_map/last/pallas_call | solution.py:318
  79.6 0.1 collective-permute-start.25
  79.7 1.7 %pick.1.even_ref = f32[1024,128]{1,0:T(8,128)S(1)} custom-call(s32[1,2048]{1,0:T(1,128)S(1)} %place.1.place_ref, f32[4096,128]{1,0:T(8,128)S(1)} %get-tuple-element.61.total), custom_call_target="tpu_custom_call" | custom-call | flops 214748368 | bytes 1677721 | tf_op jit(solution)/shard_map/pick/pallas_call | solution.py:318
  81.4 0.1 merge.5
  81.5 2.0 %collective-permute-start.28 = (bf16[256,128]{1,0:T(8,128)(2,1)S(1)}, bf16[256,128]{1,0:T(8,128)(2,1)S(1)}, u32[]{:S(2)}, u32[]{:S(2)}) collective-permute-start(bf16[256,128]{1,0:T(8,128)(2,1)S(1)} %get-tuple-element.66), channel_id=1, source_target_pairs={{0,6},{1,3},{2,4},{3,1},{4,2},{5,7},{6,0},{7,5},{8,14},{9,11},{10,... | collective-permute-start | bytes 196616 | tf_op jit(solution)/shard_map/ppermute | solution.py:340
  83.5 0.6 collective-permute-start.27
  84.0 1.9 %collective-permute-start.26 = (bf16[256,128]{1,0:T(8,128)(2,1)S(1)}, bf16[256,128]{1,0:T(8,128)(2,1)S(1)}, u32[]{:S(2)}, u32[]{:S(2)}) collective-permute-start(bf16[256,128]{1,0:T(8,128)(2,1)S(1)} %get-tuple-element.64), channel_id=1, source_target_pairs={{0,2},{1,7},{2,0},{3,5},{4,6},{5,3},{6,4},{7,1},{8,10},{9,15},{10,... | collective-permute-start | bytes 196616 | tf_op jit(solution)/shard_map/ppermute | solution.py:340
  85.9 0.1 select_reduce_fusion
  86.0 2.3 %collective-permute-done.28 = bf16[256,128]{1,0:T(8,128)(2,1)S(1)} collective-permute-done((bf16[256,128]{1,0:T(8,128)(2,1)S(1)}, bf16[256,128]{1,0:T(8,128)(2,1)S(1)}, u32[]{:S(2)}, u32[]{:S(2)}) %collective-permute-start.28) | collective-permute-done | bytes 65568 | tf_op jit(solution)/shard_map/ppermute | solution.py:340
  88.3 2.8 %collective-permute-done.27 = bf16[256,128]{1,0:T(8,128)(2,1)S(1)} collective-permute-done((bf16[256,128]{1,0:T(8,128)(2,1)S(1)}, bf16[256,128]{1,0:T(8,128)(2,1)S(1)}, u32[]{:S(2)}, u32[]{:S(2)}) %collective-permute-start.27) | collective-permute-done | bytes 65568 | tf_op jit(solution)/shard_map/ppermute | solution.py:340
  91.1 0.1 multiply_reduce_fusion
  91.2 0.8 multiply_multiply_fusion
  (26 shorter events, 0.3 us)
Async XLA Ops:
  1.1 9.4 %collective-permute-start = (bf16[512,128]{1,0:T(8,128)(2,1)S(1)}, bf16[512,128]{1,0:T(8,128)(2,1)S(1)}, u32[]{:S(2)}, u32[]{:S(2)}) collective-permute-start(bf16[512,128]{1,0:T(8,128)(2,1)S(1)} %get-tuple-element.37.refs_0_), channel_id=1, source_target_pairs={{0,8},{1,17},{2,10},{3,19},{4,12},{5,21},{6,14},{7,23},{8,0},{9,25... | collective-permute-start | bytes 393224 | tf_op jit(solution)/shard_map/ppermute | solution.py:348
  4.1 7.8 %collective-permute-start.1 = (bf16[512,128]{1,0:T(8,128)(2,1)S(1)}, bf16[512,128]{1,0:T(8,128)(2,1)S(1)}, u32[]{:S(2)}, u32[]{:S(2)}) collective-permute-start(bf16[512,128]{1,0:T(8,128)(2,1)S(1)} %get-tuple-element.37.refs_0_), channel_id=1, source_target_pairs={{0,16},{1,9},{2,18},{3,11},{4,20},{5,13},{6,22},{7,15},{8,24},{9,1... | collective-permute-start | bytes 393224 | tf_op jit(solution)/shard_map/ppermute | solution.py:348
  5.6 6.3 %collective-permute-start.2 = (bf16[512,128]{1,0:T(8,128)(2,1)S(1)}, bf16[512,128]{1,0:T(8,128)(2,1)S(1)}, u32[]{:S(2)}, u32[]{:S(2)}) collective-permute-start(bf16[512,128]{1,0:T(8,128)(2,1)S(1)} %get-tuple-element.37.refs_0_), channel_id=1, source_target_pairs={{0,24},{1,25},{2,26},{3,27},{4,28},{5,29},{6,30},{7,31},{8,16},{9,... | collective-permute-start | bytes 393224 | tf_op jit(solution)/shard_map/ppermute | solution.py:348
  14.7 2.0 %collective-permute-start.3 = (bf16[2064,128]{1,0:T(8,128)(2,1)S(1)}, bf16[2064,128]{1,0:T(8,128)(2,1)S(1)}, u32[]{:S(2)}, u32[]{:S(2)}) collective-permute-start(bf16[2064,128]{1,0:T(8,128)(2,1)S(1)} %get-tuple-element.39), channel_id=1, source_target_pairs={{0,1},{1,0},{2,3},{3,2},{4,5},{5,4},{6,7},{7,6},{8,9},{9,8},{10,11... | collective-permute-start | bytes 1585160 | tf_op jit(solution)/shard_map/ppermute | solution.py:334
  16.7 10.5 %collective-permute-start.7 = (bf16[256,128]{1,0:T(8,128)(2,1)S(1)}, bf16[256,128]{1,0:T(8,128)(2,1)S(1)}, u32[]{:S(2)}, u32[]{:S(2)}) collective-permute-start(bf16[256,128]{1,0:T(8,128)(2,1)S(1)} %get-tuple-element.48), channel_id=1, source_target_pairs={{0,2},{1,7},{2,0},{3,5},{4,6},{5,3},{6,4},{7,1},{8,10},{9,15},{10,... | collective-permute-start | bytes 196616 | tf_op jit(solution)/shard_map/ppermute | solution.py:340
  18.3 9.1 %collective-permute-start.8 = (bf16[256,128]{1,0:T(8,128)(2,1)S(1)}, bf16[256,128]{1,0:T(8,128)(2,1)S(1)}, u32[]{:S(2)}, u32[]{:S(2)}) collective-permute-start(bf16[256,128]{1,0:T(8,128)(2,1)S(1)} %get-tuple-element.49), channel_id=1, source_target_pairs={{0,4},{1,5},{2,6},{3,7},{4,0},{5,1},{6,2},{7,3},{8,12},{9,13},{10,... | collective-permute-start | bytes 196616 | tf_op jit(solution)/shard_map/ppermute | solution.py:340
  20.9 6.5 %collective-permute-start.9 = (bf16[256,128]{1,0:T(8,128)(2,1)S(1)}, bf16[256,128]{1,0:T(8,128)(2,1)S(1)}, u32[]{:S(2)}, u32[]{:S(2)}) collective-permute-start(bf16[256,128]{1,0:T(8,128)(2,1)S(1)} %get-tuple-element.50), channel_id=1, source_target_pairs={{0,6},{1,3},{2,4},{3,1},{4,2},{5,7},{6,0},{7,5},{8,14},{9,11},{10,... | collective-permute-start | bytes 196616 | tf_op jit(solution)/shard_map/ppermute | solution.py:340
  22.9 7.0 %collective-permute-start.4 = (bf16[272,128]{1,0:T(8,128)(2,1)S(1)}, bf16[272,128]{1,0:T(8,128)(2,1)S(1)}, u32[]{:S(2)}, u32[]{:S(2)}) collective-permute-start(bf16[272,128]{1,0:T(8,128)(2,1)S(1)} %get-tuple-element.42), channel_id=1, source_target_pairs={{0,2},{1,7},{2,0},{3,5},{4,6},{5,3},{6,4},{7,1},{8,10},{9,15},{10,... | collective-permute-start | bytes 208904 | tf_op jit(solution)/shard_map/ppermute | solution.py:340
  23.7 7.4 %collective-permute-start.5 = (bf16[272,128]{1,0:T(8,128)(2,1)S(1)}, bf16[272,128]{1,0:T(8,128)(2,1)S(1)}, u32[]{:S(2)}, u32[]{:S(2)}) collective-permute-start(bf16[272,128]{1,0:T(8,128)(2,1)S(1)} %get-tuple-element.43), channel_id=1, source_target_pairs={{0,4},{1,5},{2,6},{3,7},{4,0},{5,1},{6,2},{7,3},{8,12},{9,13},{10,... | collective-permute-start | bytes 208904 | tf_op jit(solution)/shard_map/ppermute | solution.py:340
  27.2 6.1 %collective-permute-start.6 = (bf16[272,128]{1,0:T(8,128)(2,1)S(1)}, bf16[272,128]{1,0:T(8,128)(2,1)S(1)}, u32[]{:S(2)}, u32[]{:S(2)}) collective-permute-start(bf16[272,128]{1,0:T(8,128)(2,1)S(1)} %get-tuple-element.44), channel_id=1, source_target_pairs={{0,6},{1,3},{2,4},{3,1},{4,2},{5,7},{6,0},{7,5},{8,14},{9,11},{10,... | collective-permute-start | bytes 208904 | tf_op jit(solution)/shard_map/ppermute | solution.py:340
  27.5 8.6 %collective-permute-start.12 = (bf16[256,128]{1,0:T(8,128)(2,1)S(1)}, bf16[256,128]{1,0:T(8,128)(2,1)S(1)}, u32[]{:S(2)}, u32[]{:S(2)}) collective-permute-start(bf16[256,128]{1,0:T(8,128)(2,1)S(1)} %state.4.refs_3_), channel_id=1, source_target_pairs={{0,8},{1,17},{2,10},{3,19},{4,12},{5,21},{6,14},{7,23},{8,0},{9,25... | collective-permute-start | bytes 196616 | tf_op jit(solution)/shard_map/ppermute | solution.py:348
  33.3 5.7 %collective-permute-start.10 = (bf16[256,128]{1,0:T(8,128)(2,1)S(1)}, bf16[256,128]{1,0:T(8,128)(2,1)S(1)}, u32[]{:S(2)}, u32[]{:S(2)}) collective-permute-start(bf16[256,128]{1,0:T(8,128)(2,1)S(1)} %state.5.refs_0_), channel_id=1, source_target_pairs={{0,8},{1,17},{2,10},{3,19},{4,12},{5,21},{6,14},{7,23},{8,0},{9,25... | collective-permute-start | bytes 196616 | tf_op jit(solution)/shard_map/ppermute | solution.py:348
  36.1 5.0 %collective-permute-start.13 = (bf16[512,128]{1,0:T(8,128)(2,1)S(1)}, bf16[512,128]{1,0:T(8,128)(2,1)S(1)}, u32[]{:S(2)}, u32[]{:S(2)}) collective-permute-start(bf16[512,128]{1,0:T(8,128)(2,1)S(1)} %pad_maximum_fusion.1), channel_id=1, source_target_pairs={{0,16},{1,9},{2,18},{3,11},{4,20},{5,13},{6,22},{7,15},{8,24},{9,1... | collective-permute-start | bytes 393224 | tf_op jit(solution)/shard_map/ppermute | solution.py:348
  39.0 5.0 %collective-permute-start.11 = (bf16[512,128]{1,0:T(8,128)(2,1)S(1)}, bf16[512,128]{1,0:T(8,128)(2,1)S(1)}, u32[]{:S(2)}, u32[]{:S(2)}) collective-permute-start(bf16[512,128]{1,0:T(8,128)(2,1)S(1)} %pad_maximum_fusion), channel_id=1, source_target_pairs={{0,16},{1,9},{2,18},{3,11},{4,20},{5,13},{6,22},{7,15},{8,24},{9,1... | collective-permute-start | bytes 393224 | tf_op jit(solution)/shard_map/ppermute | solution.py:348
  46.8 2.0 %collective-permute-start.14 = (bf16[2064,128]{1,0:T(8,128)(2,1)S(1)}, bf16[2064,128]{1,0:T(8,128)(2,1)S(1)}, u32[]{:S(2)}, u32[]{:S(2)}) collective-permute-start(bf16[2064,128]{1,0:T(8,128)(2,1)S(1)} %get-tuple-element.52), channel_id=1, source_target_pairs={{0,1},{1,0},{2,3},{3,2},{4,5},{5,4},{6,7},{7,6},{8,9},{9,8},{10,11... | collective-permute-start | bytes 1585160 | tf_op jit(solution)/shard_map/ppermute | solution.py:334
  48.9 7.6 %collective-permute-start.18 = (bf16[256,128]{1,0:T(8,128)(2,1)S(1)}, bf16[256,128]{1,0:T(8,128)(2,1)S(1)}, u32[]{:S(2)}, u32[]{:S(2)}) collective-permute-start(bf16[256,128]{1,0:T(8,128)(2,1)S(1)} %get-tuple-element.58), channel_id=1, source_target_pairs={{0,2},{1,7},{2,0},{3,5},{4,6},{5,3},{6,4},{7,1},{8,10},{9,15},{10,... | collective-permute-start | bytes 196616 | tf_op jit(solution)/shard_map/ppermute | solution.py:340
  49.0 10.7 %collective-permute-start.19 = (bf16[256,128]{1,0:T(8,128)(2,1)S(1)}, bf16[256,128]{1,0:T(8,128)(2,1)S(1)}, u32[]{:S(2)}, u32[]{:S(2)}) collective-permute-start(bf16[256,128]{1,0:T(8,128)(2,1)S(1)} %get-tuple-element.59), channel_id=1, source_target_pairs={{0,4},{1,5},{2,6},{3,7},{4,0},{5,1},{6,2},{7,3},{8,12},{9,13},{10,... | collective-permute-start | bytes 196616 | tf_op jit(solution)/shard_map/ppermute | solution.py:340
  50.2 9.4 %collective-permute-start.20 = (bf16[256,128]{1,0:T(8,128)(2,1)S(1)}, bf16[256,128]{1,0:T(8,128)(2,1)S(1)}, u32[]{:S(2)}, u32[]{:S(2)}) collective-permute-start(bf16[256,128]{1,0:T(8,128)(2,1)S(1)} %get-tuple-element.60), channel_id=1, source_target_pairs={{0,6},{1,3},{2,4},{3,1},{4,2},{5,7},{6,0},{7,5},{8,14},{9,11},{10,... | collective-permute-start | bytes 196616 | tf_op jit(solution)/shard_map/ppermute | solution.py:340
  55.1 30.8 %copy-start = (s32[256]{0:T(256)S(1)}, s32[256]{0:T(256)}, u32[]{:S(2)}) copy-start(s32[256]{0:T(256)} %param.16) | copy-start | bytes 3076
  55.1 30.8 %copy-start.1 = (f32[16]{0:T(128)S(1)}, f32[16]{0:T(128)}, u32[]{:S(2)}) copy-start(f32[16]{0:T(128)} %param.17) | copy-start | bytes 196
  55.2 6.8 %collective-permute-start.15 = (bf16[272,128]{1,0:T(8,128)(2,1)S(1)}, bf16[272,128]{1,0:T(8,128)(2,1)S(1)}, u32[]{:S(2)}, u32[]{:S(2)}) collective-permute-start(bf16[272,128]{1,0:T(8,128)(2,1)S(1)} %get-tuple-element.55), channel_id=1, source_target_pairs={{0,2},{1,7},{2,0},{3,5},{4,6},{5,3},{6,4},{7,1},{8,10},{9,15},{10,... | collective-permute-start | bytes 208904 | tf_op jit(solution)/shard_map/ppermute | solution.py:340
  55.2 8.2 %collective-permute-start.16 = (bf16[272,128]{1,0:T(8,128)(2,1)S(1)}, bf16[272,128]{1,0:T(8,128)(2,1)S(1)}, u32[]{:S(2)}, u32[]{:S(2)}) collective-permute-start(bf16[272,128]{1,0:T(8,128)(2,1)S(1)} %get-tuple-element.56), channel_id=1, source_target_pairs={{0,4},{1,5},{2,6},{3,7},{4,0},{5,1},{6,2},{7,3},{8,12},{9,13},{10,... | collective-permute-start | bytes 208904 | tf_op jit(solution)/shard_map/ppermute | solution.py:340
  56.5 6.9 %collective-permute-start.17 = (bf16[272,128]{1,0:T(8,128)(2,1)S(1)}, bf16[272,128]{1,0:T(8,128)(2,1)S(1)}, u32[]{:S(2)}, u32[]{:S(2)}) collective-permute-start(bf16[272,128]{1,0:T(8,128)(2,1)S(1)} %get-tuple-element.57), channel_id=1, source_target_pairs={{0,6},{1,3},{2,4},{3,1},{4,2},{5,7},{6,0},{7,5},{8,14},{9,11},{10,... | collective-permute-start | bytes 208904 | tf_op jit(solution)/shard_map/ppermute | solution.py:340
  59.7 6.1 %collective-permute-start.23 = (bf16[256,128]{1,0:T(8,128)(2,1)S(1)}, bf16[256,128]{1,0:T(8,128)(2,1)S(1)}, u32[]{:S(2)}, u32[]{:S(2)}) collective-permute-start(bf16[256,128]{1,0:T(8,128)(2,1)S(1)} %state.6.refs_3_), channel_id=1, source_target_pairs={{0,8},{1,17},{2,10},{3,19},{4,12},{5,21},{6,14},{7,23},{8,0},{9,25... | collective-permute-start | bytes 196616 | tf_op jit(solution)/shard_map/ppermute | solution.py:348
  63.4 5.2 %collective-permute-start.21 = (bf16[256,128]{1,0:T(8,128)(2,1)S(1)}, bf16[256,128]{1,0:T(8,128)(2,1)S(1)}, u32[]{:S(2)}, u32[]{:S(2)}) collective-permute-start(bf16[256,128]{1,0:T(8,128)(2,1)S(1)} %state.7.refs_0_), channel_id=1, source_target_pairs={{0,8},{1,17},{2,10},{3,19},{4,12},{5,21},{6,14},{7,23},{8,0},{9,25... | collective-permute-start | bytes 196616 | tf_op jit(solution)/shard_map/ppermute | solution.py:348
  65.8 5.0 %collective-permute-start.24 = (bf16[512,128]{1,0:T(8,128)(2,1)S(1)}, bf16[512,128]{1,0:T(8,128)(2,1)S(1)}, u32[]{:S(2)}, u32[]{:S(2)}) collective-permute-start(bf16[512,128]{1,0:T(8,128)(2,1)S(1)} %pad_maximum_fusion.3), channel_id=1, source_target_pairs={{0,16},{1,9},{2,18},{3,11},{4,20},{5,13},{6,22},{7,15},{8,24},{9,1... | collective-permute-start | bytes 393224 | tf_op jit(solution)/shard_map/ppermute | solution.py:348
  68.7 5.0 %collective-permute-start.22 = (bf16[512,128]{1,0:T(8,128)(2,1)S(1)}, bf16[512,128]{1,0:T(8,128)(2,1)S(1)}, u32[]{:S(2)}, u32[]{:S(2)}) collective-permute-start(bf16[512,128]{1,0:T(8,128)(2,1)S(1)} %pad_maximum_fusion.2), channel_id=1, source_target_pairs={{0,16},{1,9},{2,18},{3,11},{4,20},{5,13},{6,22},{7,15},{8,24},{9,1... | collective-permute-start | bytes 393224 | tf_op jit(solution)/shard_map/ppermute | solution.py:348
  79.6 1.8 %collective-permute-start.25 = (bf16[1024,128]{1,0:T(8,128)(2,1)S(1)}, bf16[1024,128]{1,0:T(8,128)(2,1)S(1)}, u32[]{:S(2)}, u32[]{:S(2)}) collective-permute-start(bf16[1024,128]{1,0:T(8,128)(2,1)S(1)} %get-tuple-element.62), channel_id=1, source_target_pairs={{0,1},{1,0},{2,3},{3,2},{4,5},{5,4},{6,7},{7,6},{8,9},{9,8},{10,11... | collective-permute-start | bytes 786440 | tf_op jit(solution)/shard_map/ppermute | solution.py:334
  81.5 6.8 %collective-permute-start.28 = (bf16[256,128]{1,0:T(8,128)(2,1)S(1)}, bf16[256,128]{1,0:T(8,128)(2,1)S(1)}, u32[]{:S(2)}, u32[]{:S(2)}) collective-permute-start(bf16[256,128]{1,0:T(8,128)(2,1)S(1)} %get-tuple-element.66), channel_id=1, source_target_pairs={{0,6},{1,3},{2,4},{3,1},{4,2},{5,7},{6,0},{7,5},{8,14},{9,11},{10,... | collective-permute-start | bytes 196616 | tf_op jit(solution)/shard_map/ppermute | solution.py:340
  83.5 7.6 %collective-permute-start.27 = (bf16[256,128]{1,0:T(8,128)(2,1)S(1)}, bf16[256,128]{1,0:T(8,128)(2,1)S(1)}, u32[]{:S(2)}, u32[]{:S(2)}) collective-permute-start(bf16[256,128]{1,0:T(8,128)(2,1)S(1)} %get-tuple-element.65), channel_id=1, source_target_pairs={{0,4},{1,5},{2,6},{3,7},{4,0},{5,1},{6,2},{7,3},{8,12},{9,13},{10,... | collective-permute-start | bytes 196616 | tf_op jit(solution)/shard_map/ppermute | solution.py:340
  84.0 7.1 %collective-permute-start.26 = (bf16[256,128]{1,0:T(8,128)(2,1)S(1)}, bf16[256,128]{1,0:T(8,128)(2,1)S(1)}, u32[]{:S(2)}, u32[]{:S(2)}) collective-permute-start(bf16[256,128]{1,0:T(8,128)(2,1)S(1)} %get-tuple-element.64), channel_id=1, source_target_pairs={{0,2},{1,7},{2,0},{3,5},{4,6},{5,3},{6,4},{7,1},{8,10},{9,15},{10,... | collective-permute-start | bytes 196616 | tf_op jit(solution)/shard_map/ppermute | solution.py:340

commit v10 on v8

--- a/solution.py
+++ b/solution.py
@@ -24,10 +24,6 @@
 SMEM_SPEC = pl.BlockSpec(memory_space=pltpu.SMEM)
 HBM_SPEC = pl.BlockSpec(memory_space=pltpu.HBM)
 PARAMS = pltpu.CompilerParams(vmem_limit_bytes=16 * MIB)
-
-
-def chip_slot(k, core, chips):
-    return jnp.where(core == 0, k, (chips - k) % chips)
 
 
 def row_slot(k, core, nrows):
@@ -75,8 +71,7 @@
     row = tile_row_ref[...]
     rel = (row // per_group) ^ my_col
     chunk = (1 - rel % 2) * HALVES + (row % per_group) // per_half
-    slot = chip_slot(rel // 2, (my_col + rel) % 2, chunk_tiles // per_half)
-    order = chunk * chunk_tiles + slot * per_half + row % per_half
+    order = chunk * chunk_tiles + rel // 2 * per_half + row % per_half
     order = jnp.where(iota((1, slots), 1) < count_ref[0, 0], order, row_tiles).astype(jnp.float32)
     col = tile_col_ref[...]
     source = row_slot((col // per_group) ^ my_row, my_col % 2, nrows) * per_group + col % per_group
@@ -240,8 +235,7 @@
         ids = (rows[:id_rows] * BYTE + rows[id_rows : 2 * id_rows]).astype(jnp.int32)
         rel = (ids // rows_here) ^ my_col
         chunk = (1 - rel % 2) * HALVES + ids % rows_here // half
-        slot = chip_slot(rel // 2, (my_col + rel) % 2, chips)
-        return chunk * chunk_rows + slot * half + ids % half
+        return chunk * chunk_rows + rel // 2 * half + ids % half
 
     def tail(ref):
         return ref[ref.shape[0] - extra :, :].astype(jnp.float32)
@@ -252,7 +246,7 @@
         even.append(rows)
         odd.append(pltpu.roll(rows, extra - extra // 2, 0))
     for k in range(chips):
-        for place, rows in (((chips - k) % chips, places(odd[k])), (chips + k, places(even[k]))):
+        for place, rows in ((k, places(odd[k])), (chips + k, places(even[k]))):
             for r in range(id_rows):
                 at = (place * id_rows + r) * LANES
                 place_ref[0:1, at : at + LANES] = rows[r : r + 1, :]
@@ -330,11 +324,9 @@
         return lax.ppermute(odd, "col", [(i, i ^ 1) for i in range(ncols)])
 
     def send(sent):
-        came = []
-        for slot, part in enumerate(sent, 1):
-            masks = (2 * slot, 2 * (chips - slot))
-            came.append(lax.ppermute(part, "col", [(i, i ^ masks[i % 2]) for i in range(ncols)]))
-        return came
+        return [
+            lax.ppermute(part, "col", [(i, i ^ (2 * k)) for i in range(ncols)]) for k, part in enumerate(sent, 1)
+        ]
 
     def spread(state):
         pieces = [state]

time: 86.6 us -> 87.8 us (1.014); the launches traced: 85.8 us -> 87.9 us
  starting transfers between devices: 41.8 us -> 43.2 us
  transfers between devices with their start and end apart: 33 -> 33, of which waited for: 14 -> 13; matrix products, arithmetic and copies ran while one was open for 1% -> 1% of each run, Pallas kernels for 15% -> 14%
where the time goes in v10:
time: 87.8 us; the launch traced here: 87.9 us
  starting transfers between devices  43.2 us (49%)
  Pallas kernels  23.8 us (27%)
  waiting for transfers between devices  18.3 us (21%)
  other arithmetic  1.71 us (2%)
  between operations  0.88 us (1%)
    pallas_call x18, Pallas kernels, call(): pl.pallas_call(kernel, out_shape=out_shape, grid_spec=pltpu.PrefetchScala...  23.8 us
    ppermute x15, starting transfers between devices, send(): lax.ppermute(part, 'col', [(i, i ^ 2 * k) for i in range(ncols)])  23.1 us
    ppermute x15, starting transfers between devices, spread(): pieces.append(lax.ppermute(state, ('row', 'col'), pairs))  19.9 us
    ppermute x15, waiting for transfers between devices, spread(): pieces.append(lax.ppermute(state, ('row', 'col'), pairs))  10.5 us
    ppermute x15, waiting for transfers between devices, send(): lax.ppermute(part, 'col', [(i, i ^ 2 * k) for i in range(ncols)])  7.44 us
  transfers between devices with their start and end apart: 33, of which 13 were waited for; matrix products, arithmetic and copies ran while one was open for 1% of the time, Pallas kernels for 14%

profile of v10, /device:TPU:0, one launch (start us, length us, event | category | flops | bytes accessed | tf_op | source)
XLA Modules:
  0.0 87.9 jit_solution(17673176933020815989)
XLA Ops:
  0.0 1.1 %begin.1 = (bf16[512,128]{1,0:T(8,128)(2,1)S(1)}, f32[256,128]{1,0:T(8,128)S(1)}, f32[256,128]{1,0:T(8,128)S(1)}) custom-call(s32[4,128]{1,0:T(4,128)} %bitcast.25, bf16[512,128]{1,0:T(8,128)(2,1)} %embed_hbm.1), custom_call_target="tpu_custom_call" | custom-call | tf_op jit(solution)/shard_map/begin/pallas_call | solution.py:308
  1.1 3.0 %collective-permute-start = (bf16[512,128]{1,0:T(8,128)(2,1)S(1)}, bf16[512,128]{1,0:T(8,128)(2,1)S(1)}, u32[]{:S(2)}, u32[]{:S(2)}) collective-permute-start(bf16[512,128]{1,0:T(8,128)(2,1)S(1)} %get-tuple-element.37.refs_0_), channel_id=1, source_target_pairs={{0,8},{1,17},{2,10},{3,19},{4,12},{5,21},{6,14},{7,23},{8,0},{9,25... | collective-permute-start | bytes 393224 | tf_op jit(solution)/shard_map/ppermute | solution.py:338
  4.1 1.5 %collective-permute-start.1 = (bf16[512,128]{1,0:T(8,128)(2,1)S(1)}, bf16[512,128]{1,0:T(8,128)(2,1)S(1)}, u32[]{:S(2)}, u32[]{:S(2)}) collective-permute-start(bf16[512,128]{1,0:T(8,128)(2,1)S(1)} %get-tuple-element.37.refs_0_), channel_id=1, source_target_pairs={{0,16},{1,9},{2,18},{3,11},{4,20},{5,13},{6,22},{7,15},{8,24},{9,1... | collective-permute-start | bytes 393224 | tf_op jit(solution)/shard_map/ppermute | solution.py:338
  5.6 0.0 collective-permute-start.2
  5.6 0.7 fusion.4
  7.0 3.4 %plan.1 = (s32[8,512]{1,0:T(8,128)S(1)}, bf16[256,128,128]{2,1,0:T(8,128)(2,1)S(1)}) custom-call(s32[1,1]{1,0:T(1,128)S(6)} %copy.10.count_ref, s32[1,256]{1,0:T(1,128)} %bitcast.26, s32[1,256]{1,0:T(1,128)} %bitcast.27, bf16[256,128,128]{2,1,0:T(8,128)(2,1)} %bitcast.24), custom_call_target="tpu_custom_call" | custom-call | tf_op jit(solution)/shard_map/plan/pallas_call | solution.py:308
  10.5 1.4 %collective-permute-done.1.refs_2_ = bf16[512,128]{1,0:T(8,128)(2,1)S(1)} collective-permute-done((bf16[512,128]{1,0:T(8,128)(2,1)S(1)}, bf16[512,128]{1,0:T(8,128)(2,1)S(1)}, u32[]{:S(2)}, u32[]{:S(2)}) %collective-permute-start.1) | collective-permute-done | bytes 131104 | tf_op jit(solution)/shard_map/ppermute | solution.py:338
  11.9 2.3 %odd.2 = (bf16[2064,128]{1,0:T(8,128)(2,1)S(1)}, bf16[2176,128]{1,0:T(8,128)(2,1)S(1)}) custom-call(s32[8,512]{1,0:T(8,128)S(1)} %get-tuple-element.36.plan_ref, bf16[512,128]{1,0:T(8,128)(2,1)S(1)} %get-tuple-element.37.refs_0_, bf16[512,128]{1,0:T(8,128)(2,1)S(1)} %collective-permute-done.refs_1_, bf16[512,128]{1,0:T(8,128)(2,1)S(1)} %collective-permute-done.1.refs_2_, ...), custom_call_target="tpu_custom_call" | custom-call | flops 536870912 | bytes 4194304 | tf_op jit(solution)/shard_map/odd/pallas_call | solution.py:308
  14.2 0.1 collective-permute-start.3
  14.3 1.7 %even0.2.even_ref = f32[1024,128]{1,0:T(8,128)S(1)} custom-call(s32[8,512]{1,0:T(8,128)S(1)} %get-tuple-element.36.plan_ref, bf16[2176,128]{1,0:T(8,128)(2,1)S(1)} %get-tuple-element.40.state, bf16[256,128,128]{2,1,0:T(8,128)(2,1)S(1)} %get-tuple-element.38.refs_4_.weights_ref.refs_8_), custom_call_target="tpu_custom_call" | custom-call | flops 268435456 | bytes 2097152 | tf_op jit(solution)/shard_map/even0/pallas_call | solution.py:308
  16.0 0.1 collective-permute-done.3.other_ref
  16.2 0.1 merge.3
  16.2 2.9 %collective-permute-start.7 = (bf16[256,128]{1,0:T(8,128)(2,1)S(1)}, bf16[256,128]{1,0:T(8,128)(2,1)S(1)}, u32[]{:S(2)}, u32[]{:S(2)}) collective-permute-start(bf16[256,128]{1,0:T(8,128)(2,1)S(1)} %get-tuple-element.48), channel_id=1, source_target_pairs={{0,2},{1,3},{2,0},{3,1},{4,6},{5,7},{6,4},{7,5},{8,10},{9,11},{10,... | collective-permute-start | bytes 196616 | tf_op jit(solution)/shard_map/ppermute | solution.py:328
  19.1 1.4 %collective-permute-start.8 = (bf16[256,128]{1,0:T(8,128)(2,1)S(1)}, bf16[256,128]{1,0:T(8,128)(2,1)S(1)}, u32[]{:S(2)}, u32[]{:S(2)}) collective-permute-start(bf16[256,128]{1,0:T(8,128)(2,1)S(1)} %get-tuple-element.49), channel_id=1, source_target_pairs={{0,4},{1,5},{2,6},{3,7},{4,0},{5,1},{6,2},{7,3},{8,12},{9,13},{10,... | collective-permute-start | bytes 196616 | tf_op jit(solution)/shard_map/ppermute | solution.py:328
  20.5 1.1 %collective-permute-start.9 = (bf16[256,128]{1,0:T(8,128)(2,1)S(1)}, bf16[256,128]{1,0:T(8,128)(2,1)S(1)}, u32[]{:S(2)}, u32[]{:S(2)}) collective-permute-start(bf16[256,128]{1,0:T(8,128)(2,1)S(1)} %get-tuple-element.50), channel_id=1, source_target_pairs={{0,6},{1,7},{2,4},{3,5},{4,2},{5,3},{6,0},{7,1},{8,14},{9,15},{10,... | collective-permute-start | bytes 196616 | tf_op jit(solution)/shard_map/ppermute | solution.py:328
  21.5 1.8 %even1.2 = (f32[256,128]{1,0:T(8,128)S(1)}, bf16[272,128]{1,0:T(8,128)(2,1)S(1)}, bf16[272,128]{1,0:T(8,128)(2,1)S(1)}, bf16[272,128]{1,0:T(8,128)(2,1)S(1)}) custom-call(s32[8,512]{1,0:T(8,128)S(1)} %get-tuple-element.36.plan_ref, bf16[2176,128]{1,0:T(8,128)(2,1)S(1)} %get-tuple-element.40.state, ...), custom_call_target="tpu_custom_call" | custom-call | flops 268435456 | bytes 2097152 | tf_op jit(solution)/shard_map/even1/pallas_call | solution.py:308
  23.3 1.6 %collective-permute-start.4 = (bf16[272,128]{1,0:T(8,128)(2,1)S(1)}, bf16[272,128]{1,0:T(8,128)(2,1)S(1)}, u32[]{:S(2)}, u32[]{:S(2)}) collective-permute-start(bf16[272,128]{1,0:T(8,128)(2,1)S(1)} %get-tuple-element.42), channel_id=1, source_target_pairs={{0,2},{1,3},{2,0},{3,1},{4,6},{5,7},{6,4},{7,5},{8,10},{9,11},{10,... | collective-permute-start | bytes 208904 | tf_op jit(solution)/shard_map/ppermute | solution.py:328
  24.9 1.8 %collective-permute-start.5 = (bf16[272,128]{1,0:T(8,128)(2,1)S(1)}, bf16[272,128]{1,0:T(8,128)(2,1)S(1)}, u32[]{:S(2)}, u32[]{:S(2)}) collective-permute-start(bf16[272,128]{1,0:T(8,128)(2,1)S(1)} %get-tuple-element.43), channel_id=1, source_target_pairs={{0,4},{1,5},{2,6},{3,7},{4,0},{5,1},{6,2},{7,3},{8,12},{9,13},{10,... | collective-permute-start | bytes 208904 | tf_op jit(solution)/shard_map/ppermute | solution.py:328
  26.7 1.1 %collective-permute-start.6 = (bf16[272,128]{1,0:T(8,128)(2,1)S(1)}, bf16[272,128]{1,0:T(8,128)(2,1)S(1)}, u32[]{:S(2)}, u32[]{:S(2)}) collective-permute-start(bf16[272,128]{1,0:T(8,128)(2,1)S(1)} %get-tuple-element.44), channel_id=1, source_target_pairs={{0,6},{1,7},{2,4},{3,5},{4,2},{5,3},{6,0},{7,1},{8,14},{9,15},{10,... | collective-permute-start | bytes 208904 | tf_op jit(solution)/shard_map/ppermute | solution.py:328
  27.9 0.9 %collective-permute-start.13 = (bf16[256,128]{1,0:T(8,128)(2,1)S(1)}, bf16[256,128]{1,0:T(8,128)(2,1)S(1)}, u32[]{:S(2)}, u32[]{:S(2)}) collective-permute-start(bf16[256,128]{1,0:T(8,128)(2,1)S(1)} %state.4.refs_3_.refs_4_), channel_id=1, source_target_pairs={{0,8},{1,17},{2,10},{3,19},{4,12},{5,21},{6,14},{7,23},{8,0},{9,25... | collective-permute-start | bytes 196616 | tf_op jit(solution)/shard_map/ppermute | solution.py:338
  28.8 2.5 %collective-permute-start.14 = (bf16[256,128]{1,0:T(8,128)(2,1)S(1)}, bf16[256,128]{1,0:T(8,128)(2,1)S(1)}, u32[]{:S(2)}, u32[]{:S(2)}) collective-permute-start(bf16[256,128]{1,0:T(8,128)(2,1)S(1)} %state.4.refs_3_.refs_4_), channel_id=1, source_target_pairs={{0,16},{1,9},{2,18},{3,11},{4,20},{5,13},{6,22},{7,15},{8,24},{9,1... | collective-permute-start | bytes 196616 | tf_op jit(solution)/shard_map/ppermute | solution.py:338
  31.3 0.4 collective-permute-start.15
  31.7 1.2 %collective-permute-done.5.refs_1_ = bf16[272,128]{1,0:T(8,128)(2,1)S(1)} collective-permute-done((bf16[272,128]{1,0:T(8,128)(2,1)S(1)}, bf16[272,128]{1,0:T(8,128)(2,1)S(1)}, u32[]{:S(2)}, u32[]{:S(2)}) %collective-permute-start.5) | collective-permute-done | bytes 69664 | tf_op jit(solution)/shard_map/ppermute | solution.py:328
  33.0 2.0 %collective-permute-start.10 = (bf16[256,128]{1,0:T(8,128)(2,1)S(1)}, bf16[256,128]{1,0:T(8,128)(2,1)S(1)}, u32[]{:S(2)}, u32[]{:S(2)}) collective-permute-start(bf16[256,128]{1,0:T(8,128)(2,1)S(1)} %state.5.refs_0_), channel_id=1, source_target_pairs={{0,8},{1,17},{2,10},{3,19},{4,12},{5,21},{6,14},{7,23},{8,0},{9,25... | collective-permute-start | bytes 196616 | tf_op jit(solution)/shard_map/ppermute | solution.py:338
  35.0 2.4 %collective-permute-start.11 = (bf16[256,128]{1,0:T(8,128)(2,1)S(1)}, bf16[256,128]{1,0:T(8,128)(2,1)S(1)}, u32[]{:S(2)}, u32[]{:S(2)}) collective-permute-start(bf16[256,128]{1,0:T(8,128)(2,1)S(1)} %state.5.refs_0_), channel_id=1, source_target_pairs={{0,16},{1,9},{2,18},{3,11},{4,20},{5,13},{6,22},{7,15},{8,24},{9,1... | collective-permute-start | bytes 196616 | tf_op jit(solution)/shard_map/ppermute | solution.py:338
  37.4 0.6 collective-permute-done.10.refs_1_
  38.0 1.7 %collective-permute-done.11.refs_2_ = bf16[256,128]{1,0:T(8,128)(2,1)S(1)} collective-permute-done((bf16[256,128]{1,0:T(8,128)(2,1)S(1)}, bf16[256,128]{1,0:T(8,128)(2,1)S(1)}, u32[]{:S(2)}, u32[]{:S(2)}) %collective-permute-start.11) | collective-permute-done | bytes 65568 | tf_op jit(solution)/shard_map/ppermute | solution.py:338
  39.6 2.9 %collective-permute-done.12.refs_3_ = bf16[256,128]{1,0:T(8,128)(2,1)S(1)} collective-permute-done((bf16[256,128]{1,0:T(8,128)(2,1)S(1)}, bf16[256,128]{1,0:T(8,128)(2,1)S(1)}, u32[]{:S(2)}, u32[]{:S(2)}) %collective-permute-start.12) | collective-permute-done | bytes 65568 | tf_op jit(solution)/shard_map/ppermute | solution.py:338
  42.5 2.3 %odd.3 = (bf16[2064,128]{1,0:T(8,128)(2,1)S(1)}, bf16[2176,128]{1,0:T(8,128)(2,1)S(1)}) custom-call(s32[8,512]{1,0:T(8,128)S(1)} %get-tuple-element.36.plan_ref, bf16[256,128]{1,0:T(8,128)(2,1)S(1)} %state.5.refs_0_, bf16[256,128]{1,0:T(8,128)(2,1)S(1)} %collective-permute-done.10.refs_1_, bf16[256,128]{1,0:T(8,128)(2,1)S(1)} %collective-permute-done.11.refs_2_, ...), custom_call_target="tpu_custom_call" | custom-call | flops 536870912 | bytes 4194304 | tf_op jit(solution)/shard_map/odd/pallas_call | solution.py:308
  44.9 0.1 collective-permute-start.16
  44.9 1.7 %even0.3.even_ref = f32[1024,128]{1,0:T(8,128)S(1)} custom-call(s32[8,512]{1,0:T(8,128)S(1)} %get-tuple-element.36.plan_ref, bf16[2176,128]{1,0:T(8,128)(2,1)S(1)} %get-tuple-element.51.state, bf16[256,128,128]{2,1,0:T(8,128)(2,1)S(1)} %get-tuple-element.38.refs_4_.weights_ref.refs_8_), custom_call_target="tpu_custom_call" | custom-call | flops 268435456 | bytes 2097152 | tf_op jit(solution)/shard_map/even0/pallas_call | solution.py:308
  46.7 0.2 collective-permute-done.16.other_ref
  46.8 0.1 merge.4
  46.9 0.6 collective-permute-start.20
  47.5 1.4 %collective-permute-start.21 = (bf16[256,128]{1,0:T(8,128)(2,1)S(1)}, bf16[256,128]{1,0:T(8,128)(2,1)S(1)}, u32[]{:S(2)}, u32[]{:S(2)}) collective-permute-start(bf16[256,128]{1,0:T(8,128)(2,1)S(1)} %get-tuple-element.59), channel_id=1, source_target_pairs={{0,4},{1,5},{2,6},{3,7},{4,0},{5,1},{6,2},{7,3},{8,12},{9,13},{10,... | collective-permute-start | bytes 196616 | tf_op jit(solution)/shard_map/ppermute | solution.py:328
  48.9 2.5 %collective-permute-start.22 = (bf16[256,128]{1,0:T(8,128)(2,1)S(1)}, bf16[256,128]{1,0:T(8,128)(2,1)S(1)}, u32[]{:S(2)}, u32[]{:S(2)}) collective-permute-start(bf16[256,128]{1,0:T(8,128)(2,1)S(1)} %get-tuple-element.60), channel_id=1, source_target_pairs={{0,6},{1,7},{2,4},{3,5},{4,2},{5,3},{6,0},{7,1},{8,14},{9,15},{10,... | collective-permute-start | bytes 196616 | tf_op jit(solution)/shard_map/ppermute | solution.py:328
  51.4 1.8 %even1.3 = (f32[256,128]{1,0:T(8,128)S(1)}, bf16[272,128]{1,0:T(8,128)(2,1)S(1)}, bf16[272,128]{1,0:T(8,128)(2,1)S(1)}, bf16[272,128]{1,0:T(8,128)(2,1)S(1)}) custom-call(s32[8,512]{1,0:T(8,128)S(1)} %get-tuple-element.36.plan_ref, bf16[2176,128]{1,0:T(8,128)(2,1)S(1)} %get-tuple-element.51.state, ...), custom_call_target="tpu_custom_call" | custom-call | flops 268435456 | bytes 2097152 | tf_op jit(solution)/shard_map/even1/pallas_call | solution.py:308
  53.2 0.0 copy-start
  53.2 0.1 collective-permute-start.17
  53.3 1.9 %collective-permute-start.18 = (bf16[272,128]{1,0:T(8,128)(2,1)S(1)}, bf16[272,128]{1,0:T(8,128)(2,1)S(1)}, u32[]{:S(2)}, u32[]{:S(2)}) collective-permute-start(bf16[272,128]{1,0:T(8,128)(2,1)S(1)} %get-tuple-element.56), channel_id=1, source_target_pairs={{0,4},{1,5},{2,6},{3,7},{4,0},{5,1},{6,2},{7,3},{8,12},{9,13},{10,... | collective-permute-start | bytes 208904 | tf_op jit(solution)/shard_map/ppermute | solution.py:328
  55.2 2.5 %collective-permute-start.19 = (bf16[272,128]{1,0:T(8,128)(2,1)S(1)}, bf16[272,128]{1,0:T(8,128)(2,1)S(1)}, u32[]{:S(2)}, u32[]{:S(2)}) collective-permute-start(bf16[272,128]{1,0:T(8,128)(2,1)S(1)} %get-tuple-element.57), channel_id=1, source_target_pairs={{0,6},{1,7},{2,4},{3,5},{4,2},{5,3},{6,0},{7,1},{8,14},{9,15},{10,... | collective-permute-start | bytes 208904 | tf_op jit(solution)/shard_map/ppermute | solution.py:328
  57.7 0.1 collective-permute-start.26
  57.9 1.7 %collective-permute-start.27 = (bf16[256,128]{1,0:T(8,128)(2,1)S(1)}, bf16[256,128]{1,0:T(8,128)(2,1)S(1)}, u32[]{:S(2)}, u32[]{:S(2)}) collective-permute-start(bf16[256,128]{1,0:T(8,128)(2,1)S(1)} %state.6.refs_3_.refs_4_), channel_id=1, source_target_pairs={{0,16},{1,9},{2,18},{3,11},{4,20},{5,13},{6,22},{7,15},{8,24},{9,1... | collective-permute-start | bytes 196616 | tf_op jit(solution)/shard_map/ppermute | solution.py:338
  59.5 1.8 %collective-permute-start.28 = (bf16[256,128]{1,0:T(8,128)(2,1)S(1)}, bf16[256,128]{1,0:T(8,128)(2,1)S(1)}, u32[]{:S(2)}, u32[]{:S(2)}) collective-permute-start(bf16[256,128]{1,0:T(8,128)(2,1)S(1)} %state.6.refs_3_.refs_4_), channel_id=1, source_target_pairs={{0,24},{1,25},{2,26},{3,27},{4,28},{5,29},{6,30},{7,31},{8,16},{9,... | collective-permute-start | bytes 196616 | tf_op jit(solution)/shard_map/ppermute | solution.py:338
  61.3 0.6 collective-permute-done.18.refs_1_
  61.9 0.9 %collective-permute-start.23 = (bf16[256,128]{1,0:T(8,128)(2,1)S(1)}, bf16[256,128]{1,0:T(8,128)(2,1)S(1)}, u32[]{:S(2)}, u32[]{:S(2)}) collective-permute-start(bf16[256,128]{1,0:T(8,128)(2,1)S(1)} %state.7.refs_0_), channel_id=1, source_target_pairs={{0,8},{1,17},{2,10},{3,19},{4,12},{5,21},{6,14},{7,23},{8,0},{9,25... | collective-permute-start | bytes 196616 | tf_op jit(solution)/shard_map/ppermute | solution.py:338
  62.8 1.5 %collective-permute-start.24 = (bf16[256,128]{1,0:T(8,128)(2,1)S(1)}, bf16[256,128]{1,0:T(8,128)(2,1)S(1)}, u32[]{:S(2)}, u32[]{:S(2)}) collective-permute-start(bf16[256,128]{1,0:T(8,128)(2,1)S(1)} %state.7.refs_0_), channel_id=1, source_target_pairs={{0,16},{1,9},{2,18},{3,11},{4,20},{5,13},{6,22},{7,15},{8,24},{9,1... | collective-permute-start | bytes 196616 | tf_op jit(solution)/shard_map/ppermute | solution.py:338
  64.4 1.1 %collective-permute-start.25 = (bf16[256,128]{1,0:T(8,128)(2,1)S(1)}, bf16[256,128]{1,0:T(8,128)(2,1)S(1)}, u32[]{:S(2)}, u32[]{:S(2)}) collective-permute-start(bf16[256,128]{1,0:T(8,128)(2,1)S(1)} %state.7.refs_0_), channel_id=1, source_target_pairs={{0,24},{1,25},{2,26},{3,27},{4,28},{5,29},{6,30},{7,31},{8,16},{9,... | collective-permute-start | bytes 196616 | tf_op jit(solution)/shard_map/ppermute | solution.py:338
  65.5 0.1 place.1.place_ref
  65.6 0.6 collective-permute-done.23.refs_1_
  66.2 0.9 collective-permute-done.24.refs_2_
  67.1 2.4 %collective-permute-done.25.refs_3_ = bf16[256,128]{1,0:T(8,128)(2,1)S(1)} collective-permute-done((bf16[256,128]{1,0:T(8,128)(2,1)S(1)}, bf16[256,128]{1,0:T(8,128)(2,1)S(1)}, u32[]{:S(2)}, u32[]{:S(2)}) %collective-permute-start.25) | collective-permute-done | bytes 65568 | tf_op jit(solution)/shard_map/ppermute | solution.py:338
  69.5 5.4 %last.1 = (bf16[1024,128]{1,0:T(8,128)(2,1)S(1)}, f32[4096,128]{1,0:T(8,128)S(1)}) custom-call(s32[8,512]{1,0:T(8,128)S(1)} %get-tuple-element.36.plan_ref, s32[1,2048]{1,0:T(1,128)S(1)} %place.1.place_ref, bf16[256,128]{1,0:T(8,128)(2,1)S(1)} %state.7.refs_0_, bf16[256,128]{1,0:T(8,128)(2,1)S(1)} %collective-permute-done.23.refs_1_, ...), custom_call_target="tpu_custom_call" | custom-call | flops 1073741824 | bytes 8388608 | tf_op jit(solution)/shard_map/last/pallas_call | solution.py:308
  74.9 0.1 collective-permute-start.29
  75.0 1.7 %pick.1.even_ref = f32[1024,128]{1,0:T(8,128)S(1)} custom-call(s32[1,2048]{1,0:T(1,128)S(1)} %place.1.place_ref, f32[4096,128]{1,0:T(8,128)S(1)} %get-tuple-element.61.total), custom_call_target="tpu_custom_call" | custom-call | flops 214748368 | bytes 1677721 | tf_op jit(solution)/shard_map/pick/pallas_call | solution.py:308
  76.8 0.1 merge.5
  76.8 1.4 %collective-permute-start.32 = (bf16[256,128]{1,0:T(8,128)(2,1)S(1)}, bf16[256,128]{1,0:T(8,128)(2,1)S(1)}, u32[]{:S(2)}, u32[]{:S(2)}) collective-permute-start(bf16[256,128]{1,0:T(8,128)(2,1)S(1)} %get-tuple-element.66), channel_id=1, source_target_pairs={{0,6},{1,7},{2,4},{3,5},{4,2},{5,3},{6,0},{7,1},{8,14},{9,15},{10,... | collective-permute-start | bytes 196616 | tf_op jit(solution)/shard_map/ppermute | solution.py:328
  78.2 2.1 %collective-permute-start.31 = (bf16[256,128]{1,0:T(8,128)(2,1)S(1)}, bf16[256,128]{1,0:T(8,128)(2,1)S(1)}, u32[]{:S(2)}, u32[]{:S(2)}) collective-permute-start(bf16[256,128]{1,0:T(8,128)(2,1)S(1)} %get-tuple-element.65), channel_id=1, source_target_pairs={{0,4},{1,5},{2,6},{3,7},{4,0},{5,1},{6,2},{7,3},{8,12},{9,13},{10,... | collective-permute-start | bytes 196616 | tf_op jit(solution)/shard_map/ppermute | solution.py:328
  80.3 1.0 %collective-permute-start.30 = (bf16[256,128]{1,0:T(8,128)(2,1)S(1)}, bf16[256,128]{1,0:T(8,128)(2,1)S(1)}, u32[]{:S(2)}, u32[]{:S(2)}) collective-permute-start(bf16[256,128]{1,0:T(8,128)(2,1)S(1)} %get-tuple-element.64), channel_id=1, source_target_pairs={{0,2},{1,3},{2,0},{3,1},{4,6},{5,7},{6,4},{7,5},{8,10},{9,11},{10,... | collective-permute-start | bytes 196616 | tf_op jit(solution)/shard_map/ppermute | solution.py:328
  81.3 0.1 select_reduce_fusion
  81.4 2.3 %collective-permute-done.32 = bf16[256,128]{1,0:T(8,128)(2,1)S(1)} collective-permute-done((bf16[256,128]{1,0:T(8,128)(2,1)S(1)}, bf16[256,128]{1,0:T(8,128)(2,1)S(1)}, u32[]{:S(2)}, u32[]{:S(2)}) %collective-permute-start.32) | collective-permute-done | bytes 65568 | tf_op jit(solution)/shard_map/ppermute | solution.py:328
  83.7 3.3 %collective-permute-done.31 = bf16[256,128]{1,0:T(8,128)(2,1)S(1)} collective-permute-done((bf16[256,128]{1,0:T(8,128)(2,1)S(1)}, bf16[256,128]{1,0:T(8,128)(2,1)S(1)}, u32[]{:S(2)}, u32[]{:S(2)}) %collective-permute-start.31) | collective-permute-done | bytes 65568 | tf_op jit(solution)/shard_map/ppermute | solution.py:328
  87.0 0.1 multiply_reduce_fusion
  87.1 0.8 multiply_multiply_fusion
  (30 shorter events, 0.3 us)
Async XLA Ops:
  1.1 9.4 %collective-permute-start = (bf16[512,128]{1,0:T(8,128)(2,1)S(1)}, bf16[512,128]{1,0:T(8,128)(2,1)S(1)}, u32[]{:S(2)}, u32[]{:S(2)}) collective-permute-start(bf16[512,128]{1,0:T(8,128)(2,1)S(1)} %get-tuple-element.37.refs_0_), channel_id=1, source_target_pairs={{0,8},{1,17},{2,10},{3,19},{4,12},{5,21},{6,14},{7,23},{8,0},{9,25... | collective-permute-start | bytes 393224 | tf_op jit(solution)/shard_map/ppermute | solution.py:338
  4.1 7.8 %collective-permute-start.1 = (bf16[512,128]{1,0:T(8,128)(2,1)S(1)}, bf16[512,128]{1,0:T(8,128)(2,1)S(1)}, u32[]{:S(2)}, u32[]{:S(2)}) collective-permute-start(bf16[512,128]{1,0:T(8,128)(2,1)S(1)} %get-tuple-element.37.refs_0_), channel_id=1, source_target_pairs={{0,16},{1,9},{2,18},{3,11},{4,20},{5,13},{6,22},{7,15},{8,24},{9,1... | collective-permute-start | bytes 393224 | tf_op jit(solution)/shard_map/ppermute | solution.py:338
  5.6 6.3 %collective-permute-start.2 = (bf16[512,128]{1,0:T(8,128)(2,1)S(1)}, bf16[512,128]{1,0:T(8,128)(2,1)S(1)}, u32[]{:S(2)}, u32[]{:S(2)}) collective-permute-start(bf16[512,128]{1,0:T(8,128)(2,1)S(1)} %get-tuple-element.37.refs_0_), channel_id=1, source_target_pairs={{0,24},{1,25},{2,26},{3,27},{4,28},{5,29},{6,30},{7,31},{8,16},{9,... | collective-permute-start | bytes 393224 | tf_op jit(solution)/shard_map/ppermute | solution.py:338
  14.2 2.0 %collective-permute-start.3 = (bf16[2064,128]{1,0:T(8,128)(2,1)S(1)}, bf16[2064,128]{1,0:T(8,128)(2,1)S(1)}, u32[]{:S(2)}, u32[]{:S(2)}) collective-permute-start(bf16[2064,128]{1,0:T(8,128)(2,1)S(1)} %get-tuple-element.39), channel_id=1, source_target_pairs={{0,1},{1,0},{2,3},{3,2},{4,5},{5,4},{6,7},{7,6},{8,9},{9,8},{10,11... | collective-permute-start | bytes 1585160 | tf_op jit(solution)/shard_map/ppermute | solution.py:324
  16.2 10.5 %collective-permute-start.7 = (bf16[256,128]{1,0:T(8,128)(2,1)S(1)}, bf16[256,128]{1,0:T(8,128)(2,1)S(1)}, u32[]{:S(2)}, u32[]{:S(2)}) collective-permute-start(bf16[256,128]{1,0:T(8,128)(2,1)S(1)} %get-tuple-element.48), channel_id=1, source_target_pairs={{0,2},{1,3},{2,0},{3,1},{4,6},{5,7},{6,4},{7,5},{8,10},{9,11},{10,... | collective-permute-start | bytes 196616 | tf_op jit(solution)/shard_map/ppermute | solution.py:328
  19.1 8.7 %collective-permute-start.8 = (bf16[256,128]{1,0:T(8,128)(2,1)S(1)}, bf16[256,128]{1,0:T(8,128)(2,1)S(1)}, u32[]{:S(2)}, u32[]{:S(2)}) collective-permute-start(bf16[256,128]{1,0:T(8,128)(2,1)S(1)} %get-tuple-element.49), channel_id=1, source_target_pairs={{0,4},{1,5},{2,6},{3,7},{4,0},{5,1},{6,2},{7,3},{8,12},{9,13},{10,... | collective-permute-start | bytes 196616 | tf_op jit(solution)/shard_map/ppermute | solution.py:328
  20.5 7.3 %collective-permute-start.9 = (bf16[256,128]{1,0:T(8,128)(2,1)S(1)}, bf16[256,128]{1,0:T(8,128)(2,1)S(1)}, u32[]{:S(2)}, u32[]{:S(2)}) collective-permute-start(bf16[256,128]{1,0:T(8,128)(2,1)S(1)} %get-tuple-element.50), channel_id=1, source_target_pairs={{0,6},{1,7},{2,4},{3,5},{4,2},{5,3},{6,0},{7,1},{8,14},{9,15},{10,... | collective-permute-start | bytes 196616 | tf_op jit(solution)/shard_map/ppermute | solution.py:328
  23.3 7.9 %collective-permute-start.4 = (bf16[272,128]{1,0:T(8,128)(2,1)S(1)}, bf16[272,128]{1,0:T(8,128)(2,1)S(1)}, u32[]{:S(2)}, u32[]{:S(2)}) collective-permute-start(bf16[272,128]{1,0:T(8,128)(2,1)S(1)} %get-tuple-element.42), channel_id=1, source_target_pairs={{0,2},{1,3},{2,0},{3,1},{4,6},{5,7},{6,4},{7,5},{8,10},{9,11},{10,... | collective-permute-start | bytes 208904 | tf_op jit(solution)/shard_map/ppermute | solution.py:328
  24.9 8.1 %collective-permute-start.5 = (bf16[272,128]{1,0:T(8,128)(2,1)S(1)}, bf16[272,128]{1,0:T(8,128)(2,1)S(1)}, u32[]{:S(2)}, u32[]{:S(2)}) collective-permute-start(bf16[272,128]{1,0:T(8,128)(2,1)S(1)} %get-tuple-element.43), channel_id=1, source_target_pairs={{0,4},{1,5},{2,6},{3,7},{4,0},{5,1},{6,2},{7,3},{8,12},{9,13},{10,... | collective-permute-start | bytes 208904 | tf_op jit(solution)/shard_map/ppermute | solution.py:328
  26.7 6.2 %collective-permute-start.6 = (bf16[272,128]{1,0:T(8,128)(2,1)S(1)}, bf16[272,128]{1,0:T(8,128)(2,1)S(1)}, u32[]{:S(2)}, u32[]{:S(2)}) collective-permute-start(bf16[272,128]{1,0:T(8,128)(2,1)S(1)} %get-tuple-element.44), channel_id=1, source_target_pairs={{0,6},{1,7},{2,4},{3,5},{4,2},{5,3},{6,0},{7,1},{8,14},{9,15},{10,... | collective-permute-start | bytes 208904 | tf_op jit(solution)/shard_map/ppermute | solution.py:328
  27.9 9.5 %collective-permute-start.13 = (bf16[256,128]{1,0:T(8,128)(2,1)S(1)}, bf16[256,128]{1,0:T(8,128)(2,1)S(1)}, u32[]{:S(2)}, u32[]{:S(2)}) collective-permute-start(bf16[256,128]{1,0:T(8,128)(2,1)S(1)} %state.4.refs_3_.refs_4_), channel_id=1, source_target_pairs={{0,8},{1,17},{2,10},{3,19},{4,12},{5,21},{6,14},{7,23},{8,0},{9,25... | collective-permute-start | bytes 196616 | tf_op jit(solution)/shard_map/ppermute | solution.py:338
  28.8 8.6 %collective-permute-start.14 = (bf16[256,128]{1,0:T(8,128)(2,1)S(1)}, bf16[256,128]{1,0:T(8,128)(2,1)S(1)}, u32[]{:S(2)}, u32[]{:S(2)}) collective-permute-start(bf16[256,128]{1,0:T(8,128)(2,1)S(1)} %state.4.refs_3_.refs_4_), channel_id=1, source_target_pairs={{0,16},{1,9},{2,18},{3,11},{4,20},{5,13},{6,22},{7,15},{8,24},{9,1... | collective-permute-start | bytes 196616 | tf_op jit(solution)/shard_map/ppermute | solution.py:338
  31.3 6.1 %collective-permute-start.15 = (bf16[256,128]{1,0:T(8,128)(2,1)S(1)}, bf16[256,128]{1,0:T(8,128)(2,1)S(1)}, u32[]{:S(2)}, u32[]{:S(2)}) collective-permute-start(bf16[256,128]{1,0:T(8,128)(2,1)S(1)} %state.4.refs_3_.refs_4_), channel_id=1, source_target_pairs={{0,24},{1,25},{2,26},{3,27},{4,28},{5,29},{6,30},{7,31},{8,16},{9,... | collective-permute-start | bytes 196616 | tf_op jit(solution)/shard_map/ppermute | solution.py:338
  33.0 4.9 %collective-permute-start.10 = (bf16[256,128]{1,0:T(8,128)(2,1)S(1)}, bf16[256,128]{1,0:T(8,128)(2,1)S(1)}, u32[]{:S(2)}, u32[]{:S(2)}) collective-permute-start(bf16[256,128]{1,0:T(8,128)(2,1)S(1)} %state.5.refs_0_), channel_id=1, source_target_pairs={{0,8},{1,17},{2,10},{3,19},{4,12},{5,21},{6,14},{7,23},{8,0},{9,25... | collective-permute-start | bytes 196616 | tf_op jit(solution)/shard_map/ppermute | solution.py:338
  35.0 4.6 %collective-permute-start.11 = (bf16[256,128]{1,0:T(8,128)(2,1)S(1)}, bf16[256,128]{1,0:T(8,128)(2,1)S(1)}, u32[]{:S(2)}, u32[]{:S(2)}) collective-permute-start(bf16[256,128]{1,0:T(8,128)(2,1)S(1)} %state.5.refs_0_), channel_id=1, source_target_pairs={{0,16},{1,9},{2,18},{3,11},{4,20},{5,13},{6,22},{7,15},{8,24},{9,1... | collective-permute-start | bytes 196616 | tf_op jit(solution)/shard_map/ppermute | solution.py:338
  37.4 5.2 %collective-permute-start.12 = (bf16[256,128]{1,0:T(8,128)(2,1)S(1)}, bf16[256,128]{1,0:T(8,128)(2,1)S(1)}, u32[]{:S(2)}, u32[]{:S(2)}) collective-permute-start(bf16[256,128]{1,0:T(8,128)(2,1)S(1)} %state.5.refs_0_), channel_id=1, source_target_pairs={{0,24},{1,25},{2,26},{3,27},{4,28},{5,29},{6,30},{7,31},{8,16},{9,... | collective-permute-start | bytes 196616 | tf_op jit(solution)/shard_map/ppermute | solution.py:338
  44.9 2.0 %collective-permute-start.16 = (bf16[2064,128]{1,0:T(8,128)(2,1)S(1)}, bf16[2064,128]{1,0:T(8,128)(2,1)S(1)}, u32[]{:S(2)}, u32[]{:S(2)}) collective-permute-start(bf16[2064,128]{1,0:T(8,128)(2,1)S(1)} %get-tuple-element.52), channel_id=1, source_target_pairs={{0,1},{1,0},{2,3},{3,2},{4,5},{5,4},{6,7},{7,6},{8,9},{9,8},{10,11... | collective-permute-start | bytes 1585160 | tf_op jit(solution)/shard_map/ppermute | solution.py:324
  46.9 8.3 %collective-permute-start.20 = (bf16[256,128]{1,0:T(8,128)(2,1)S(1)}, bf16[256,128]{1,0:T(8,128)(2,1)S(1)}, u32[]{:S(2)}, u32[]{:S(2)}) collective-permute-start(bf16[256,128]{1,0:T(8,128)(2,1)S(1)} %get-tuple-element.58), channel_id=1, source_target_pairs={{0,2},{1,3},{2,0},{3,1},{4,6},{5,7},{6,4},{7,5},{8,10},{9,11},{10,... | collective-permute-start | bytes 196616 | tf_op jit(solution)/shard_map/ppermute | solution.py:328
  47.5 10.2 %collective-permute-start.21 = (bf16[256,128]{1,0:T(8,128)(2,1)S(1)}, bf16[256,128]{1,0:T(8,128)(2,1)S(1)}, u32[]{:S(2)}, u32[]{:S(2)}) collective-permute-start(bf16[256,128]{1,0:T(8,128)(2,1)S(1)} %get-tuple-element.59), channel_id=1, source_target_pairs={{0,4},{1,5},{2,6},{3,7},{4,0},{5,1},{6,2},{7,3},{8,12},{9,13},{10,... | collective-permute-start | bytes 196616 | tf_op jit(solution)/shard_map/ppermute | solution.py:328
  48.9 8.8 %collective-permute-start.22 = (bf16[256,128]{1,0:T(8,128)(2,1)S(1)}, bf16[256,128]{1,0:T(8,128)(2,1)S(1)}, u32[]{:S(2)}, u32[]{:S(2)}) collective-permute-start(bf16[256,128]{1,0:T(8,128)(2,1)S(1)} %get-tuple-element.60), channel_id=1, source_target_pairs={{0,6},{1,7},{2,4},{3,5},{4,2},{5,3},{6,0},{7,1},{8,14},{9,15},{10,... | collective-permute-start | bytes 196616 | tf_op jit(solution)/shard_map/ppermute | solution.py:328
  53.2 28.1 %copy-start = (s32[256]{0:T(256)S(1)}, s32[256]{0:T(256)}, u32[]{:S(2)}) copy-start(s32[256]{0:T(256)} %param.16) | copy-start | bytes 3076
  53.2 28.1 %copy-start.1 = (f32[16]{0:T(128)S(1)}, f32[16]{0:T(128)}, u32[]{:S(2)}) copy-start(f32[16]{0:T(128)} %param.17) | copy-start | bytes 196
  53.2 6.3 %collective-permute-start.17 = (bf16[272,128]{1,0:T(8,128)(2,1)S(1)}, bf16[272,128]{1,0:T(8,128)(2,1)S(1)}, u32[]{:S(2)}, u32[]{:S(2)}) collective-permute-start(bf16[272,128]{1,0:T(8,128)(2,1)S(1)} %get-tuple-element.55), channel_id=1, source_target_pairs={{0,2},{1,3},{2,0},{3,1},{4,6},{5,7},{6,4},{7,5},{8,10},{9,11},{10,... | collective-permute-start | bytes 208904 | tf_op jit(solution)/shard_map/ppermute | solution.py:328
  53.3 8.5 %collective-permute-start.18 = (bf16[272,128]{1,0:T(8,128)(2,1)S(1)}, bf16[272,128]{1,0:T(8,128)(2,1)S(1)}, u32[]{:S(2)}, u32[]{:S(2)}) collective-permute-start(bf16[272,128]{1,0:T(8,128)(2,1)S(1)} %get-tuple-element.56), channel_id=1, source_target_pairs={{0,4},{1,5},{2,6},{3,7},{4,0},{5,1},{6,2},{7,3},{8,12},{9,13},{10,... | collective-permute-start | bytes 208904 | tf_op jit(solution)/shard_map/ppermute | solution.py:328
  55.2 6.7 %collective-permute-start.19 = (bf16[272,128]{1,0:T(8,128)(2,1)S(1)}, bf16[272,128]{1,0:T(8,128)(2,1)S(1)}, u32[]{:S(2)}, u32[]{:S(2)}) collective-permute-start(bf16[272,128]{1,0:T(8,128)(2,1)S(1)} %get-tuple-element.57), channel_id=1, source_target_pairs={{0,6},{1,7},{2,4},{3,5},{4,2},{5,3},{6,0},{7,1},{8,14},{9,15},{10,... | collective-permute-start | bytes 208904 | tf_op jit(solution)/shard_map/ppermute | solution.py:328
  57.7 6.6 %collective-permute-start.26 = (bf16[256,128]{1,0:T(8,128)(2,1)S(1)}, bf16[256,128]{1,0:T(8,128)(2,1)S(1)}, u32[]{:S(2)}, u32[]{:S(2)}) collective-permute-start(bf16[256,128]{1,0:T(8,128)(2,1)S(1)} %state.6.refs_3_.refs_4_), channel_id=1, source_target_pairs={{0,8},{1,17},{2,10},{3,19},{4,12},{5,21},{6,14},{7,23},{8,0},{9,25... | collective-permute-start | bytes 196616 | tf_op jit(solution)/shard_map/ppermute | solution.py:338
  57.9 7.7 %collective-permute-start.27 = (bf16[256,128]{1,0:T(8,128)(2,1)S(1)}, bf16[256,128]{1,0:T(8,128)(2,1)S(1)}, u32[]{:S(2)}, u32[]{:S(2)}) collective-permute-start(bf16[256,128]{1,0:T(8,128)(2,1)S(1)} %state.6.refs_3_.refs_4_), channel_id=1, source_target_pairs={{0,16},{1,9},{2,18},{3,11},{4,20},{5,13},{6,22},{7,15},{8,24},{9,1... | collective-permute-start | bytes 196616 | tf_op jit(solution)/shard_map/ppermute | solution.py:338
  59.5 6.0 %collective-permute-start.28 = (bf16[256,128]{1,0:T(8,128)(2,1)S(1)}, bf16[256,128]{1,0:T(8,128)(2,1)S(1)}, u32[]{:S(2)}, u32[]{:S(2)}) collective-permute-start(bf16[256,128]{1,0:T(8,128)(2,1)S(1)} %state.6.refs_3_.refs_4_), channel_id=1, source_target_pairs={{0,24},{1,25},{2,26},{3,27},{4,28},{5,29},{6,30},{7,31},{8,16},{9,... | collective-permute-start | bytes 196616 | tf_op jit(solution)/shard_map/ppermute | solution.py:338
  61.9 4.3 %collective-permute-start.23 = (bf16[256,128]{1,0:T(8,128)(2,1)S(1)}, bf16[256,128]{1,0:T(8,128)(2,1)S(1)}, u32[]{:S(2)}, u32[]{:S(2)}) collective-permute-start(bf16[256,128]{1,0:T(8,128)(2,1)S(1)} %state.7.refs_0_), channel_id=1, source_target_pairs={{0,8},{1,17},{2,10},{3,19},{4,12},{5,21},{6,14},{7,23},{8,0},{9,25... | collective-permute-start | bytes 196616 | tf_op jit(solution)/shard_map/ppermute | solution.py:338
  62.8 4.3 %collective-permute-start.24 = (bf16[256,128]{1,0:T(8,128)(2,1)S(1)}, bf16[256,128]{1,0:T(8,128)(2,1)S(1)}, u32[]{:S(2)}, u32[]{:S(2)}) collective-permute-start(bf16[256,128]{1,0:T(8,128)(2,1)S(1)} %state.7.refs_0_), channel_id=1, source_target_pairs={{0,16},{1,9},{2,18},{3,11},{4,20},{5,13},{6,22},{7,15},{8,24},{9,1... | collective-permute-start | bytes 196616 | tf_op jit(solution)/shard_map/ppermute | solution.py:338
  64.4 5.2 %collective-permute-start.25 = (bf16[256,128]{1,0:T(8,128)(2,1)S(1)}, bf16[256,128]{1,0:T(8,128)(2,1)S(1)}, u32[]{:S(2)}, u32[]{:S(2)}) collective-permute-start(bf16[256,128]{1,0:T(8,128)(2,1)S(1)} %state.7.refs_0_), channel_id=1, source_target_pairs={{0,24},{1,25},{2,26},{3,27},{4,28},{5,29},{6,30},{7,31},{8,16},{9,... | collective-permute-start | bytes 196616 | tf_op jit(solution)/shard_map/ppermute | solution.py:338
  74.9 1.8 %collective-permute-start.29 = (bf16[1024,128]{1,0:T(8,128)(2,1)S(1)}, bf16[1024,128]{1,0:T(8,128)(2,1)S(1)}, u32[]{:S(2)}, u32[]{:S(2)}) collective-permute-start(bf16[1024,128]{1,0:T(8,128)(2,1)S(1)} %get-tuple-element.62), channel_id=1, source_target_pairs={{0,1},{1,0},{2,3},{3,2},{4,5},{5,4},{6,7},{7,6},{8,9},{9,8},{10,11... | collective-permute-start | bytes 786440 | tf_op jit(solution)/shard_map/ppermute | solution.py:324
  76.8 6.9 %collective-permute-start.32 = (bf16[256,128]{1,0:T(8,128)(2,1)S(1)}, bf16[256,128]{1,0:T(8,128)(2,1)S(1)}, u32[]{:S(2)}, u32[]{:S(2)}) collective-permute-start(bf16[256,128]{1,0:T(8,128)(2,1)S(1)} %get-tuple-element.66), channel_id=1, source_target_pairs={{0,6},{1,7},{2,4},{3,5},{4,2},{5,3},{6,0},{7,1},{8,14},{9,15},{10,... | collective-permute-start | bytes 196616 | tf_op jit(solution)/shard_map/ppermute | solution.py:328
  78.2 8.8 %collective-permute-start.31 = (bf16[256,128]{1,0:T(8,128)(2,1)S(1)}, bf16[256,128]{1,0:T(8,128)(2,1)S(1)}, u32[]{:S(2)}, u32[]{:S(2)}) collective-permute-start(bf16[256,128]{1,0:T(8,128)(2,1)S(1)} %get-tuple-element.65), channel_id=1, source_target_pairs={{0,4},{1,5},{2,6},{3,7},{4,0},{5,1},{6,2},{7,3},{8,12},{9,13},{10,... | collective-permute-start | bytes 196616 | tf_op jit(solution)/shard_map/ppermute | solution.py:328
  80.3 6.7 %collective-permute-start.30 = (bf16[256,128]{1,0:T(8,128)(2,1)S(1)}, bf16[256,128]{1,0:T(8,128)(2,1)S(1)}, u32[]{:S(2)}, u32[]{:S(2)}) collective-permute-start(bf16[256,128]{1,0:T(8,128)(2,1)S(1)} %get-tuple-element.64), channel_id=1, source_target_pairs={{0,2},{1,3},{2,0},{3,1},{4,6},{5,7},{6,4},{7,5},{8,10},{9,11},{10,... | collective-permute-start | bytes 196616 | tf_op jit(solution)/shard_map/ppermute | solution.py:328
